TPU v7x, 32 devices: a whole 2x2x4 slice. The times are simulated.
32 devices in a mesh: blk: 8 (over z, x), grp: 4 (over y, core).
Axes of the slice: x: 2, y: 2, z: 4, core: 2. Of those that a mesh axis runs over, the one named last changes fastest.
Arguments:
- amplitudes: bfloat16 [1920, 1920], P('blk'), may hold values from -6 to 6
- hole_panel: bfloat16 [1920, 8, 1920], P(None, 'blk', 'grp'), may hold values from -0.375 to 0.375
- virt_fock: bfloat16 [1920, 1920], replicated, may hold values from -0.125 to 0.125
- irrep_sizes: int32 [8], replicated, may hold values from 1 to 480, 1920 in all
- pair_irreps: int32 [8], P('blk'), may hold values from 0 to 7
Outputs:
- dressed: bfloat16 [1920, 8, 1920], P('grp', 'blk')
Inputs may be any that keep to these rules, and one draw needn't show every extreme that they name: `irrep_sizes`: the 8 entries sum to 1920.
All inputs are finite; a program needn't handle non-finite values.
Results may differ from a plain program's by a relative error of at most 0.0049.
Values may be sent and summed in bfloat16 or wider, within the bound.
No kernel may reach another device: no remote copies, remote signals or barrier semaphores. Data moves between devices by JAX's collectives and lax.ppermute only.
A program may use at most 128 MiB of HBM per device.

v0:
```python
import jax
import jax.numpy as jnp
from jax import lax
from jax.sharding import PartitionSpec as P


def irrep_of(positions, block_sizes):
    bounds = jnp.cumsum(block_sizes)[:-1]
    return jnp.sum((positions[:, None] >= bounds[None, :]).astype(jnp.int32), axis=1)


def local(amplitudes, hole_panel, virt_fock, irrep_sizes, pair_irreps):
    virtuals = amplitudes.shape[1]
    occ_local = hole_panel.shape[1]
    quarter = hole_panel.shape[2]
    col_start = lax.axis_index("grp") * quarter
    rows_irrep = irrep_of(jnp.arange(virtuals, dtype=jnp.int32), irrep_sizes)
    cols_irrep = irrep_of(col_start + jnp.arange(quarter, dtype=jnp.int32), irrep_sizes)
    allowed = (
        jnp.bitwise_xor(rows_irrep[:, None, None], cols_irrep[None, None, :])
        == pair_irreps[None, :, None]
    )
    masked = jnp.where(allowed, hole_panel, jnp.zeros((), jnp.bfloat16))
    flattened = masked.reshape(virtuals, occ_local * quarter)
    coupled = jnp.dot(
        lax.all_gather(amplitudes, "blk", axis=0, tiled=True),
        flattened,
        preferred_element_type=jnp.float32,
    ).astype(jnp.bfloat16)
    coupled = coupled.reshape(virtuals, occ_local, quarter)
    fock_rows = lax.dynamic_slice_in_dim(virt_fock, col_start, quarter, 0)
    summed = lax.psum_scatter(
        jnp.einsum("ajb,be->aje", coupled, fock_rows, preferred_element_type=jnp.float32),
        "grp",
        scatter_dimension=0,
        tiled=True,
    )
    return summed.astype(jnp.bfloat16)


def solution(mesh):
    in_specs = (P("blk", None), P(None, "blk", "grp"), P(), P(), P("blk"))
    out_specs = P("grp", "blk", None)
    return jax.shard_map(local, mesh=mesh, in_specs=in_specs, out_specs=out_specs, check_vma=False)
```

profile of v0, /device:TPU:4, one launch (start us, length us, event | category | flops | bytes accessed | tf_op | source)
XLA Modules:
  0.0 259.1 jit_solution(8742748554231771793)
XLA Ops:
  6.5 0.0 all-gather.2.cloned.1.call-start
  6.5 0.7 all-gather.2.cloned.1.call-update
  7.3 0.0 reduce-scatter.2.cloned.1.call-start
  8.0 0.8 reduce-window.4
  8.8 0.1 convert_reduce_fusion
  8.9 0.1 convert_reduce_fusion.1
  9.0 114.2 %all-gather.2.cloned.1.call-done = bf16[1920,1920]{1,0:T(8,128)(2,1)} async-done(((bf16[240,1920]{1,0:T(8,128)(2,1)}), bf16[1920,1920]{1,0:T(8,128)(2,1)}) %all-gather.2.cloned.1.call-update) | async-done | bytes 7372816 | tf_op jit(solution)/shard_map/all_gather | solution.py:26
  123.2 15.0 %convolution_bitcast_fusion = f32[1920,1,1920]{2,0,1:T(8,128)} fusion(bf16[1920,1920]{1,0:T(8,128)(2,1)} %param.7, s32[]{:T(128)S(6)} %select_n.8, bf16[1920,1920]{1,0:T(8,128)(2,1)} %all-gather.2.cloned.1.call-done, bf16[1920,1,480]{0,2,1:T(8,128)(2,1)} %param.6, s32[]{:T(128)} %bitcast.12, s32[480]{0:T(512)S(1)} %convert_reduce_fusion.1, ...), kind=kOutput, calls=%fused_computation | convolution fusion | flops 7081574400 | bytes 25814916 | tf_op jit(solution)/shard_map/ajb,be->aje/dot_general | solution.py:33
  138.2 0.0 reduce-scatter.2.cloned.1.call-update
  138.2 110.6 %reduce-scatter.2.cloned.1.call-done = f32[480,1,1920]{2,0,1:T(8,128)} async-done(((f32[1920,1,1920]{2,0,1:T(8,128)}), f32[480,1,1920]{2,0,1:T(8,128)}) %reduce-scatter.2.cloned.1.call-update) | async-done | bytes 3686416 | tf_op jit(solution)/shard_map/reduce_scatter | solution.py:32
  248.8 3.5 %convert_element_type.16 = bf16[480,1,1920]{2,0,1:T(8,128)(2,1)} convert(f32[480,1,1920]{2,0,1:T(8,128)} %reduce-scatter.2.cloned.1.call-done) | non-fusion elementwise | flops 921600 | bytes 5529600 | tf_op jit(solution)/shard_map/convert_element_type | solution.py:38
  (2 shorter events, 0.0 us)
Async XLA Ops:
  6.5 116.6 %all-gather.2.cloned.1.call-start = ((), (), s32[]{:S(2)}) async-start(), calls=%async_computation.1 | async-start | bytes 8294400 | tf_op jit(solution)/shard_map/all_gather | solution.py:26
  7.3 241.5 %reduce-scatter.2.cloned.1.call-start = ((), (), s32[]{:S(2)}) async-start(), calls=%async_computation.2 | async-start | bytes 18432000 | tf_op jit(solution)/shard_map/reduce_scatter | solution.py:32
Sparse Core Ops, SparseCore 0:
  9.5 113.5 all-gather.1
  138.3 110.4 reduce-scatter.1
where the time goes:
time: 262 us; the launch traced here: 259 us
  waiting for transfers between devices  226 us (86%)
  matrix products  15 us (6%)
  between operations  14.1 us (5%)
  other arithmetic  4.48 us (2%)
    all_gather x1, waiting for transfers between devices, local(): lax.all_gather(amplitudes, 'blk', axis=0, tiled=True)  114 us
    reduce_scatter x1, waiting for transfers between devices, local(): lax.psum_scatter(jnp.einsum('ajb,be->aje', coupled, fock_rows, preferred_...  111 us
    dot_general x1, matrix products, local(): jnp.einsum('ajb,be->aje', coupled, fock_rows, preferred_element_type=jnp....  15 us
  transfers between devices with their start and end apart: 2, of which 2 were waited for; matrix products, arithmetic and copies ran while one was open for 0% of the time, Pallas kernels for 0%

commit v1 on v0

v1 whole, which is shorter than its diff:
```python
import jax
import jax.numpy as jnp
from jax import lax
from jax.sharding import PartitionSpec as P

LANES = 128


def irrep_of(positions, block_sizes):
    bounds = jnp.cumsum(block_sizes)[:-1]
    return jnp.sum((positions[:, None] >= bounds[None, :]).astype(jnp.int32), axis=1)


def swapped_bits(position, count):
    half = count // 2
    return (position % 2) * half + position // 2 if count % 2 == 0 else position


def make_local(blocks, groups):
    members = blocks // groups

    def device(hi, lo, grp):
        return (hi * members + lo) * groups + grp

    first = [
        (device(grp, lo, swapped_bits(hi, groups)), device(hi, lo, grp))
        for hi in range(groups)
        for lo in range(members)
        for grp in range(groups)
    ]

    def shifted(by):
        return [
            (device(hi, (lo + by) % members, grp), device(hi, lo, grp))
            for hi in range(groups)
            for lo in range(members)
            for grp in range(groups)
        ]

    def local(amplitudes, hole_panel, virt_fock, irrep_sizes, pair_irreps):
        rows, virtuals = amplitudes.shape
        quarter = hole_panel.shape[2]
        fold = -(-(virtuals // 4) // LANES) * LANES
        copies = -(-virtuals // fold)
        axes = ("blk", "grp")
        group = lax.axis_index("grp")
        member = lax.axis_index("blk") % members

        pieces = 2
        step = rows // pieces
        held = [
            lax.ppermute(amplitudes[k * step:(k + 1) * step], axes, first) for k in range(pieces)
        ]
        arrived = [held]
        for by in range(1, members):
            arrived.append([lax.ppermute(piece, axes, shifted(by)) for piece in held])

        labels = irrep_of(jnp.arange(virtuals, dtype=jnp.int32), irrep_sizes)
        wanted = jnp.bitwise_xor(labels, pair_irreps[0])
        own_wanted = lax.dynamic_slice_in_dim(wanted, group * quarter, quarter, 0)
        panel = jnp.swapaxes(hole_panel[:, 0, :], 0, 1)
        masked = jnp.where(own_wanted[:, None] == labels[None, :], panel, jnp.zeros((), panel.dtype))
        padded = jnp.pad(masked, ((0, 0), (0, copies * fold - virtuals)))
        folded = sum(padded[:, k * fold:(k + 1) * fold] for k in range(copies))

        grid = lambda step_of: [(p * groups + step_of(g), p * groups + g) for p in range(blocks) for g in range(groups)]
        if groups == 4:
            across = lax.ppermute(folded, axes, grid(lambda g: g ^ 2))
            beside = lax.ppermute(folded, axes, grid(lambda g: g ^ 1))
            both = lax.ppermute(across, axes, grid(lambda g: g ^ 1))
            stack = jnp.stack([folded, beside, across, both])
            full = jnp.concatenate([stack[group ^ k] for k in range(groups)])
        else:
            full = lax.all_gather(folded, "grp", axis=0, tiled=True)
        spread = jnp.concatenate([full] * copies, axis=1)[:, :virtuals]
        dense = jnp.where(wanted[:, None] == labels[None, :], spread, jnp.zeros((), full.dtype))

        parts = []
        for pieces_in in arrived:
            mine = jnp.concatenate(pieces_in)
            coupled = lax.dot_general(
                mine, dense, (((1,), (1,)), ((), ())), preferred_element_type=jnp.float32
            ).astype(jnp.bfloat16)
            parts.append(
                jnp.dot(coupled, virt_fock, preferred_element_type=jnp.float32).astype(jnp.bfloat16)
            )
        result = jnp.zeros((members * rows, virtuals), jnp.bfloat16)
        for by, part in enumerate(parts):
            place = (member + by) % members * rows
            result = lax.dynamic_update_slice_in_dim(result, part, place, 0)
        return result[:, None, :]

    return local


def solution(mesh):
    in_specs = (P("blk", None), P(None, "blk", "grp"), P(), P(), P("blk"))
    out_specs = P("grp", "blk", None)
    local = make_local(mesh.shape["blk"], mesh.shape["grp"])
    return jax.shard_map(local, mesh=mesh, in_specs=in_specs, out_specs=out_specs, check_vma=False)
```

time: 262 us -> 193 us (0.74)
  the two profiles are of different devices: /device:TPU:4 before, /device:TPU:1 now
where the time goes in v1:
time: 193 us
  other arithmetic  118 us (61%)
  waiting for transfers between devices  35.6 us (18%)
  matrix products  20.4 us (11%)
  starting transfers between devices  14.6 us (8%)
  local copies, waits for them, and re-layouts  2.6 us (1%)
    select_n x1, other arithmetic, local(): jnp.where(wanted[:, None] == labels[None, :], spread, jnp.zeros((), full....  113 us
    ppermute x2, waiting for transfers between devices, local(): lax.ppermute(amplitudes[k * step:(k + 1) * step], axes, first)  25.4 us
    dot_general x2, matrix products, local(): jnp.dot(coupled, virt_fock, preferred_element_type=jnp.float32)  20.4 us
    ppermute x1, waiting for transfers between devices, local(): across = lax.ppermute(folded, axes, grid(lambda g: g ^ 2))  10.2 us
    ppermute x2, starting transfers between devices, local(): lax.ppermute(amplitudes[k * step:(k + 1) * step], axes, first)  7.52 us
  transfers between devices with their start and end apart: 7, of which 3 were waited for; matrix products, arithmetic and copies ran while one was open for 65% of the time, Pallas kernels for 0%

profile of v1, /device:TPU:1, one launch (start us, length us, event | category | flops | bytes accessed | tf_op | source)
XLA Modules:
  0.0 192.5 jit_solution(5162938782795199932)
XLA Ops:
  0.0 0.0 copy-start.1
  0.0 0.9 reduce-window.4
  0.9 0.1 convert_reduce_fusion
  1.7 0.1 dynamic_slice.15
  1.8 2.1 %compare_select_fusion.1 = bf16[480,1920]{1,0:T(8,128)(2,1)S(1)} fusion(bf16[1920,1,480]{0,2,1:T(8,128)(2,1)} %param.6, s32[1920]{0:T(1024)S(1)} %convert_reduce_fusion, s32[480]{0:T(512)S(1)} %dynamic_slice.15), kind=kLoop, calls=%fused_computation.16 | loop fusion | flops 1843200 | bytes 3696000 | tf_op jit(solution)/shard_map/jit(_where)/select_n | solution.py:62
  3.8 1.0 fusion.17
  4.8 2.1 %collective-permute-start.3 = (bf16[480,512]{1,0:T(8,128)(2,1)}, bf16[480,512]{1,0:T(8,128)(2,1)S(1)}, u32[]{:S(2)}, u32[]{:S(2)}) collective-permute-start(bf16[480,512]{1,0:T(8,128)(2,1)} %fusion.17), channel_id=1, source_target_pairs={{2,0},{3,1},{0,2},{1,3},{6,4},{7,5},{4,6},{5,7},{10,8},{11,9},{8,1... | collective-permute-start | bytes 1474568 | tf_op jit(solution)/shard_map/ppermute | solution.py:68
  6.9 1.0 collective-permute-start.2
  7.9 10.2 %collective-permute-done.3 = bf16[480,512]{1,0:T(8,128)(2,1)S(1)} collective-permute-done((bf16[480,512]{1,0:T(8,128)(2,1)}, bf16[480,512]{1,0:T(8,128)(2,1)S(1)}, u32[]{:S(2)}, u32[]{:S(2)}) %collective-permute-start.3) | collective-permute-done | bytes 491552 | tf_op jit(solution)/shard_map/ppermute | solution.py:68
  18.1 1.2 collective-permute-start.4
  19.3 0.0 copy-done.1
  19.3 1.0 fusion.22
  20.3 4.3 %collective-permute-start = (bf16[120,1920]{1,0:T(8,128)(2,1)}, bf16[120,1920]{1,0:T(8,128)(2,1)S(1)}, u32[]{:S(2)}, u32[]{:S(2)}) collective-permute-start(bf16[120,1920]{1,0:T(8,128)(2,1)} %get-tuple-element.9), channel_id=1, source_target_pairs={{0,0},{8,1},{16,2},{24,3},{4,4},{12,5},{20,6},{28,7},{2,8},{10,9},... | collective-permute-start | bytes 1382408 | tf_op jit(solution)/shard_map/ppermute | solution.py:52
  24.7 3.2 %collective-permute-start.1 = (bf16[120,1920]{1,0:T(8,128)(2,1)}, bf16[120,1920]{1,0:T(8,128)(2,1)S(1)}, u32[]{:S(2)}, u32[]{:S(2)}) collective-permute-start(bf16[120,1920]{1,0:T(8,128)(2,1)} %get-tuple-element.10), channel_id=1, source_target_pairs={{0,0},{8,1},{16,2},{24,3},{4,4},{12,5},{20,6},{28,7},{2,8},{10,9},... | collective-permute-start | bytes 1382408 | tf_op jit(solution)/shard_map/ppermute | solution.py:52
  27.9 0.2 fusion.27
  28.2 21.9 %collective-permute-done = bf16[120,1920]{1,0:T(8,128)(2,1)S(1)} collective-permute-done((bf16[120,1920]{1,0:T(8,128)(2,1)}, bf16[120,1920]{1,0:T(8,128)(2,1)S(1)}, u32[]{:S(2)}, u32[]{:S(2)}) %collective-permute-start) | collective-permute-done | bytes 460832 | tf_op jit(solution)/shard_map/ppermute | solution.py:52
  50.1 1.4 collective-permute-start.5
  51.5 3.5 %collective-permute-done.1 = bf16[120,1920]{1,0:T(8,128)(2,1)S(1)} collective-permute-done((bf16[120,1920]{1,0:T(8,128)(2,1)}, bf16[120,1920]{1,0:T(8,128)(2,1)S(1)}, u32[]{:S(2)}, u32[]{:S(2)}) %collective-permute-start.1) | collective-permute-done | bytes 460832 | tf_op jit(solution)/shard_map/ppermute | solution.py:52
  55.0 1.4 collective-permute-start.6
  56.5 0.0 collective-permute-done.2
  56.5 0.0 collective-permute-done.4
  56.5 1.4 pad_maximum_fusion.12
  57.9 0.1 dynamic-slice_bitcast_fusion.3
  58.1 112.7 %compare_select_fusion = bf16[1920,1920]{1,0:T(8,128)(2,1)} fusion(bf16[480,512]{1,0:T(8,128)(2,1)S(1)} %get-tuple-element.6, bf16[480,512]{1,0:T(8,128)(2,1)S(1)} %get-tuple-element.7, bf16[480,512]{1,0:T(8,128)(2,1)S(1)} %get-tuple-element.8, bf16[480,512]{1,0:T(8,128)(2,1)S(1)} %get-tuple-element.5, s32[1920]{0:T(1024)S(1)} %convert_reduce_fusion, ...), kind=kLoop, calls=%fused_computation | loop fusion | flops 125337600 | bytes 9354240 | tf_op jit(solution)/shard_map/jit(_where)/select_n | solution.py:76
  170.8 0.1 broadcast_in_dim.22
  170.9 9.6 %fusion.4 = bf16[480,1,1920]{2,0,1:T(8,128)(2,1)S(1)} fusion(bf16[480,1,1920]{2,0,1:T(8,128)(2,1)S(1)} %broadcast_in_dim.22, s32[]{:T(128)S(6)} %select_n.53, bf16[1920,1920]{1,0:T(8,128)(2,1)} %param.7, bf16[1920,1920]{1,0:T(8,128)(2,1)} %compare_select_fusion, bf16[120,1920]{1,0:T(8,128)(2,1)S(1)} %collective-permute-done.1, ...), kind=kOutput, calls=%fused_computation.22 | convolution fusion | flops 3541708800 | bytes 16588804 | tf_op jit(solution)/shard_map/dot_general | solution.py:85
  180.5 0.0 copy-start
  180.5 0.0 collective-permute-done.5
  180.5 0.0 collective-permute-done.6
  180.6 1.2 copy-done
  181.8 10.8 %fusion.6 = bf16[480,1,1920]{2,0,1:T(8,128)(2,1)} fusion(bf16[480,1,1920]{2,0,1:T(8,128)(2,1)} %copy-done, s32[]{:T(128)S(6)} %select_n.55, bf16[1920,1920]{1,0:T(8,128)(2,1)} %param.7, bf16[1920,1920]{1,0:T(8,128)(2,1)} %compare_select_fusion, bf16[120,1920]{1,0:T(8,128)(2,1)} %collective-permute-done.6, bf16[120,1920]{1,0:T(8,128)(2,1)} %collective-permute-done.5), kind=kOutput, calls=%fused_computation.24 | convolution fusion | flops 3541708800 | bytes 16588804 | tf_op jit(solution)/shard_map/dot_general | solution.py:85
  (2 shorter events, 0.0 us)
Async XLA Ops:
  0.0 19.3 %copy-start.1 = (bf16[240,1920]{1,0:T(8,128)(2,1)S(1)}, bf16[240,1920]{1,0:T(8,128)(2,1)}, u32[]{:S(2)}) copy-start(bf16[240,1920]{1,0:T(8,128)(2,1)} %param.5) | copy-start | bytes 2764804
  4.8 13.2 %collective-permute-start.3 = (bf16[480,512]{1,0:T(8,128)(2,1)}, bf16[480,512]{1,0:T(8,128)(2,1)S(1)}, u32[]{:S(2)}, u32[]{:S(2)}) collective-permute-start(bf16[480,512]{1,0:T(8,128)(2,1)} %fusion.17), channel_id=1, source_target_pairs={{2,0},{3,1},{0,2},{1,3},{6,4},{7,5},{4,6},{5,7},{10,8},{11,9},{8,1... | collective-permute-start | bytes 1474568 | tf_op jit(solution)/shard_map/ppermute | solution.py:68
  6.9 49.6 %collective-permute-start.2 = (bf16[480,512]{1,0:T(8,128)(2,1)}, bf16[480,512]{1,0:T(8,128)(2,1)}, u32[]{:S(2)}, u32[]{:S(2)}) collective-permute-start(bf16[480,512]{1,0:T(8,128)(2,1)} %fusion.17), channel_id=1, source_target_pairs={{1,0},{0,1},{3,2},{2,3},{5,4},{4,5},{7,6},{6,7},{9,8},{8,9},{11,10... | collective-permute-start | bytes 1474568 | tf_op jit(solution)/shard_map/ppermute | solution.py:69
  18.1 38.4 %collective-permute-start.4 = (bf16[480,512]{1,0:T(8,128)(2,1)S(1)}, bf16[480,512]{1,0:T(8,128)(2,1)}, u32[]{:S(2)}, u32[]{:S(2)}) collective-permute-start(bf16[480,512]{1,0:T(8,128)(2,1)S(1)} %collective-permute-done.3), channel_id=1, source_target_pairs={{1,0},{0,1},{3,2},{2,3},{5,4},{4,5},{7,6},{6,7},{9,8},{8,9},{11,10... | collective-permute-start | bytes 1474568 | tf_op jit(solution)/shard_map/ppermute | solution.py:70
  20.3 29.8 %collective-permute-start = (bf16[120,1920]{1,0:T(8,128)(2,1)}, bf16[120,1920]{1,0:T(8,128)(2,1)S(1)}, u32[]{:S(2)}, u32[]{:S(2)}) collective-permute-start(bf16[120,1920]{1,0:T(8,128)(2,1)} %get-tuple-element.9), channel_id=1, source_target_pairs={{0,0},{8,1},{16,2},{24,3},{4,4},{12,5},{20,6},{28,7},{2,8},{10,9},... | collective-permute-start | bytes 1382408 | tf_op jit(solution)/shard_map/ppermute | solution.py:52
  24.7 30.4 %collective-permute-start.1 = (bf16[120,1920]{1,0:T(8,128)(2,1)}, bf16[120,1920]{1,0:T(8,128)(2,1)S(1)}, u32[]{:S(2)}, u32[]{:S(2)}) collective-permute-start(bf16[120,1920]{1,0:T(8,128)(2,1)} %get-tuple-element.10), channel_id=1, source_target_pairs={{0,0},{8,1},{16,2},{24,3},{4,4},{12,5},{20,6},{28,7},{2,8},{10,9},... | collective-permute-start | bytes 1382408 | tf_op jit(solution)/shard_map/ppermute | solution.py:52
  50.1 130.4 %collective-permute-start.5 = (bf16[120,1920]{1,0:T(8,128)(2,1)S(1)}, bf16[120,1920]{1,0:T(8,128)(2,1)}, u32[]{:S(2)}, u32[]{:S(2)}) collective-permute-start(bf16[120,1920]{1,0:T(8,128)(2,1)S(1)} %collective-permute-done), channel_id=1, source_target_pairs={{4,0},{5,1},{6,2},{7,3},{0,4},{1,5},{2,6},{3,7},{12,8},{13,9},{14,... | collective-permute-start | bytes 1382408 | tf_op jit(solution)/shard_map/ppermute | solution.py:56
  55.0 125.5 %collective-permute-start.6 = (bf16[120,1920]{1,0:T(8,128)(2,1)S(1)}, bf16[120,1920]{1,0:T(8,128)(2,1)}, u32[]{:S(2)}, u32[]{:S(2)}) collective-permute-start(bf16[120,1920]{1,0:T(8,128)(2,1)S(1)} %collective-permute-done.1), channel_id=1, source_target_pairs={{4,0},{5,1},{6,2},{7,3},{0,4},{1,5},{2,6},{3,7},{12,8},{13,9},{14,... | collective-permute-start | bytes 1382408 | tf_op jit(solution)/shard_map/ppermute | solution.py:56
  180.5 1.2 copy-start

commit v2 on v0

v2 whole, which is shorter than its diff:
```python
import functools

import jax
import jax.numpy as jnp
from jax import lax
from jax.experimental import pallas as pl
from jax.experimental.pallas import tpu as pltpu
from jax.sharding import PartitionSpec as P

LANES = 128
SUBLANES = 16
MIB = 1 << 20


def rounded(value, unit):
    return -(-value // unit) * unit


def fill_bounds(sizes, bounds):
    total = jnp.int32(0)
    for r in range(sizes.shape[0]):
        bounds[r] = total
        total = total + sizes[r]
    bounds[sizes.shape[0]] = total


def wanted_range(b, pair, bounds, irreps):
    low, high = jnp.zeros_like(b), jnp.zeros_like(b)
    for r in range(irreps):
        partner = jnp.bitwise_xor(pair[0], r)
        inside = (b >= bounds[r]) & (b < bounds[r + 1])
        low = jnp.where(inside, bounds[partner], low)
        high = jnp.where(inside, bounds[partner + 1], high)
    return low, high


def fold_kernel(sizes, pair, panel, folded, bounds):
    quarter, virtuals = panel.shape
    fold = folded.shape[1]
    fill_bounds(sizes, bounds)
    start = lax.axis_index("grp") * quarter
    step = 32 if quarter % 32 == 0 else SUBLANES

    @pl.loop(0, quarter // step)
    def _(i):
        first = pl.multiple_of(i * step, step)
        here = pl.ds(first, step)
        b = start + first + lax.broadcasted_iota(jnp.int32, (step, LANES), 0)
        low, high = wanted_range(b, pair, bounds, sizes.shape[0])
        lane = lax.broadcasted_iota(jnp.int32, (step, LANES), 1)
        low, high = low - lane, high - lane
        for place in range(0, fold, LANES):
            total = jnp.zeros((step, LANES), jnp.float32)
            for c in range(place, virtuals, fold):
                value = panel[here, c:c + LANES].astype(jnp.float32)
                total = jnp.where((low <= c) & (high > c), value, total)
            folded[here, place:place + LANES] = total.astype(folded.dtype)


def fold_panel(panel, sizes, pair, fold):
    quarter, virtuals = panel.shape
    return pl.pallas_call(
        fold_kernel,
        out_shape=jax.ShapeDtypeStruct((quarter, fold), panel.dtype),
        in_specs=[
            pl.BlockSpec(memory_space=pltpu.SMEM),
            pl.BlockSpec(memory_space=pltpu.SMEM),
            pl.BlockSpec(memory_space=pltpu.VMEM),
        ],
        out_specs=pl.BlockSpec(memory_space=pltpu.VMEM),
        scratch_shapes=[pltpu.SMEM((sizes.shape[0] + 1,), jnp.int32)],
        compiler_params=pltpu.CompilerParams(vmem_limit_bytes=8 * MIB),
        cost_estimate=pl.CostEstimate(
            flops=0, bytes_accessed=2 * quarter * (virtuals + fold), transcendentals=0
        ),
        name="fold_panel",
    )(sizes, pair, panel)


def spread_kernel(slots, sizes, pair, fock, *refs):
    count = len(slots)
    folded, (dense, fock_out, bounds, turned, sems) = refs[:count], refs[count:]
    quarter, fold = folded[0].shape
    virtuals = dense.shape[1]
    width = dense.shape[2]
    group = lax.axis_index("grp")
    copies = []
    for k, slot in enumerate(slots):
        first = pl.multiple_of(jnp.bitwise_xor(group, slot) * quarter, SUBLANES)
        copies.append(pltpu.make_async_copy(
            fock.at[pl.ds(first, quarter)], fock_out.at[k, pl.ds(0, quarter)], sems.at[k]
        ))
        copies[-1].start()
    fill_bounds(sizes, bounds)
    step = 32
    for k, slot in enumerate(slots):
        if width > quarter:
            fock_out[k, quarter:width, :] = jnp.zeros((width - quarter, virtuals), fock_out.dtype)
        values = folded[k][...].astype(jnp.float32)
        if width > quarter:
            values = jnp.concatenate([values, jnp.zeros((width - quarter, fold), jnp.float32)])
        turned[...] = values.T
        start = jnp.bitwise_xor(group, slot) * quarter
        b = start + lax.broadcasted_iota(jnp.int32, (8, width), 1)
        low, high = wanted_range(b, pair, bounds, sizes.shape[0])
        low = jnp.concatenate([low] * (step // 8))
        high = jnp.concatenate([high] * (step // 8))

        @pl.loop(0, virtuals // step)
        def _(i):
            first = pl.multiple_of(i * step, step)
            source = pl.multiple_of(lax.rem(first, fold), step)
            c = first + lax.broadcasted_iota(jnp.int32, (step, width), 0)
            kept = jnp.where((c >= low) & (c < high), turned[pl.ds(source, step), :], 0.0)
            dense[k, pl.ds(first, step), :] = kept.astype(dense.dtype)

    for copy in copies:
        copy.wait()


def spread(slots, folded, fock, sizes, pair):
    quarter, fold = folded[0].shape
    virtuals = fock.shape[0]
    width = rounded(quarter, LANES)
    count = len(slots)
    smem = pl.BlockSpec(memory_space=pltpu.SMEM)
    vmem = pl.BlockSpec(memory_space=pltpu.VMEM)
    return pl.pallas_call(
        functools.partial(spread_kernel, slots),
        out_shape=(
            pltpu.VMEM((count, virtuals, width), fock.dtype),
            pltpu.VMEM((count, width, virtuals), fock.dtype),
        ),
        in_specs=[smem, smem, pl.BlockSpec(memory_space=pl.ANY)] + [vmem] * count,
        out_specs=(vmem, vmem),
        scratch_shapes=[
            pltpu.SMEM((sizes.shape[0] + 1,), jnp.int32),
            pltpu.VMEM((fold, width), jnp.float32),
            pltpu.SemaphoreType.DMA((count,)),
        ],
        compiler_params=pltpu.CompilerParams(vmem_limit_bytes=16 * MIB),
        cost_estimate=pl.CostEstimate(
            flops=0, bytes_accessed=6 * count * quarter * virtuals, transcendentals=0
        ),
        name="spread_panel",
    )(sizes, pair, fock, *folded)


def column_tiles(total, tile):
    return [(first, min(tile, total - first)) for first in range(0, total, tile)]


def dress_kernel(by, offset, rows, members, sets, has_base, *refs):
    amplitudes, refs = refs[0], refs[1:]
    dense, focks, refs = refs[:sets], refs[sets:2 * sets], refs[2 * sets:]
    if has_base:
        refs = refs[1:]
    result, coupled, dressed, sems = refs
    height = amplitudes.shape[0]
    virtuals = amplitudes.shape[1]
    width = dense[0].shape[2]
    slots = [(part, k) for part in range(sets) for k in range(dense[part].shape[0])]
    member = lax.rem(lax.axis_index("blk") + by, members)
    place = pl.multiple_of(member * rows + offset, SUBLANES)
    for s, (part, k) in enumerate(slots):
        for first, tile in column_tiles(width, 256):
            coupled[:, s * width + first:s * width + first + tile] = jnp.dot(
                amplitudes[...], dense[part][k, :, first:first + tile],
                preferred_element_type=jnp.float32,
            ).astype(coupled.dtype)
    copies = []
    for t, (first, tile) in enumerate(column_tiles(virtuals, 512)):
        total = jnp.zeros((height, tile), jnp.float32)
        for s, (part, k) in enumerate(slots):
            total = total + jnp.dot(
                coupled[:, s * width:(s + 1) * width], focks[part][k, :, first:first + tile],
                preferred_element_type=jnp.float32,
            )
        dressed[:, first:first + tile] = total.astype(dressed.dtype)
        copies.append(pltpu.make_async_copy(
            dressed.at[:, pl.ds(first, tile)],
            result.at[pl.ds(place, height), pl.ds(first, tile)],
            sems.at[t],
        ))
        copies[-1].start()
    for copy in copies:
        copy.wait()


def dress(amplitudes, dense, focks, base, by, offset, rows, members, out_rows):
    height, virtuals = amplitudes.shape
    width = dense[0].shape[2]
    slots = sum(d.shape[0] for d in dense)
    vmem = pl.BlockSpec(memory_space=pltpu.VMEM)
    anywhere = pl.BlockSpec(memory_space=pl.ANY)
    pinned = [pltpu.with_memory_space_constraint(x, pltpu.VMEM) for x in (*dense, *focks)]
    bases = [] if base is None else [base]
    return pl.pallas_call(
        functools.partial(dress_kernel, by, offset, rows, members, len(dense), base is not None),
        out_shape=jax.ShapeDtypeStruct((out_rows, virtuals), amplitudes.dtype),
        in_specs=[vmem] * (1 + len(pinned)) + [anywhere] * len(bases),
        out_specs=anywhere,
        input_output_aliases={} if base is None else {1 + len(pinned): 0},
        scratch_shapes=[
            pltpu.VMEM((height, slots * width), amplitudes.dtype),
            pltpu.VMEM((height, virtuals), amplitudes.dtype),
            pltpu.SemaphoreType.DMA((len(column_tiles(virtuals, 512)),)),
        ],
        compiler_params=pltpu.CompilerParams(vmem_limit_bytes=16 * MIB),
        cost_estimate=pl.CostEstimate(
            flops=4 * height * virtuals * virtuals,
            bytes_accessed=4 * height * virtuals,
            transcendentals=0,
        ),
        name="dress_rows",
    )(amplitudes, *pinned, *bases)


def make_local(blocks, groups):
    members = blocks // groups
    axes = ("blk", "grp")

    def device(hi, lo, grp):
        return (hi * members + lo) * groups + grp

    everyone = [(h, l, g) for h in range(groups) for l in range(members) for g in range(groups)]

    def source_copy(hi, grp):
        if groups != 4:
            return hi
        order = {0: (0, 2, 1, 3), 1: (3, 1, 2, 0), 2: (0, 3, 2, 1), 3: (2, 0, 1, 3)}
        return order[grp][hi]

    to_group = [(device(g, l, source_copy(h, g)), device(h, l, g)) for h, l, g in everyone]

    def to_member(by):
        return [(device(h, (l + by) % members, g), device(h, l, g)) for h, l, g in everyone]

    def to_slot(slot):
        return [(device(h, l, g ^ slot), device(h, l, g)) for h, l, g in everyone]

    def local(amplitudes, hole_panel, virt_fock, irrep_sizes, pair_irreps):
        rows, virtuals = amplitudes.shape
        out_rows = rows * members
        fold = rounded(virtuals // 4, LANES)
        panel = jnp.swapaxes(hole_panel[:, 0, :], 0, 1)

        if rows % SUBLANES == 0:
            half = rounded(rows // 2, SUBLANES)
            spans = [(0, half), (half, rows - half)]
        else:
            spans = [(0, rows)]
        held = [
            lax.ppermute(lax.slice_in_dim(amplitudes, first, first + size), axes, to_group)
            for first, size in spans
        ]
        arrived = {(0, k): piece for k, piece in enumerate(held)}
        for k, piece in enumerate(held):
            for by in range(1, members):
                arrived[by, k] = lax.ppermute(piece, axes, to_member(by))

        own = fold_panel(panel, irrep_sizes, pair_irreps, fold)
        across = lax.ppermute(own, axes, to_slot(2))
        beside = lax.ppermute(own, axes, to_slot(1))
        near_dense, near_fock = spread((0, 1), (own, beside), virt_fock, irrep_sizes, pair_irreps)
        both = lax.ppermute(across, axes, to_slot(1))
        far_dense, far_fock = spread((2, 3), (across, both), virt_fock, irrep_sizes, pair_irreps)
        dense, focks = (near_dense, far_dense), (near_fock, far_fock)

        if rows % SUBLANES == 0:
            pieces = [(jnp.concatenate(held), 0, 0)]
            pieces += [
                (arrived[by, k], by, spans[k][0]) for by in range(1, members) for k in range(len(spans))
            ]
            result = None
            for piece, by, offset in pieces:
                result = dress(piece, dense, focks, result, by, offset, rows, members, out_rows)
        else:
            member = lax.axis_index("blk") % members
            stacked = jnp.stack([arrived[by, 0] for by in range(members)])
            ordered = jnp.roll(stacked, member, axis=0).reshape(out_rows, virtuals)
            result = dress(ordered, dense, focks, None, 0, 0, 0, members, out_rows)
        return result[:, None, :]

    return local


def solution(mesh):
    in_specs = (P("blk", None), P(None, "blk", "grp"), P(), P(), P("blk"))
    out_specs = P("grp", "blk", None)
    local = make_local(mesh.shape["blk"], mesh.shape["grp"])
    return jax.shard_map(local, mesh=mesh, in_specs=in_specs, out_specs=out_specs, check_vma=False)
```

time: 262 us -> 60 us (0.23)
  waiting for transfers between devices: 226 us -> 22 us
  Pallas kernels: 0 us -> 18.8 us
  matrix products: 15 us -> 0 us
  between operations: 14.1 us -> 0.78 us
  starting transfers between devices: 0.04 us -> 11.9 us
  local copies, waits for them, and re-layouts: 0.01 us -> 5.32 us
  other arithmetic: 4.48 us -> 0.07 us
    all_gather x1 -> x0, waiting for transfers between devices: 114 us -> none  [local(): lax.all_gather(amplitudes, 'blk', axis=0, tiled=True)]
    reduce_scatter x1 -> x0, waiting for transfers between devices: 111 us -> none  [local(): lax.psum_scatter(jnp.einsum('ajb,be->aje', coupled, fock_rows, preferred_...]
    ppermute x0 -> x7, waiting for transfers between devices: none -> 22 us  [the longest x1 10.2 us: local(): across = lax.ppermute(own, axes, to_slot(2))]
    pallas_call x0 -> x6, Pallas kernels: none -> 18.8 us  [the longest x3 11 us: dress(): pl.pallas_call(functools.partial(dress_kernel, by, offset, rows, members,...]
    dot_general x1 -> x0, matrix products: 15 us -> none  [local(): jnp.einsum('ajb,be->aje', coupled, fock_rows, preferred_element_type=jnp....]
    ppermute x0 -> x7, starting transfers between devices: none -> 11.9 us  [the longest x2 6.84 us: local(): lax.ppermute(lax.slice_in_dim(amplitudes, first, first + size), axes, to_...]
    unnamed x0 -> x12, local copies, waits for them, and re-layouts: none -> 5.25 us
    convert_element_type x1 -> x0, other arithmetic: 3.46 us -> none  [local(): return summed.astype(jnp.bfloat16)]
  transfers between devices with their start and end apart: 2 -> 7, of which waited for: 2 -> 3; matrix products, arithmetic and copies ran while one was open for 0% -> 0% of each run, Pallas kernels for 0% -> 24%
where the time goes in v2:
time: 60 us; the launch traced here: 58.9 us
  waiting for transfers between devices  22 us (37%)
  Pallas kernels  18.8 us (31%)
  starting transfers between devices  11.9 us (20%)
  local copies, waits for them, and re-layouts  5.32 us (9%)
  between operations  0.78 us (1%)
    pallas_call x3, Pallas kernels, dress(): pl.pallas_call(functools.partial(dress_kernel, by, offset, rows, members,...  11 us
    ppermute x1, waiting for transfers between devices, local(): across = lax.ppermute(own, axes, to_slot(2))  10.2 us
    ppermute x2, waiting for transfers between devices, local(): lax.ppermute(lax.slice_in_dim(amplitudes, first, first + size), axes, to_...  6.88 us
    ppermute x2, starting transfers between devices, local(): lax.ppermute(lax.slice_in_dim(amplitudes, first, first + size), axes, to_...  6.84 us
    pallas_call x2, Pallas kernels, spread(): pl.pallas_call(functools.partial(spread_kernel, slots), out_shape=(pltpu....  6.18 us
    unnamed x12, local copies, waits for them, and re-layouts  5.25 us
    ppermute x2, waiting for transfers between devices, local(): arrived[by, k] = lax.ppermute(piece, axes, to_member(by))  4.87 us
    ppermute x2, starting transfers between devices, local(): arrived[by, k] = lax.ppermute(piece, axes, to_member(by))  2.8 us
  transfers between devices with their start and end apart: 7, of which 3 were waited for; matrix products, arithmetic and copies ran while one was open for 0% of the time, Pallas kernels for 24%

profile of v2, /device:TPU:4, one launch (start us, length us, event | category | flops | bytes accessed | tf_op | source)
XLA Modules:
  0.0 58.9 jit_solution(13851155231837666931)
XLA Ops:
  0.7 0.0 copy-start.2
  0.7 1.5 %copy-done.2 = bf16[1920,1,480]{0,2,1:T(8,128)(2,1)S(1)} copy-done((bf16[1920,1,480]{0,2,1:T(8,128)(2,1)S(1)}, bf16[1920,1,480]{0,2,1:T(8,128)(2,1)}, u32[]{:S(2)}) %copy-start.2) | copy-done | bytes 1843224
  2.2 0.7 %copy-done.3 = s32[8]{0:T(128)S(1)} copy-done((s32[8]{0:T(128)S(1)}, s32[8]{0:T(128)}, u32[]{:S(2)}) %copy-start.3) | copy-done | bytes 56
  2.8 0.0 copy-start.5
  2.8 0.0 copy-start.4
  2.8 1.6 %fold_panel.1.refs_0_ = bf16[480,512]{1,0:T(8,128)(2,1)S(1)} custom-call(s32[8]{0:T(128)S(1)} %copy-done.3, s32[1]{0:T(128)S(6)} %copy.10.pair, bf16[480,1920]{1,0:T(8,128)(2,1)S(1)} %bitcast.4), custom_call_target="tpu_custom_call" | custom-call | bytes 2334720 | tf_op jit(solution)/shard_map/fold_panel/pallas_call | solution.py:62
  4.4 0.1 collective-permute-start.3
  4.5 0.0 copy-done.5
  4.6 4.9 %collective-permute-start.5 = (bf16[128,1920]{1,0:T(8,128)(2,1)S(1)}, bf16[128,1920]{1,0:T(8,128)(2,1)S(1)}, u32[]{:S(2)}, u32[]{:S(2)}) collective-permute-start(bf16[128,1920]{1,0:T(8,128)(2,1)S(1)} %slice.7), channel_id=1, source_target_pairs={{0,0},{11,1},{16,2},{26,3},{4,4},{15,5},{20,6},{30,7},{2,8},{9,9},... | collective-permute-start | bytes 1474568 | tf_op jit(solution)/shard_map/ppermute | solution.py:254
  9.5 2.2 %collective-permute-start.2 = (bf16[480,512]{1,0:T(8,128)(2,1)S(1)}, bf16[480,512]{1,0:T(8,128)(2,1)S(1)}, u32[]{:S(2)}, u32[]{:S(2)}) collective-permute-start(bf16[480,512]{1,0:T(8,128)(2,1)S(1)} %fold_panel.1.refs_0_), channel_id=1, source_target_pairs={{1,0},{0,1},{3,2},{2,3},{5,4},{4,5},{7,6},{6,7},{9,8},{8,9},{11,10... | collective-permute-start | bytes 1474568 | tf_op jit(solution)/shard_map/ppermute | solution.py:264
  11.7 1.9 %collective-permute-start = (bf16[112,1920]{1,0:T(8,128)(2,1)S(1)}, bf16[112,1920]{1,0:T(8,128)(2,1)S(1)}, u32[]{:S(2)}, u32[]{:S(2)}) collective-permute-start(bf16[112,1920]{1,0:T(8,128)(2,1)S(1)} %slice.6), channel_id=1, source_target_pairs={{0,0},{11,1},{16,2},{26,3},{4,4},{15,5},{20,6},{30,7},{2,8},{9,9},... | collective-permute-start | bytes 1290248 | tf_op jit(solution)/shard_map/ppermute | solution.py:254
  13.6 10.2 %collective-permute-done.3.refs_0_ = bf16[480,512]{1,0:T(8,128)(2,1)S(1)} collective-permute-done((bf16[480,512]{1,0:T(8,128)(2,1)S(1)}, bf16[480,512]{1,0:T(8,128)(2,1)S(1)}, u32[]{:S(2)}, u32[]{:S(2)}) %collective-permute-start.3) | collective-permute-done | bytes 491552 | tf_op jit(solution)/shard_map/ppermute | solution.py:263
  23.9 0.0 collective-permute-start.4
  23.9 6.9 %collective-permute-done = bf16[112,1920]{1,0:T(8,128)(2,1)S(1)} collective-permute-done((bf16[112,1920]{1,0:T(8,128)(2,1)S(1)}, bf16[112,1920]{1,0:T(8,128)(2,1)S(1)}, u32[]{:S(2)}, u32[]{:S(2)}) %collective-permute-start) | collective-permute-done | bytes 430112 | tf_op jit(solution)/shard_map/ppermute | solution.py:254
  30.8 2.8 %collective-permute-start.1 = (bf16[112,1920]{1,0:T(8,128)(2,1)S(1)}, bf16[112,1920]{1,0:T(8,128)(2,1)S(1)}, u32[]{:S(2)}, u32[]{:S(2)}) collective-permute-start(bf16[112,1920]{1,0:T(8,128)(2,1)S(1)} %collective-permute-done), channel_id=1, source_target_pairs={{4,0},{5,1},{6,2},{7,3},{0,4},{1,5},{2,6},{3,7},{12,8},{13,9},{14,... | collective-permute-start | bytes 1290248 | tf_op jit(solution)/shard_map/ppermute | solution.py:260
  33.5 0.0 collective-permute-done.5
  33.5 0.0 collective-permute-start.6
  33.6 0.0 collective-permute-done.2.refs_1_
  33.6 0.0 copy-done.4
  33.6 0.0 copy-start
  33.6 3.1 %copy-done = bf16[1920,1920]{1,0:T(8,128)(2,1)S(1)} copy-done((bf16[1920,1920]{1,0:T(8,128)(2,1)S(1)}, bf16[1920,1920]{1,0:T(8,128)(2,1)}, u32[]{:S(2)}) %copy-start) | copy-done | bytes 7372824
  36.7 0.0 copy-start.1
  36.7 3.1 %spread_panel.2 = (bf16[2,1920,512]{2,1,0:T(8,128)(2,1)S(1)}, bf16[2,512,1920]{2,1,0:T(8,128)(2,1)S(1)}) custom-call(s32[8]{0:T(128)S(1)} %copy-done.4, s32[1]{0:T(128)S(6)} %copy.10.pair, bf16[1920,1920]{1,0:T(8,128)(2,1)S(1)} %copy-done, bf16[480,512]{1,0:T(8,128)(2,1)S(1)} %fold_panel.1.refs_0_, bf16[480,512]{1,0:T(8,128)(2,1)S(1)} %collective-permute-done.2.refs_1_), custom_call_target="tpu_custom_call" | custom-call | bytes 11059200 | tf_op jit(solution)/shard_map/spread_panel/pallas_call | solution.py:128
  39.8 0.1 pad_maximum_fusion.refs_0_
  39.8 0.0 collective-permute-done.4.refs_1_
  39.8 0.0 copy-done.1
  39.9 3.1 %spread_panel.3 = (bf16[2,1920,512]{2,1,0:T(8,128)(2,1)S(1)}, bf16[2,512,1920]{2,1,0:T(8,128)(2,1)S(1)}) custom-call(s32[8]{0:T(128)S(1)} %copy-done.4, s32[1]{0:T(128)S(6)} %copy.10.pair, bf16[1920,1920]{1,0:T(8,128)(2,1)S(1)} %copy-done.1, bf16[480,512]{1,0:T(8,128)(2,1)S(1)} %collective-permute-done.3.refs_0_, ...), custom_call_target="tpu_custom_call" | custom-call | bytes 11059200 | tf_op jit(solution)/shard_map/spread_panel/pallas_call | solution.py:128
  43.0 5.0 %dress_rows.3.refs_5_ = bf16[480,1920]{1,0:T(8,128)(2,1)} custom-call(bf16[240,1920]{1,0:T(8,128)(2,1)S(1)} %pad_maximum_fusion.refs_0_, bf16[2,1920,512]{2,1,0:T(8,128)(2,1)S(1)} %get-tuple-element.9.refs_1_, bf16[2,1920,512]{2,1,0:T(8,128)(2,1)S(1)} %get-tuple-element.10.refs_2_, bf16[2,512,1920]{2,1,0:T(8,128)(2,1)S(1)} %get-tuple-element.11.refs_3_, ...), custom_call_target="tpu_custom_call" | custom-call | flops 3538944000 | bytes 1843200 | tf_op jit(solution)/shard_map/dress_rows/pallas_call | solution.py:198
  47.9 4.9 %collective-permute-done.6.refs_0_ = bf16[128,1920]{1,0:T(8,128)(2,1)S(1)} collective-permute-done((bf16[128,1920]{1,0:T(8,128)(2,1)S(1)}, bf16[128,1920]{1,0:T(8,128)(2,1)S(1)}, u32[]{:S(2)}, u32[]{:S(2)}) %collective-permute-start.6) | collective-permute-done | bytes 491552 | tf_op jit(solution)/shard_map/ppermute | solution.py:260
  52.8 3.0 %dress_rows.4.refs_5_ = bf16[480,1920]{1,0:T(8,128)(2,1)} custom-call(bf16[128,1920]{1,0:T(8,128)(2,1)S(1)} %collective-permute-done.6.refs_0_, bf16[2,1920,512]{2,1,0:T(8,128)(2,1)S(1)} %get-tuple-element.9.refs_1_, bf16[2,1920,512]{2,1,0:T(8,128)(2,1)S(1)} %get-tuple-element.10.refs_2_, ...), custom_call_target="tpu_custom_call", output_to_operand_aliasing={{}: (5, {})} | custom-call | flops 1887436800 | bytes 983040 | tf_op jit(solution)/shard_map/dress_rows/pallas_call | solution.py:198
  55.8 0.0 collective-permute-done.1.refs_0_
  55.9 3.0 %dress_rows.5 = bf16[480,1920]{1,0:T(8,128)(2,1)} custom-call(bf16[112,1920]{1,0:T(8,128)(2,1)S(1)} %collective-permute-done.1.refs_0_, bf16[2,1920,512]{2,1,0:T(8,128)(2,1)S(1)} %get-tuple-element.9.refs_1_, bf16[2,1920,512]{2,1,0:T(8,128)(2,1)S(1)} %get-tuple-element.10.refs_2_, ...), custom_call_target="tpu_custom_call", output_to_operand_aliasing={{}: (5, {})} | custom-call | flops 1651507200 | bytes 860160 | tf_op jit(solution)/shard_map/dress_rows/pallas_call | solution.py:198
  (3 shorter events, 0.1 us)
Async XLA Ops:
  0.7 1.5 %copy-start.2 = (bf16[1920,1,480]{0,2,1:T(8,128)(2,1)S(1)}, bf16[1920,1,480]{0,2,1:T(8,128)(2,1)}, u32[]{:S(2)}) copy-start(bf16[1920,1,480]{0,2,1:T(8,128)(2,1)} %param.6) | copy-start | bytes 5529604
  2.2 0.7 %copy-start.3 = (s32[8]{0:T(128)S(1)}, s32[8]{0:T(128)}, u32[]{:S(2)}) copy-start(s32[8]{0:T(128)} %sizes.5) | copy-start | bytes 100
  2.8 1.7 %copy-start.5 = (bf16[240,1920]{1,0:T(8,128)(2,1)S(1)}, bf16[240,1920]{1,0:T(8,128)(2,1)}, u32[]{:S(2)}) copy-start(bf16[240,1920]{1,0:T(8,128)(2,1)} %param.5) | copy-start | bytes 2764804
  2.8 30.8 %copy-start.4 = (s32[8]{0:T(128)S(1)}, s32[8]{0:T(128)}, u32[]{:S(2)}) copy-start(s32[8]{0:T(128)} %sizes.5) | copy-start | bytes 100
  4.4 19.5 %collective-permute-start.3 = (bf16[480,512]{1,0:T(8,128)(2,1)S(1)}, bf16[480,512]{1,0:T(8,128)(2,1)S(1)}, u32[]{:S(2)}, u32[]{:S(2)}) collective-permute-start(bf16[480,512]{1,0:T(8,128)(2,1)S(1)} %fold_panel.1.refs_0_), channel_id=1, source_target_pairs={{2,0},{3,1},{0,2},{1,3},{6,4},{7,5},{4,6},{5,7},{10,8},{11,9},{8,1... | collective-permute-start | bytes 1474568 | tf_op jit(solution)/shard_map/ppermute | solution.py:263
  4.6 29.0 %collective-permute-start.5 = (bf16[128,1920]{1,0:T(8,128)(2,1)S(1)}, bf16[128,1920]{1,0:T(8,128)(2,1)S(1)}, u32[]{:S(2)}, u32[]{:S(2)}) collective-permute-start(bf16[128,1920]{1,0:T(8,128)(2,1)S(1)} %slice.7), channel_id=1, source_target_pairs={{0,0},{11,1},{16,2},{26,3},{4,4},{15,5},{20,6},{30,7},{2,8},{9,9},... | collective-permute-start | bytes 1474568 | tf_op jit(solution)/shard_map/ppermute | solution.py:254
  9.5 24.1 %collective-permute-start.2 = (bf16[480,512]{1,0:T(8,128)(2,1)S(1)}, bf16[480,512]{1,0:T(8,128)(2,1)S(1)}, u32[]{:S(2)}, u32[]{:S(2)}) collective-permute-start(bf16[480,512]{1,0:T(8,128)(2,1)S(1)} %fold_panel.1.refs_0_), channel_id=1, source_target_pairs={{1,0},{0,1},{3,2},{2,3},{5,4},{4,5},{7,6},{6,7},{9,8},{8,9},{11,10... | collective-permute-start | bytes 1474568 | tf_op jit(solution)/shard_map/ppermute | solution.py:264
  11.7 19.0 %collective-permute-start = (bf16[112,1920]{1,0:T(8,128)(2,1)S(1)}, bf16[112,1920]{1,0:T(8,128)(2,1)S(1)}, u32[]{:S(2)}, u32[]{:S(2)}) collective-permute-start(bf16[112,1920]{1,0:T(8,128)(2,1)S(1)} %slice.6), channel_id=1, source_target_pairs={{0,0},{11,1},{16,2},{26,3},{4,4},{15,5},{20,6},{30,7},{2,8},{9,9},... | collective-permute-start | bytes 1290248 | tf_op jit(solution)/shard_map/ppermute | solution.py:254
  23.9 16.0 %collective-permute-start.4 = (bf16[480,512]{1,0:T(8,128)(2,1)S(1)}, bf16[480,512]{1,0:T(8,128)(2,1)S(1)}, u32[]{:S(2)}, u32[]{:S(2)}) collective-permute-start(bf16[480,512]{1,0:T(8,128)(2,1)S(1)} %collective-permute-done.3.refs_0_), channel_id=1, source_target_pairs={{1,0},{0,1},{3,2},{2,3},{5,4},{4,5},{7,6},{6,7},{9,8},{8,9},{11,10... | collective-permute-start | bytes 1474568 | tf_op jit(solution)/shard_map/ppermute | solution.py:266
  30.8 25.1 %collective-permute-start.1 = (bf16[112,1920]{1,0:T(8,128)(2,1)S(1)}, bf16[112,1920]{1,0:T(8,128)(2,1)S(1)}, u32[]{:S(2)}, u32[]{:S(2)}) collective-permute-start(bf16[112,1920]{1,0:T(8,128)(2,1)S(1)} %collective-permute-done), channel_id=1, source_target_pairs={{4,0},{5,1},{6,2},{7,3},{0,4},{1,5},{2,6},{3,7},{12,8},{13,9},{14,... | collective-permute-start | bytes 1290248 | tf_op jit(solution)/shard_map/ppermute | solution.py:260
  33.5 19.3 %collective-permute-start.6 = (bf16[128,1920]{1,0:T(8,128)(2,1)S(1)}, bf16[128,1920]{1,0:T(8,128)(2,1)S(1)}, u32[]{:S(2)}, u32[]{:S(2)}) collective-permute-start(bf16[128,1920]{1,0:T(8,128)(2,1)S(1)} %collective-permute-done.5), channel_id=1, source_target_pairs={{4,0},{5,1},{6,2},{7,3},{0,4},{1,5},{2,6},{3,7},{12,8},{13,9},{14,... | collective-permute-start | bytes 1474568 | tf_op jit(solution)/shard_map/ppermute | solution.py:260
  33.6 3.1 %copy-start = (bf16[1920,1920]{1,0:T(8,128)(2,1)S(1)}, bf16[1920,1920]{1,0:T(8,128)(2,1)}, u32[]{:S(2)}) copy-start(bf16[1920,1920]{1,0:T(8,128)(2,1)} %fock.3) | copy-start | bytes 22118404
  36.7 3.2 %copy-start.1 = (bf16[1920,1920]{1,0:T(8,128)(2,1)S(1)}, bf16[1920,1920]{1,0:T(8,128)(2,1)}, u32[]{:S(2)}) copy-start(bf16[1920,1920]{1,0:T(8,128)(2,1)} %fock.3) | copy-start | bytes 22118404

commit v3 on v2

--- a/solution.py
+++ b/solution.py
@@ -140,10 +140,24 @@
         ],
         compiler_params=pltpu.CompilerParams(vmem_limit_bytes=16 * MIB),
         cost_estimate=pl.CostEstimate(
-            flops=0, bytes_accessed=6 * count * quarter * virtuals, transcendentals=0
+            flops=0, bytes_accessed=count * quarter * fold, transcendentals=0
         ),
         name="spread_panel",
     )(sizes, pair, fock, *folded)
+
+
+def after(array, *others):
+    anywhere = pl.BlockSpec(memory_space=pl.ANY)
+    return pl.pallas_call(
+        lambda *refs: None,
+        out_shape=jax.ShapeDtypeStruct(array.shape, array.dtype),
+        in_specs=[anywhere] * (1 + len(others)),
+        out_specs=anywhere,
+        input_output_aliases={0: 0},
+        compiler_params=pltpu.CompilerParams(vmem_limit_bytes=MIB),
+        cost_estimate=pl.CostEstimate(flops=0, bytes_accessed=0, transcendentals=0),
+        name="after",
+    )(array, *others)
 
 
 def column_tiles(total, tile):
@@ -254,17 +268,24 @@
             lax.ppermute(lax.slice_in_dim(amplitudes, first, first + size), axes, to_group)
             for first, size in spans
         ]
+
+        own = fold_panel(panel, irrep_sizes, pair_irreps, fold)
+        across = lax.ppermute(own, axes, to_slot(2))
+        beside = lax.ppermute(own, axes, to_slot(1))
+        fock = pltpu.with_memory_space_constraint(virt_fock, pltpu.HBM)
+        near_dense, near_fock = spread((0, 1), (own, beside), fock, irrep_sizes, pair_irreps)
+        across = after(across, near_dense)
+        both = lax.ppermute(across, axes, to_slot(1))
+
+        held[0] = after(held[0], near_dense)
+        for k in range(1, len(held)):
+            held[k] = after(held[k], held[k - 1])
         arrived = {(0, k): piece for k, piece in enumerate(held)}
         for k, piece in enumerate(held):
             for by in range(1, members):
                 arrived[by, k] = lax.ppermute(piece, axes, to_member(by))
 
-        own = fold_panel(panel, irrep_sizes, pair_irreps, fold)
-        across = lax.ppermute(own, axes, to_slot(2))
-        beside = lax.ppermute(own, axes, to_slot(1))
-        near_dense, near_fock = spread((0, 1), (own, beside), virt_fock, irrep_sizes, pair_irreps)
-        both = lax.ppermute(across, axes, to_slot(1))
-        far_dense, far_fock = spread((2, 3), (across, both), virt_fock, irrep_sizes, pair_irreps)
+        far_dense, far_fock = spread((2, 3), (across, both), fock, irrep_sizes, pair_irreps)
         dense, focks = (near_dense, far_dense), (near_fock, far_fock)
 
         if rows % SUBLANES == 0:

time: 60 us -> 54.1 us (0.902)
  the two profiles are of different devices: /device:TPU:4 before, /device:TPU:28 now
where the time goes in v3:
time: 54.1 us; the launch traced here: 53.9 us
  waiting for transfers between devices  21.5 us (40%)
  Pallas kernels  18.3 us (34%)
  starting transfers between devices  11.1 us (21%)
  local copies, waits for them, and re-layouts  2.23 us (4%)
  between operations  0.78 us (1%)
    ppermute x1, waiting for transfers between devices, local(): across = lax.ppermute(own, axes, to_slot(2))  11.7 us
    pallas_call x3, Pallas kernels, dress(): pl.pallas_call(functools.partial(dress_kernel, by, offset, rows, members,...  11.1 us
    ppermute x2, waiting for transfers between devices, local(): arrived[by, k] = lax.ppermute(piece, axes, to_member(by))  9.79 us
    ppermute x2, starting transfers between devices, local(): lax.ppermute(lax.slice_in_dim(amplitudes, first, first + size), axes, to_...  8.32 us
    pallas_call x2, Pallas kernels, spread(): pl.pallas_call(functools.partial(spread_kernel, slots), out_shape=(pltpu....  5.62 us
    unnamed x8, local copies, waits for them, and re-layouts  2.16 us
    ppermute x2, starting transfers between devices, local(): arrived[by, k] = lax.ppermute(piece, axes, to_member(by))  2.09 us
    pallas_call x1, Pallas kernels, fold_panel(): pl.pallas_call(fold_kernel, out_shape=jax.ShapeDtypeStruct((quarter, fold...  1.59 us
  transfers between devices with their start and end apart: 7, of which 3 were waited for; matrix products, arithmetic and copies ran while one was open for 0% of the time, Pallas kernels for 25%

profile of v3, /device:TPU:28, one launch (start us, length us, event | category | flops | bytes accessed | tf_op | source)
XLA Modules:
  0.0 53.9 jit_solution(6322732227836793528)
XLA Ops:
  0.7 0.0 copy-start
  0.7 1.5 %copy-done = bf16[1920,1,480]{0,2,1:T(8,128)(2,1)S(1)} copy-done((bf16[1920,1,480]{0,2,1:T(8,128)(2,1)S(1)}, bf16[1920,1,480]{0,2,1:T(8,128)(2,1)}, u32[]{:S(2)}) %copy-start) | copy-done | bytes 1843224
  2.2 0.0 copy-start.1
  2.2 0.7 %copy-done.1 = s32[8]{0:T(128)S(1)} copy-done((s32[8]{0:T(128)S(1)}, s32[8]{0:T(128)}, u32[]{:S(2)}) %copy-start.1) | copy-done | bytes 56
  2.8 0.0 copy-start.3
  2.8 0.0 copy-start.2
  2.8 1.6 %fold_panel.1.refs_0_ = bf16[480,512]{1,0:T(8,128)(2,1)S(1)} custom-call(s32[8]{0:T(128)S(1)} %copy-done.1, s32[1]{0:T(128)S(6)} %copy.16.pair, bf16[480,1920]{1,0:T(8,128)(2,1)S(1)} %bitcast.4), custom_call_target="tpu_custom_call" | custom-call | bytes 2334720 | tf_op jit(solution)/shard_map/fold_panel/pallas_call | solution.py:62
  4.4 0.1 collective-permute-start.2
  4.5 0.6 %collective-permute-start.4 = (bf16[480,512]{1,0:T(8,128)(2,1)S(1)}, bf16[480,512]{1,0:T(8,128)(2,1)S(1)}, u32[]{:S(2)}, u32[]{:S(2)}) collective-permute-start(bf16[480,512]{1,0:T(8,128)(2,1)S(1)} %fold_panel.1.refs_0_), channel_id=1, source_target_pairs={{2,0},{3,1},{0,2},{1,3},{6,4},{7,5},{4,6},{5,7},{10,8},{11,9},{8,1... | collective-permute-start | bytes 1474568 | tf_op jit(solution)/shard_map/ppermute | solution.py:273
  5.1 0.0 copy-done.3
  5.1 1.9 %collective-permute-start.1 = (bf16[128,1920]{1,0:T(8,128)(2,1)S(1)}, bf16[128,1920]{1,0:T(8,128)(2,1)S(1)}, u32[]{:S(2)}, u32[]{:S(2)}) collective-permute-start(bf16[128,1920]{1,0:T(8,128)(2,1)S(1)} %slice.7), channel_id=1, source_target_pairs={{0,0},{11,1},{16,2},{26,3},{4,4},{15,5},{20,6},{30,7},{2,8},{9,9},... | collective-permute-start | bytes 1474568 | tf_op jit(solution)/shard_map/ppermute | solution.py:268
  7.1 6.4 %collective-permute-start = (bf16[112,1920]{1,0:T(8,128)(2,1)S(1)}, bf16[112,1920]{1,0:T(8,128)(2,1)S(1)}, u32[]{:S(2)}, u32[]{:S(2)}) collective-permute-start(bf16[112,1920]{1,0:T(8,128)(2,1)S(1)} %slice.6), channel_id=1, source_target_pairs={{0,0},{11,1},{16,2},{26,3},{4,4},{15,5},{20,6},{30,7},{2,8},{9,9},... | collective-permute-start | bytes 1290248 | tf_op jit(solution)/shard_map/ppermute | solution.py:268
  13.5 0.0 collective-permute-done.2.refs_1_
  13.5 0.0 copy-done.2
  13.5 2.8 %spread_panel.2 = (bf16[2,1920,512]{2,1,0:T(8,128)(2,1)S(1)}, bf16[2,512,1920]{2,1,0:T(8,128)(2,1)S(1)}) custom-call(s32[8]{0:T(128)S(1)} %copy-done.2, s32[1]{0:T(128)S(6)} %copy.16.pair, bf16[1920,1920]{1,0:T(8,128)(2,1)} %fock.3, bf16[480,512]{1,0:T(8,128)(2,1)S(1)} %fold_panel.1.refs_0_, bf16[480,512]{1,0:T(8,128)(2,1)S(1)} %collective-permute-done.2.refs_1_), custom_call_target="tpu_custom_call" | custom-call | bytes 491520 | tf_op jit(solution)/shard_map/spread_panel/pallas_call | solution.py:128
  16.3 11.7 %collective-permute-done.4.refs_0_ = bf16[480,512]{1,0:T(8,128)(2,1)S(1)} collective-permute-done((bf16[480,512]{1,0:T(8,128)(2,1)S(1)}, bf16[480,512]{1,0:T(8,128)(2,1)S(1)}, u32[]{:S(2)}, u32[]{:S(2)}) %collective-permute-start.4) | collective-permute-done | bytes 491552 | tf_op jit(solution)/shard_map/ppermute | solution.py:273
  28.0 0.0 collective-permute-start.5
  28.0 0.0 collective-permute-done.1.refs_0_
  28.0 1.6 %collective-permute-start.6 = (bf16[128,1920]{1,0:T(8,128)(2,1)S(1)}, bf16[128,1920]{1,0:T(8,128)(2,1)S(1)}, u32[]{:S(2)}, u32[]{:S(2)}) collective-permute-start(bf16[128,1920]{1,0:T(8,128)(2,1)S(1)} %after.3.refs_1_), channel_id=1, source_target_pairs={{4,0},{5,1},{6,2},{7,3},{0,4},{1,5},{2,6},{3,7},{12,8},{13,9},{14,... | collective-permute-start | bytes 1474568 | tf_op jit(solution)/shard_map/ppermute | solution.py:286
  29.6 0.0 collective-permute-done.refs_0_
  29.6 0.5 collective-permute-start.3
  30.1 0.1 pad_maximum_fusion.refs_0_
  30.2 0.0 collective-permute-done.5.refs_1_
  30.2 2.8 %spread_panel.3 = (bf16[2,1920,512]{2,1,0:T(8,128)(2,1)S(1)}, bf16[2,512,1920]{2,1,0:T(8,128)(2,1)S(1)}) custom-call(s32[8]{0:T(128)S(1)} %copy-done.2, s32[1]{0:T(128)S(6)} %copy.16.pair, bf16[1920,1920]{1,0:T(8,128)(2,1)} %fock.3, bf16[480,512]{1,0:T(8,128)(2,1)S(1)} %after.5.refs_0_, bf16[480,512]{1,0:T(8,128)(2,1)S(1)} %collective-permute-done.5.refs_1_), custom_call_target="tpu_custom_call" | custom-call | bytes 491520 | tf_op jit(solution)/shard_map/spread_panel/pallas_call | solution.py:128
  33.0 5.0 %dress_rows.3.refs_5_ = bf16[480,1920]{1,0:T(8,128)(2,1)} custom-call(bf16[240,1920]{1,0:T(8,128)(2,1)S(1)} %pad_maximum_fusion.refs_0_, bf16[2,1920,512]{2,1,0:T(8,128)(2,1)S(1)} %get-tuple-element.9.refs_1_, bf16[2,1920,512]{2,1,0:T(8,128)(2,1)S(1)} %get-tuple-element.10.refs_2_, bf16[2,512,1920]{2,1,0:T(8,128)(2,1)S(1)} %get-tuple-element.11.refs_3_, ...), custom_call_target="tpu_custom_call" | custom-call | flops 3538944000 | bytes 1843200 | tf_op jit(solution)/shard_map/dress_rows/pallas_call | solution.py:212
  38.0 4.1 %collective-permute-done.6.refs_0_ = bf16[128,1920]{1,0:T(8,128)(2,1)S(1)} collective-permute-done((bf16[128,1920]{1,0:T(8,128)(2,1)S(1)}, bf16[128,1920]{1,0:T(8,128)(2,1)S(1)}, u32[]{:S(2)}, u32[]{:S(2)}) %collective-permute-start.6) | collective-permute-done | bytes 491552 | tf_op jit(solution)/shard_map/ppermute | solution.py:286
  42.1 3.1 %dress_rows.4.refs_5_ = bf16[480,1920]{1,0:T(8,128)(2,1)} custom-call(bf16[128,1920]{1,0:T(8,128)(2,1)S(1)} %collective-permute-done.6.refs_0_, bf16[2,1920,512]{2,1,0:T(8,128)(2,1)S(1)} %get-tuple-element.9.refs_1_, bf16[2,1920,512]{2,1,0:T(8,128)(2,1)S(1)} %get-tuple-element.10.refs_2_, ...), custom_call_target="tpu_custom_call", output_to_operand_aliasing={{}: (5, {})} | custom-call | flops 1887436800 | bytes 983040 | tf_op jit(solution)/shard_map/dress_rows/pallas_call | solution.py:212
  45.2 5.7 %collective-permute-done.3.refs_0_ = bf16[112,1920]{1,0:T(8,128)(2,1)S(1)} collective-permute-done((bf16[112,1920]{1,0:T(8,128)(2,1)S(1)}, bf16[112,1920]{1,0:T(8,128)(2,1)S(1)}, u32[]{:S(2)}, u32[]{:S(2)}) %collective-permute-start.3) | collective-permute-done | bytes 430112 | tf_op jit(solution)/shard_map/ppermute | solution.py:286
  50.9 3.1 %dress_rows.5 = bf16[480,1920]{1,0:T(8,128)(2,1)} custom-call(bf16[112,1920]{1,0:T(8,128)(2,1)S(1)} %collective-permute-done.3.refs_0_, bf16[2,1920,512]{2,1,0:T(8,128)(2,1)S(1)} %get-tuple-element.9.refs_1_, bf16[2,1920,512]{2,1,0:T(8,128)(2,1)S(1)} %get-tuple-element.10.refs_2_, ...), custom_call_target="tpu_custom_call", output_to_operand_aliasing={{}: (5, {})} | custom-call | flops 1651507200 | bytes 860160 | tf_op jit(solution)/shard_map/dress_rows/pallas_call | solution.py:212
  (5 shorter events, 0.1 us)
Async XLA Ops:
  0.7 1.5 %copy-start = (bf16[1920,1,480]{0,2,1:T(8,128)(2,1)S(1)}, bf16[1920,1,480]{0,2,1:T(8,128)(2,1)}, u32[]{:S(2)}) copy-start(bf16[1920,1,480]{0,2,1:T(8,128)(2,1)} %param.6) | copy-start | bytes 5529604
  2.2 0.7 %copy-start.1 = (s32[8]{0:T(128)S(1)}, s32[8]{0:T(128)}, u32[]{:S(2)}) copy-start(s32[8]{0:T(128)} %sizes.5) | copy-start | bytes 100
  2.8 2.3 %copy-start.3 = (bf16[240,1920]{1,0:T(8,128)(2,1)S(1)}, bf16[240,1920]{1,0:T(8,128)(2,1)}, u32[]{:S(2)}) copy-start(bf16[240,1920]{1,0:T(8,128)(2,1)} %param.5) | copy-start | bytes 2764804
  2.8 10.7 %copy-start.2 = (s32[8]{0:T(128)S(1)}, s32[8]{0:T(128)}, u32[]{:S(2)}) copy-start(s32[8]{0:T(128)} %sizes.5) | copy-start | bytes 100
  4.4 9.1 %collective-permute-start.2 = (bf16[480,512]{1,0:T(8,128)(2,1)S(1)}, bf16[480,512]{1,0:T(8,128)(2,1)S(1)}, u32[]{:S(2)}, u32[]{:S(2)}) collective-permute-start(bf16[480,512]{1,0:T(8,128)(2,1)S(1)} %fold_panel.1.refs_0_), channel_id=1, source_target_pairs={{1,0},{0,1},{3,2},{2,3},{5,4},{4,5},{7,6},{6,7},{9,8},{8,9},{11,10... | collective-permute-start | bytes 1474568 | tf_op jit(solution)/shard_map/ppermute | solution.py:274
  4.5 23.5 %collective-permute-start.4 = (bf16[480,512]{1,0:T(8,128)(2,1)S(1)}, bf16[480,512]{1,0:T(8,128)(2,1)S(1)}, u32[]{:S(2)}, u32[]{:S(2)}) collective-permute-start(bf16[480,512]{1,0:T(8,128)(2,1)S(1)} %fold_panel.1.refs_0_), channel_id=1, source_target_pairs={{2,0},{3,1},{0,2},{1,3},{6,4},{7,5},{4,6},{5,7},{10,8},{11,9},{8,1... | collective-permute-start | bytes 1474568 | tf_op jit(solution)/shard_map/ppermute | solution.py:273
  5.1 22.9 %collective-permute-start.1 = (bf16[128,1920]{1,0:T(8,128)(2,1)S(1)}, bf16[128,1920]{1,0:T(8,128)(2,1)S(1)}, u32[]{:S(2)}, u32[]{:S(2)}) collective-permute-start(bf16[128,1920]{1,0:T(8,128)(2,1)S(1)} %slice.7), channel_id=1, source_target_pairs={{0,0},{11,1},{16,2},{26,3},{4,4},{15,5},{20,6},{30,7},{2,8},{9,9},... | collective-permute-start | bytes 1474568 | tf_op jit(solution)/shard_map/ppermute | solution.py:268
  7.1 22.5 %collective-permute-start = (bf16[112,1920]{1,0:T(8,128)(2,1)S(1)}, bf16[112,1920]{1,0:T(8,128)(2,1)S(1)}, u32[]{:S(2)}, u32[]{:S(2)}) collective-permute-start(bf16[112,1920]{1,0:T(8,128)(2,1)S(1)} %slice.6), channel_id=1, source_target_pairs={{0,0},{11,1},{16,2},{26,3},{4,4},{15,5},{20,6},{30,7},{2,8},{9,9},... | collective-permute-start | bytes 1290248 | tf_op jit(solution)/shard_map/ppermute | solution.py:268
  28.0 2.2 %collective-permute-start.5 = (bf16[480,512]{1,0:T(8,128)(2,1)S(1)}, bf16[480,512]{1,0:T(8,128)(2,1)S(1)}, u32[]{:S(2)}, u32[]{:S(2)}) collective-permute-start(bf16[480,512]{1,0:T(8,128)(2,1)S(1)} %after.5.refs_0_), channel_id=1, source_target_pairs={{1,0},{0,1},{3,2},{2,3},{5,4},{4,5},{7,6},{6,7},{9,8},{8,9},{11,10... | collective-permute-start | bytes 1474568 | tf_op jit(solution)/shard_map/ppermute | solution.py:278
  28.0 14.1 %collective-permute-start.6 = (bf16[128,1920]{1,0:T(8,128)(2,1)S(1)}, bf16[128,1920]{1,0:T(8,128)(2,1)S(1)}, u32[]{:S(2)}, u32[]{:S(2)}) collective-permute-start(bf16[128,1920]{1,0:T(8,128)(2,1)S(1)} %after.3.refs_1_), channel_id=1, source_target_pairs={{4,0},{5,1},{6,2},{7,3},{0,4},{1,5},{2,6},{3,7},{12,8},{13,9},{14,... | collective-permute-start | bytes 1474568 | tf_op jit(solution)/shard_map/ppermute | solution.py:286
  29.6 21.3 %collective-permute-start.3 = (bf16[112,1920]{1,0:T(8,128)(2,1)S(1)}, bf16[112,1920]{1,0:T(8,128)(2,1)S(1)}, u32[]{:S(2)}, u32[]{:S(2)}) collective-permute-start(bf16[112,1920]{1,0:T(8,128)(2,1)S(1)} %after.4), channel_id=1, source_target_pairs={{4,0},{5,1},{6,2},{7,3},{0,4},{1,5},{2,6},{3,7},{12,8},{13,9},{14,... | collective-permute-start | bytes 1290248 | tf_op jit(solution)/shard_map/ppermute | solution.py:286

commit v4 on v3

--- a/solution.py
+++ b/solution.py
@@ -10,6 +10,7 @@
 LANES = 128
 SUBLANES = 16
 MIB = 1 << 20
+NOTHING = pl.CostEstimate(flops=0, bytes_accessed=0, transcendentals=0)
 
 
 def rounded(value, unit):
@@ -70,9 +71,7 @@
         out_specs=pl.BlockSpec(memory_space=pltpu.VMEM),
         scratch_shapes=[pltpu.SMEM((sizes.shape[0] + 1,), jnp.int32)],
         compiler_params=pltpu.CompilerParams(vmem_limit_bytes=8 * MIB),
-        cost_estimate=pl.CostEstimate(
-            flops=0, bytes_accessed=2 * quarter * (virtuals + fold), transcendentals=0
-        ),
+        cost_estimate=NOTHING,
         name="fold_panel",
     )(sizes, pair, panel)
 
@@ -139,9 +138,7 @@
             pltpu.SemaphoreType.DMA((count,)),
         ],
         compiler_params=pltpu.CompilerParams(vmem_limit_bytes=16 * MIB),
-        cost_estimate=pl.CostEstimate(
-            flops=0, bytes_accessed=count * quarter * fold, transcendentals=0
-        ),
+        cost_estimate=NOTHING,
         name="spread_panel",
     )(sizes, pair, fock, *folded)
 
@@ -155,7 +152,7 @@
         out_specs=anywhere,
         input_output_aliases={0: 0},
         compiler_params=pltpu.CompilerParams(vmem_limit_bytes=MIB),
-        cost_estimate=pl.CostEstimate(flops=0, bytes_accessed=0, transcendentals=0),
+        cost_estimate=NOTHING,
         name="after",
     )(array, *others)
 
@@ -164,18 +161,22 @@
     return [(first, min(tile, total - first)) for first in range(0, total, tile)]
 
 
-def dress_kernel(by, offset, rows, members, sets, has_base, *refs):
+def dress_kernel(spans, rows, members, sets, has_base, *refs):
     amplitudes, refs = refs[0], refs[1:]
     dense, focks, refs = refs[:sets], refs[sets:2 * sets], refs[2 * sets:]
     if has_base:
         refs = refs[1:]
-    result, coupled, dressed, sems = refs
+    result, token, coupled, dressed, sems = refs
+    token[...] = jnp.zeros_like(token)
     height = amplitudes.shape[0]
     virtuals = amplitudes.shape[1]
     width = dense[0].shape[2]
     slots = [(part, k) for part in range(sets) for k in range(dense[part].shape[0])]
-    member = lax.rem(lax.axis_index("blk") + by, members)
-    place = pl.multiple_of(member * rows + offset, SUBLANES)
+    block = lax.axis_index("blk")
+    places = [
+        pl.multiple_of(lax.rem(block + by, members) * rows + offset, SUBLANES)
+        for by, offset, _ in spans
+    ]
     for s, (part, k) in enumerate(slots):
         for first, tile in column_tiles(width, 256):
             coupled[:, s * width + first:s * width + first + tile] = jnp.dot(
@@ -191,17 +192,20 @@
                 preferred_element_type=jnp.float32,
             )
         dressed[:, first:first + tile] = total.astype(dressed.dtype)
-        copies.append(pltpu.make_async_copy(
-            dressed.at[:, pl.ds(first, tile)],
-            result.at[pl.ds(place, height), pl.ds(first, tile)],
-            sems.at[t],
-        ))
-        copies[-1].start()
+        begin = 0
+        for p, (_, _, size) in enumerate(spans):
+            copies.append(pltpu.make_async_copy(
+                dressed.at[pl.ds(begin, size), pl.ds(first, tile)],
+                result.at[pl.ds(places[p], size), pl.ds(first, tile)],
+                sems.at[p, t],
+            ))
+            copies[-1].start()
+            begin += size
     for copy in copies:
         copy.wait()
 
 
-def dress(amplitudes, dense, focks, base, by, offset, rows, members, out_rows):
+def dress(amplitudes, spans, dense, focks, base, rows, members, out_rows):
     height, virtuals = amplitudes.shape
     width = dense[0].shape[2]
     slots = sum(d.shape[0] for d in dense)
@@ -210,22 +214,21 @@
     pinned = [pltpu.with_memory_space_constraint(x, pltpu.VMEM) for x in (*dense, *focks)]
     bases = [] if base is None else [base]
     return pl.pallas_call(
-        functools.partial(dress_kernel, by, offset, rows, members, len(dense), base is not None),
-        out_shape=jax.ShapeDtypeStruct((out_rows, virtuals), amplitudes.dtype),
+        functools.partial(dress_kernel, spans, rows, members, len(dense), base is not None),
+        out_shape=(
+            jax.ShapeDtypeStruct((out_rows, virtuals), amplitudes.dtype),
+            pltpu.VMEM((8, LANES), jnp.int32),
+        ),
         in_specs=[vmem] * (1 + len(pinned)) + [anywhere] * len(bases),
-        out_specs=anywhere,
+        out_specs=(anywhere, vmem),
         input_output_aliases={} if base is None else {1 + len(pinned): 0},
         scratch_shapes=[
             pltpu.VMEM((height, slots * width), amplitudes.dtype),
             pltpu.VMEM((height, virtuals), amplitudes.dtype),
-            pltpu.SemaphoreType.DMA((len(column_tiles(virtuals, 512)),)),
+            pltpu.SemaphoreType.DMA((len(spans), len(column_tiles(virtuals, 512)))),
         ],
         compiler_params=pltpu.CompilerParams(vmem_limit_bytes=16 * MIB),
-        cost_estimate=pl.CostEstimate(
-            flops=4 * height * virtuals * virtuals,
-            bytes_accessed=4 * height * virtuals,
-            transcendentals=0,
-        ),
+        cost_estimate=NOTHING,
         name="dress_rows",
     )(amplitudes, *pinned, *bases)
 
@@ -259,48 +262,38 @@
         fold = rounded(virtuals // 4, LANES)
         panel = jnp.swapaxes(hole_panel[:, 0, :], 0, 1)
 
-        if rows % SUBLANES == 0:
-            half = rounded(rows // 2, SUBLANES)
-            spans = [(0, half), (half, rows - half)]
-        else:
-            spans = [(0, rows)]
-        held = [
-            lax.ppermute(lax.slice_in_dim(amplitudes, first, first + size), axes, to_group)
-            for first, size in spans
-        ]
-
         own = fold_panel(panel, irrep_sizes, pair_irreps, fold)
         across = lax.ppermute(own, axes, to_slot(2))
         beside = lax.ppermute(own, axes, to_slot(1))
+
+        early = rounded(rows * 3 // 5, SUBLANES) if rows % SUBLANES == 0 else rows
+        top = lax.ppermute(amplitudes[:early], axes, to_group)
+        tops = [top] + [lax.ppermute(top, axes, to_member(by)) for by in range(1, members)]
+        if early < rows:
+            low = amplitudes[early:]
+            lows = [low] + [lax.ppermute(low, axes, to_member(by)) for by in range(1, members)]
+            lows = lax.ppermute(after(jnp.concatenate(lows), top), axes, to_group)
+
         fock = pltpu.with_memory_space_constraint(virt_fock, pltpu.HBM)
         near_dense, near_fock = spread((0, 1), (own, beside), fock, irrep_sizes, pair_irreps)
-        across = after(across, near_dense)
+        across = after(across, near_dense, top)
         both = lax.ppermute(across, axes, to_slot(1))
-
-        held[0] = after(held[0], near_dense)
-        for k in range(1, len(held)):
-            held[k] = after(held[k], held[k - 1])
-        arrived = {(0, k): piece for k, piece in enumerate(held)}
-        for k, piece in enumerate(held):
-            for by in range(1, members):
-                arrived[by, k] = lax.ppermute(piece, axes, to_member(by))
-
         far_dense, far_fock = spread((2, 3), (across, both), fock, irrep_sizes, pair_irreps)
         dense, focks = (near_dense, far_dense), (near_fock, far_fock)
 
-        if rows % SUBLANES == 0:
-            pieces = [(jnp.concatenate(held), 0, 0)]
-            pieces += [
-                (arrived[by, k], by, spans[k][0]) for by in range(1, members) for k in range(len(spans))
-            ]
+        if early < rows:
             result = None
-            for piece, by, offset in pieces:
-                result = dress(piece, dense, focks, result, by, offset, rows, members, out_rows)
+            for by, piece in enumerate(tops):
+                spans = [(by, 0, early)]
+                result, token = dress(piece, spans, dense, focks, result, rows, members, out_rows)
+            spans = [(by, early, rows - early) for by in range(members)]
+            lows = after(lows, token)
+            result, _ = dress(lows, spans, dense, focks, result, rows, members, out_rows)
         else:
             member = lax.axis_index("blk") % members
-            stacked = jnp.stack([arrived[by, 0] for by in range(members)])
-            ordered = jnp.roll(stacked, member, axis=0).reshape(out_rows, virtuals)
-            result = dress(ordered, dense, focks, None, 0, 0, 0, members, out_rows)
+            ordered = jnp.roll(jnp.stack(tops), member, axis=0).reshape(out_rows, virtuals)
+            spans = [(0, 0, out_rows)]
+            result, _ = dress(ordered, spans, dense, focks, None, 0, members, out_rows)
         return result[:, None, :]
 
     return local

time: 54.1 us -> 50.7 us (0.937)
  the two profiles are of different devices: /device:TPU:28 before, /device:TPU:4 now
where the time goes in v4:
time: 50.7 us; the launch traced here: 50.5 us
  Pallas kernels  19.3 us (38%)
  waiting for transfers between devices  16.9 us (33%)
  starting transfers between devices  11.2 us (22%)
  local copies, waits for them, and re-layouts  2.25 us (4%)
  between operations  0.75 us (1%)
    pallas_call x3, Pallas kernels, dress(): pl.pallas_call(functools.partial(dress_kernel, spans, rows, members, len(...  12.1 us
    ppermute x1, waiting for transfers between devices, local(): top = lax.ppermute(amplitudes[:early], axes, to_group)  11.2 us
    pallas_call x2, Pallas kernels, spread(): pl.pallas_call(functools.partial(spread_kernel, slots), out_shape=(pltpu....  5.61 us
    ppermute x1, waiting for transfers between devices, local(): lows = lax.ppermute(after(jnp.concatenate(lows), top), axes, to_group)  3.44 us
    ppermute x1, starting transfers between devices, local(): top = lax.ppermute(amplitudes[:early], axes, to_group)  3.43 us
    ppermute x1, starting transfers between devices, local(): beside = lax.ppermute(own, axes, to_slot(1))  2.21 us
    ppermute x1, starting transfers between devices, local(): lows = lax.ppermute(after(jnp.concatenate(lows), top), axes, to_group)  1.91 us
    pallas_call x1, Pallas kernels, fold_panel(): pl.pallas_call(fold_kernel, out_shape=jax.ShapeDtypeStruct((quarter, fold...  1.6 us
  transfers between devices with their start and end apart: 7, of which 4 were waited for; matrix products, arithmetic and copies ran while one was open for 2% of the time, Pallas kernels for 29%

profile of v4, /device:TPU:4, one launch (start us, length us, event | category | flops | bytes accessed | tf_op | source)
XLA Modules:
  0.0 50.5 jit_solution(4894743121840809836)
XLA Ops:
  0.0 0.0 copy-start
  0.0 0.0 copy-start.1
  0.0 1.1 %slice.6 = bf16[96,1920]{1,0:T(8,128)(2,1)S(1)} slice(bf16[240,1920]{1,0:T(8,128)(2,1)} %param.5), slice={[144:240], [0:1920]} | slice | bytes 737280 | tf_op jit(solution)/shard_map/slice | solution.py:273
  1.2 1.6 %collective-permute-start = (bf16[96,1920]{1,0:T(8,128)(2,1)S(1)}, bf16[96,1920]{1,0:T(8,128)(2,1)S(1)}, u32[]{:S(2)}, u32[]{:S(2)}) collective-permute-start(bf16[96,1920]{1,0:T(8,128)(2,1)S(1)} %slice.6), channel_id=1, source_target_pairs={{4,0},{5,1},{6,2},{7,3},{0,4},{1,5},{2,6},{3,7},{12,8},{13,9},{14,... | collective-permute-start | bytes 1105928 | tf_op jit(solution)/shard_map/ppermute | solution.py:274
  2.7 1.1 %slice.7 = bf16[144,1920]{1,0:T(8,128)(2,1)S(1)} slice(bf16[240,1920]{1,0:T(8,128)(2,1)} %param.5), slice={[0:144], [0:1920]} | slice | bytes 1105920 | tf_op jit(solution)/shard_map/slice | solution.py:270
  3.8 3.4 %collective-permute-start.1 = (bf16[144,1920]{1,0:T(8,128)(2,1)S(1)}, bf16[144,1920]{1,0:T(8,128)(2,1)S(1)}, u32[]{:S(2)}, u32[]{:S(2)}) collective-permute-start(bf16[144,1920]{1,0:T(8,128)(2,1)S(1)} %slice.7), channel_id=1, source_target_pairs={{0,0},{11,1},{16,2},{26,3},{4,4},{15,5},{20,6},{30,7},{2,8},{9,9},... | collective-permute-start | bytes 1658888 | tf_op jit(solution)/shard_map/ppermute | solution.py:270
  7.9 0.0 copy-done
  7.9 0.0 copy-done.1
  7.9 1.6 %fold_panel.1.refs_0_ = bf16[480,512]{1,0:T(8,128)(2,1)S(1)} custom-call(s32[8]{0:T(128)S(1)} %copy-done.1, s32[1]{0:T(128)S(6)} %copy.16.pair, bf16[480,1920]{1,0:T(8,128)(2,1)S(1)} %bitcast.4), custom_call_target="tpu_custom_call" | custom-call | tf_op jit(solution)/shard_map/fold_panel/pallas_call | solution.py:63
  9.5 2.2 %collective-permute-start.4 = (bf16[480,512]{1,0:T(8,128)(2,1)S(1)}, bf16[480,512]{1,0:T(8,128)(2,1)S(1)}, u32[]{:S(2)}, u32[]{:S(2)}) collective-permute-start(bf16[480,512]{1,0:T(8,128)(2,1)S(1)} %fold_panel.1.refs_0_), channel_id=1, source_target_pairs={{1,0},{0,1},{3,2},{2,3},{5,4},{4,5},{7,6},{6,7},{9,8},{8,9},{11,10... | collective-permute-start | bytes 1474568 | tf_op jit(solution)/shard_map/ppermute | solution.py:267
  11.7 0.0 collective-permute-start.5
  11.7 0.0 collective-permute-done
  11.7 0.1 pad_maximum_fusion.refs_0_
  11.8 11.2 %collective-permute-done.1.refs_1_.refs_2_.refs_0_ = bf16[144,1920]{1,0:T(8,128)(2,1)S(1)} collective-permute-done((bf16[144,1920]{1,0:T(8,128)(2,1)S(1)}, bf16[144,1920]{1,0:T(8,128)(2,1)S(1)}, u32[]{:S(2)}, u32[]{:S(2)}) %collective-permute-start.1) | collective-permute-done | bytes 552992 | tf_op jit(solution)/shard_map/ppermute | solution.py:270
  23.0 1.9 %collective-permute-start.2 = (bf16[192,1920]{1,0:T(8,128)(2,1)S(1)}, bf16[192,1920]{1,0:T(8,128)(2,1)S(1)}, u32[]{:S(2)}, u32[]{:S(2)}) collective-permute-start(bf16[192,1920]{1,0:T(8,128)(2,1)S(1)} %after.3), channel_id=1, source_target_pairs={{0,0},{11,1},{16,2},{26,3},{4,4},{15,5},{20,6},{30,7},{2,8},{9,9},... | collective-permute-start | bytes 2211848 | tf_op jit(solution)/shard_map/ppermute | solution.py:275
  24.9 0.6 %collective-permute-start.3 = (bf16[144,1920]{1,0:T(8,128)(2,1)S(1)}, bf16[144,1920]{1,0:T(8,128)(2,1)S(1)}, u32[]{:S(2)}, u32[]{:S(2)}) collective-permute-start(bf16[144,1920]{1,0:T(8,128)(2,1)S(1)} %collective-permute-done.1.refs_1_.refs_2_.refs_0_), channel_id=1, source_target_pairs={{4,0},{5,1},{6,2},{7,3},{0,4},{1,5},{2,6},{3,7},{12,8},{13,9},{14,... | collective-permute-start | bytes 1658888 | tf_op jit(solution)/shard_map/ppermute | solution.py:271
  25.5 0.0 collective-permute-done.4.refs_1_
  25.5 2.8 %spread_panel.2 = (bf16[2,1920,512]{2,1,0:T(8,128)(2,1)S(1)}, bf16[2,512,1920]{2,1,0:T(8,128)(2,1)S(1)}) custom-call(s32[8]{0:T(128)S(1)} %copy-done.1, s32[1]{0:T(128)S(6)} %copy.16.pair, bf16[1920,1920]{1,0:T(8,128)(2,1)} %fock.3, bf16[480,512]{1,0:T(8,128)(2,1)S(1)} %fold_panel.1.refs_0_, bf16[480,512]{1,0:T(8,128)(2,1)S(1)} %collective-permute-done.4.refs_1_), custom_call_target="tpu_custom_call" | custom-call | tf_op jit(solution)/shard_map/spread_panel/pallas_call | solution.py:127
  28.4 0.8 %collective-permute-done.5.refs_0_ = bf16[480,512]{1,0:T(8,128)(2,1)S(1)} collective-permute-done((bf16[480,512]{1,0:T(8,128)(2,1)S(1)}, bf16[480,512]{1,0:T(8,128)(2,1)S(1)}, u32[]{:S(2)}, u32[]{:S(2)}) %collective-permute-start.5) | collective-permute-done | bytes 491552 | tf_op jit(solution)/shard_map/ppermute | solution.py:266
  29.1 1.5 %collective-permute-start.6 = (bf16[480,512]{1,0:T(8,128)(2,1)S(1)}, bf16[480,512]{1,0:T(8,128)(2,1)S(1)}, u32[]{:S(2)}, u32[]{:S(2)}) collective-permute-start(bf16[480,512]{1,0:T(8,128)(2,1)S(1)} %after.4.refs_0_), channel_id=1, source_target_pairs={{1,0},{0,1},{3,2},{2,3},{5,4},{4,5},{7,6},{6,7},{9,8},{8,9},{11,10... | collective-permute-start | bytes 1474568 | tf_op jit(solution)/shard_map/ppermute | solution.py:280
  30.6 1.5 %collective-permute-done.6.refs_1_ = bf16[480,512]{1,0:T(8,128)(2,1)S(1)} collective-permute-done((bf16[480,512]{1,0:T(8,128)(2,1)S(1)}, bf16[480,512]{1,0:T(8,128)(2,1)S(1)}, u32[]{:S(2)}, u32[]{:S(2)}) %collective-permute-start.6) | collective-permute-done | bytes 491552 | tf_op jit(solution)/shard_map/ppermute | solution.py:280
  32.1 2.8 %spread_panel.3 = (bf16[2,1920,512]{2,1,0:T(8,128)(2,1)S(1)}, bf16[2,512,1920]{2,1,0:T(8,128)(2,1)S(1)}) custom-call(s32[8]{0:T(128)S(1)} %copy-done.1, s32[1]{0:T(128)S(6)} %copy.16.pair, bf16[1920,1920]{1,0:T(8,128)(2,1)} %fock.3, bf16[480,512]{1,0:T(8,128)(2,1)S(1)} %after.4.refs_0_, bf16[480,512]{1,0:T(8,128)(2,1)S(1)} %collective-permute-done.6.refs_1_), custom_call_target="tpu_custom_call" | custom-call | tf_op jit(solution)/shard_map/spread_panel/pallas_call | solution.py:127
  34.9 3.9 %dress_rows.3 = (bf16[480,1920]{1,0:T(8,128)(2,1)}, s32[8,128]{1,0:T(8,128)}) custom-call(bf16[144,1920]{1,0:T(8,128)(2,1)S(1)} %collective-permute-done.1.refs_1_.refs_2_.refs_0_, bf16[2,1920,512]{2,1,0:T(8,128)(2,1)S(1)} %get-tuple-element.13.refs_1_, bf16[2,1920,512]{2,1,0:T(8,128)(2,1)S(1)} %get-tuple-element.14.refs_2_, ...), custom_call_target="tpu_custom_call" | custom-call | tf_op jit(solution)/shard_map/dress_rows/pallas_call | solution.py:216
  38.8 0.0 collective-permute-done.3.refs_0_
  38.9 3.4 %dress_rows.4 = (bf16[480,1920]{1,0:T(8,128)(2,1)}, s32[8,128]{1,0:T(8,128)S(1)}) custom-call(bf16[144,1920]{1,0:T(8,128)(2,1)S(1)} %collective-permute-done.3.refs_0_, bf16[2,1920,512]{2,1,0:T(8,128)(2,1)S(1)} %get-tuple-element.13.refs_1_, bf16[2,1920,512]{2,1,0:T(8,128)(2,1)S(1)} %get-tuple-element.14.refs_2_, ...), custom_call_target="tpu_custom_call", output_to_operand_aliasing={{0}: (5, {})} | custom-call | tf_op jit(solution)/shard_map/dress_rows/pallas_call | solution.py:216
  42.2 3.4 %collective-permute-done.2.refs_0_ = bf16[192,1920]{1,0:T(8,128)(2,1)S(1)} collective-permute-done((bf16[192,1920]{1,0:T(8,128)(2,1)S(1)}, bf16[192,1920]{1,0:T(8,128)(2,1)S(1)}, u32[]{:S(2)}, u32[]{:S(2)}) %collective-permute-start.2) | collective-permute-done | bytes 737312 | tf_op jit(solution)/shard_map/ppermute | solution.py:275
  45.7 4.8 %dress_rows.5 = (bf16[480,1920]{1,0:T(8,128)(2,1)}, s32[8,128]{1,0:T(8,128)}) custom-call(bf16[192,1920]{1,0:T(8,128)(2,1)S(1)} %after.5.refs_0_, bf16[2,1920,512]{2,1,0:T(8,128)(2,1)S(1)} %get-tuple-element.13.refs_1_, bf16[2,1920,512]{2,1,0:T(8,128)(2,1)S(1)} %get-tuple-element.14.refs_2_, ...), custom_call_target="tpu_custom_call", output_to_operand_aliasing={{0}: (5, {})} | custom-call | tf_op jit(solution)/shard_map/dress_rows/pallas_call | solution.py:216
  (3 shorter events, 0.0 us)
Async XLA Ops:
  0.0 7.9 %copy-start = (bf16[1920,1,480]{0,2,1:T(8,128)(2,1)S(1)}, bf16[1920,1,480]{0,2,1:T(8,128)(2,1)}, u32[]{:S(2)}) copy-start(bf16[1920,1,480]{0,2,1:T(8,128)(2,1)} %param.6) | copy-start | bytes 5529604
  0.0 7.9 %copy-start.1 = (s32[8]{0:T(128)S(1)}, s32[8]{0:T(128)}, u32[]{:S(2)}) copy-start(s32[8]{0:T(128)} %sizes.5) | copy-start | bytes 100
  1.2 10.6 %collective-permute-start = (bf16[96,1920]{1,0:T(8,128)(2,1)S(1)}, bf16[96,1920]{1,0:T(8,128)(2,1)S(1)}, u32[]{:S(2)}, u32[]{:S(2)}) collective-permute-start(bf16[96,1920]{1,0:T(8,128)(2,1)S(1)} %slice.6), channel_id=1, source_target_pairs={{4,0},{5,1},{6,2},{7,3},{0,4},{1,5},{2,6},{3,7},{12,8},{13,9},{14,... | collective-permute-start | bytes 1105928 | tf_op jit(solution)/shard_map/ppermute | solution.py:274
  3.8 19.2 %collective-permute-start.1 = (bf16[144,1920]{1,0:T(8,128)(2,1)S(1)}, bf16[144,1920]{1,0:T(8,128)(2,1)S(1)}, u32[]{:S(2)}, u32[]{:S(2)}) collective-permute-start(bf16[144,1920]{1,0:T(8,128)(2,1)S(1)} %slice.7), channel_id=1, source_target_pairs={{0,0},{11,1},{16,2},{26,3},{4,4},{15,5},{20,6},{30,7},{2,8},{9,9},... | collective-permute-start | bytes 1658888 | tf_op jit(solution)/shard_map/ppermute | solution.py:270
  9.5 16.0 %collective-permute-start.4 = (bf16[480,512]{1,0:T(8,128)(2,1)S(1)}, bf16[480,512]{1,0:T(8,128)(2,1)S(1)}, u32[]{:S(2)}, u32[]{:S(2)}) collective-permute-start(bf16[480,512]{1,0:T(8,128)(2,1)S(1)} %fold_panel.1.refs_0_), channel_id=1, source_target_pairs={{1,0},{0,1},{3,2},{2,3},{5,4},{4,5},{7,6},{6,7},{9,8},{8,9},{11,10... | collective-permute-start | bytes 1474568 | tf_op jit(solution)/shard_map/ppermute | solution.py:267
  11.7 17.4 %collective-permute-start.5 = (bf16[480,512]{1,0:T(8,128)(2,1)S(1)}, bf16[480,512]{1,0:T(8,128)(2,1)S(1)}, u32[]{:S(2)}, u32[]{:S(2)}) collective-permute-start(bf16[480,512]{1,0:T(8,128)(2,1)S(1)} %fold_panel.1.refs_0_), channel_id=1, source_target_pairs={{2,0},{3,1},{0,2},{1,3},{6,4},{7,5},{4,6},{5,7},{10,8},{11,9},{8,1... | collective-permute-start | bytes 1474568 | tf_op jit(solution)/shard_map/ppermute | solution.py:266
  23.0 22.6 %collective-permute-start.2 = (bf16[192,1920]{1,0:T(8,128)(2,1)S(1)}, bf16[192,1920]{1,0:T(8,128)(2,1)S(1)}, u32[]{:S(2)}, u32[]{:S(2)}) collective-permute-start(bf16[192,1920]{1,0:T(8,128)(2,1)S(1)} %after.3), channel_id=1, source_target_pairs={{0,0},{11,1},{16,2},{26,3},{4,4},{15,5},{20,6},{30,7},{2,8},{9,9},... | collective-permute-start | bytes 2211848 | tf_op jit(solution)/shard_map/ppermute | solution.py:275
  24.9 13.9 %collective-permute-start.3 = (bf16[144,1920]{1,0:T(8,128)(2,1)S(1)}, bf16[144,1920]{1,0:T(8,128)(2,1)S(1)}, u32[]{:S(2)}, u32[]{:S(2)}) collective-permute-start(bf16[144,1920]{1,0:T(8,128)(2,1)S(1)} %collective-permute-done.1.refs_1_.refs_2_.refs_0_), channel_id=1, source_target_pairs={{4,0},{5,1},{6,2},{7,3},{0,4},{1,5},{2,6},{3,7},{12,8},{13,9},{14,... | collective-permute-start | bytes 1658888 | tf_op jit(solution)/shard_map/ppermute | solution.py:271
  29.1 3.0 %collective-permute-start.6 = (bf16[480,512]{1,0:T(8,128)(2,1)S(1)}, bf16[480,512]{1,0:T(8,128)(2,1)S(1)}, u32[]{:S(2)}, u32[]{:S(2)}) collective-permute-start(bf16[480,512]{1,0:T(8,128)(2,1)S(1)} %after.4.refs_0_), channel_id=1, source_target_pairs={{1,0},{0,1},{3,2},{2,3},{5,4},{4,5},{7,6},{6,7},{9,8},{8,9},{11,10... | collective-permute-start | bytes 1474568 | tf_op jit(solution)/shard_map/ppermute | solution.py:280

commit v5 on v4

--- a/solution.py
+++ b/solution.py
@@ -35,11 +35,37 @@
     return low, high
 
 
+def cut_kernel(whole, *refs):
+    pieces, sems = refs[:-1], refs[-1]
+    copies, first = [], 0
+    for k, piece in enumerate(pieces):
+        size = piece.shape[0]
+        copies.append(pltpu.make_async_copy(whole.at[pl.ds(first, size)], piece, sems.at[k]))
+        copies[-1].start()
+        first += size
+    for copy in copies:
+        copy.wait()
+
+
+def cut(whole, sizes):
+    vmem = pl.BlockSpec(memory_space=pltpu.VMEM)
+    return pl.pallas_call(
+        cut_kernel,
+        out_shape=[pltpu.VMEM((size, whole.shape[1]), whole.dtype) for size in sizes],
+        in_specs=[pl.BlockSpec(memory_space=pl.ANY)],
+        out_specs=[vmem] * len(sizes),
+        scratch_shapes=[pltpu.SemaphoreType.DMA((len(sizes),))],
+        compiler_params=pltpu.CompilerParams(vmem_limit_bytes=4 * MIB),
+        cost_estimate=NOTHING,
+        name="cut_rows",
+    )(pltpu.with_memory_space_constraint(whole, pltpu.HBM))
+
+
 def fold_kernel(sizes, pair, panel, folded, bounds):
     quarter, virtuals = panel.shape
     fold = folded.shape[1]
     fill_bounds(sizes, bounds)
-    start = lax.axis_index("grp") * quarter
+    start = (lax.axis_index("grp") * pl.num_programs(0) + pl.program_id(0)) * quarter
     step = 32 if quarter % 32 == 0 else SUBLANES
 
     @pl.loop(0, quarter // step)
@@ -60,20 +86,22 @@
 
 def fold_panel(panel, sizes, pair, fold):
     quarter, virtuals = panel.shape
+    chunk = quarter // 5 if quarter % (5 * SUBLANES) == 0 else quarter
     return pl.pallas_call(
         fold_kernel,
+        grid=(quarter // chunk,),
         out_shape=jax.ShapeDtypeStruct((quarter, fold), panel.dtype),
         in_specs=[
             pl.BlockSpec(memory_space=pltpu.SMEM),
             pl.BlockSpec(memory_space=pltpu.SMEM),
-            pl.BlockSpec(memory_space=pltpu.VMEM),
+            pl.BlockSpec((chunk, virtuals), lambda i: (i, 0)),
         ],
-        out_specs=pl.BlockSpec(memory_space=pltpu.VMEM),
+        out_specs=pl.BlockSpec((chunk, fold), lambda i: (i, 0)),
         scratch_shapes=[pltpu.SMEM((sizes.shape[0] + 1,), jnp.int32)],
         compiler_params=pltpu.CompilerParams(vmem_limit_bytes=8 * MIB),
         cost_estimate=NOTHING,
         name="fold_panel",
-    )(sizes, pair, panel)
+    )(sizes, pair, pltpu.with_memory_space_constraint(panel, pltpu.HBM))
 
 
 def spread_kernel(slots, sizes, pair, fock, *refs):
@@ -261,25 +289,32 @@
         out_rows = rows * members
         fold = rounded(virtuals // 4, LANES)
         panel = jnp.swapaxes(hole_panel[:, 0, :], 0, 1)
+        irrep_sizes = pltpu.with_memory_space_constraint(irrep_sizes, pltpu.HBM)
 
         own = fold_panel(panel, irrep_sizes, pair_irreps, fold)
         across = lax.ppermute(own, axes, to_slot(2))
         beside = lax.ppermute(own, axes, to_slot(1))
 
-        early = rounded(rows * 3 // 5, SUBLANES) if rows % SUBLANES == 0 else rows
-        top = lax.ppermute(amplitudes[:early], axes, to_group)
+        early = rounded(rows * 2 // 3, SUBLANES) if rows % SUBLANES == 0 else rows
+        if early < rows:
+            top, low = cut(amplitudes, (early, rows - early))
+            top = lax.ppermute(top, axes, to_group)
+            lows = [low] + [lax.ppermute(low, axes, to_member(by)) for by in range(1, members)]
+        else:
+            top = lax.ppermute(amplitudes, axes, to_group)
+
+        fock = pltpu.with_memory_space_constraint(virt_fock, pltpu.HBM)
+        near_dense, near_fock = spread((0, 1), (own, beside), fock, irrep_sizes, pair_irreps)
+        top = after(top, near_dense)
         tops = [top] + [lax.ppermute(top, axes, to_member(by)) for by in range(1, members)]
         if early < rows:
-            low = amplitudes[early:]
-            lows = [low] + [lax.ppermute(low, axes, to_member(by)) for by in range(1, members)]
             lows = lax.ppermute(after(jnp.concatenate(lows), top), axes, to_group)
-
-        fock = pltpu.with_memory_space_constraint(virt_fock, pltpu.HBM)
-        near_dense, near_fock = spread((0, 1), (own, beside), fock, irrep_sizes, pair_irreps)
         across = after(across, near_dense, top)
         both = lax.ppermute(across, axes, to_slot(1))
-        far_dense, far_fock = spread((2, 3), (across, both), fock, irrep_sizes, pair_irreps)
-        dense, focks = (near_dense, far_dense), (near_fock, far_fock)
+        far_dense, far_fock = spread((2,), (across,), fock, irrep_sizes, pair_irreps)
+        both = after(both, far_dense)
+        last_dense, last_fock = spread((3,), (both,), fock, irrep_sizes, pair_irreps)
+        dense, focks = (near_dense, far_dense, last_dense), (near_fock, far_fock, last_fock)
 
         if early < rows:
             result = None

time: 50.7 us -> 50.4 us (level)
  the two profiles are of different devices: /device:TPU:4 before, /device:TPU:1 now
where the time goes in v5:
time: 50.4 us; the launch traced here: 50.1 us
  Pallas kernels  24.5 us (49%)
  starting transfers between devices  15.2 us (30%)
  waiting for transfers between devices  9.52 us (19%)
  between operations  0.78 us (2%)
    pallas_call x3, Pallas kernels, dress(): pl.pallas_call(functools.partial(dress_kernel, spans, rows, members, len(...  12 us
    pallas_call x3, Pallas kernels, spread(): pl.pallas_call(functools.partial(spread_kernel, slots), out_shape=(pltpu....  7.54 us
    ppermute x1, waiting for transfers between devices, local(): across = lax.ppermute(own, axes, to_slot(2))  6.78 us
    ppermute x1, starting transfers between devices, local(): top = lax.ppermute(top, axes, to_group)  5.61 us
    pallas_call x1, Pallas kernels, fold_panel(): pl.pallas_call(fold_kernel, grid=(quarter // chunk,), out_shape=jax.Shape...  3.72 us
    ppermute x1, starting transfers between devices, local(): lows = lax.ppermute(after(jnp.concatenate(lows), top), axes, to_group)  3.48 us
    ppermute x1, waiting for transfers between devices, local(): top = lax.ppermute(top, axes, to_group)  2.72 us
    ppermute x1, starting transfers between devices, local(): across = lax.ppermute(own, axes, to_slot(2))  2.2 us
  transfers between devices with their start and end apart: 7, of which 2 were waited for; matrix products, arithmetic and copies ran while one was open for 0% of the time, Pallas kernels for 38%

profile of v5, /device:TPU:1, one launch (start us, length us, event | category | flops | bytes accessed | tf_op | source)
XLA Modules:
  0.0 50.1 jit_solution(2958071247903262475)
XLA Ops:
  0.0 1.2 %cut_rows.1 = (bf16[160,1920]{1,0:T(8,128)(2,1)S(1)}, bf16[80,1920]{1,0:T(8,128)(2,1)S(1)}) custom-call(bf16[240,1920]{1,0:T(8,128)(2,1)} %whole.1), custom_call_target="tpu_custom_call" | custom-call | tf_op jit(solution)/shard_map/cut_rows/pallas_call | solution.py:52
  1.2 5.6 %collective-permute-start.1 = (bf16[160,1920]{1,0:T(8,128)(2,1)S(1)}, bf16[160,1920]{1,0:T(8,128)(2,1)S(1)}, u32[]{:S(2)}, u32[]{:S(2)}) collective-permute-start(bf16[160,1920]{1,0:T(8,128)(2,1)S(1)} %get-tuple-element.18), channel_id=1, source_target_pairs={{0,0},{11,1},{16,2},{26,3},{4,4},{15,5},{20,6},{30,7},{2,8},{9,9},... | collective-permute-start | bytes 1843208 | tf_op jit(solution)/shard_map/ppermute | solution.py:301
  7.4 3.7 %fold_panel.1.refs_0_ = bf16[480,512]{1,0:T(8,128)(2,1)S(1)} custom-call(s32[8]{0:T(128)} %sizes.7, s32[1]{0:T(128)S(6)} %copy.20.pair, bf16[480,1920]{1,0:T(8,128)(2,1)} %bitcast.4), custom_call_target="tpu_custom_call" | custom-call | tf_op jit(solution)/shard_map/fold_panel/pallas_call | solution.py:90
  11.2 0.1 collective-permute-start.2
  11.2 1.3 %collective-permute-start = (bf16[80,1920]{1,0:T(8,128)(2,1)S(1)}, bf16[80,1920]{1,0:T(8,128)(2,1)S(1)}, u32[]{:S(2)}, u32[]{:S(2)}) collective-permute-start(bf16[80,1920]{1,0:T(8,128)(2,1)S(1)} %get-tuple-element.17), channel_id=1, source_target_pairs={{4,0},{5,1},{6,2},{7,3},{0,4},{1,5},{2,6},{3,7},{12,8},{13,9},{14,... | collective-permute-start | bytes 921608 | tf_op jit(solution)/shard_map/ppermute | solution.py:302
  12.5 2.2 %collective-permute-start.5 = (bf16[480,512]{1,0:T(8,128)(2,1)S(1)}, bf16[480,512]{1,0:T(8,128)(2,1)S(1)}, u32[]{:S(2)}, u32[]{:S(2)}) collective-permute-start(bf16[480,512]{1,0:T(8,128)(2,1)S(1)} %fold_panel.1.refs_0_), channel_id=1, source_target_pairs={{2,0},{3,1},{0,2},{1,3},{6,4},{7,5},{4,6},{5,7},{10,8},{11,9},{8,1... | collective-permute-start | bytes 1474568 | tf_op jit(solution)/shard_map/ppermute | solution.py:295
  14.7 0.0 collective-permute-done.2.refs_1_
  14.7 2.9 %spread_panel.3 = (bf16[2,1920,512]{2,1,0:T(8,128)(2,1)S(1)}, bf16[2,512,1920]{2,1,0:T(8,128)(2,1)S(1)}) custom-call(s32[8]{0:T(128)} %sizes.7, s32[1]{0:T(128)S(6)} %copy.20.pair, bf16[1920,1920]{1,0:T(8,128)(2,1)} %fock.5, bf16[480,512]{1,0:T(8,128)(2,1)S(1)} %fold_panel.1.refs_0_, bf16[480,512]{1,0:T(8,128)(2,1)S(1)} %collective-permute-done.2.refs_1_), custom_call_target="tpu_custom_call" | custom-call | tf_op jit(solution)/shard_map/spread_panel/pallas_call | solution.py:155
  17.7 2.7 %collective-permute-done.1.refs_0_ = bf16[160,1920]{1,0:T(8,128)(2,1)S(1)} collective-permute-done((bf16[160,1920]{1,0:T(8,128)(2,1)S(1)}, bf16[160,1920]{1,0:T(8,128)(2,1)S(1)}, u32[]{:S(2)}, u32[]{:S(2)}) %collective-permute-start.1) | collective-permute-done | bytes 614432 | tf_op jit(solution)/shard_map/ppermute | solution.py:301
  20.4 1.3 %collective-permute-start.4 = (bf16[160,1920]{1,0:T(8,128)(2,1)S(1)}, bf16[160,1920]{1,0:T(8,128)(2,1)S(1)}, u32[]{:S(2)}, u32[]{:S(2)}) collective-permute-start(bf16[160,1920]{1,0:T(8,128)(2,1)S(1)} %after.5.refs_1_.refs_2_.refs_0_), channel_id=1, source_target_pairs={{4,0},{5,1},{6,2},{7,3},{0,4},{1,5},{2,6},{3,7},{12,8},{13,9},{14,... | collective-permute-start | bytes 1843208 | tf_op jit(solution)/shard_map/ppermute | solution.py:309
  21.7 0.0 collective-permute-done
  21.8 3.5 %collective-permute-start.3 = (bf16[160,1920]{1,0:T(8,128)(2,1)S(1)}, bf16[160,1920]{1,0:T(8,128)(2,1)S(1)}, u32[]{:S(2)}, u32[]{:S(2)}) collective-permute-start(bf16[160,1920]{1,0:T(8,128)(2,1)S(1)} %after.6), channel_id=1, source_target_pairs={{0,0},{11,1},{16,2},{26,3},{4,4},{15,5},{20,6},{30,7},{2,8},{9,9},... | collective-permute-start | bytes 1843208 | tf_op jit(solution)/shard_map/ppermute | solution.py:311
  25.3 6.8 %collective-permute-done.5.refs_0_ = bf16[480,512]{1,0:T(8,128)(2,1)S(1)} collective-permute-done((bf16[480,512]{1,0:T(8,128)(2,1)S(1)}, bf16[480,512]{1,0:T(8,128)(2,1)S(1)}, u32[]{:S(2)}, u32[]{:S(2)}) %collective-permute-start.5) | collective-permute-done | bytes 491552 | tf_op jit(solution)/shard_map/ppermute | solution.py:295
  32.0 1.3 %collective-permute-start.6 = (bf16[480,512]{1,0:T(8,128)(2,1)S(1)}, bf16[480,512]{1,0:T(8,128)(2,1)S(1)}, u32[]{:S(2)}, u32[]{:S(2)}) collective-permute-start(bf16[480,512]{1,0:T(8,128)(2,1)S(1)} %after.7.refs_0_), channel_id=1, source_target_pairs={{1,0},{0,1},{3,2},{2,3},{5,4},{4,5},{7,6},{6,7},{9,8},{8,9},{11,10... | collective-permute-start | bytes 1474568 | tf_op jit(solution)/shard_map/ppermute | solution.py:313
  33.3 2.3 %spread_panel.4 = (bf16[1,1920,512]{2,1,0:T(8,128)(2,1)S(1)}, bf16[1,512,1920]{2,1,0:T(8,128)(2,1)S(1)}) custom-call(s32[8]{0:T(128)} %sizes.7, s32[1]{0:T(128)S(6)} %copy.20.pair, bf16[1920,1920]{1,0:T(8,128)(2,1)} %fock.5, bf16[480,512]{1,0:T(8,128)(2,1)S(1)} %after.7.refs_0_), custom_call_target="tpu_custom_call" | custom-call | tf_op jit(solution)/shard_map/spread_panel/pallas_call | solution.py:155
  35.6 0.0 collective-permute-done.6.refs_0_
  35.6 2.3 %spread_panel.5 = (bf16[1,1920,512]{2,1,0:T(8,128)(2,1)S(1)}, bf16[1,512,1920]{2,1,0:T(8,128)(2,1)S(1)}) custom-call(s32[8]{0:T(128)} %sizes.7, s32[1]{0:T(128)S(6)} %copy.20.pair, bf16[1920,1920]{1,0:T(8,128)(2,1)} %fock.5, bf16[480,512]{1,0:T(8,128)(2,1)S(1)} %after.8.refs_0_), custom_call_target="tpu_custom_call" | custom-call | tf_op jit(solution)/shard_map/spread_panel/pallas_call | solution.py:155
  38.0 4.2 %dress_rows.3 = (bf16[480,1920]{1,0:T(8,128)(2,1)}, s32[8,128]{1,0:T(8,128)}) custom-call(bf16[160,1920]{1,0:T(8,128)(2,1)S(1)} %after.5.refs_1_.refs_2_.refs_0_, bf16[2,1920,512]{2,1,0:T(8,128)(2,1)S(1)} %get-tuple-element.19.refs_1_, bf16[1,1920,512]{2,1,0:T(8,128)(2,1)S(1)} %get-tuple-element.20.refs_1_.refs_2_, ...), custom_call_target="tpu_custom_call" | custom-call | tf_op jit(solution)/shard_map/dress_rows/pallas_call | solution.py:244
  42.2 0.0 collective-permute-done.4.refs_0_
  42.2 3.6 %dress_rows.4 = (bf16[480,1920]{1,0:T(8,128)(2,1)}, s32[8,128]{1,0:T(8,128)S(1)}) custom-call(bf16[160,1920]{1,0:T(8,128)(2,1)S(1)} %collective-permute-done.4.refs_0_, bf16[2,1920,512]{2,1,0:T(8,128)(2,1)S(1)} %get-tuple-element.19.refs_1_, bf16[1,1920,512]{2,1,0:T(8,128)(2,1)S(1)} %get-tuple-element.20.refs_1_.refs_2_, ...), custom_call_target="tpu_custom_call", output_to_operand_aliasing={{0}: (7, {})} | custom-call | tf_op jit(solution)/shard_map/dress_rows/pallas_call | solution.py:244
  45.8 0.0 collective-permute-done.3.refs_0_
  45.8 4.2 %dress_rows.5 = (bf16[480,1920]{1,0:T(8,128)(2,1)}, s32[8,128]{1,0:T(8,128)}) custom-call(bf16[160,1920]{1,0:T(8,128)(2,1)S(1)} %after.9.refs_0_, bf16[2,1920,512]{2,1,0:T(8,128)(2,1)S(1)} %get-tuple-element.19.refs_1_, bf16[1,1920,512]{2,1,0:T(8,128)(2,1)S(1)} %get-tuple-element.20.refs_1_.refs_2_, ...), custom_call_target="tpu_custom_call", output_to_operand_aliasing={{0}: (7, {})} | custom-call | tf_op jit(solution)/shard_map/dress_rows/pallas_call | solution.py:244
  (6 shorter events, 0.1 us)
Async XLA Ops:
  1.2 19.2 %collective-permute-start.1 = (bf16[160,1920]{1,0:T(8,128)(2,1)S(1)}, bf16[160,1920]{1,0:T(8,128)(2,1)S(1)}, u32[]{:S(2)}, u32[]{:S(2)}) collective-permute-start(bf16[160,1920]{1,0:T(8,128)(2,1)S(1)} %get-tuple-element.18), channel_id=1, source_target_pairs={{0,0},{11,1},{16,2},{26,3},{4,4},{15,5},{20,6},{30,7},{2,8},{9,9},... | collective-permute-start | bytes 1843208 | tf_op jit(solution)/shard_map/ppermute | solution.py:301
  11.2 3.6 %collective-permute-start.2 = (bf16[480,512]{1,0:T(8,128)(2,1)S(1)}, bf16[480,512]{1,0:T(8,128)(2,1)S(1)}, u32[]{:S(2)}, u32[]{:S(2)}) collective-permute-start(bf16[480,512]{1,0:T(8,128)(2,1)S(1)} %fold_panel.1.refs_0_), channel_id=1, source_target_pairs={{1,0},{0,1},{3,2},{2,3},{5,4},{4,5},{7,6},{6,7},{9,8},{8,9},{11,10... | collective-permute-start | bytes 1474568 | tf_op jit(solution)/shard_map/ppermute | solution.py:296
  11.2 10.5 %collective-permute-start = (bf16[80,1920]{1,0:T(8,128)(2,1)S(1)}, bf16[80,1920]{1,0:T(8,128)(2,1)S(1)}, u32[]{:S(2)}, u32[]{:S(2)}) collective-permute-start(bf16[80,1920]{1,0:T(8,128)(2,1)S(1)} %get-tuple-element.17), channel_id=1, source_target_pairs={{4,0},{5,1},{6,2},{7,3},{0,4},{1,5},{2,6},{3,7},{12,8},{13,9},{14,... | collective-permute-start | bytes 921608 | tf_op jit(solution)/shard_map/ppermute | solution.py:302
  12.5 19.5 %collective-permute-start.5 = (bf16[480,512]{1,0:T(8,128)(2,1)S(1)}, bf16[480,512]{1,0:T(8,128)(2,1)S(1)}, u32[]{:S(2)}, u32[]{:S(2)}) collective-permute-start(bf16[480,512]{1,0:T(8,128)(2,1)S(1)} %fold_panel.1.refs_0_), channel_id=1, source_target_pairs={{2,0},{3,1},{0,2},{1,3},{6,4},{7,5},{4,6},{5,7},{10,8},{11,9},{8,1... | collective-permute-start | bytes 1474568 | tf_op jit(solution)/shard_map/ppermute | solution.py:295
  20.4 21.8 %collective-permute-start.4 = (bf16[160,1920]{1,0:T(8,128)(2,1)S(1)}, bf16[160,1920]{1,0:T(8,128)(2,1)S(1)}, u32[]{:S(2)}, u32[]{:S(2)}) collective-permute-start(bf16[160,1920]{1,0:T(8,128)(2,1)S(1)} %after.5.refs_1_.refs_2_.refs_0_), channel_id=1, source_target_pairs={{4,0},{5,1},{6,2},{7,3},{0,4},{1,5},{2,6},{3,7},{12,8},{13,9},{14,... | collective-permute-start | bytes 1843208 | tf_op jit(solution)/shard_map/ppermute | solution.py:309
  21.8 24.0 %collective-permute-start.3 = (bf16[160,1920]{1,0:T(8,128)(2,1)S(1)}, bf16[160,1920]{1,0:T(8,128)(2,1)S(1)}, u32[]{:S(2)}, u32[]{:S(2)}) collective-permute-start(bf16[160,1920]{1,0:T(8,128)(2,1)S(1)} %after.6), channel_id=1, source_target_pairs={{0,0},{11,1},{16,2},{26,3},{4,4},{15,5},{20,6},{30,7},{2,8},{9,9},... | collective-permute-start | bytes 1843208 | tf_op jit(solution)/shard_map/ppermute | solution.py:311
  32.0 3.6 %collective-permute-start.6 = (bf16[480,512]{1,0:T(8,128)(2,1)S(1)}, bf16[480,512]{1,0:T(8,128)(2,1)S(1)}, u32[]{:S(2)}, u32[]{:S(2)}) collective-permute-start(bf16[480,512]{1,0:T(8,128)(2,1)S(1)} %after.7.refs_0_), channel_id=1, source_target_pairs={{1,0},{0,1},{3,2},{2,3},{5,4},{4,5},{7,6},{6,7},{9,8},{8,9},{11,10... | collective-permute-start | bytes 1474568 | tf_op jit(solution)/shard_map/ppermute | solution.py:313

commit v6 on v5

--- a/solution.py
+++ b/solution.py
@@ -61,68 +61,81 @@
     )(pltpu.with_memory_space_constraint(whole, pltpu.HBM))
 
 
-def fold_kernel(sizes, pair, panel, folded, bounds):
+def fold_kernel(chunk, sizes, pair, source, folded, again, panel, bounds, sems):
     quarter, virtuals = panel.shape
     fold = folded.shape[1]
+    copies = []
+    for k in range(quarter // chunk):
+        rows = pl.ds(k * chunk, chunk)
+        copies.append(pltpu.make_async_copy(source.at[rows], panel.at[rows], sems.at[k]))
+        copies[-1].start()
     fill_bounds(sizes, bounds)
-    start = (lax.axis_index("grp") * pl.num_programs(0) + pl.program_id(0)) * quarter
-    step = 32 if quarter % 32 == 0 else SUBLANES
-
-    @pl.loop(0, quarter // step)
-    def _(i):
-        first = pl.multiple_of(i * step, step)
-        here = pl.ds(first, step)
-        b = start + first + lax.broadcasted_iota(jnp.int32, (step, LANES), 0)
-        low, high = wanted_range(b, pair, bounds, sizes.shape[0])
-        lane = lax.broadcasted_iota(jnp.int32, (step, LANES), 1)
-        low, high = low - lane, high - lane
-        for place in range(0, fold, LANES):
-            total = jnp.zeros((step, LANES), jnp.float32)
-            for c in range(place, virtuals, fold):
-                value = panel[here, c:c + LANES].astype(jnp.float32)
-                total = jnp.where((low <= c) & (high > c), value, total)
-            folded[here, place:place + LANES] = total.astype(folded.dtype)
+    start = lax.axis_index("grp") * quarter
+    step = 32 if chunk % 32 == 0 else SUBLANES
+    for k, copy in enumerate(copies):
+        copy.wait()
+
+        @pl.loop(0, chunk // step)
+        def _(i):
+            first = pl.multiple_of(k * chunk + i * step, SUBLANES)
+            here = pl.ds(first, step)
+            b = start + first + lax.broadcasted_iota(jnp.int32, (step, LANES), 0)
+            low, high = wanted_range(b, pair, bounds, sizes.shape[0])
+            lane = lax.broadcasted_iota(jnp.int32, (step, LANES), 1)
+            low, high = low - lane, high - lane
+            for place in range(0, fold, LANES):
+                total = jnp.zeros((step, LANES), jnp.float32)
+                for c in range(place, virtuals, fold):
+                    value = panel[here, c:c + LANES].astype(jnp.float32)
+                    total = jnp.where((low <= c) & (high > c), value, total)
+                total = total.astype(folded.dtype)
+                folded[here, place:place + LANES] = total
+                again[here, place:place + LANES] = total
 
 
 def fold_panel(panel, sizes, pair, fold):
     quarter, virtuals = panel.shape
     chunk = quarter // 5 if quarter % (5 * SUBLANES) == 0 else quarter
-    return pl.pallas_call(
-        fold_kernel,
-        grid=(quarter // chunk,),
-        out_shape=jax.ShapeDtypeStruct((quarter, fold), panel.dtype),
-        in_specs=[
-            pl.BlockSpec(memory_space=pltpu.SMEM),
-            pl.BlockSpec(memory_space=pltpu.SMEM),
-            pl.BlockSpec((chunk, virtuals), lambda i: (i, 0)),
+    smem = pl.BlockSpec(memory_space=pltpu.SMEM)
+    return pl.pallas_call(
+        functools.partial(fold_kernel, chunk),
+        out_shape=[pltpu.VMEM((quarter, fold), panel.dtype)] * 2,
+        in_specs=[smem, smem, pl.BlockSpec(memory_space=pl.ANY)],
+        out_specs=[pl.BlockSpec(memory_space=pltpu.VMEM)] * 2,
+        scratch_shapes=[
+            pltpu.VMEM((quarter, virtuals), panel.dtype),
+            pltpu.SMEM((sizes.shape[0] + 1,), jnp.int32),
+            pltpu.SemaphoreType.DMA((quarter // chunk,)),
         ],
-        out_specs=pl.BlockSpec((chunk, fold), lambda i: (i, 0)),
-        scratch_shapes=[pltpu.SMEM((sizes.shape[0] + 1,), jnp.int32)],
         compiler_params=pltpu.CompilerParams(vmem_limit_bytes=8 * MIB),
         cost_estimate=NOTHING,
         name="fold_panel",
     )(sizes, pair, pltpu.with_memory_space_constraint(panel, pltpu.HBM))
 
 
-def spread_kernel(slots, sizes, pair, fock, *refs):
-    count = len(slots)
-    folded, (dense, fock_out, bounds, turned, sems) = refs[:count], refs[count:]
+def spread_kernel(slots, fock_slots, sizes, pair, *refs):
+    count, loads = len(slots), len(fock_slots)
+    folded, refs = refs[:count], refs[count:]
+    if loads:
+        (fock, dense, fock_out, bounds, turned, sems) = refs
+    else:
+        (dense, bounds, turned) = refs
     quarter, fold = folded[0].shape
     virtuals = dense.shape[1]
     width = dense.shape[2]
     group = lax.axis_index("grp")
     copies = []
-    for k, slot in enumerate(slots):
+    for k, slot in enumerate(fock_slots):
         first = pl.multiple_of(jnp.bitwise_xor(group, slot) * quarter, SUBLANES)
         copies.append(pltpu.make_async_copy(
             fock.at[pl.ds(first, quarter)], fock_out.at[k, pl.ds(0, quarter)], sems.at[k]
         ))
         copies[-1].start()
+        if width > quarter:
+            fock_out[k, quarter:width, :] = jnp.zeros((width - quarter, virtuals), fock_out.dtype)
     fill_bounds(sizes, bounds)
     step = 32
     for k, slot in enumerate(slots):
-        if width > quarter:
-            fock_out[k, quarter:width, :] = jnp.zeros((width - quarter, virtuals), fock_out.dtype)
         values = folded[k][...].astype(jnp.float32)
         if width > quarter:
             values = jnp.concatenate([values, jnp.zeros((width - quarter, fold), jnp.float32)])
@@ -145,30 +158,32 @@
         copy.wait()
 
 
-def spread(slots, folded, fock, sizes, pair):
+def spread(slots, folded, sizes, pair, virtuals, fock=None, fock_slots=()):
     quarter, fold = folded[0].shape
-    virtuals = fock.shape[0]
     width = rounded(quarter, LANES)
-    count = len(slots)
+    count, loads = len(slots), len(fock_slots)
     smem = pl.BlockSpec(memory_space=pltpu.SMEM)
     vmem = pl.BlockSpec(memory_space=pltpu.VMEM)
-    return pl.pallas_call(
-        functools.partial(spread_kernel, slots),
-        out_shape=(
-            pltpu.VMEM((count, virtuals, width), fock.dtype),
-            pltpu.VMEM((count, width, virtuals), fock.dtype),
-        ),
-        in_specs=[smem, smem, pl.BlockSpec(memory_space=pl.ANY)] + [vmem] * count,
-        out_specs=(vmem, vmem),
-        scratch_shapes=[
-            pltpu.SMEM((sizes.shape[0] + 1,), jnp.int32),
-            pltpu.VMEM((fold, width), jnp.float32),
-            pltpu.SemaphoreType.DMA((count,)),
-        ],
-        compiler_params=pltpu.CompilerParams(vmem_limit_bytes=16 * MIB),
+    out_shape = [pltpu.VMEM((count, virtuals, width), folded[0].dtype)]
+    scratch = [
+        pltpu.SMEM((sizes.shape[0] + 1,), jnp.int32),
+        pltpu.VMEM((fold, width), jnp.float32),
+    ]
+    extra = []
+    if loads:
+        out_shape.append(pltpu.VMEM((loads, width, virtuals), fock.dtype))
+        scratch.append(pltpu.SemaphoreType.DMA((loads,)))
+        extra.append(pltpu.with_memory_space_constraint(fock, pltpu.HBM))
+    return pl.pallas_call(
+        functools.partial(spread_kernel, slots, fock_slots),
+        out_shape=out_shape,
+        in_specs=[smem, smem] + [vmem] * count + [pl.BlockSpec(memory_space=pl.ANY)] * len(extra),
+        out_specs=[vmem] * len(out_shape),
+        scratch_shapes=scratch,
+        compiler_params=pltpu.CompilerParams(vmem_limit_bytes=8 * MIB),
         cost_estimate=NOTHING,
         name="spread_panel",
-    )(sizes, pair, fock, *folded)
+    )(sizes, pair, *folded, *extra)
 
 
 def after(array, *others):
@@ -190,8 +205,8 @@
 
 
 def dress_kernel(spans, rows, members, sets, has_base, *refs):
-    amplitudes, refs = refs[0], refs[1:]
-    dense, focks, refs = refs[:sets], refs[sets:2 * sets], refs[2 * sets:]
+    amplitudes, fock, refs = refs[0], refs[1], refs[2:]
+    dense, refs = refs[:sets], refs[sets:]
     if has_base:
         refs = refs[1:]
     result, token, coupled, dressed, sems = refs
@@ -216,7 +231,7 @@
         total = jnp.zeros((height, tile), jnp.float32)
         for s, (part, k) in enumerate(slots):
             total = total + jnp.dot(
-                coupled[:, s * width:(s + 1) * width], focks[part][k, :, first:first + tile],
+                coupled[:, s * width:(s + 1) * width], fock[s, :, first:first + tile],
                 preferred_element_type=jnp.float32,
             )
         dressed[:, first:first + tile] = total.astype(dressed.dtype)
@@ -233,13 +248,13 @@
         copy.wait()
 
 
-def dress(amplitudes, spans, dense, focks, base, rows, members, out_rows):
+def dress(amplitudes, spans, dense, fock, base, rows, members, out_rows):
     height, virtuals = amplitudes.shape
     width = dense[0].shape[2]
     slots = sum(d.shape[0] for d in dense)
     vmem = pl.BlockSpec(memory_space=pltpu.VMEM)
     anywhere = pl.BlockSpec(memory_space=pl.ANY)
-    pinned = [pltpu.with_memory_space_constraint(x, pltpu.VMEM) for x in (*dense, *focks)]
+    pinned = [pltpu.with_memory_space_constraint(x, pltpu.VMEM) for x in (fock, *dense)]
     bases = [] if base is None else [base]
     return pl.pallas_call(
         functools.partial(dress_kernel, spans, rows, members, len(dense), base is not None),
@@ -291,44 +306,47 @@
         panel = jnp.swapaxes(hole_panel[:, 0, :], 0, 1)
         irrep_sizes = pltpu.with_memory_space_constraint(irrep_sizes, pltpu.HBM)
 
-        own = fold_panel(panel, irrep_sizes, pair_irreps, fold)
+        own, own_again = fold_panel(panel, irrep_sizes, pair_irreps, fold)
         across = lax.ppermute(own, axes, to_slot(2))
-        beside = lax.ppermute(own, axes, to_slot(1))
-
-        early = rounded(rows * 2 // 3, SUBLANES) if rows % SUBLANES == 0 else rows
+
+        early = rounded(rows * 3 // 5, SUBLANES) if rows % SUBLANES == 0 else rows
         if early < rows:
             top, low = cut(amplitudes, (early, rows - early))
             top = lax.ppermute(top, axes, to_group)
             lows = [low] + [lax.ppermute(low, axes, to_member(by)) for by in range(1, members)]
+            lows = jnp.concatenate(lows)
         else:
             top = lax.ppermute(amplitudes, axes, to_group)
 
-        fock = pltpu.with_memory_space_constraint(virt_fock, pltpu.HBM)
-        near_dense, near_fock = spread((0, 1), (own, beside), fock, irrep_sizes, pair_irreps)
-        top = after(top, near_dense)
+        spread_one = lambda slot, folded, *fock: spread(
+            (slot,), (folded,), irrep_sizes, pair_irreps, virtuals, *fock
+        )
+        first, fock = spread_one(0, own, virt_fock, range(groups))
+        if early < rows:
+            top = after(top, first)
+            lows = after(lows, top)
+            lows = lax.ppermute(lows, axes, to_group)
         tops = [top] + [lax.ppermute(top, axes, to_member(by)) for by in range(1, members)]
-        if early < rows:
-            lows = lax.ppermute(after(jnp.concatenate(lows), top), axes, to_group)
-        across = after(across, near_dense, top)
+        beside = lax.ppermute(after(own_again, across), axes, to_slot(1))
         both = lax.ppermute(across, axes, to_slot(1))
-        far_dense, far_fock = spread((2,), (across,), fock, irrep_sizes, pair_irreps)
-        both = after(both, far_dense)
-        last_dense, last_fock = spread((3,), (both,), fock, irrep_sizes, pair_irreps)
-        dense, focks = (near_dense, far_dense, last_dense), (near_fock, far_fock, last_fock)
+        third, = spread_one(2, across)
+        second, = spread_one(1, after(beside, third))
+        fourth, = spread_one(3, after(both, third))
+        dense = (first, second, third, fourth)
 
         if early < rows:
             result = None
             for by, piece in enumerate(tops):
                 spans = [(by, 0, early)]
-                result, token = dress(piece, spans, dense, focks, result, rows, members, out_rows)
+                result, token = dress(piece, spans, dense, fock, result, rows, members, out_rows)
             spans = [(by, early, rows - early) for by in range(members)]
             lows = after(lows, token)
-            result, _ = dress(lows, spans, dense, focks, result, rows, members, out_rows)
+            result, _ = dress(lows, spans, dense, fock, result, rows, members, out_rows)
         else:
             member = lax.axis_index("blk") % members
             ordered = jnp.roll(jnp.stack(tops), member, axis=0).reshape(out_rows, virtuals)
             spans = [(0, 0, out_rows)]
-            result, _ = dress(ordered, spans, dense, focks, None, 0, members, out_rows)
+            result, _ = dress(ordered, spans, dense, fock, None, 0, members, out_rows)
         return result[:, None, :]
 
     return local

time: 50.4 us -> 50.3 us (level)
  the two profiles are of different devices: /device:TPU:1 before, /device:TPU:4 now
where the time goes in v6:
time: 50.3 us; the launch traced here: 49.4 us
  Pallas kernels  25.3 us (50%)
  waiting for transfers between devices  15 us (30%)
  starting transfers between devices  8.28 us (16%)
  between operations  0.79 us (2%)
    pallas_call x3, Pallas kernels, dress(): pl.pallas_call(functools.partial(dress_kernel, spans, rows, members, len(...  12 us
    pallas_call x4, Pallas kernels, spread(): pl.pallas_call(functools.partial(spread_kernel, slots, fock_slots), out_s...  9.32 us
    ppermute x1, waiting for transfers between devices, local(): top = lax.ppermute(top, axes, to_group)  8.21 us
    ppermute x1, waiting for transfers between devices, local(): lows = lax.ppermute(lows, axes, to_group)  3.52 us
    ppermute x1, starting transfers between devices, local(): top = lax.ppermute(top, axes, to_group)  3.42 us
    ppermute x1, waiting for transfers between devices, local(): across = lax.ppermute(own, axes, to_slot(2))  2.93 us
    pallas_call x1, Pallas kernels, fold_panel(): pl.pallas_call(functools.partial(fold_kernel, chunk), out_shape=[pltpu.VM...  2.75 us
    ppermute x1, starting transfers between devices, local(): lows = lax.ppermute(lows, axes, to_group)  1.91 us
  transfers between devices with their start and end apart: 7, of which 4 were waited for; matrix products, arithmetic and copies ran while one was open for 0% of the time, Pallas kernels for 39%

profile of v6, /device:TPU:4, one launch (start us, length us, event | category | flops | bytes accessed | tf_op | source)
XLA Modules:
  0.0 49.4 jit_solution(125944063297818026)
XLA Ops:
  0.0 1.2 %cut_rows.1 = (bf16[144,1920]{1,0:T(8,128)(2,1)S(1)}, bf16[96,1920]{1,0:T(8,128)(2,1)S(1)}) custom-call(bf16[240,1920]{1,0:T(8,128)(2,1)} %whole.1), custom_call_target="tpu_custom_call" | custom-call | tf_op jit(solution)/shard_map/cut_rows/pallas_call | solution.py:52
  1.2 1.6 %collective-permute-start = (bf16[96,1920]{1,0:T(8,128)(2,1)S(1)}, bf16[96,1920]{1,0:T(8,128)(2,1)S(1)}, u32[]{:S(2)}, u32[]{:S(2)}) collective-permute-start(bf16[96,1920]{1,0:T(8,128)(2,1)S(1)} %get-tuple-element.15), channel_id=1, source_target_pairs={{4,0},{5,1},{6,2},{7,3},{0,4},{1,5},{2,6},{3,7},{12,8},{13,9},{14,... | collective-permute-start | bytes 1105928 | tf_op jit(solution)/shard_map/ppermute | solution.py:316
  2.7 3.4 %collective-permute-start.1 = (bf16[144,1920]{1,0:T(8,128)(2,1)S(1)}, bf16[144,1920]{1,0:T(8,128)(2,1)S(1)}, u32[]{:S(2)}, u32[]{:S(2)}) collective-permute-start(bf16[144,1920]{1,0:T(8,128)(2,1)S(1)} %get-tuple-element.16), channel_id=1, source_target_pairs={{0,0},{11,1},{16,2},{26,3},{4,4},{15,5},{20,6},{30,7},{2,8},{9,9},... | collective-permute-start | bytes 1658888 | tf_op jit(solution)/shard_map/ppermute | solution.py:315
  6.8 2.7 %fold_panel.1 = (bf16[480,512]{1,0:T(8,128)(2,1)S(1)}, bf16[480,512]{1,0:T(8,128)(2,1)S(1)}) custom-call(s32[8]{0:T(128)} %sizes.9, s32[1]{0:T(128)S(6)} %copy.22.pair, bf16[480,1920]{1,0:T(8,128)(2,1)} %bitcast.4), custom_call_target="tpu_custom_call" | custom-call | tf_op jit(solution)/shard_map/fold_panel/pallas_call | solution.py:100
  9.6 0.1 collective-permute-start.4
  9.6 4.0 %spread_panel.4 = (bf16[1,1920,512]{2,1,0:T(8,128)(2,1)S(1)}, bf16[4,512,1920]{2,1,0:T(8,128)(2,1)S(1)}) custom-call(s32[8]{0:T(128)} %sizes.9, s32[1]{0:T(128)S(6)} %copy.22.pair, bf16[480,512]{1,0:T(8,128)(2,1)S(1)} %get-tuple-element.17.refs_0_, bf16[1920,1920]{1,0:T(8,128)(2,1)} %refs_1_.1), custom_call_target="tpu_custom_call" | custom-call | tf_op jit(solution)/shard_map/spread_panel/pallas_call | solution.py:177
  13.7 0.0 collective-permute-done
  13.7 0.1 pad_maximum_fusion.refs_0_
  13.7 8.2 %collective-permute-done.1.refs_0_ = bf16[144,1920]{1,0:T(8,128)(2,1)S(1)} collective-permute-done((bf16[144,1920]{1,0:T(8,128)(2,1)S(1)}, bf16[144,1920]{1,0:T(8,128)(2,1)S(1)}, u32[]{:S(2)}, u32[]{:S(2)}) %collective-permute-start.1) | collective-permute-done | bytes 552992 | tf_op jit(solution)/shard_map/ppermute | solution.py:315
  21.9 1.9 %collective-permute-start.2 = (bf16[192,1920]{1,0:T(8,128)(2,1)S(1)}, bf16[192,1920]{1,0:T(8,128)(2,1)S(1)}, u32[]{:S(2)}, u32[]{:S(2)}) collective-permute-start(bf16[192,1920]{1,0:T(8,128)(2,1)S(1)} %after.7), channel_id=1, source_target_pairs={{0,0},{11,1},{16,2},{26,3},{4,4},{15,5},{20,6},{30,7},{2,8},{9,9},... | collective-permute-start | bytes 2211848 | tf_op jit(solution)/shard_map/ppermute | solution.py:328
  23.9 0.6 %collective-permute-start.3 = (bf16[144,1920]{1,0:T(8,128)(2,1)S(1)}, bf16[144,1920]{1,0:T(8,128)(2,1)S(1)}, u32[]{:S(2)}, u32[]{:S(2)}) collective-permute-start(bf16[144,1920]{1,0:T(8,128)(2,1)S(1)} %after.6.refs_1_.refs_0_), channel_id=1, source_target_pairs={{4,0},{5,1},{6,2},{7,3},{0,4},{1,5},{2,6},{3,7},{12,8},{13,9},{14,... | collective-permute-start | bytes 1658888 | tf_op jit(solution)/shard_map/ppermute | solution.py:329
  24.5 2.9 %collective-permute-done.4.refs_1_.refs_0_ = bf16[480,512]{1,0:T(8,128)(2,1)S(1)} collective-permute-done((bf16[480,512]{1,0:T(8,128)(2,1)S(1)}, bf16[480,512]{1,0:T(8,128)(2,1)S(1)}, u32[]{:S(2)}, u32[]{:S(2)}) %collective-permute-start.4) | collective-permute-done | bytes 491552 | tf_op jit(solution)/shard_map/ppermute | solution.py:310
  27.4 0.7 %collective-permute-start.5 = (bf16[480,512]{1,0:T(8,128)(2,1)S(1)}, bf16[480,512]{1,0:T(8,128)(2,1)S(1)}, u32[]{:S(2)}, u32[]{:S(2)}) collective-permute-start(bf16[480,512]{1,0:T(8,128)(2,1)S(1)} %after.8), channel_id=1, source_target_pairs={{1,0},{0,1},{3,2},{2,3},{5,4},{4,5},{7,6},{6,7},{9,8},{8,9},{11,10... | collective-permute-start | bytes 1474568 | tf_op jit(solution)/shard_map/ppermute | solution.py:330
  28.1 0.0 collective-permute-start.6
  28.1 1.8 %spread_panel.5.refs_1_.refs_4_ = bf16[1,1920,512]{2,1,0:T(8,128)(2,1)S(1)} custom-call(s32[8]{0:T(128)} %sizes.9, s32[1]{0:T(128)S(6)} %copy.22.pair, bf16[480,512]{1,0:T(8,128)(2,1)S(1)} %collective-permute-done.4.refs_1_.refs_0_), custom_call_target="tpu_custom_call" | custom-call | tf_op jit(solution)/shard_map/spread_panel/pallas_call | solution.py:177
  29.9 0.0 collective-permute-done.5.refs_0_
  29.9 1.8 %spread_panel.6.refs_3_ = bf16[1,1920,512]{2,1,0:T(8,128)(2,1)S(1)} custom-call(s32[8]{0:T(128)} %sizes.9, s32[1]{0:T(128)S(6)} %copy.22.pair, bf16[480,512]{1,0:T(8,128)(2,1)S(1)} %after.9.refs_0_), custom_call_target="tpu_custom_call" | custom-call | tf_op jit(solution)/shard_map/spread_panel/pallas_call | solution.py:177
  31.7 0.0 collective-permute-done.6.refs_0_
  31.7 1.8 %spread_panel.7.refs_5_ = bf16[1,1920,512]{2,1,0:T(8,128)(2,1)S(1)} custom-call(s32[8]{0:T(128)} %sizes.9, s32[1]{0:T(128)S(6)} %copy.22.pair, bf16[480,512]{1,0:T(8,128)(2,1)S(1)} %after.10.refs_0_), custom_call_target="tpu_custom_call" | custom-call | tf_op jit(solution)/shard_map/spread_panel/pallas_call | solution.py:177
  33.5 3.9 %dress_rows.3 = (bf16[480,1920]{1,0:T(8,128)(2,1)}, s32[8,128]{1,0:T(8,128)}) custom-call(bf16[144,1920]{1,0:T(8,128)(2,1)S(1)} %after.6.refs_1_.refs_0_, bf16[4,512,1920]{2,1,0:T(8,128)(2,1)S(1)} %get-tuple-element.19.refs_1_, bf16[1,1920,512]{2,1,0:T(8,128)(2,1)S(1)} %get-tuple-element.18.refs_1_.refs_2_, bf16[1,1920,512]{2,1,0:T(8,128)(2,1)S(1)} %spread_panel.6.refs_3_, ...), custom_call_target="tpu_custom_call" | custom-call | tf_op jit(solution)/shard_map/dress_rows/pallas_call | solution.py:259
  37.4 0.3 collective-permute-done.3.refs_0_
  37.7 3.3 %dress_rows.4 = (bf16[480,1920]{1,0:T(8,128)(2,1)}, s32[8,128]{1,0:T(8,128)S(1)}) custom-call(bf16[144,1920]{1,0:T(8,128)(2,1)S(1)} %collective-permute-done.3.refs_0_, bf16[4,512,1920]{2,1,0:T(8,128)(2,1)S(1)} %get-tuple-element.19.refs_1_, bf16[1,1920,512]{2,1,0:T(8,128)(2,1)S(1)} %get-tuple-element.18.refs_1_.refs_2_, ...), custom_call_target="tpu_custom_call", output_to_operand_aliasing={{0}: (6, {})} | custom-call | tf_op jit(solution)/shard_map/dress_rows/pallas_call | solution.py:259
  41.1 3.5 %collective-permute-done.2.refs_0_ = bf16[192,1920]{1,0:T(8,128)(2,1)S(1)} collective-permute-done((bf16[192,1920]{1,0:T(8,128)(2,1)S(1)}, bf16[192,1920]{1,0:T(8,128)(2,1)S(1)}, u32[]{:S(2)}, u32[]{:S(2)}) %collective-permute-start.2) | collective-permute-done | bytes 737312 | tf_op jit(solution)/shard_map/ppermute | solution.py:328
  44.6 4.8 %dress_rows.5 = (bf16[480,1920]{1,0:T(8,128)(2,1)}, s32[8,128]{1,0:T(8,128)}) custom-call(bf16[192,1920]{1,0:T(8,128)(2,1)S(1)} %after.11.refs_0_, bf16[4,512,1920]{2,1,0:T(8,128)(2,1)S(1)} %get-tuple-element.19.refs_1_, bf16[1,1920,512]{2,1,0:T(8,128)(2,1)S(1)} %get-tuple-element.18.refs_1_.refs_2_, ...), custom_call_target="tpu_custom_call", output_to_operand_aliasing={{0}: (6, {})} | custom-call | tf_op jit(solution)/shard_map/dress_rows/pallas_call | solution.py:259
  (6 shorter events, 0.0 us)
Async XLA Ops:
  1.2 12.5 %collective-permute-start = (bf16[96,1920]{1,0:T(8,128)(2,1)S(1)}, bf16[96,1920]{1,0:T(8,128)(2,1)S(1)}, u32[]{:S(2)}, u32[]{:S(2)}) collective-permute-start(bf16[96,1920]{1,0:T(8,128)(2,1)S(1)} %get-tuple-element.15), channel_id=1, source_target_pairs={{4,0},{5,1},{6,2},{7,3},{0,4},{1,5},{2,6},{3,7},{12,8},{13,9},{14,... | collective-permute-start | bytes 1105928 | tf_op jit(solution)/shard_map/ppermute | solution.py:316
  2.7 19.2 %collective-permute-start.1 = (bf16[144,1920]{1,0:T(8,128)(2,1)S(1)}, bf16[144,1920]{1,0:T(8,128)(2,1)S(1)}, u32[]{:S(2)}, u32[]{:S(2)}) collective-permute-start(bf16[144,1920]{1,0:T(8,128)(2,1)S(1)} %get-tuple-element.16), channel_id=1, source_target_pairs={{0,0},{11,1},{16,2},{26,3},{4,4},{15,5},{20,6},{30,7},{2,8},{9,9},... | collective-permute-start | bytes 1658888 | tf_op jit(solution)/shard_map/ppermute | solution.py:315
  9.6 17.8 %collective-permute-start.4 = (bf16[480,512]{1,0:T(8,128)(2,1)S(1)}, bf16[480,512]{1,0:T(8,128)(2,1)S(1)}, u32[]{:S(2)}, u32[]{:S(2)}) collective-permute-start(bf16[480,512]{1,0:T(8,128)(2,1)S(1)} %get-tuple-element.17.refs_0_), channel_id=1, source_target_pairs={{2,0},{3,1},{0,2},{1,3},{6,4},{7,5},{4,6},{5,7},{10,8},{11,9},{8,1... | collective-permute-start | bytes 1474568 | tf_op jit(solution)/shard_map/ppermute | solution.py:310
  21.9 22.6 %collective-permute-start.2 = (bf16[192,1920]{1,0:T(8,128)(2,1)S(1)}, bf16[192,1920]{1,0:T(8,128)(2,1)S(1)}, u32[]{:S(2)}, u32[]{:S(2)}) collective-permute-start(bf16[192,1920]{1,0:T(8,128)(2,1)S(1)} %after.7), channel_id=1, source_target_pairs={{0,0},{11,1},{16,2},{26,3},{4,4},{15,5},{20,6},{30,7},{2,8},{9,9},... | collective-permute-start | bytes 2211848 | tf_op jit(solution)/shard_map/ppermute | solution.py:328
  23.9 13.9 %collective-permute-start.3 = (bf16[144,1920]{1,0:T(8,128)(2,1)S(1)}, bf16[144,1920]{1,0:T(8,128)(2,1)S(1)}, u32[]{:S(2)}, u32[]{:S(2)}) collective-permute-start(bf16[144,1920]{1,0:T(8,128)(2,1)S(1)} %after.6.refs_1_.refs_0_), channel_id=1, source_target_pairs={{4,0},{5,1},{6,2},{7,3},{0,4},{1,5},{2,6},{3,7},{12,8},{13,9},{14,... | collective-permute-start | bytes 1658888 | tf_op jit(solution)/shard_map/ppermute | solution.py:329
  27.4 2.5 %collective-permute-start.5 = (bf16[480,512]{1,0:T(8,128)(2,1)S(1)}, bf16[480,512]{1,0:T(8,128)(2,1)S(1)}, u32[]{:S(2)}, u32[]{:S(2)}) collective-permute-start(bf16[480,512]{1,0:T(8,128)(2,1)S(1)} %after.8), channel_id=1, source_target_pairs={{1,0},{0,1},{3,2},{2,3},{5,4},{4,5},{7,6},{6,7},{9,8},{8,9},{11,10... | collective-permute-start | bytes 1474568 | tf_op jit(solution)/shard_map/ppermute | solution.py:330
  28.1 3.6 %collective-permute-start.6 = (bf16[480,512]{1,0:T(8,128)(2,1)S(1)}, bf16[480,512]{1,0:T(8,128)(2,1)S(1)}, u32[]{:S(2)}, u32[]{:S(2)}) collective-permute-start(bf16[480,512]{1,0:T(8,128)(2,1)S(1)} %collective-permute-done.4.refs_1_.refs_0_), channel_id=1, source_target_pairs={{1,0},{0,1},{3,2},{2,3},{5,4},{4,5},{7,6},{6,7},{9,8},{8,9},{11,10... | collective-permute-start | bytes 1474568 | tf_op jit(solution)/shard_map/ppermute | solution.py:331

commit v7 on v6

--- a/solution.py
+++ b/solution.py
@@ -75,7 +75,7 @@
     for k, copy in enumerate(copies):
         copy.wait()
 
-        @pl.loop(0, chunk // step)
+        @pl.loop(0, chunk // step, unroll=True)
         def _(i):
             first = pl.multiple_of(k * chunk + i * step, SUBLANES)
             here = pl.ds(first, step)
@@ -146,7 +146,7 @@
         low = jnp.concatenate([low] * (step // 8))
         high = jnp.concatenate([high] * (step // 8))
 
-        @pl.loop(0, virtuals // step)
+        @pl.loop(0, virtuals // step, unroll=4)
         def _(i):
             first = pl.multiple_of(i * step, step)
             source = pl.multiple_of(lax.rem(first, fold), step)
@@ -309,7 +309,7 @@
         own, own_again = fold_panel(panel, irrep_sizes, pair_irreps, fold)
         across = lax.ppermute(own, axes, to_slot(2))
 
-        early = rounded(rows * 3 // 5, SUBLANES) if rows % SUBLANES == 0 else rows
+        early = rounded(rows * 2 // 3, SUBLANES) if rows % SUBLANES == 0 else rows
         if early < rows:
             top, low = cut(amplitudes, (early, rows - early))
             top = lax.ppermute(top, axes, to_group)
@@ -327,10 +327,11 @@
             lows = after(lows, top)
             lows = lax.ppermute(lows, axes, to_group)
         tops = [top] + [lax.ppermute(top, axes, to_member(by)) for by in range(1, members)]
-        beside = lax.ppermute(after(own_again, across), axes, to_slot(1))
+        beside = lax.ppermute(own_again, axes, to_slot(1))
+        second, = spread_one(1, beside)
+        across = after(across, second)
         both = lax.ppermute(across, axes, to_slot(1))
         third, = spread_one(2, across)
-        second, = spread_one(1, after(beside, third))
         fourth, = spread_one(3, after(both, third))
         dense = (first, second, third, fourth)
 

time: 50.3 us -> 48 us (0.954)
  waiting for transfers between devices: 15 us -> 11.1 us
  starting transfers between devices: 8.28 us -> 10.9 us
  Pallas kernels: 25.3 us -> 24.7 us
    ppermute x1, waiting for transfers between devices: 8.21 us -> 6.13 us  [local(): top = lax.ppermute(top, axes, to_group)]
    ppermute x1, starting transfers between devices: 0.72 us -> 1.93 us  [local(): beside = lax.ppermute(own_again, axes, to_slot(1))]
    ppermute x1, starting transfers between devices: 0.6 us -> 1.49 us  [local(): lax.ppermute(top, axes, to_member(by))]
    ppermute x1, waiting for transfers between devices: 3.52 us -> 2.74 us  [local(): lows = lax.ppermute(lows, axes, to_group)]
    ppermute x1, waiting for transfers between devices: 2.93 us -> 2.17 us  [local(): across = lax.ppermute(own, axes, to_slot(2))]
    ppermute x1, starting transfers between devices: 0.01 us -> 0.54 us  [local(): both = lax.ppermute(across, axes, to_slot(1))]
  transfers between devices with their start and end apart: 7 -> 7, of which waited for: 4 -> 3; matrix products, arithmetic and copies ran while one was open for 0% -> 0% of each run, Pallas kernels for 39% -> 41%
where the time goes in v7:
time: 48 us; the launch traced here: 47.4 us
  Pallas kernels  24.7 us (51%)
  waiting for transfers between devices  11.1 us (23%)
  starting transfers between devices  10.9 us (23%)
  between operations  0.78 us (2%)
    pallas_call x3, Pallas kernels, dress(): pl.pallas_call(functools.partial(dress_kernel, spans, rows, members, len(...  12 us
    pallas_call x4, Pallas kernels, spread(): pl.pallas_call(functools.partial(spread_kernel, slots, fock_slots), out_s...  8.84 us
    ppermute x1, waiting for transfers between devices, local(): top = lax.ppermute(top, axes, to_group)  6.13 us
    ppermute x1, starting transfers between devices, local(): top = lax.ppermute(top, axes, to_group)  3.43 us
    ppermute x1, waiting for transfers between devices, local(): lows = lax.ppermute(lows, axes, to_group)  2.74 us
    pallas_call x1, Pallas kernels, fold_panel(): pl.pallas_call(functools.partial(fold_kernel, chunk), out_shape=[pltpu.VM...  2.7 us
    ppermute x1, waiting for transfers between devices, local(): across = lax.ppermute(own, axes, to_slot(2))  2.17 us
    ppermute x1, starting transfers between devices, local(): beside = lax.ppermute(own_again, axes, to_slot(1))  1.93 us
  transfers between devices with their start and end apart: 7, of which 3 were waited for; matrix products, arithmetic and copies ran while one was open for 0% of the time, Pallas kernels for 41%

profile of v7, /device:TPU:4, one launch (start us, length us, event | category | flops | bytes accessed | tf_op | source)
XLA Modules:
  0.0 47.4 jit_solution(1367413695277571431)
XLA Ops:
  0.0 1.2 %cut_rows.1 = (bf16[160,1920]{1,0:T(8,128)(2,1)S(1)}, bf16[80,1920]{1,0:T(8,128)(2,1)S(1)}) custom-call(bf16[240,1920]{1,0:T(8,128)(2,1)} %whole.1), custom_call_target="tpu_custom_call" | custom-call | tf_op jit(solution)/shard_map/cut_rows/pallas_call | solution.py:52
  1.2 3.4 %collective-permute-start.1 = (bf16[160,1920]{1,0:T(8,128)(2,1)S(1)}, bf16[160,1920]{1,0:T(8,128)(2,1)S(1)}, u32[]{:S(2)}, u32[]{:S(2)}) collective-permute-start(bf16[160,1920]{1,0:T(8,128)(2,1)S(1)} %get-tuple-element.16), channel_id=1, source_target_pairs={{0,0},{11,1},{16,2},{26,3},{4,4},{15,5},{20,6},{30,7},{2,8},{9,9},... | collective-permute-start | bytes 1843208 | tf_op jit(solution)/shard_map/ppermute | solution.py:315
  4.6 1.6 %collective-permute-start = (bf16[80,1920]{1,0:T(8,128)(2,1)S(1)}, bf16[80,1920]{1,0:T(8,128)(2,1)S(1)}, u32[]{:S(2)}, u32[]{:S(2)}) collective-permute-start(bf16[80,1920]{1,0:T(8,128)(2,1)S(1)} %get-tuple-element.15), channel_id=1, source_target_pairs={{4,0},{5,1},{6,2},{7,3},{0,4},{1,5},{2,6},{3,7},{12,8},{13,9},{14,... | collective-permute-start | bytes 921608 | tf_op jit(solution)/shard_map/ppermute | solution.py:316
  6.8 2.7 %fold_panel.1 = (bf16[480,512]{1,0:T(8,128)(2,1)S(1)}, bf16[480,512]{1,0:T(8,128)(2,1)S(1)}) custom-call(s32[8]{0:T(128)} %sizes.9, s32[1]{0:T(128)S(6)} %copy.20.pair, bf16[480,1920]{1,0:T(8,128)(2,1)} %bitcast.4), custom_call_target="tpu_custom_call" | custom-call | tf_op jit(solution)/shard_map/fold_panel/pallas_call | solution.py:100
  9.5 1.9 %collective-permute-start.4 = (bf16[480,512]{1,0:T(8,128)(2,1)S(1)}, bf16[480,512]{1,0:T(8,128)(2,1)S(1)}, u32[]{:S(2)}, u32[]{:S(2)}) collective-permute-start(bf16[480,512]{1,0:T(8,128)(2,1)S(1)} %get-tuple-element.20), channel_id=1, source_target_pairs={{1,0},{0,1},{3,2},{2,3},{5,4},{4,5},{7,6},{6,7},{9,8},{8,9},{11,10... | collective-permute-start | bytes 1474568 | tf_op jit(solution)/shard_map/ppermute | solution.py:330
  11.5 0.0 collective-permute-start.5
  11.5 4.0 %spread_panel.4 = (bf16[1,1920,512]{2,1,0:T(8,128)(2,1)S(1)}, bf16[4,512,1920]{2,1,0:T(8,128)(2,1)S(1)}) custom-call(s32[8]{0:T(128)} %sizes.9, s32[1]{0:T(128)S(6)} %copy.20.pair, bf16[480,512]{1,0:T(8,128)(2,1)S(1)} %get-tuple-element.17.refs_0_, bf16[1920,1920]{1,0:T(8,128)(2,1)} %refs_1_.1), custom_call_target="tpu_custom_call" | custom-call | tf_op jit(solution)/shard_map/spread_panel/pallas_call | solution.py:177
  15.5 6.1 %collective-permute-done.1.refs_0_ = bf16[160,1920]{1,0:T(8,128)(2,1)S(1)} collective-permute-done((bf16[160,1920]{1,0:T(8,128)(2,1)S(1)}, bf16[160,1920]{1,0:T(8,128)(2,1)S(1)}, u32[]{:S(2)}, u32[]{:S(2)}) %collective-permute-start.1) | collective-permute-done | bytes 614432 | tf_op jit(solution)/shard_map/ppermute | solution.py:315
  21.6 1.5 %collective-permute-start.3 = (bf16[160,1920]{1,0:T(8,128)(2,1)S(1)}, bf16[160,1920]{1,0:T(8,128)(2,1)S(1)}, u32[]{:S(2)}, u32[]{:S(2)}) collective-permute-start(bf16[160,1920]{1,0:T(8,128)(2,1)S(1)} %after.5.refs_1_.refs_0_), channel_id=1, source_target_pairs={{4,0},{5,1},{6,2},{7,3},{0,4},{1,5},{2,6},{3,7},{12,8},{13,9},{14,... | collective-permute-start | bytes 1843208 | tf_op jit(solution)/shard_map/ppermute | solution.py:329
  23.1 0.0 collective-permute-done
  23.2 1.9 %collective-permute-start.2 = (bf16[160,1920]{1,0:T(8,128)(2,1)S(1)}, bf16[160,1920]{1,0:T(8,128)(2,1)S(1)}, u32[]{:S(2)}, u32[]{:S(2)}) collective-permute-start(bf16[160,1920]{1,0:T(8,128)(2,1)S(1)} %after.6), channel_id=1, source_target_pairs={{0,0},{11,1},{16,2},{26,3},{4,4},{15,5},{20,6},{30,7},{2,8},{9,9},... | collective-permute-start | bytes 1843208 | tf_op jit(solution)/shard_map/ppermute | solution.py:328
  25.1 0.0 collective-permute-done.4.refs_0_
  25.1 1.6 %spread_panel.5.refs_1_.refs_3_ = bf16[1,1920,512]{2,1,0:T(8,128)(2,1)S(1)} custom-call(s32[8]{0:T(128)} %sizes.9, s32[1]{0:T(128)S(6)} %copy.20.pair, bf16[480,512]{1,0:T(8,128)(2,1)S(1)} %collective-permute-done.4.refs_0_), custom_call_target="tpu_custom_call" | custom-call | tf_op jit(solution)/shard_map/spread_panel/pallas_call | solution.py:177
  26.7 2.2 %collective-permute-done.5.refs_0_ = bf16[480,512]{1,0:T(8,128)(2,1)S(1)} collective-permute-done((bf16[480,512]{1,0:T(8,128)(2,1)S(1)}, bf16[480,512]{1,0:T(8,128)(2,1)S(1)}, u32[]{:S(2)}, u32[]{:S(2)}) %collective-permute-start.5) | collective-permute-done | bytes 491552 | tf_op jit(solution)/shard_map/ppermute | solution.py:310
  28.9 0.5 %collective-permute-start.6 = (bf16[480,512]{1,0:T(8,128)(2,1)S(1)}, bf16[480,512]{1,0:T(8,128)(2,1)S(1)}, u32[]{:S(2)}, u32[]{:S(2)}) collective-permute-start(bf16[480,512]{1,0:T(8,128)(2,1)S(1)} %after.7.refs_0_), channel_id=1, source_target_pairs={{1,0},{0,1},{3,2},{2,3},{5,4},{4,5},{7,6},{6,7},{9,8},{8,9},{11,10... | collective-permute-start | bytes 1474568 | tf_op jit(solution)/shard_map/ppermute | solution.py:333
  29.4 1.6 %spread_panel.6.refs_1_.refs_4_ = bf16[1,1920,512]{2,1,0:T(8,128)(2,1)S(1)} custom-call(s32[8]{0:T(128)} %sizes.9, s32[1]{0:T(128)S(6)} %copy.20.pair, bf16[480,512]{1,0:T(8,128)(2,1)S(1)} %after.7.refs_0_), custom_call_target="tpu_custom_call" | custom-call | tf_op jit(solution)/shard_map/spread_panel/pallas_call | solution.py:177
  31.0 0.0 collective-permute-done.6.refs_0_
  31.1 1.6 %spread_panel.7.refs_5_ = bf16[1,1920,512]{2,1,0:T(8,128)(2,1)S(1)} custom-call(s32[8]{0:T(128)} %sizes.9, s32[1]{0:T(128)S(6)} %copy.20.pair, bf16[480,512]{1,0:T(8,128)(2,1)S(1)} %after.8.refs_0_), custom_call_target="tpu_custom_call" | custom-call | tf_op jit(solution)/shard_map/spread_panel/pallas_call | solution.py:177
  32.7 4.2 %dress_rows.3 = (bf16[480,1920]{1,0:T(8,128)(2,1)}, s32[8,128]{1,0:T(8,128)}) custom-call(bf16[160,1920]{1,0:T(8,128)(2,1)S(1)} %after.5.refs_1_.refs_0_, bf16[4,512,1920]{2,1,0:T(8,128)(2,1)S(1)} %get-tuple-element.19.refs_1_, bf16[1,1920,512]{2,1,0:T(8,128)(2,1)S(1)} %get-tuple-element.18.refs_1_.refs_2_, ...), custom_call_target="tpu_custom_call" | custom-call | tf_op jit(solution)/shard_map/dress_rows/pallas_call | solution.py:259
  36.9 0.0 collective-permute-done.3.refs_0_
  36.9 3.6 %dress_rows.4 = (bf16[480,1920]{1,0:T(8,128)(2,1)}, s32[8,128]{1,0:T(8,128)S(1)}) custom-call(bf16[160,1920]{1,0:T(8,128)(2,1)S(1)} %collective-permute-done.3.refs_0_, bf16[4,512,1920]{2,1,0:T(8,128)(2,1)S(1)} %get-tuple-element.19.refs_1_, bf16[1,1920,512]{2,1,0:T(8,128)(2,1)S(1)} %get-tuple-element.18.refs_1_.refs_2_, ...), custom_call_target="tpu_custom_call", output_to_operand_aliasing={{0}: (6, {})} | custom-call | tf_op jit(solution)/shard_map/dress_rows/pallas_call | solution.py:259
  40.5 2.7 %collective-permute-done.2.refs_0_ = bf16[160,1920]{1,0:T(8,128)(2,1)S(1)} collective-permute-done((bf16[160,1920]{1,0:T(8,128)(2,1)S(1)}, bf16[160,1920]{1,0:T(8,128)(2,1)S(1)}, u32[]{:S(2)}, u32[]{:S(2)}) %collective-permute-start.2) | collective-permute-done | bytes 614432 | tf_op jit(solution)/shard_map/ppermute | solution.py:328
  43.2 4.2 %dress_rows.5 = (bf16[480,1920]{1,0:T(8,128)(2,1)}, s32[8,128]{1,0:T(8,128)}) custom-call(bf16[160,1920]{1,0:T(8,128)(2,1)S(1)} %after.9.refs_0_, bf16[4,512,1920]{2,1,0:T(8,128)(2,1)S(1)} %get-tuple-element.19.refs_1_, bf16[1,1920,512]{2,1,0:T(8,128)(2,1)S(1)} %get-tuple-element.18.refs_1_.refs_2_, ...), custom_call_target="tpu_custom_call", output_to_operand_aliasing={{0}: (6, {})} | custom-call | tf_op jit(solution)/shard_map/dress_rows/pallas_call | solution.py:259
  (6 shorter events, 0.1 us)
Async XLA Ops:
  1.2 20.4 %collective-permute-start.1 = (bf16[160,1920]{1,0:T(8,128)(2,1)S(1)}, bf16[160,1920]{1,0:T(8,128)(2,1)S(1)}, u32[]{:S(2)}, u32[]{:S(2)}) collective-permute-start(bf16[160,1920]{1,0:T(8,128)(2,1)S(1)} %get-tuple-element.16), channel_id=1, source_target_pairs={{0,0},{11,1},{16,2},{26,3},{4,4},{15,5},{20,6},{30,7},{2,8},{9,9},... | collective-permute-start | bytes 1843208 | tf_op jit(solution)/shard_map/ppermute | solution.py:315
  4.6 18.5 %collective-permute-start = (bf16[80,1920]{1,0:T(8,128)(2,1)S(1)}, bf16[80,1920]{1,0:T(8,128)(2,1)S(1)}, u32[]{:S(2)}, u32[]{:S(2)}) collective-permute-start(bf16[80,1920]{1,0:T(8,128)(2,1)S(1)} %get-tuple-element.15), channel_id=1, source_target_pairs={{4,0},{5,1},{6,2},{7,3},{0,4},{1,5},{2,6},{3,7},{12,8},{13,9},{14,... | collective-permute-start | bytes 921608 | tf_op jit(solution)/shard_map/ppermute | solution.py:316
  9.5 15.6 %collective-permute-start.4 = (bf16[480,512]{1,0:T(8,128)(2,1)S(1)}, bf16[480,512]{1,0:T(8,128)(2,1)S(1)}, u32[]{:S(2)}, u32[]{:S(2)}) collective-permute-start(bf16[480,512]{1,0:T(8,128)(2,1)S(1)} %get-tuple-element.20), channel_id=1, source_target_pairs={{1,0},{0,1},{3,2},{2,3},{5,4},{4,5},{7,6},{6,7},{9,8},{8,9},{11,10... | collective-permute-start | bytes 1474568 | tf_op jit(solution)/shard_map/ppermute | solution.py:330
  11.5 17.4 %collective-permute-start.5 = (bf16[480,512]{1,0:T(8,128)(2,1)S(1)}, bf16[480,512]{1,0:T(8,128)(2,1)S(1)}, u32[]{:S(2)}, u32[]{:S(2)}) collective-permute-start(bf16[480,512]{1,0:T(8,128)(2,1)S(1)} %get-tuple-element.17.refs_0_), channel_id=1, source_target_pairs={{2,0},{3,1},{0,2},{1,3},{6,4},{7,5},{4,6},{5,7},{10,8},{11,9},{8,1... | collective-permute-start | bytes 1474568 | tf_op jit(solution)/shard_map/ppermute | solution.py:310
  21.6 15.3 %collective-permute-start.3 = (bf16[160,1920]{1,0:T(8,128)(2,1)S(1)}, bf16[160,1920]{1,0:T(8,128)(2,1)S(1)}, u32[]{:S(2)}, u32[]{:S(2)}) collective-permute-start(bf16[160,1920]{1,0:T(8,128)(2,1)S(1)} %after.5.refs_1_.refs_0_), channel_id=1, source_target_pairs={{4,0},{5,1},{6,2},{7,3},{0,4},{1,5},{2,6},{3,7},{12,8},{13,9},{14,... | collective-permute-start | bytes 1843208 | tf_op jit(solution)/shard_map/ppermute | solution.py:329
  23.2 20.1 %collective-permute-start.2 = (bf16[160,1920]{1,0:T(8,128)(2,1)S(1)}, bf16[160,1920]{1,0:T(8,128)(2,1)S(1)}, u32[]{:S(2)}, u32[]{:S(2)}) collective-permute-start(bf16[160,1920]{1,0:T(8,128)(2,1)S(1)} %after.6), channel_id=1, source_target_pairs={{0,0},{11,1},{16,2},{26,3},{4,4},{15,5},{20,6},{30,7},{2,8},{9,9},... | collective-permute-start | bytes 1843208 | tf_op jit(solution)/shard_map/ppermute | solution.py:328
  28.9 2.2 %collective-permute-start.6 = (bf16[480,512]{1,0:T(8,128)(2,1)S(1)}, bf16[480,512]{1,0:T(8,128)(2,1)S(1)}, u32[]{:S(2)}, u32[]{:S(2)}) collective-permute-start(bf16[480,512]{1,0:T(8,128)(2,1)S(1)} %after.7.refs_0_), channel_id=1, source_target_pairs={{1,0},{0,1},{3,2},{2,3},{5,4},{4,5},{7,6},{6,7},{9,8},{8,9},{11,10... | collective-permute-start | bytes 1474568 | tf_op jit(solution)/shard_map/ppermute | solution.py:333

commit v8 on v7

--- a/solution.py
+++ b/solution.py
@@ -113,77 +113,80 @@
     )(sizes, pair, pltpu.with_memory_space_constraint(panel, pltpu.HBM))
 
 
-def spread_kernel(slots, fock_slots, sizes, pair, *refs):
-    count, loads = len(slots), len(fock_slots)
-    folded, refs = refs[:count], refs[count:]
-    if loads:
-        (fock, dense, fock_out, bounds, turned, sems) = refs
+def spread_kernel(slot, groups, first, sizes, pair, folded, other, *refs):
+    if first:
+        dense, fock_out, bounds, turned, sems = refs
     else:
-        (dense, bounds, turned) = refs
-    quarter, fold = folded[0].shape
-    virtuals = dense.shape[1]
-    width = dense.shape[2]
+        dense, bounds, turned = refs
+    quarter, fold = folded.shape
+    virtuals, total = dense.shape
+    width = total // groups
     group = lax.axis_index("grp")
     copies = []
-    for k, slot in enumerate(fock_slots):
-        first = pl.multiple_of(jnp.bitwise_xor(group, slot) * quarter, SUBLANES)
-        copies.append(pltpu.make_async_copy(
-            fock.at[pl.ds(first, quarter)], fock_out.at[k, pl.ds(0, quarter)], sems.at[k]
-        ))
-        copies[-1].start()
-        if width > quarter:
-            fock_out[k, quarter:width, :] = jnp.zeros((width - quarter, virtuals), fock_out.dtype)
+    if first:
+        for k in range(groups):
+            start = pl.multiple_of(jnp.bitwise_xor(group, k) * quarter, SUBLANES)
+            copies.append(pltpu.make_async_copy(
+                other.at[pl.ds(start, quarter)], fock_out.at[pl.ds(k * width, quarter)], sems.at[k]
+            ))
+            copies[-1].start()
+            if width > quarter:
+                fock_out[k * width + quarter:(k + 1) * width, :] = jnp.zeros(
+                    (width - quarter, virtuals), fock_out.dtype
+                )
     fill_bounds(sizes, bounds)
     step = 32
-    for k, slot in enumerate(slots):
-        values = folded[k][...].astype(jnp.float32)
-        if width > quarter:
-            values = jnp.concatenate([values, jnp.zeros((width - quarter, fold), jnp.float32)])
-        turned[...] = values.T
-        start = jnp.bitwise_xor(group, slot) * quarter
-        b = start + lax.broadcasted_iota(jnp.int32, (8, width), 1)
-        low, high = wanted_range(b, pair, bounds, sizes.shape[0])
-        low = jnp.concatenate([low] * (step // 8))
-        high = jnp.concatenate([high] * (step // 8))
-
-        @pl.loop(0, virtuals // step, unroll=4)
-        def _(i):
-            first = pl.multiple_of(i * step, step)
-            source = pl.multiple_of(lax.rem(first, fold), step)
-            c = first + lax.broadcasted_iota(jnp.int32, (step, width), 0)
-            kept = jnp.where((c >= low) & (c < high), turned[pl.ds(source, step), :], 0.0)
-            dense[k, pl.ds(first, step), :] = kept.astype(dense.dtype)
+    values = folded[...].astype(jnp.float32)
+    if width > quarter:
+        values = jnp.concatenate([values, jnp.zeros((width - quarter, fold), jnp.float32)])
+    turned[...] = values.T
+    start = jnp.bitwise_xor(group, slot) * quarter
+    b = start + lax.broadcasted_iota(jnp.int32, (8, width), 1)
+    low, high = wanted_range(b, pair, bounds, sizes.shape[0])
+    low = jnp.concatenate([low] * (step // 8))
+    high = jnp.concatenate([high] * (step // 8))
+
+    @pl.loop(0, virtuals // step, unroll=4)
+    def _(i):
+        row = pl.multiple_of(i * step, step)
+        source = pl.multiple_of(lax.rem(row, fold), step)
+        c = row + lax.broadcasted_iota(jnp.int32, (step, width), 0)
+        kept = jnp.where((c >= low) & (c < high), turned[pl.ds(source, step), :], 0.0)
+        dense[pl.ds(row, step), slot * width:(slot + 1) * width] = kept.astype(dense.dtype)
 
     for copy in copies:
         copy.wait()
 
 
-def spread(slots, folded, sizes, pair, virtuals, fock=None, fock_slots=()):
-    quarter, fold = folded[0].shape
+def spread(slot, groups, folded, sizes, pair, *, fock=None, dense=None):
+    quarter, fold = folded.shape
+    first = dense is None
+    virtuals = fock.shape[0] if first else dense.shape[0]
     width = rounded(quarter, LANES)
-    count, loads = len(slots), len(fock_slots)
     smem = pl.BlockSpec(memory_space=pltpu.SMEM)
     vmem = pl.BlockSpec(memory_space=pltpu.VMEM)
-    out_shape = [pltpu.VMEM((count, virtuals, width), folded[0].dtype)]
+    out_shape = [pltpu.VMEM((virtuals, groups * width), folded.dtype)]
     scratch = [
         pltpu.SMEM((sizes.shape[0] + 1,), jnp.int32),
         pltpu.VMEM((fold, width), jnp.float32),
     ]
-    extra = []
-    if loads:
-        out_shape.append(pltpu.VMEM((loads, width, virtuals), fock.dtype))
-        scratch.append(pltpu.SemaphoreType.DMA((loads,)))
-        extra.append(pltpu.with_memory_space_constraint(fock, pltpu.HBM))
-    return pl.pallas_call(
-        functools.partial(spread_kernel, slots, fock_slots),
+    if first:
+        out_shape.append(pltpu.VMEM((groups * width, virtuals), fock.dtype))
+        scratch.append(pltpu.SemaphoreType.DMA((groups,)))
+        other = pltpu.with_memory_space_constraint(fock, pltpu.HBM)
+    else:
+        other = pltpu.with_memory_space_constraint(dense, pltpu.VMEM)
+    return pl.pallas_call(
+        functools.partial(spread_kernel, slot, groups, first),
         out_shape=out_shape,
-        in_specs=[smem, smem] + [vmem] * count + [pl.BlockSpec(memory_space=pl.ANY)] * len(extra),
+        in_specs=[smem, smem, vmem, pl.BlockSpec(memory_space=pl.ANY)],
         out_specs=[vmem] * len(out_shape),
+        input_output_aliases={} if first else {3: 0},
         scratch_shapes=scratch,
         compiler_params=pltpu.CompilerParams(vmem_limit_bytes=8 * MIB),
         cost_estimate=NOTHING,
         name="spread_panel",
-    )(sizes, pair, *folded, *extra)
+    )(sizes, pair, folded, other)
 
 
 def after(array, *others):
@@ -204,37 +207,26 @@
     return [(first, min(tile, total - first)) for first in range(0, total, tile)]
 
 
-def dress_kernel(spans, rows, members, sets, has_base, *refs):
-    amplitudes, fock, refs = refs[0], refs[1], refs[2:]
-    dense, refs = refs[:sets], refs[sets:]
+def dress_kernel(spans, rows, members, has_base, amplitudes, dense, fock, *refs):
     if has_base:
         refs = refs[1:]
     result, token, coupled, dressed, sems = refs
     token[...] = jnp.zeros_like(token)
-    height = amplitudes.shape[0]
-    virtuals = amplitudes.shape[1]
-    width = dense[0].shape[2]
-    slots = [(part, k) for part in range(sets) for k in range(dense[part].shape[0])]
+    virtuals, total = dense.shape
     block = lax.axis_index("blk")
     places = [
         pl.multiple_of(lax.rem(block + by, members) * rows + offset, SUBLANES)
         for by, offset, _ in spans
     ]
-    for s, (part, k) in enumerate(slots):
-        for first, tile in column_tiles(width, 256):
-            coupled[:, s * width + first:s * width + first + tile] = jnp.dot(
-                amplitudes[...], dense[part][k, :, first:first + tile],
-                preferred_element_type=jnp.float32,
-            ).astype(coupled.dtype)
+    for first, tile in column_tiles(total, 512):
+        coupled[:, first:first + tile] = jnp.dot(
+            amplitudes[...], dense[:, first:first + tile], preferred_element_type=jnp.float32
+        ).astype(coupled.dtype)
     copies = []
     for t, (first, tile) in enumerate(column_tiles(virtuals, 512)):
-        total = jnp.zeros((height, tile), jnp.float32)
-        for s, (part, k) in enumerate(slots):
-            total = total + jnp.dot(
-                coupled[:, s * width:(s + 1) * width], fock[s, :, first:first + tile],
-                preferred_element_type=jnp.float32,
-            )
-        dressed[:, first:first + tile] = total.astype(dressed.dtype)
+        dressed[:, first:first + tile] = jnp.dot(
+            coupled[...], fock[:, first:first + tile], preferred_element_type=jnp.float32
+        ).astype(dressed.dtype)
         begin = 0
         for p, (_, _, size) in enumerate(spans):
             copies.append(pltpu.make_async_copy(
@@ -250,23 +242,21 @@
 
 def dress(amplitudes, spans, dense, fock, base, rows, members, out_rows):
     height, virtuals = amplitudes.shape
-    width = dense[0].shape[2]
-    slots = sum(d.shape[0] for d in dense)
     vmem = pl.BlockSpec(memory_space=pltpu.VMEM)
     anywhere = pl.BlockSpec(memory_space=pl.ANY)
-    pinned = [pltpu.with_memory_space_constraint(x, pltpu.VMEM) for x in (fock, *dense)]
+    pinned = [pltpu.with_memory_space_constraint(x, pltpu.VMEM) for x in (dense, fock)]
     bases = [] if base is None else [base]
     return pl.pallas_call(
-        functools.partial(dress_kernel, spans, rows, members, len(dense), base is not None),
+        functools.partial(dress_kernel, spans, rows, members, base is not None),
         out_shape=(
             jax.ShapeDtypeStruct((out_rows, virtuals), amplitudes.dtype),
             pltpu.VMEM((8, LANES), jnp.int32),
         ),
-        in_specs=[vmem] * (1 + len(pinned)) + [anywhere] * len(bases),
+        in_specs=[vmem] * 3 + [anywhere] * len(bases),
         out_specs=(anywhere, vmem),
-        input_output_aliases={} if base is None else {1 + len(pinned): 0},
+        input_output_aliases={} if base is None else {3: 0},
         scratch_shapes=[
-            pltpu.VMEM((height, slots * width), amplitudes.dtype),
+            pltpu.VMEM((height, dense.shape[1]), amplitudes.dtype),
             pltpu.VMEM((height, virtuals), amplitudes.dtype),
             pltpu.SemaphoreType.DMA((len(spans), len(column_tiles(virtuals, 512)))),
         ],
@@ -285,13 +275,13 @@
 
     everyone = [(h, l, g) for h in range(groups) for l in range(members) for g in range(groups)]
 
-    def source_copy(hi, grp):
-        if groups != 4:
-            return hi
-        order = {0: (0, 2, 1, 3), 1: (3, 1, 2, 0), 2: (0, 3, 2, 1), 3: (2, 0, 1, 3)}
-        return order[grp][hi]
-
-    to_group = [(device(g, l, source_copy(h, g)), device(h, l, g)) for h, l, g in everyone]
+    if groups == 4:
+        copies = ((None, 1, 0, 3), (0, None, 2, 1), (0, 2, None, 3), (2, 0, 3, None))
+    else:
+        copies = [[None if h == g else h for h in range(groups)] for g in range(groups)]
+    to_group = [
+        (device(g, l, copies[g][h]), device(h, l, g)) for h, l, g in everyone if h != g
+    ]
 
     def to_member(by):
         return [(device(h, (l + by) % members, g), device(h, l, g)) for h, l, g in everyone]
@@ -308,32 +298,34 @@
 
         own, own_again = fold_panel(panel, irrep_sizes, pair_irreps, fold)
         across = lax.ppermute(own, axes, to_slot(2))
+        beside = lax.ppermute(own_again, axes, to_slot(1))
+
+        owner = lax.axis_index("blk") // members == lax.axis_index("grp")
+
+        def arrived(piece, kept):
+            return jnp.where(owner, kept, piece)
 
         early = rounded(rows * 2 // 3, SUBLANES) if rows % SUBLANES == 0 else rows
         if early < rows:
             top, low = cut(amplitudes, (early, rows - early))
-            top = lax.ppermute(top, axes, to_group)
             lows = [low] + [lax.ppermute(low, axes, to_member(by)) for by in range(1, members)]
             lows = jnp.concatenate(lows)
         else:
-            top = lax.ppermute(amplitudes, axes, to_group)
-
-        spread_one = lambda slot, folded, *fock: spread(
-            (slot,), (folded,), irrep_sizes, pair_irreps, virtuals, *fock
-        )
-        first, fock = spread_one(0, own, virt_fock, range(groups))
+            top = amplitudes
+        top = arrived(lax.ppermute(top, axes, to_group), top)
+
+        spread_one = functools.partial(spread, sizes=irrep_sizes, pair=pair_irreps)
+        dense, fock = spread_one(0, groups, own, fock=virt_fock)
+        top = after(top, fock)
         if early < rows:
-            top = after(top, first)
             lows = after(lows, top)
-            lows = lax.ppermute(lows, axes, to_group)
+            late = lax.ppermute(lows, axes, to_group)
         tops = [top] + [lax.ppermute(top, axes, to_member(by)) for by in range(1, members)]
-        beside = lax.ppermute(own_again, axes, to_slot(1))
-        second, = spread_one(1, beside)
-        across = after(across, second)
+        dense, = spread_one(1, groups, beside, dense=dense)
+        across = after(across, dense)
         both = lax.ppermute(across, axes, to_slot(1))
-        third, = spread_one(2, across)
-        fourth, = spread_one(3, after(both, third))
-        dense = (first, second, third, fourth)
+        dense, = spread_one(2, groups, across, dense=dense)
+        dense, = spread_one(3, groups, both, dense=dense)
 
         if early < rows:
             result = None
@@ -341,7 +333,7 @@
                 spans = [(by, 0, early)]
                 result, token = dress(piece, spans, dense, fock, result, rows, members, out_rows)
             spans = [(by, early, rows - early) for by in range(members)]
-            lows = after(lows, token)
+            lows = arrived(after(late, token), lows)
             result, _ = dress(lows, spans, dense, fock, result, rows, members, out_rows)
         else:
             member = lax.axis_index("blk") % members

time: 48 us -> 51.8 us (1.079)
  local copies, waits for them, and re-layouts: 0 us -> 9.79 us
  waiting for transfers between devices: 11.1 us -> 2.36 us
  other arithmetic: 0.04 us -> 1.77 us
    unnamed x0 -> x12, local copies, waits for them, and re-layouts: none -> 9.79 us
    ppermute x2, waiting for transfers between devices: 8.88 us -> 2 us  [the longest x1 2 us: local(): late = lax.ppermute(lows, axes, to_group)]
    ppermute x2, starting transfers between devices: 5.35 us -> 2.58 us  [the longest x1 1.29 us: local(): top = arrived(lax.ppermute(top, axes, to_group), top)]
    ppermute x1, starting transfers between devices: 1.93 us -> 4.34 us  [local(): beside = lax.ppermute(own_again, axes, to_slot(1))]
    ppermute x1, waiting for transfers between devices: 2.17 us -> 0.01 us  [local(): across = lax.ppermute(own, axes, to_slot(2))]
    concatenate x1, other arithmetic: 0.04 us -> 1.55 us  [local(): lows = jnp.concatenate(lows)]
    ppermute x1, starting transfers between devices: 0.54 us -> 1.32 us  [local(): both = lax.ppermute(across, axes, to_slot(1))]
  transfers between devices with their start and end apart: 7 -> 7, of which waited for: 3 -> 2; matrix products, arithmetic and copies ran while one was open for 0% -> 3% of each run, Pallas kernels for 41% -> 39%
where the time goes in v8:
time: 51.8 us; the launch traced here: 50.8 us
  Pallas kernels  25.1 us (48%)
  starting transfers between devices  11.1 us (21%)
  local copies, waits for them, and re-layouts  9.79 us (19%)
  waiting for transfers between devices  2.36 us (5%)
  other arithmetic  1.77 us (3%)
  between operations  0.82 us (2%)
    pallas_call x3, Pallas kernels, dress(): pl.pallas_call(functools.partial(dress_kernel, spans, rows, members, base...  12.1 us
    unnamed x12, local copies, waits for them, and re-layouts  9.79 us
    pallas_call x4, Pallas kernels, spread(): pl.pallas_call(functools.partial(spread_kernel, slot, groups, first), out...  9.1 us
    ppermute x1, starting transfers between devices, local(): beside = lax.ppermute(own_again, axes, to_slot(1))  4.34 us
    pallas_call x1, Pallas kernels, fold_panel(): pl.pallas_call(functools.partial(fold_kernel, chunk), out_shape=[pltpu.VM...  2.7 us
    ppermute x1, waiting for transfers between devices, local(): late = lax.ppermute(lows, axes, to_group)  2 us
    concatenate x1, other arithmetic, local(): lows = jnp.concatenate(lows)  1.55 us
    ppermute x1, starting transfers between devices, local(): lax.ppermute(low, axes, to_member(by))  1.49 us
  transfers between devices with their start and end apart: 7, of which 2 were waited for; matrix products, arithmetic and copies ran while one was open for 3% of the time, Pallas kernels for 39%

profile of v8, /device:TPU:4, one launch (start us, length us, event | category | flops | bytes accessed | tf_op | source)
XLA Modules:
  0.0 50.8 jit_solution(1905838733726042323)
XLA Ops:
  0.0 1.2 %cut_rows.1 = (bf16[160,1920]{1,0:T(8,128)(2,1)S(1)}, bf16[80,1920]{1,0:T(8,128)(2,1)S(1)}) custom-call(bf16[240,1920]{1,0:T(8,128)(2,1)} %whole.1), custom_call_target="tpu_custom_call" | custom-call | tf_op jit(solution)/shard_map/cut_rows/pallas_call | solution.py:52
  1.2 1.3 %collective-permute-start.1 = (bf16[160,1920]{1,0:T(8,128)(2,1)S(1)}, bf16[160,1920]{1,0:T(8,128)(2,1)S(1)}, u32[]{:S(2)}, u32[]{:S(2)}) collective-permute-start(bf16[160,1920]{1,0:T(8,128)(2,1)S(1)} %get-tuple-element.16), channel_id=1, source_target_pairs={{8,1},{16,2},{26,3},{12,5},{20,6},{30,7},{1,8},{18,10},{24,11},{5,... | collective-permute-start | bytes 1843208 | tf_op jit(solution)/shard_map/ppermute | solution.py:315
  3.1 2.7 %fold_panel.1 = (bf16[480,512]{1,0:T(8,128)(2,1)S(1)}, bf16[480,512]{1,0:T(8,128)(2,1)S(1)}) custom-call(s32[8]{0:T(128)} %sizes.9, s32[1]{0:T(128)S(6)} %copy.24.pair, bf16[480,1920]{1,0:T(8,128)(2,1)} %bitcast.6), custom_call_target="tpu_custom_call" | custom-call | tf_op jit(solution)/shard_map/fold_panel/pallas_call | solution.py:100
  5.8 4.3 %collective-permute-start.5 = (bf16[480,512]{1,0:T(8,128)(2,1)S(1)}, bf16[480,512]{1,0:T(8,128)(2,1)S(1)}, u32[]{:S(2)}, u32[]{:S(2)}) collective-permute-start(bf16[480,512]{1,0:T(8,128)(2,1)S(1)} %get-tuple-element.19), channel_id=1, source_target_pairs={{1,0},{0,1},{3,2},{2,3},{5,4},{4,5},{7,6},{6,7},{9,8},{8,9},{11,10... | collective-permute-start | bytes 1474568 | tf_op jit(solution)/shard_map/ppermute | solution.py:301
  10.2 0.0 collective-permute-start.4
  10.2 1.5 %collective-permute-start = (bf16[80,1920]{1,0:T(8,128)(2,1)S(1)}, bf16[80,1920]{1,0:T(8,128)(2,1)}, u32[]{:S(2)}, u32[]{:S(2)}) collective-permute-start(bf16[80,1920]{1,0:T(8,128)(2,1)S(1)} %get-tuple-element.15), channel_id=1, source_target_pairs={{4,0},{5,1},{6,2},{7,3},{0,4},{1,5},{2,6},{3,7},{12,8},{13,9},{14,... | collective-permute-start | bytes 921608 | tf_op jit(solution)/shard_map/ppermute | solution.py:311
  11.7 4.0 %spread_panel.4 = (bf16[1920,2048]{1,0:T(8,128)(2,1)S(1)}, bf16[2048,1920]{1,0:T(8,128)(2,1)S(1)}) custom-call(s32[8]{0:T(128)} %sizes.9, s32[1]{0:T(128)S(6)} %copy.24.pair, bf16[480,512]{1,0:T(8,128)(2,1)S(1)} %get-tuple-element.17.folded, bf16[1920,1920]{1,0:T(8,128)(2,1)} %other.1), custom_call_target="tpu_custom_call" | custom-call | tf_op jit(solution)/shard_map/spread_panel/pallas_call | solution.py:179
  15.7 3.1 %copy-done = bf16[1920,2048]{1,0:T(8,128)(2,1)} copy-done((bf16[1920,2048]{1,0:T(8,128)(2,1)}, bf16[1920,2048]{1,0:T(8,128)(2,1)S(1)}, u32[]{:S(2)}) %copy-start) | copy-done | bytes 7864344
  18.8 3.0 %copy-done.2 = bf16[2048,1920]{1,0:T(8,128)(2,1)} copy-done((bf16[2048,1920]{1,0:T(8,128)(2,1)}, bf16[2048,1920]{1,0:T(8,128)(2,1)S(1)}, u32[]{:S(2)}) %copy-start.2) | copy-done | bytes 7864344
  21.9 0.0 collective-permute-done.1
  21.9 0.1 broadcast_select_fusion.1.refs_0_
  22.0 3.2 %copy-done.3 = bf16[2048,1920]{1,0:T(8,128)(2,1)S(1)} copy-done((bf16[2048,1920]{1,0:T(8,128)(2,1)S(1)}, bf16[2048,1920]{1,0:T(8,128)(2,1)}, u32[]{:S(2)}) %copy-start.3) | copy-done | bytes 7864344
  25.2 1.3 %collective-permute-start.3 = (bf16[160,1920]{1,0:T(8,128)(2,1)S(1)}, bf16[160,1920]{1,0:T(8,128)(2,1)S(1)}, u32[]{:S(2)}, u32[]{:S(2)}) collective-permute-start(bf16[160,1920]{1,0:T(8,128)(2,1)S(1)} %after.4.refs_1_.amplitudes), channel_id=1, source_target_pairs={{4,0},{5,1},{6,2},{7,3},{0,4},{1,5},{2,6},{3,7},{12,8},{13,9},{14,... | collective-permute-start | bytes 1843208 | tf_op jit(solution)/shard_map/ppermute | solution.py:323
  26.6 0.0 collective-permute-done
  26.6 1.6 %pad_maximum_fusion.refs_0_ = bf16[160,1920]{1,0:T(8,128)(2,1)S(1)} fusion(bf16[80,1920]{1,0:T(8,128)(2,1)} %collective-permute-done, bf16[80,1920]{1,0:T(8,128)(2,1)S(1)} %get-tuple-element.15), kind=kLoop, calls=%fused_computation | loop fusion | flops 1228800 | bytes 1228800 | tf_op jit(solution)/shard_map/concatenate | solution.py:312
  28.1 1.3 %collective-permute-start.2 = (bf16[160,1920]{1,0:T(8,128)(2,1)S(1)}, bf16[160,1920]{1,0:T(8,128)(2,1)S(1)}, u32[]{:S(2)}, u32[]{:S(2)}) collective-permute-start(bf16[160,1920]{1,0:T(8,128)(2,1)S(1)} %after.5), channel_id=1, source_target_pairs={{8,1},{16,2},{26,3},{12,5},{20,6},{30,7},{1,8},{18,10},{24,11},{5,... | collective-permute-start | bytes 1843208 | tf_op jit(solution)/shard_map/ppermute | solution.py:322
  29.4 0.0 collective-permute-done.5.folded
  29.4 0.0 copy-done.1
  29.4 1.6 %spread_panel.5.refs_1_.other = bf16[1920,2048]{1,0:T(8,128)(2,1)S(1)} custom-call(s32[8]{0:T(128)} %sizes.9, s32[1]{0:T(128)S(6)} %copy.24.pair, bf16[480,512]{1,0:T(8,128)(2,1)S(1)} %collective-permute-done.5.folded, bf16[1920,2048]{1,0:T(8,128)(2,1)S(1)} %copy-done.1), custom_call_target="tpu_custom_call", output_to_operand_aliasing={{}: (3, {})} | custom-call | tf_op jit(solution)/shard_map/spread_panel/pallas_call | solution.py:179
  31.1 0.0 collective-permute-done.4.refs_0_
  31.1 1.3 %collective-permute-start.6 = (bf16[480,512]{1,0:T(8,128)(2,1)S(1)}, bf16[480,512]{1,0:T(8,128)(2,1)S(1)}, u32[]{:S(2)}, u32[]{:S(2)}) collective-permute-start(bf16[480,512]{1,0:T(8,128)(2,1)S(1)} %after.6.folded), channel_id=1, source_target_pairs={{1,0},{0,1},{3,2},{2,3},{5,4},{4,5},{7,6},{6,7},{9,8},{8,9},{11,10... | collective-permute-start | bytes 1474568 | tf_op jit(solution)/shard_map/ppermute | solution.py:326
  32.4 1.7 %spread_panel.6.other = bf16[1920,2048]{1,0:T(8,128)(2,1)S(1)} custom-call(s32[8]{0:T(128)} %sizes.9, s32[1]{0:T(128)S(6)} %copy.24.pair, bf16[480,512]{1,0:T(8,128)(2,1)S(1)} %after.6.folded, bf16[1920,2048]{1,0:T(8,128)(2,1)S(1)} %spread_panel.5.refs_1_.other), custom_call_target="tpu_custom_call", output_to_operand_aliasing={{}: (3, {})} | custom-call | tf_op jit(solution)/shard_map/spread_panel/pallas_call | solution.py:179
  34.2 0.0 slice-start.1
  34.2 0.0 collective-permute-done.6.folded
  34.2 1.7 %spread_panel.7.dense = bf16[1920,2048]{1,0:T(8,128)(2,1)S(1)} custom-call(s32[8]{0:T(128)} %sizes.9, s32[1]{0:T(128)S(6)} %copy.24.pair, bf16[480,512]{1,0:T(8,128)(2,1)S(1)} %collective-permute-done.6.folded, bf16[1920,2048]{1,0:T(8,128)(2,1)S(1)} %spread_panel.6.other), custom_call_target="tpu_custom_call", output_to_operand_aliasing={{}: (3, {})} | custom-call | tf_op jit(solution)/shard_map/spread_panel/pallas_call | solution.py:179
  35.9 0.4 slice-done.1
  36.3 4.2 %dress_rows.3 = (bf16[480,1920]{1,0:T(8,128)(2,1)}, s32[8,128]{1,0:T(8,128)}) custom-call(bf16[160,1920]{1,0:T(8,128)(2,1)S(1)} %after.4.refs_1_.amplitudes, bf16[1920,2048]{1,0:T(8,128)(2,1)S(1)} %spread_panel.7.dense, bf16[2048,1920]{1,0:T(8,128)(2,1)S(1)} %bitcast.5), custom_call_target="tpu_custom_call" | custom-call | tf_op jit(solution)/shard_map/dress_rows/pallas_call | solution.py:249
  40.5 0.3 collective-permute-done.3.amplitudes
  40.9 3.6 %dress_rows.4 = (bf16[480,1920]{1,0:T(8,128)(2,1)}, s32[8,128]{1,0:T(8,128)S(1)}) custom-call(bf16[160,1920]{1,0:T(8,128)(2,1)S(1)} %collective-permute-done.3.amplitudes, bf16[1920,2048]{1,0:T(8,128)(2,1)S(1)} %spread_panel.7.dense, bf16[2048,1920]{1,0:T(8,128)(2,1)S(1)} %bitcast.5, ...), custom_call_target="tpu_custom_call", output_to_operand_aliasing={{0}: (3, {})} | custom-call | tf_op jit(solution)/shard_map/dress_rows/pallas_call | solution.py:249
  44.5 2.0 %collective-permute-done.2.refs_0_ = bf16[160,1920]{1,0:T(8,128)(2,1)S(1)} collective-permute-done((bf16[160,1920]{1,0:T(8,128)(2,1)S(1)}, bf16[160,1920]{1,0:T(8,128)(2,1)S(1)}, u32[]{:S(2)}, u32[]{:S(2)}) %collective-permute-start.2) | collective-permute-done | bytes 614432 | tf_op jit(solution)/shard_map/ppermute | solution.py:322
  46.5 0.1 broadcast_select_fusion.amplitudes
  46.6 4.2 %dress_rows.5 = (bf16[480,1920]{1,0:T(8,128)(2,1)}, s32[8,128]{1,0:T(8,128)}) custom-call(bf16[160,1920]{1,0:T(8,128)(2,1)S(1)} %broadcast_select_fusion.amplitudes, bf16[1920,2048]{1,0:T(8,128)(2,1)S(1)} %spread_panel.7.dense, bf16[2048,1920]{1,0:T(8,128)(2,1)S(1)} %bitcast.5, ...), custom_call_target="tpu_custom_call", output_to_operand_aliasing={{0}: (3, {})} | custom-call | tf_op jit(solution)/shard_map/dress_rows/pallas_call | solution.py:249
  (11 shorter events, 0.0 us)
Async XLA Ops:
  1.2 20.7 %collective-permute-start.1 = (bf16[160,1920]{1,0:T(8,128)(2,1)S(1)}, bf16[160,1920]{1,0:T(8,128)(2,1)S(1)}, u32[]{:S(2)}, u32[]{:S(2)}) collective-permute-start(bf16[160,1920]{1,0:T(8,128)(2,1)S(1)} %get-tuple-element.16), channel_id=1, source_target_pairs={{8,1},{16,2},{26,3},{12,5},{20,6},{30,7},{1,8},{18,10},{24,11},{5,... | collective-permute-start | bytes 1843208 | tf_op jit(solution)/shard_map/ppermute | solution.py:315
  5.8 23.6 %collective-permute-start.5 = (bf16[480,512]{1,0:T(8,128)(2,1)S(1)}, bf16[480,512]{1,0:T(8,128)(2,1)S(1)}, u32[]{:S(2)}, u32[]{:S(2)}) collective-permute-start(bf16[480,512]{1,0:T(8,128)(2,1)S(1)} %get-tuple-element.19), channel_id=1, source_target_pairs={{1,0},{0,1},{3,2},{2,3},{5,4},{4,5},{7,6},{6,7},{9,8},{8,9},{11,10... | collective-permute-start | bytes 1474568 | tf_op jit(solution)/shard_map/ppermute | solution.py:301
  10.2 20.9 %collective-permute-start.4 = (bf16[480,512]{1,0:T(8,128)(2,1)S(1)}, bf16[480,512]{1,0:T(8,128)(2,1)S(1)}, u32[]{:S(2)}, u32[]{:S(2)}) collective-permute-start(bf16[480,512]{1,0:T(8,128)(2,1)S(1)} %get-tuple-element.17.folded), channel_id=1, source_target_pairs={{2,0},{3,1},{0,2},{1,3},{6,4},{7,5},{4,6},{5,7},{10,8},{11,9},{8,1... | collective-permute-start | bytes 1474568 | tf_op jit(solution)/shard_map/ppermute | solution.py:300
  10.2 16.4 %collective-permute-start = (bf16[80,1920]{1,0:T(8,128)(2,1)S(1)}, bf16[80,1920]{1,0:T(8,128)(2,1)}, u32[]{:S(2)}, u32[]{:S(2)}) collective-permute-start(bf16[80,1920]{1,0:T(8,128)(2,1)S(1)} %get-tuple-element.15), channel_id=1, source_target_pairs={{4,0},{5,1},{6,2},{7,3},{0,4},{1,5},{2,6},{3,7},{12,8},{13,9},{14,... | collective-permute-start | bytes 921608 | tf_op jit(solution)/shard_map/ppermute | solution.py:311
  15.7 3.1 %copy-start = (bf16[1920,2048]{1,0:T(8,128)(2,1)}, bf16[1920,2048]{1,0:T(8,128)(2,1)S(1)}, u32[]{:S(2)}) copy-start(bf16[1920,2048]{1,0:T(8,128)(2,1)S(1)} %get-tuple-element.20.other) | copy-start | bytes 23592964
  18.8 3.0 %copy-start.2 = (bf16[2048,1920]{1,0:T(8,128)(2,1)}, bf16[2048,1920]{1,0:T(8,128)(2,1)S(1)}, u32[]{:S(2)}) copy-start(bf16[2048,1920]{1,0:T(8,128)(2,1)S(1)} %get-tuple-element.18.refs_1_.fock) | copy-start | bytes 23592964
  22.0 3.2 %copy-start.3 = (bf16[2048,1920]{1,0:T(8,128)(2,1)S(1)}, bf16[2048,1920]{1,0:T(8,128)(2,1)}, u32[]{:S(2)}) copy-start(bf16[2048,1920]{1,0:T(8,128)(2,1)} %copy-done.2) | copy-start | bytes 23592964
  25.2 4.2 %copy-start.1 = (bf16[1920,2048]{1,0:T(8,128)(2,1)S(1)}, bf16[1920,2048]{1,0:T(8,128)(2,1)}, u32[]{:S(2)}) copy-start(bf16[1920,2048]{1,0:T(8,128)(2,1)} %copy-done) | copy-start | bytes 23592964
  25.2 15.6 %collective-permute-start.3 = (bf16[160,1920]{1,0:T(8,128)(2,1)S(1)}, bf16[160,1920]{1,0:T(8,128)(2,1)S(1)}, u32[]{:S(2)}, u32[]{:S(2)}) collective-permute-start(bf16[160,1920]{1,0:T(8,128)(2,1)S(1)} %after.4.refs_1_.amplitudes), channel_id=1, source_target_pairs={{4,0},{5,1},{6,2},{7,3},{0,4},{1,5},{2,6},{3,7},{12,8},{13,9},{14,... | collective-permute-start | bytes 1843208 | tf_op jit(solution)/shard_map/ppermute | solution.py:323
  28.1 18.4 %collective-permute-start.2 = (bf16[160,1920]{1,0:T(8,128)(2,1)S(1)}, bf16[160,1920]{1,0:T(8,128)(2,1)S(1)}, u32[]{:S(2)}, u32[]{:S(2)}) collective-permute-start(bf16[160,1920]{1,0:T(8,128)(2,1)S(1)} %after.5), channel_id=1, source_target_pairs={{8,1},{16,2},{26,3},{12,5},{20,6},{30,7},{1,8},{18,10},{24,11},{5,... | collective-permute-start | bytes 1843208 | tf_op jit(solution)/shard_map/ppermute | solution.py:322
  31.1 3.1 %collective-permute-start.6 = (bf16[480,512]{1,0:T(8,128)(2,1)S(1)}, bf16[480,512]{1,0:T(8,128)(2,1)S(1)}, u32[]{:S(2)}, u32[]{:S(2)}) collective-permute-start(bf16[480,512]{1,0:T(8,128)(2,1)S(1)} %after.6.folded), channel_id=1, source_target_pairs={{1,0},{0,1},{3,2},{2,3},{5,4},{4,5},{7,6},{6,7},{9,8},{8,9},{11,10... | collective-permute-start | bytes 1474568 | tf_op jit(solution)/shard_map/ppermute | solution.py:326
  32.4 3.5 %slice-start = ((s8[7864320]{0:T(1024)(128)(4,1)}), s8[4194304]{0:T(1024)(128)(4,1)S(1)}, s32[]{:S(2)}) async-start(s8[7864320]{0:T(1024)(128)(4,1)} %bitcast.4), calls=%async_computation | async-start | bytes 8388608
  34.2 2.1 %slice-start.1 = ((s8[7864320]{0:T(1024)(128)(4,1)}), s8[3670016]{0:T(1024)(128)(4,1)S(1)}, s32[]{:S(2)}) async-start(s8[7864320]{0:T(1024)(128)(4,1)} %bitcast.4), calls=%async_computation.1 | async-start | bytes 7340032

commit v9 on v8

--- a/solution.py
+++ b/solution.py
@@ -115,9 +115,10 @@
 
 def spread_kernel(slot, groups, first, sizes, pair, folded, other, *refs):
     if first:
-        dense, fock_out, bounds, turned, sems = refs
+        dense, token, fock_out, bounds, turned, sems = refs
     else:
-        dense, bounds, turned = refs
+        dense, token, bounds, turned = refs
+    token[...] = jnp.zeros_like(token)
     quarter, fold = folded.shape
     virtuals, total = dense.shape
     width = total // groups
@@ -165,7 +166,9 @@
     width = rounded(quarter, LANES)
     smem = pl.BlockSpec(memory_space=pltpu.SMEM)
     vmem = pl.BlockSpec(memory_space=pltpu.VMEM)
-    out_shape = [pltpu.VMEM((virtuals, groups * width), folded.dtype)]
+    out_shape = [
+        pltpu.VMEM((virtuals, groups * width), folded.dtype), pltpu.VMEM((8, LANES), jnp.int32)
+    ]
     scratch = [
         pltpu.SMEM((sizes.shape[0] + 1,), jnp.int32),
         pltpu.VMEM((fold, width), jnp.float32),
@@ -315,17 +318,17 @@
         top = arrived(lax.ppermute(top, axes, to_group), top)
 
         spread_one = functools.partial(spread, sizes=irrep_sizes, pair=pair_irreps)
-        dense, fock = spread_one(0, groups, own, fock=virt_fock)
-        top = after(top, fock)
+        dense, token, fock = spread_one(0, groups, own, fock=virt_fock)
+        top = after(top, token)
         if early < rows:
             lows = after(lows, top)
             late = lax.ppermute(lows, axes, to_group)
         tops = [top] + [lax.ppermute(top, axes, to_member(by)) for by in range(1, members)]
-        dense, = spread_one(1, groups, beside, dense=dense)
-        across = after(across, dense)
+        dense, token = spread_one(1, groups, beside, dense=dense)
+        across = after(across, token)
         both = lax.ppermute(across, axes, to_slot(1))
-        dense, = spread_one(2, groups, across, dense=dense)
-        dense, = spread_one(3, groups, both, dense=dense)
+        dense, _ = spread_one(2, groups, across, dense=dense)
+        dense, _ = spread_one(3, groups, both, dense=dense)
 
         if early < rows:
             result = None

time: 51.8 us -> 57.7 us (1.11)
  the two profiles are of different devices: /device:TPU:4 before, /device:TPU:1 now
where the time goes in v9:
time: 57.7 us; the launch traced here: 57.4 us
  Pallas kernels  26.2 us (45%)
  local copies, waits for them, and re-layouts  15.8 us (27%)
  starting transfers between devices  13.4 us (23%)
  other arithmetic  1.2 us (2%)
  between operations  0.81 us (1%)
    unnamed x14, local copies, waits for them, and re-layouts  15.8 us
    pallas_call x3, Pallas kernels, dress(): pl.pallas_call(functools.partial(dress_kernel, spans, rows, members, base...  12.1 us
    pallas_call x4, Pallas kernels, spread(): pl.pallas_call(functools.partial(spread_kernel, slot, groups, first), out...  10.2 us
    ppermute x1, starting transfers between devices, local(): top = arrived(lax.ppermute(top, axes, to_group), top)  4.59 us
    pallas_call x1, Pallas kernels, fold_panel(): pl.pallas_call(functools.partial(fold_kernel, chunk), out_shape=[pltpu.VM...  2.7 us
    ppermute x1, starting transfers between devices, local(): both = lax.ppermute(across, axes, to_slot(1))  1.98 us
    ppermute x1, starting transfers between devices, local(): late = lax.ppermute(lows, axes, to_group)  1.92 us
    ppermute x1, starting transfers between devices, local(): across = lax.ppermute(own, axes, to_slot(2))  1.84 us
  transfers between devices with their start and end apart: 7, of which 0 were waited for; matrix products, arithmetic and copies ran while one was open for 2% of the time, Pallas kernels for 36%

profile of v9, /device:TPU:1, one launch (start us, length us, event | category | flops | bytes accessed | tf_op | source)
XLA Modules:
  0.0 57.4 jit_solution(11279457347265447807)
XLA Ops:
  0.0 1.2 %cut_rows.1 = (bf16[160,1920]{1,0:T(8,128)(2,1)S(1)}, bf16[80,1920]{1,0:T(8,128)(2,1)S(1)}) custom-call(bf16[240,1920]{1,0:T(8,128)(2,1)} %whole.1), custom_call_target="tpu_custom_call" | custom-call | tf_op jit(solution)/shard_map/cut_rows/pallas_call | solution.py:52
  1.2 4.6 %collective-permute-start.1 = (bf16[160,1920]{1,0:T(8,128)(2,1)S(1)}, bf16[160,1920]{1,0:T(8,128)(2,1)S(1)}, u32[]{:S(2)}, u32[]{:S(2)}) collective-permute-start(bf16[160,1920]{1,0:T(8,128)(2,1)S(1)} %get-tuple-element.21), channel_id=1, source_target_pairs={{8,1},{16,2},{26,3},{12,5},{20,6},{30,7},{1,8},{18,10},{24,11},{5,... | collective-permute-start | bytes 1843208 | tf_op jit(solution)/shard_map/ppermute | solution.py:318
  6.4 2.7 %fold_panel.1 = (bf16[480,512]{1,0:T(8,128)(2,1)S(1)}, bf16[480,512]{1,0:T(8,128)(2,1)S(1)}) custom-call(s32[8]{0:T(128)} %sizes.9, s32[1]{0:T(128)S(6)} %copy.24.pair, bf16[480,1920]{1,0:T(8,128)(2,1)} %bitcast.6), custom_call_target="tpu_custom_call" | custom-call | tf_op jit(solution)/shard_map/fold_panel/pallas_call | solution.py:100
  9.1 1.5 %collective-permute-start.5 = (bf16[480,512]{1,0:T(8,128)(2,1)S(1)}, bf16[480,512]{1,0:T(8,128)(2,1)S(1)}, u32[]{:S(2)}, u32[]{:S(2)}) collective-permute-start(bf16[480,512]{1,0:T(8,128)(2,1)S(1)} %get-tuple-element.24), channel_id=1, source_target_pairs={{1,0},{0,1},{3,2},{2,3},{5,4},{4,5},{7,6},{6,7},{9,8},{8,9},{11,10... | collective-permute-start | bytes 1474568 | tf_op jit(solution)/shard_map/ppermute | solution.py:304
  10.6 1.8 %collective-permute-start.4 = (bf16[480,512]{1,0:T(8,128)(2,1)S(1)}, bf16[480,512]{1,0:T(8,128)(2,1)S(1)}, u32[]{:S(2)}, u32[]{:S(2)}) collective-permute-start(bf16[480,512]{1,0:T(8,128)(2,1)S(1)} %get-tuple-element.22.folded), channel_id=1, source_target_pairs={{2,0},{3,1},{0,2},{1,3},{6,4},{7,5},{4,6},{5,7},{10,8},{11,9},{8,1... | collective-permute-start | bytes 1474568 | tf_op jit(solution)/shard_map/ppermute | solution.py:303
  12.5 1.2 %collective-permute-start = (bf16[80,1920]{1,0:T(8,128)(2,1)S(1)}, bf16[80,1920]{1,0:T(8,128)(2,1)}, u32[]{:S(2)}, u32[]{:S(2)}) collective-permute-start(bf16[80,1920]{1,0:T(8,128)(2,1)S(1)} %get-tuple-element.20), channel_id=1, source_target_pairs={{4,0},{5,1},{6,2},{7,3},{0,4},{1,5},{2,6},{3,7},{12,8},{13,9},{14,... | collective-permute-start | bytes 921608 | tf_op jit(solution)/shard_map/ppermute | solution.py:314
  13.7 4.0 %spread_panel.4 = (bf16[1920,2048]{1,0:T(8,128)(2,1)S(1)}, s32[8,128]{1,0:T(8,128)S(1)}, bf16[2048,1920]{1,0:T(8,128)(2,1)S(1)}) custom-call(s32[8]{0:T(128)} %sizes.9, s32[1]{0:T(128)S(6)} %copy.24.pair, bf16[480,512]{1,0:T(8,128)(2,1)S(1)} %get-tuple-element.22.folded, bf16[1920,1920]{1,0:T(8,128)(2,1)} %other.1), custom_call_target="tpu_custom_call" | custom-call | tf_op jit(solution)/shard_map/spread_panel/pallas_call | solution.py:182
  17.7 3.1 %copy-done = bf16[1920,2048]{1,0:T(8,128)(2,1)} copy-done((bf16[1920,2048]{1,0:T(8,128)(2,1)}, bf16[1920,2048]{1,0:T(8,128)(2,1)S(1)}, u32[]{:S(2)}) %copy-start) | copy-done | bytes 7864344
  20.8 3.0 %copy-done.4 = bf16[2048,1920]{1,0:T(8,128)(2,1)} copy-done((bf16[2048,1920]{1,0:T(8,128)(2,1)}, bf16[2048,1920]{1,0:T(8,128)(2,1)S(1)}, u32[]{:S(2)}) %copy-start.4) | copy-done | bytes 7864344
  23.9 0.0 collective-permute-done.1
  23.9 0.1 broadcast_select_fusion.1.refs_0_
  24.0 0.3 collective-permute-start.3
  24.3 0.0 collective-permute-done
  24.3 1.0 %pad_maximum_fusion.refs_0_ = bf16[160,1920]{1,0:T(8,128)(2,1)S(1)} fusion(bf16[80,1920]{1,0:T(8,128)(2,1)} %collective-permute-done, bf16[80,1920]{1,0:T(8,128)(2,1)S(1)} %get-tuple-element.20), kind=kLoop, calls=%fused_computation | loop fusion | flops 1228800 | bytes 1228800 | tf_op jit(solution)/shard_map/concatenate | solution.py:315
  25.3 1.9 %collective-permute-start.2 = (bf16[160,1920]{1,0:T(8,128)(2,1)S(1)}, bf16[160,1920]{1,0:T(8,128)(2,1)S(1)}, u32[]{:S(2)}, u32[]{:S(2)}) collective-permute-start(bf16[160,1920]{1,0:T(8,128)(2,1)S(1)} %after.5), channel_id=1, source_target_pairs={{8,1},{16,2},{26,3},{12,5},{20,6},{30,7},{1,8},{18,10},{24,11},{5,... | collective-permute-start | bytes 1843208 | tf_op jit(solution)/shard_map/ppermute | solution.py:325
  27.3 0.0 collective-permute-done.5.folded
  27.3 3.2 %copy-done.1 = bf16[1920,2048]{1,0:T(8,128)(2,1)S(1)} copy-done((bf16[1920,2048]{1,0:T(8,128)(2,1)S(1)}, bf16[1920,2048]{1,0:T(8,128)(2,1)}, u32[]{:S(2)}) %copy-start.1) | copy-done | bytes 7864344
  30.5 1.6 %spread_panel.5 = (bf16[1920,2048]{1,0:T(8,128)(2,1)S(1)}, s32[8,128]{1,0:T(8,128)S(1)}) custom-call(s32[8]{0:T(128)} %sizes.9, s32[1]{0:T(128)S(6)} %copy.24.pair, bf16[480,512]{1,0:T(8,128)(2,1)S(1)} %collective-permute-done.5.folded, bf16[1920,2048]{1,0:T(8,128)(2,1)S(1)} %copy-done.1), custom_call_target="tpu_custom_call", output_to_operand_aliasing={{0}: (3, {})} | custom-call | tf_op jit(solution)/shard_map/spread_panel/pallas_call | solution.py:182
  32.1 0.0 collective-permute-done.4.refs_0_
  32.1 2.0 %collective-permute-start.6 = (bf16[480,512]{1,0:T(8,128)(2,1)S(1)}, bf16[480,512]{1,0:T(8,128)(2,1)S(1)}, u32[]{:S(2)}, u32[]{:S(2)}) collective-permute-start(bf16[480,512]{1,0:T(8,128)(2,1)S(1)} %after.6.folded), channel_id=1, source_target_pairs={{1,0},{0,1},{3,2},{2,3},{5,4},{4,5},{7,6},{6,7},{9,8},{8,9},{11,10... | collective-permute-start | bytes 1474568 | tf_op jit(solution)/shard_map/ppermute | solution.py:329
  34.1 2.3 %spread_panel.6 = (bf16[1920,2048]{1,0:T(8,128)(2,1)S(1)}, s32[8,128]{1,0:T(8,128)}) custom-call(s32[8]{0:T(128)} %sizes.9, s32[1]{0:T(128)S(6)} %copy.24.pair, bf16[480,512]{1,0:T(8,128)(2,1)S(1)} %after.6.folded, bf16[1920,2048]{1,0:T(8,128)(2,1)S(1)} %get-tuple-element.27.other), custom_call_target="tpu_custom_call", output_to_operand_aliasing={{0}: (3, {})} | custom-call | tf_op jit(solution)/shard_map/spread_panel/pallas_call | solution.py:182
  36.4 0.0 collective-permute-done.6.folded
  36.5 2.3 %spread_panel.7 = (bf16[1920,2048]{1,0:T(8,128)(2,1)S(1)}, s32[8,128]{1,0:T(8,128)}) custom-call(s32[8]{0:T(128)} %sizes.9, s32[1]{0:T(128)S(6)} %copy.24.pair, bf16[480,512]{1,0:T(8,128)(2,1)S(1)} %collective-permute-done.6.folded, bf16[1920,2048]{1,0:T(8,128)(2,1)S(1)} %get-tuple-element.28.other), custom_call_target="tpu_custom_call", output_to_operand_aliasing={{0}: (3, {})} | custom-call | tf_op jit(solution)/shard_map/spread_panel/pallas_call | solution.py:182
  38.8 3.1 %copy-done.2 = bf16[1920,2048]{1,0:T(8,128)(2,1)} copy-done((bf16[1920,2048]{1,0:T(8,128)(2,1)}, bf16[1920,2048]{1,0:T(8,128)(2,1)S(1)}, u32[]{:S(2)}) %copy-start.2) | copy-done | bytes 7864344
  41.9 0.0 slice-done
  41.9 3.2 %copy-done.3 = bf16[1920,2048]{1,0:T(8,128)(2,1)S(1)} copy-done((bf16[1920,2048]{1,0:T(8,128)(2,1)S(1)}, bf16[1920,2048]{1,0:T(8,128)(2,1)}, u32[]{:S(2)}) %copy-start.3) | copy-done | bytes 7864344
  45.1 4.2 %dress_rows.3 = (bf16[480,1920]{1,0:T(8,128)(2,1)}, s32[8,128]{1,0:T(8,128)}) custom-call(bf16[160,1920]{1,0:T(8,128)(2,1)S(1)} %after.4.refs_1_.amplitudes, bf16[1920,2048]{1,0:T(8,128)(2,1)S(1)} %copy-done.3, bf16[2048,1920]{1,0:T(8,128)(2,1)S(1)} %bitcast.5), custom_call_target="tpu_custom_call" | custom-call | tf_op jit(solution)/shard_map/dress_rows/pallas_call | solution.py:252
  49.3 0.0 collective-permute-done.3.amplitudes
  49.3 3.7 %dress_rows.4 = (bf16[480,1920]{1,0:T(8,128)(2,1)}, s32[8,128]{1,0:T(8,128)S(1)}) custom-call(bf16[160,1920]{1,0:T(8,128)(2,1)S(1)} %collective-permute-done.3.amplitudes, bf16[1920,2048]{1,0:T(8,128)(2,1)S(1)} %copy-done.3, bf16[2048,1920]{1,0:T(8,128)(2,1)S(1)} %bitcast.5, bf16[480,1920]{1,0:T(8,128)(2,1)} %get-tuple-element.31.refs_0_), custom_call_target="tpu_custom_call", output_to_operand_aliasing={{0}: (3, {})} | custom-call | tf_op jit(solution)/shard_map/dress_rows/pallas_call | solution.py:252
  53.1 0.0 collective-permute-done.2.refs_0_
  53.1 0.1 broadcast_select_fusion.amplitudes
  53.2 4.2 %dress_rows.5 = (bf16[480,1920]{1,0:T(8,128)(2,1)}, s32[8,128]{1,0:T(8,128)}) custom-call(bf16[160,1920]{1,0:T(8,128)(2,1)S(1)} %broadcast_select_fusion.amplitudes, bf16[1920,2048]{1,0:T(8,128)(2,1)S(1)} %copy-done.3, bf16[2048,1920]{1,0:T(8,128)(2,1)S(1)} %bitcast.5, bf16[480,1920]{1,0:T(8,128)(2,1)} %get-tuple-element.33.refs_0_), custom_call_target="tpu_custom_call", output_to_operand_aliasing={{0}: (3, {})} | custom-call | tf_op jit(solution)/shard_map/dress_rows/pallas_call | solution.py:252
  (13 shorter events, 0.0 us)
Async XLA Ops:
  1.2 22.7 %collective-permute-start.1 = (bf16[160,1920]{1,0:T(8,128)(2,1)S(1)}, bf16[160,1920]{1,0:T(8,128)(2,1)S(1)}, u32[]{:S(2)}, u32[]{:S(2)}) collective-permute-start(bf16[160,1920]{1,0:T(8,128)(2,1)S(1)} %get-tuple-element.21), channel_id=1, source_target_pairs={{8,1},{16,2},{26,3},{12,5},{20,6},{30,7},{1,8},{18,10},{24,11},{5,... | collective-permute-start | bytes 1843208 | tf_op jit(solution)/shard_map/ppermute | solution.py:318
  9.1 18.1 %collective-permute-start.5 = (bf16[480,512]{1,0:T(8,128)(2,1)S(1)}, bf16[480,512]{1,0:T(8,128)(2,1)S(1)}, u32[]{:S(2)}, u32[]{:S(2)}) collective-permute-start(bf16[480,512]{1,0:T(8,128)(2,1)S(1)} %get-tuple-element.24), channel_id=1, source_target_pairs={{1,0},{0,1},{3,2},{2,3},{5,4},{4,5},{7,6},{6,7},{9,8},{8,9},{11,10... | collective-permute-start | bytes 1474568 | tf_op jit(solution)/shard_map/ppermute | solution.py:304
  10.6 21.5 %collective-permute-start.4 = (bf16[480,512]{1,0:T(8,128)(2,1)S(1)}, bf16[480,512]{1,0:T(8,128)(2,1)S(1)}, u32[]{:S(2)}, u32[]{:S(2)}) collective-permute-start(bf16[480,512]{1,0:T(8,128)(2,1)S(1)} %get-tuple-element.22.folded), channel_id=1, source_target_pairs={{2,0},{3,1},{0,2},{1,3},{6,4},{7,5},{4,6},{5,7},{10,8},{11,9},{8,1... | collective-permute-start | bytes 1474568 | tf_op jit(solution)/shard_map/ppermute | solution.py:303
  12.5 11.8 %collective-permute-start = (bf16[80,1920]{1,0:T(8,128)(2,1)S(1)}, bf16[80,1920]{1,0:T(8,128)(2,1)}, u32[]{:S(2)}, u32[]{:S(2)}) collective-permute-start(bf16[80,1920]{1,0:T(8,128)(2,1)S(1)} %get-tuple-element.20), channel_id=1, source_target_pairs={{4,0},{5,1},{6,2},{7,3},{0,4},{1,5},{2,6},{3,7},{12,8},{13,9},{14,... | collective-permute-start | bytes 921608 | tf_op jit(solution)/shard_map/ppermute | solution.py:314
  17.7 3.1 %copy-start = (bf16[1920,2048]{1,0:T(8,128)(2,1)}, bf16[1920,2048]{1,0:T(8,128)(2,1)S(1)}, u32[]{:S(2)}) copy-start(bf16[1920,2048]{1,0:T(8,128)(2,1)S(1)} %get-tuple-element.25.other) | copy-start | bytes 23592964
  20.8 3.0 %copy-start.4 = (bf16[2048,1920]{1,0:T(8,128)(2,1)}, bf16[2048,1920]{1,0:T(8,128)(2,1)S(1)}, u32[]{:S(2)}) copy-start(bf16[2048,1920]{1,0:T(8,128)(2,1)S(1)} %get-tuple-element.30.fock) | copy-start | bytes 23592964
  24.0 25.3 %collective-permute-start.3 = (bf16[160,1920]{1,0:T(8,128)(2,1)S(1)}, bf16[160,1920]{1,0:T(8,128)(2,1)S(1)}, u32[]{:S(2)}, u32[]{:S(2)}) collective-permute-start(bf16[160,1920]{1,0:T(8,128)(2,1)S(1)} %after.4.refs_1_.amplitudes), channel_id=1, source_target_pairs={{4,0},{5,1},{6,2},{7,3},{0,4},{1,5},{2,6},{3,7},{12,8},{13,9},{14,... | collective-permute-start | bytes 1843208 | tf_op jit(solution)/shard_map/ppermute | solution.py:326
  25.3 27.7 %collective-permute-start.2 = (bf16[160,1920]{1,0:T(8,128)(2,1)S(1)}, bf16[160,1920]{1,0:T(8,128)(2,1)S(1)}, u32[]{:S(2)}, u32[]{:S(2)}) collective-permute-start(bf16[160,1920]{1,0:T(8,128)(2,1)S(1)} %after.5), channel_id=1, source_target_pairs={{8,1},{16,2},{26,3},{12,5},{20,6},{30,7},{1,8},{18,10},{24,11},{5,... | collective-permute-start | bytes 1843208 | tf_op jit(solution)/shard_map/ppermute | solution.py:325
  27.3 3.2 %copy-start.1 = (bf16[1920,2048]{1,0:T(8,128)(2,1)S(1)}, bf16[1920,2048]{1,0:T(8,128)(2,1)}, u32[]{:S(2)}) copy-start(bf16[1920,2048]{1,0:T(8,128)(2,1)} %copy-done) | copy-start | bytes 23592964
  32.1 4.3 %collective-permute-start.6 = (bf16[480,512]{1,0:T(8,128)(2,1)S(1)}, bf16[480,512]{1,0:T(8,128)(2,1)S(1)}, u32[]{:S(2)}, u32[]{:S(2)}) collective-permute-start(bf16[480,512]{1,0:T(8,128)(2,1)S(1)} %after.6.folded), channel_id=1, source_target_pairs={{1,0},{0,1},{3,2},{2,3},{5,4},{4,5},{7,6},{6,7},{9,8},{8,9},{11,10... | collective-permute-start | bytes 1474568 | tf_op jit(solution)/shard_map/ppermute | solution.py:329
  34.1 7.8 %slice-start = ((s8[7864320]{0:T(1024)(128)(4,1)}), s8[4194304]{0:T(1024)(128)(4,1)S(1)}, s32[]{:S(2)}) async-start(s8[7864320]{0:T(1024)(128)(4,1)} %bitcast.4), calls=%async_computation | async-start | bytes 8388608
  36.5 5.5 %slice-start.1 = ((s8[7864320]{0:T(1024)(128)(4,1)}), s8[3670016]{0:T(1024)(128)(4,1)S(1)}, s32[]{:S(2)}) async-start(s8[7864320]{0:T(1024)(128)(4,1)} %bitcast.4), calls=%async_computation.1 | async-start | bytes 7340032
  38.8 3.1 %copy-start.2 = (bf16[1920,2048]{1,0:T(8,128)(2,1)}, bf16[1920,2048]{1,0:T(8,128)(2,1)S(1)}, u32[]{:S(2)}) copy-start(bf16[1920,2048]{1,0:T(8,128)(2,1)S(1)} %get-tuple-element.29.dense) | copy-start | bytes 23592964
  41.9 3.2 %copy-start.3 = (bf16[1920,2048]{1,0:T(8,128)(2,1)S(1)}, bf16[1920,2048]{1,0:T(8,128)(2,1)}, u32[]{:S(2)}) copy-start(bf16[1920,2048]{1,0:T(8,128)(2,1)} %copy-done.2) | copy-start | bytes 23592964

commit v10 on v9

--- a/solution.py
+++ b/solution.py
@@ -206,6 +206,31 @@
     )(array, *others)
 
 
+def owned_kernel(members, received, kept, *refs):
+    out, sem = refs[-2:]
+
+    @pl.when(lax.div(lax.axis_index("blk"), members) == lax.axis_index("grp"))
+    def _():
+        copy = pltpu.make_async_copy(kept, out, sem)
+        copy.start()
+        copy.wait()
+
+
+def owned(received, kept, members, *others):
+    anywhere = pl.BlockSpec(memory_space=pl.ANY)
+    return pl.pallas_call(
+        functools.partial(owned_kernel, members),
+        out_shape=jax.ShapeDtypeStruct(received.shape, received.dtype),
+        in_specs=[anywhere] * (2 + len(others)),
+        out_specs=anywhere,
+        input_output_aliases={0: 0},
+        scratch_shapes=[pltpu.SemaphoreType.DMA],
+        compiler_params=pltpu.CompilerParams(vmem_limit_bytes=MIB),
+        cost_estimate=NOTHING,
+        name="owned_rows",
+    )(received, kept, *others)
+
+
 def column_tiles(total, tile):
     return [(first, min(tile, total - first)) for first in range(0, total, tile)]
 
@@ -303,11 +328,6 @@
         across = lax.ppermute(own, axes, to_slot(2))
         beside = lax.ppermute(own_again, axes, to_slot(1))
 
-        owner = lax.axis_index("blk") // members == lax.axis_index("grp")
-
-        def arrived(piece, kept):
-            return jnp.where(owner, kept, piece)
-
         early = rounded(rows * 2 // 3, SUBLANES) if rows % SUBLANES == 0 else rows
         if early < rows:
             top, low = cut(amplitudes, (early, rows - early))
@@ -315,11 +335,10 @@
             lows = jnp.concatenate(lows)
         else:
             top = amplitudes
-        top = arrived(lax.ppermute(top, axes, to_group), top)
 
         spread_one = functools.partial(spread, sizes=irrep_sizes, pair=pair_irreps)
         dense, token, fock = spread_one(0, groups, own, fock=virt_fock)
-        top = after(top, token)
+        top = owned(lax.ppermute(top, axes, to_group), top, members, token)
         if early < rows:
             lows = after(lows, top)
             late = lax.ppermute(lows, axes, to_group)
@@ -336,7 +355,7 @@
                 spans = [(by, 0, early)]
                 result, token = dress(piece, spans, dense, fock, result, rows, members, out_rows)
             spans = [(by, early, rows - early) for by in range(members)]
-            lows = arrived(after(late, token), lows)
+            lows = owned(late, lows, members, token)
             result, _ = dress(lows, spans, dense, fock, result, rows, members, out_rows)
         else:
             member = lax.axis_index("blk") % members

time: 57.7 us -> 50.1 us (0.87)
  the two profiles are of different devices: /device:TPU:1 before, /device:TPU:27 now
where the time goes in v10:
time: 50.1 us; the launch traced here: 49.8 us
  Pallas kernels  26 us (52%)
  waiting for transfers between devices  16.4 us (33%)
  starting transfers between devices  6.57 us (13%)
  between operations  0.77 us (2%)
    pallas_call x3, Pallas kernels, dress(): pl.pallas_call(functools.partial(dress_kernel, spans, rows, members, base...  12.1 us
    pallas_call x4, Pallas kernels, spread(): pl.pallas_call(functools.partial(spread_kernel, slot, groups, first), out...  9.98 us
    ppermute x1, waiting for transfers between devices, local(): across = lax.ppermute(own, axes, to_slot(2))  9.95 us
    ppermute x1, waiting for transfers between devices, local(): top = owned(lax.ppermute(top, axes, to_group), top, members, token)  6.48 us
    pallas_call x1, Pallas kernels, fold_panel(): pl.pallas_call(functools.partial(fold_kernel, chunk), out_shape=[pltpu.VM...  2.7 us
    ppermute x1, starting transfers between devices, local(): beside = lax.ppermute(own_again, axes, to_slot(1))  2.37 us
    ppermute x1, starting transfers between devices, local(): top = owned(lax.ppermute(top, axes, to_group), top, members, token)  1.29 us
    ppermute x1, starting transfers between devices, local(): late = lax.ppermute(lows, axes, to_group)  1.29 us
  transfers between devices with their start and end apart: 7, of which 2 were waited for; matrix products, arithmetic and copies ran while one was open for 0% of the time, Pallas kernels for 41%

profile of v10, /device:TPU:27, one launch (start us, length us, event | category | flops | bytes accessed | tf_op | source)
XLA Modules:
  0.0 49.8 jit_solution(4369438496878491057)
XLA Ops:
  0.0 1.2 %cut_rows.1 = (bf16[160,1920]{1,0:T(8,128)(2,1)S(1)}, bf16[80,1920]{1,0:T(8,128)(2,1)S(1)}) custom-call(bf16[240,1920]{1,0:T(8,128)(2,1)} %whole.1), custom_call_target="tpu_custom_call" | custom-call | tf_op jit(solution)/shard_map/cut_rows/pallas_call | solution.py:52
  1.2 1.3 %collective-permute-start.1 = (bf16[160,1920]{1,0:T(8,128)(2,1)S(1)}, bf16[160,1920]{1,0:T(8,128)(2,1)S(1)}, u32[]{:S(2)}, u32[]{:S(2)}) collective-permute-start(bf16[160,1920]{1,0:T(8,128)(2,1)S(1)} %get-tuple-element.21.kept), channel_id=1, source_target_pairs={{8,1},{16,2},{26,3},{12,5},{20,6},{30,7},{1,8},{18,10},{24,11},{5,... | collective-permute-start | bytes 1843208 | tf_op jit(solution)/shard_map/ppermute | solution.py:341
  2.5 0.3 collective-permute-start
  3.4 2.7 %fold_panel.1 = (bf16[480,512]{1,0:T(8,128)(2,1)S(1)}, bf16[480,512]{1,0:T(8,128)(2,1)S(1)}) custom-call(s32[8]{0:T(128)} %sizes.9, s32[1]{0:T(128)S(6)} %copy.24.pair, bf16[480,1920]{1,0:T(8,128)(2,1)} %bitcast.4), custom_call_target="tpu_custom_call" | custom-call | tf_op jit(solution)/shard_map/fold_panel/pallas_call | solution.py:100
  6.2 2.4 %collective-permute-start.5 = (bf16[480,512]{1,0:T(8,128)(2,1)S(1)}, bf16[480,512]{1,0:T(8,128)(2,1)S(1)}, u32[]{:S(2)}, u32[]{:S(2)}) collective-permute-start(bf16[480,512]{1,0:T(8,128)(2,1)S(1)} %get-tuple-element.24), channel_id=1, source_target_pairs={{1,0},{0,1},{3,2},{2,3},{5,4},{4,5},{7,6},{6,7},{9,8},{8,9},{11,10... | collective-permute-start | bytes 1474568 | tf_op jit(solution)/shard_map/ppermute | solution.py:329
  8.5 0.5 %collective-permute-start.4 = (bf16[480,512]{1,0:T(8,128)(2,1)S(1)}, bf16[480,512]{1,0:T(8,128)(2,1)S(1)}, u32[]{:S(2)}, u32[]{:S(2)}) collective-permute-start(bf16[480,512]{1,0:T(8,128)(2,1)S(1)} %get-tuple-element.22.folded), channel_id=1, source_target_pairs={{2,0},{3,1},{0,2},{1,3},{6,4},{7,5},{4,6},{5,7},{10,8},{11,9},{8,1... | collective-permute-start | bytes 1474568 | tf_op jit(solution)/shard_map/ppermute | solution.py:328
  9.1 4.0 %spread_panel.4 = (bf16[1920,2048]{1,0:T(8,128)(2,1)S(1)}, s32[8,128]{1,0:T(8,128)S(1)}, bf16[2048,1920]{1,0:T(8,128)(2,1)S(1)}) custom-call(s32[8]{0:T(128)} %sizes.9, s32[1]{0:T(128)S(6)} %copy.24.pair, bf16[480,512]{1,0:T(8,128)(2,1)S(1)} %get-tuple-element.22.folded, bf16[1920,1920]{1,0:T(8,128)(2,1)} %other.1), custom_call_target="tpu_custom_call" | custom-call | tf_op jit(solution)/shard_map/spread_panel/pallas_call | solution.py:182
  13.1 6.5 %collective-permute-done.1.received = bf16[160,1920]{1,0:T(8,128)(2,1)S(1)} collective-permute-done((bf16[160,1920]{1,0:T(8,128)(2,1)S(1)}, bf16[160,1920]{1,0:T(8,128)(2,1)S(1)}, u32[]{:S(2)}, u32[]{:S(2)}) %collective-permute-start.1) | collective-permute-done | bytes 614432 | tf_op jit(solution)/shard_map/ppermute | solution.py:341
  19.6 0.3 collective-permute-start.3
  19.9 0.0 collective-permute-done
  19.9 1.3 %collective-permute-start.2 = (bf16[160,1920]{1,0:T(8,128)(2,1)S(1)}, bf16[160,1920]{1,0:T(8,128)(2,1)S(1)}, u32[]{:S(2)}, u32[]{:S(2)}) collective-permute-start(bf16[160,1920]{1,0:T(8,128)(2,1)S(1)} %after.2.kept), channel_id=1, source_target_pairs={{8,1},{16,2},{26,3},{12,5},{20,6},{30,7},{1,8},{18,10},{24,11},{5,... | collective-permute-start | bytes 1843208 | tf_op jit(solution)/shard_map/ppermute | solution.py:344
  21.2 0.0 collective-permute-done.5.folded
  21.3 1.6 %spread_panel.5 = (bf16[1920,2048]{1,0:T(8,128)(2,1)S(1)}, s32[8,128]{1,0:T(8,128)S(1)}) custom-call(s32[8]{0:T(128)} %sizes.9, s32[1]{0:T(128)S(6)} %copy.24.pair, bf16[480,512]{1,0:T(8,128)(2,1)S(1)} %collective-permute-done.5.folded, bf16[1920,2048]{1,0:T(8,128)(2,1)S(1)} %get-tuple-element.25.other), custom_call_target="tpu_custom_call", output_to_operand_aliasing={{0}: (3, {})} | custom-call | tf_op jit(solution)/shard_map/spread_panel/pallas_call | solution.py:182
  22.9 10.0 %collective-permute-done.4.refs_0_ = bf16[480,512]{1,0:T(8,128)(2,1)S(1)} collective-permute-done((bf16[480,512]{1,0:T(8,128)(2,1)S(1)}, bf16[480,512]{1,0:T(8,128)(2,1)S(1)}, u32[]{:S(2)}, u32[]{:S(2)}) %collective-permute-start.4) | collective-permute-done | bytes 491552 | tf_op jit(solution)/shard_map/ppermute | solution.py:328
  32.8 0.4 collective-permute-start.6
  33.3 2.2 %spread_panel.6 = (bf16[1920,2048]{1,0:T(8,128)(2,1)S(1)}, s32[8,128]{1,0:T(8,128)}) custom-call(s32[8]{0:T(128)} %sizes.9, s32[1]{0:T(128)S(6)} %copy.24.pair, bf16[480,512]{1,0:T(8,128)(2,1)S(1)} %after.3.folded, bf16[1920,2048]{1,0:T(8,128)(2,1)S(1)} %get-tuple-element.27.other), custom_call_target="tpu_custom_call", output_to_operand_aliasing={{0}: (3, {})} | custom-call | tf_op jit(solution)/shard_map/spread_panel/pallas_call | solution.py:182
  35.5 0.0 collective-permute-done.6.folded
  35.5 2.2 %spread_panel.7 = (bf16[1920,2048]{1,0:T(8,128)(2,1)S(1)}, s32[8,128]{1,0:T(8,128)}) custom-call(s32[8]{0:T(128)} %sizes.9, s32[1]{0:T(128)S(6)} %copy.24.pair, bf16[480,512]{1,0:T(8,128)(2,1)S(1)} %collective-permute-done.6.folded, bf16[1920,2048]{1,0:T(8,128)(2,1)S(1)} %get-tuple-element.28.other), custom_call_target="tpu_custom_call", output_to_operand_aliasing={{0}: (3, {})} | custom-call | tf_op jit(solution)/shard_map/spread_panel/pallas_call | solution.py:182
  37.7 4.2 %dress_rows.3 = (bf16[480,1920]{1,0:T(8,128)(2,1)}, s32[8,128]{1,0:T(8,128)}) custom-call(bf16[160,1920]{1,0:T(8,128)(2,1)S(1)} %owned_rows.2.refs_1_.amplitudes, bf16[1920,2048]{1,0:T(8,128)(2,1)S(1)} %get-tuple-element.29.dense, bf16[2048,1920]{1,0:T(8,128)(2,1)S(1)} %get-tuple-element.30.fock), custom_call_target="tpu_custom_call" | custom-call | tf_op jit(solution)/shard_map/dress_rows/pallas_call | solution.py:277
  41.9 0.0 collective-permute-done.3.amplitudes
  41.9 3.7 %dress_rows.4 = (bf16[480,1920]{1,0:T(8,128)(2,1)}, s32[8,128]{1,0:T(8,128)S(1)}) custom-call(bf16[160,1920]{1,0:T(8,128)(2,1)S(1)} %collective-permute-done.3.amplitudes, bf16[1920,2048]{1,0:T(8,128)(2,1)S(1)} %get-tuple-element.29.dense, bf16[2048,1920]{1,0:T(8,128)(2,1)S(1)} %get-tuple-element.30.fock, ...), custom_call_target="tpu_custom_call", output_to_operand_aliasing={{0}: (3, {})} | custom-call | tf_op jit(solution)/shard_map/dress_rows/pallas_call | solution.py:277
  45.5 0.0 collective-permute-done.2.received
  45.6 4.2 %dress_rows.5 = (bf16[480,1920]{1,0:T(8,128)(2,1)}, s32[8,128]{1,0:T(8,128)}) custom-call(bf16[160,1920]{1,0:T(8,128)(2,1)S(1)} %owned_rows.3.amplitudes, bf16[1920,2048]{1,0:T(8,128)(2,1)S(1)} %get-tuple-element.29.dense, bf16[2048,1920]{1,0:T(8,128)(2,1)S(1)} %get-tuple-element.30.fock, ...), custom_call_target="tpu_custom_call", output_to_operand_aliasing={{0}: (3, {})} | custom-call | tf_op jit(solution)/shard_map/dress_rows/pallas_call | solution.py:277
  (5 shorter events, 0.1 us)
Async XLA Ops:
  1.2 18.4 %collective-permute-start.1 = (bf16[160,1920]{1,0:T(8,128)(2,1)S(1)}, bf16[160,1920]{1,0:T(8,128)(2,1)S(1)}, u32[]{:S(2)}, u32[]{:S(2)}) collective-permute-start(bf16[160,1920]{1,0:T(8,128)(2,1)S(1)} %get-tuple-element.21.kept), channel_id=1, source_target_pairs={{8,1},{16,2},{26,3},{12,5},{20,6},{30,7},{1,8},{18,10},{24,11},{5,... | collective-permute-start | bytes 1843208 | tf_op jit(solution)/shard_map/ppermute | solution.py:341
  2.5 17.4 %collective-permute-start = (bf16[80,1920]{1,0:T(8,128)(2,1)S(1)}, bf16[80,1920]{1,0:T(8,128)(2,1)S(1)}, u32[]{:S(2)}, u32[]{:S(2)}) collective-permute-start(bf16[80,1920]{1,0:T(8,128)(2,1)S(1)} %get-tuple-element.20), channel_id=1, source_target_pairs={{4,0},{5,1},{6,2},{7,3},{0,4},{1,5},{2,6},{3,7},{12,8},{13,9},{14,... | collective-permute-start | bytes 921608 | tf_op jit(solution)/shard_map/ppermute | solution.py:334
  6.2 15.1 %collective-permute-start.5 = (bf16[480,512]{1,0:T(8,128)(2,1)S(1)}, bf16[480,512]{1,0:T(8,128)(2,1)S(1)}, u32[]{:S(2)}, u32[]{:S(2)}) collective-permute-start(bf16[480,512]{1,0:T(8,128)(2,1)S(1)} %get-tuple-element.24), channel_id=1, source_target_pairs={{1,0},{0,1},{3,2},{2,3},{5,4},{4,5},{7,6},{6,7},{9,8},{8,9},{11,10... | collective-permute-start | bytes 1474568 | tf_op jit(solution)/shard_map/ppermute | solution.py:329
  8.5 24.3 %collective-permute-start.4 = (bf16[480,512]{1,0:T(8,128)(2,1)S(1)}, bf16[480,512]{1,0:T(8,128)(2,1)S(1)}, u32[]{:S(2)}, u32[]{:S(2)}) collective-permute-start(bf16[480,512]{1,0:T(8,128)(2,1)S(1)} %get-tuple-element.22.folded), channel_id=1, source_target_pairs={{2,0},{3,1},{0,2},{1,3},{6,4},{7,5},{4,6},{5,7},{10,8},{11,9},{8,1... | collective-permute-start | bytes 1474568 | tf_op jit(solution)/shard_map/ppermute | solution.py:328
  19.6 22.3 %collective-permute-start.3 = (bf16[160,1920]{1,0:T(8,128)(2,1)S(1)}, bf16[160,1920]{1,0:T(8,128)(2,1)S(1)}, u32[]{:S(2)}, u32[]{:S(2)}) collective-permute-start(bf16[160,1920]{1,0:T(8,128)(2,1)S(1)} %owned_rows.2.refs_1_.amplitudes), channel_id=1, source_target_pairs={{4,0},{5,1},{6,2},{7,3},{0,4},{1,5},{2,6},{3,7},{12,8},{13,9},{14,... | collective-permute-start | bytes 1843208 | tf_op jit(solution)/shard_map/ppermute | solution.py:345
  19.9 25.6 %collective-permute-start.2 = (bf16[160,1920]{1,0:T(8,128)(2,1)S(1)}, bf16[160,1920]{1,0:T(8,128)(2,1)S(1)}, u32[]{:S(2)}, u32[]{:S(2)}) collective-permute-start(bf16[160,1920]{1,0:T(8,128)(2,1)S(1)} %after.2.kept), channel_id=1, source_target_pairs={{8,1},{16,2},{26,3},{12,5},{20,6},{30,7},{1,8},{18,10},{24,11},{5,... | collective-permute-start | bytes 1843208 | tf_op jit(solution)/shard_map/ppermute | solution.py:344
  32.8 2.6 %collective-permute-start.6 = (bf16[480,512]{1,0:T(8,128)(2,1)S(1)}, bf16[480,512]{1,0:T(8,128)(2,1)S(1)}, u32[]{:S(2)}, u32[]{:S(2)}) collective-permute-start(bf16[480,512]{1,0:T(8,128)(2,1)S(1)} %after.3.folded), channel_id=1, source_target_pairs={{1,0},{0,1},{3,2},{2,3},{5,4},{4,5},{7,6},{6,7},{9,8},{8,9},{11,10... | collective-permute-start | bytes 1474568 | tf_op jit(solution)/shard_map/ppermute | solution.py:348

commit v11 on v10

--- a/solution.py
+++ b/solution.py
@@ -10,6 +10,7 @@
 LANES = 128
 SUBLANES = 16
 MIB = 1 << 20
+TOKEN = pltpu.VMEM((8, LANES), jnp.int32)
 NOTHING = pl.CostEstimate(flops=0, bytes_accessed=0, transcendentals=0)
 
 
@@ -113,12 +114,14 @@
     )(sizes, pair, pltpu.with_memory_space_constraint(panel, pltpu.HBM))
 
 
-def spread_kernel(slot, groups, first, sizes, pair, folded, other, *refs):
+def spread_kernel(slot, groups, first, signed, sizes, pair, folded, other, dense, *refs):
+    if signed:
+        refs[0][...] = jnp.zeros_like(refs[0])
+        refs = refs[1:]
     if first:
-        dense, token, fock_out, bounds, turned, sems = refs
+        fock_out, bounds, turned, sems = refs
     else:
-        dense, token, bounds, turned = refs
-    token[...] = jnp.zeros_like(token)
+        bounds, turned = refs
     quarter, fold = folded.shape
     virtuals, total = dense.shape
     width = total // groups
@@ -159,16 +162,14 @@
         copy.wait()
 
 
-def spread(slot, groups, folded, sizes, pair, *, fock=None, dense=None):
+def spread(slot, groups, folded, sizes, pair, *, fock=None, dense=None, signed=False):
     quarter, fold = folded.shape
     first = dense is None
     virtuals = fock.shape[0] if first else dense.shape[0]
     width = rounded(quarter, LANES)
     smem = pl.BlockSpec(memory_space=pltpu.SMEM)
     vmem = pl.BlockSpec(memory_space=pltpu.VMEM)
-    out_shape = [
-        pltpu.VMEM((virtuals, groups * width), folded.dtype), pltpu.VMEM((8, LANES), jnp.int32)
-    ]
+    out_shape = [pltpu.VMEM((virtuals, groups * width), folded.dtype)] + [TOKEN] * signed
     scratch = [
         pltpu.SMEM((sizes.shape[0] + 1,), jnp.int32),
         pltpu.VMEM((fold, width), jnp.float32),
@@ -180,7 +181,7 @@
     else:
         other = pltpu.with_memory_space_constraint(dense, pltpu.VMEM)
     return pl.pallas_call(
-        functools.partial(spread_kernel, slot, groups, first),
+        functools.partial(spread_kernel, slot, groups, first, signed),
         out_shape=out_shape,
         in_specs=[smem, smem, vmem, pl.BlockSpec(memory_space=pl.ANY)],
         out_specs=[vmem] * len(out_shape),
@@ -235,59 +236,81 @@
     return [(first, min(tile, total - first)) for first in range(0, total, tile)]
 
 
-def dress_kernel(spans, rows, members, has_base, amplitudes, dense, fock, *refs):
-    if has_base:
+def dress_kernel(job, amplitudes, dense, fock, *refs):
+    columns, spans, rows, members, has_sums, has_base, signed = job
+    if has_sums:
+        sums, refs = refs[0], refs[1:]
+    refs = refs[has_base:]
+    result, refs = refs[0], refs[1:]
+    if signed:
+        refs[0][...] = jnp.zeros_like(refs[0])
         refs = refs[1:]
-    result, token, coupled, dressed, sems = refs
-    token[...] = jnp.zeros_like(token)
-    virtuals, total = dense.shape
-    block = lax.axis_index("blk")
-    places = [
-        pl.multiple_of(lax.rem(block + by, members) * rows + offset, SUBLANES)
-        for by, offset, _ in spans
-    ]
-    for first, tile in column_tiles(total, 512):
+    virtuals = dense.shape[0]
+    begin, end = columns
+    coupled = refs[0]
+    for first, tile in column_tiles(end - begin, 512):
         coupled[:, first:first + tile] = jnp.dot(
-            amplitudes[...], dense[:, first:first + tile], preferred_element_type=jnp.float32
+            amplitudes[...], dense[:, begin + first:begin + first + tile],
+            preferred_element_type=jnp.float32,
         ).astype(coupled.dtype)
+    if spans:
+        dressed, sems = refs[1:]
+        block = lax.axis_index("blk")
+        places = [
+            pl.multiple_of(lax.rem(block + by, members) * rows + offset, SUBLANES)
+            for by, offset, _ in spans
+        ]
     copies = []
     for t, (first, tile) in enumerate(column_tiles(virtuals, 512)):
-        dressed[:, first:first + tile] = jnp.dot(
-            coupled[...], fock[:, first:first + tile], preferred_element_type=jnp.float32
-        ).astype(dressed.dtype)
-        begin = 0
+        here = slice(first, first + tile)
+        total = jnp.dot(
+            coupled[...], fock[begin:end, here], preferred_element_type=jnp.float32
+        )
+        if has_sums:
+            total = total + sums[:, here]
+        if not spans:
+            result[:, here] = total
+            continue
+        dressed[:, here] = total.astype(dressed.dtype)
+        top = 0
         for p, (_, _, size) in enumerate(spans):
             copies.append(pltpu.make_async_copy(
-                dressed.at[pl.ds(begin, size), pl.ds(first, tile)],
+                dressed.at[pl.ds(top, size), pl.ds(first, tile)],
                 result.at[pl.ds(places[p], size), pl.ds(first, tile)],
                 sems.at[p, t],
             ))
             copies[-1].start()
-            begin += size
+            top += size
     for copy in copies:
         copy.wait()
 
 
-def dress(amplitudes, spans, dense, fock, base, rows, members, out_rows):
+def dress(amplitudes, dense, fock, *, columns=None, sums=None, spans=(), base=None, rows=0, members=1,
+          out_rows=0, signed=False):
     height, virtuals = amplitudes.shape
+    begin, end = columns or (0, dense.shape[1])
     vmem = pl.BlockSpec(memory_space=pltpu.VMEM)
     anywhere = pl.BlockSpec(memory_space=pl.ANY)
-    pinned = [pltpu.with_memory_space_constraint(x, pltpu.VMEM) for x in (dense, fock)]
+    pinned = [dense, fock] + ([] if sums is None else [sums])
+    pinned = [pltpu.with_memory_space_constraint(x, pltpu.VMEM) for x in pinned]
     bases = [] if base is None else [base]
-    return pl.pallas_call(
-        functools.partial(dress_kernel, spans, rows, members, base is not None),
-        out_shape=(
-            jax.ShapeDtypeStruct((out_rows, virtuals), amplitudes.dtype),
-            pltpu.VMEM((8, LANES), jnp.int32),
-        ),
-        in_specs=[vmem] * 3 + [anywhere] * len(bases),
-        out_specs=(anywhere, vmem),
-        input_output_aliases={} if base is None else {3: 0},
-        scratch_shapes=[
-            pltpu.VMEM((height, dense.shape[1]), amplitudes.dtype),
+    scratch = [pltpu.VMEM((height, end - begin), amplitudes.dtype)]
+    if spans:
+        out_shape = [jax.ShapeDtypeStruct((out_rows, virtuals), amplitudes.dtype)]
+        scratch += [
             pltpu.VMEM((height, virtuals), amplitudes.dtype),
             pltpu.SemaphoreType.DMA((len(spans), len(column_tiles(virtuals, 512)))),
-        ],
+        ]
+    else:
+        out_shape = [pltpu.VMEM((height, virtuals), jnp.float32)]
+    job = ((begin, end), spans, rows, members, sums is not None, base is not None, signed)
+    return pl.pallas_call(
+        functools.partial(dress_kernel, job),
+        out_shape=out_shape + [TOKEN] * signed,
+        in_specs=[vmem] * (1 + len(pinned)) + [anywhere] * len(bases),
+        out_specs=[anywhere if spans else vmem] + [vmem] * signed,
+        input_output_aliases={} if base is None else {1 + len(pinned): 0},
+        scratch_shapes=scratch,
         compiler_params=pltpu.CompilerParams(vmem_limit_bytes=16 * MIB),
         cost_estimate=NOTHING,
         name="dress_rows",
@@ -337,31 +360,39 @@
             top = amplitudes
 
         spread_one = functools.partial(spread, sizes=irrep_sizes, pair=pair_irreps)
-        dense, token, fock = spread_one(0, groups, own, fock=virt_fock)
+        dense, token, fock = spread_one(0, groups, own, fock=virt_fock, signed=True)
         top = owned(lax.ppermute(top, axes, to_group), top, members, token)
         if early < rows:
             lows = after(lows, top)
             late = lax.ppermute(lows, axes, to_group)
         tops = [top] + [lax.ppermute(top, axes, to_member(by)) for by in range(1, members)]
-        dense, token = spread_one(1, groups, beside, dense=dense)
-        across = after(across, token)
+        dense, = spread_one(1, groups, beside, dense=dense)
+        near = 2 * dense.shape[1] // groups
+        if early < rows:
+            sums, token = dress(top, dense, fock, columns=(0, near), signed=True)
+            across = after(across, token)
         both = lax.ppermute(across, axes, to_slot(1))
-        dense, _ = spread_one(2, groups, across, dense=dense)
-        dense, _ = spread_one(3, groups, both, dense=dense)
+        dense, = spread_one(2, groups, across, dense=dense)
+        dense, = spread_one(3, groups, both, dense=dense)
 
         if early < rows:
-            result = None
-            for by, piece in enumerate(tops):
-                spans = [(by, 0, early)]
-                result, token = dress(piece, spans, dense, fock, result, rows, members, out_rows)
-            spans = [(by, early, rows - early) for by in range(members)]
-            lows = owned(late, lows, members, token)
-            result, _ = dress(lows, spans, dense, fock, result, rows, members, out_rows)
+            place = dict(rows=rows, members=members, out_rows=out_rows)
+            result, = dress(
+                top, dense, fock, columns=(near, dense.shape[1]), sums=sums, spans=((0, 0, early),),
+                **place,
+            )
+            for by in range(1, members):
+                result, *token = dress(
+                    tops[by], dense, fock, spans=((by, 0, early),), base=result,
+                    signed=by == members - 1, **place,
+                )
+            lows = owned(late, lows, members, *token)
+            spans = tuple((by, early, rows - early) for by in range(members))
+            result, = dress(lows, dense, fock, spans=spans, base=result, **place)
         else:
             member = lax.axis_index("blk") % members
             ordered = jnp.roll(jnp.stack(tops), member, axis=0).reshape(out_rows, virtuals)
-            spans = [(0, 0, out_rows)]
-            result, _ = dress(ordered, spans, dense, fock, None, 0, members, out_rows)
+            result, = dress(ordered, dense, fock, spans=((0, 0, out_rows),), out_rows=out_rows)
         return result[:, None, :]
 
     return local

time: 50.1 us -> 46.4 us (0.926)
  Pallas kernels: 26 us -> 23.8 us
  waiting for transfers between devices: 16.4 us -> 14.9 us
    pallas_call x7 -> x8, Pallas kernels: 22.1 us -> 19.9 us  [the longest x4 11.1 us: dress(): pl.pallas_call(functools.partial(dress_kernel, job), out_shape=out_shape...]
    ppermute x1, waiting for transfers between devices: 9.95 us -> 8.47 us  [local(): across = lax.ppermute(own, axes, to_slot(2))]
where the time goes in v11:
time: 46.4 us; the launch traced here: 46.1 us
  Pallas kernels  23.8 us (51%)
  waiting for transfers between devices  14.9 us (32%)
  starting transfers between devices  6.56 us (14%)
  between operations  0.81 us (2%)
    pallas_call x4, Pallas kernels, dress(): pl.pallas_call(functools.partial(dress_kernel, job), out_shape=out_shape...  11.1 us
    pallas_call x4, Pallas kernels, spread(): pl.pallas_call(functools.partial(spread_kernel, slot, groups, first, sign...  8.84 us
    ppermute x1, waiting for transfers between devices, local(): across = lax.ppermute(own, axes, to_slot(2))  8.47 us
    ppermute x1, waiting for transfers between devices, local(): top = owned(lax.ppermute(top, axes, to_group), top, members, token)  6.42 us
    pallas_call x1, Pallas kernels, fold_panel(): pl.pallas_call(functools.partial(fold_kernel, chunk), out_shape=[pltpu.VM...  2.7 us
    ppermute x1, starting transfers between devices, local(): beside = lax.ppermute(own_again, axes, to_slot(1))  2.37 us
    ppermute x1, starting transfers between devices, local(): top = owned(lax.ppermute(top, axes, to_group), top, members, token)  1.29 us
    ppermute x1, starting transfers between devices, local(): late = lax.ppermute(lows, axes, to_group)  1.28 us
  transfers between devices with their start and end apart: 7, of which 2 were waited for; matrix products, arithmetic and copies ran while one was open for 0% of the time, Pallas kernels for 41%

profile of v11, /device:TPU:27, one launch (start us, length us, event | category | flops | bytes accessed | tf_op | source)
XLA Modules:
  0.0 46.1 jit_solution(1573360102409260997)
XLA Ops:
  0.0 1.2 %cut_rows.1 = (bf16[160,1920]{1,0:T(8,128)(2,1)S(1)}, bf16[80,1920]{1,0:T(8,128)(2,1)S(1)}) custom-call(bf16[240,1920]{1,0:T(8,128)(2,1)} %whole.1), custom_call_target="tpu_custom_call" | custom-call | tf_op jit(solution)/shard_map/cut_rows/pallas_call | solution.py:53
  1.2 1.3 %collective-permute-start.1 = (bf16[160,1920]{1,0:T(8,128)(2,1)S(1)}, bf16[160,1920]{1,0:T(8,128)(2,1)S(1)}, u32[]{:S(2)}, u32[]{:S(2)}) collective-permute-start(bf16[160,1920]{1,0:T(8,128)(2,1)S(1)} %get-tuple-element.17.kept), channel_id=1, source_target_pairs={{8,1},{16,2},{26,3},{12,5},{20,6},{30,7},{1,8},{18,10},{24,11},{5,... | collective-permute-start | bytes 1843208 | tf_op jit(solution)/shard_map/ppermute | solution.py:364
  2.5 0.3 collective-permute-start
  3.4 2.7 %fold_panel.1 = (bf16[480,512]{1,0:T(8,128)(2,1)S(1)}, bf16[480,512]{1,0:T(8,128)(2,1)S(1)}) custom-call(s32[8]{0:T(128)} %sizes.9, s32[1]{0:T(128)S(6)} %copy.24.pair, bf16[480,1920]{1,0:T(8,128)(2,1)} %bitcast.4), custom_call_target="tpu_custom_call" | custom-call | tf_op jit(solution)/shard_map/fold_panel/pallas_call | solution.py:101
  6.2 2.4 %collective-permute-start.5 = (bf16[480,512]{1,0:T(8,128)(2,1)S(1)}, bf16[480,512]{1,0:T(8,128)(2,1)S(1)}, u32[]{:S(2)}, u32[]{:S(2)}) collective-permute-start(bf16[480,512]{1,0:T(8,128)(2,1)S(1)} %get-tuple-element.20), channel_id=1, source_target_pairs={{1,0},{0,1},{3,2},{2,3},{5,4},{4,5},{7,6},{6,7},{9,8},{8,9},{11,10... | collective-permute-start | bytes 1474568 | tf_op jit(solution)/shard_map/ppermute | solution.py:352
  8.5 0.5 %collective-permute-start.4 = (bf16[480,512]{1,0:T(8,128)(2,1)S(1)}, bf16[480,512]{1,0:T(8,128)(2,1)S(1)}, u32[]{:S(2)}, u32[]{:S(2)}) collective-permute-start(bf16[480,512]{1,0:T(8,128)(2,1)S(1)} %get-tuple-element.18.folded), channel_id=1, source_target_pairs={{2,0},{3,1},{0,2},{1,3},{6,4},{7,5},{4,6},{5,7},{10,8},{11,9},{8,1... | collective-permute-start | bytes 1474568 | tf_op jit(solution)/shard_map/ppermute | solution.py:351
  9.1 4.0 %spread_panel.4 = (bf16[1920,2048]{1,0:T(8,128)(2,1)S(1)}, s32[8,128]{1,0:T(8,128)S(1)}, bf16[2048,1920]{1,0:T(8,128)(2,1)S(1)}) custom-call(s32[8]{0:T(128)} %sizes.9, s32[1]{0:T(128)S(6)} %copy.24.pair, bf16[480,512]{1,0:T(8,128)(2,1)S(1)} %get-tuple-element.18.folded, bf16[1920,1920]{1,0:T(8,128)(2,1)} %other.1), custom_call_target="tpu_custom_call" | custom-call | tf_op jit(solution)/shard_map/spread_panel/pallas_call | solution.py:183
  13.1 0.0 collective-permute-done
  13.1 6.4 %collective-permute-done.1.received = bf16[160,1920]{1,0:T(8,128)(2,1)S(1)} collective-permute-done((bf16[160,1920]{1,0:T(8,128)(2,1)S(1)}, bf16[160,1920]{1,0:T(8,128)(2,1)S(1)}, u32[]{:S(2)}, u32[]{:S(2)}) %collective-permute-start.1) | collective-permute-done | bytes 614432 | tf_op jit(solution)/shard_map/ppermute | solution.py:364
  19.6 0.3 collective-permute-start.3
  19.9 1.3 %collective-permute-start.2 = (bf16[160,1920]{1,0:T(8,128)(2,1)S(1)}, bf16[160,1920]{1,0:T(8,128)(2,1)S(1)}, u32[]{:S(2)}, u32[]{:S(2)}) collective-permute-start(bf16[160,1920]{1,0:T(8,128)(2,1)S(1)} %after.2.kept), channel_id=1, source_target_pairs={{8,1},{16,2},{26,3},{12,5},{20,6},{30,7},{1,8},{18,10},{24,11},{5,... | collective-permute-start | bytes 1843208 | tf_op jit(solution)/shard_map/ppermute | solution.py:367
  21.2 0.0 collective-permute-done.5.folded
  21.2 1.6 %spread_panel.5.dense.other = bf16[1920,2048]{1,0:T(8,128)(2,1)S(1)} custom-call(s32[8]{0:T(128)} %sizes.9, s32[1]{0:T(128)S(6)} %copy.24.pair, bf16[480,512]{1,0:T(8,128)(2,1)S(1)} %collective-permute-done.5.folded, bf16[1920,2048]{1,0:T(8,128)(2,1)S(1)} %get-tuple-element.21.other), custom_call_target="tpu_custom_call", output_to_operand_aliasing={{}: (3, {})} | custom-call | tf_op jit(solution)/shard_map/spread_panel/pallas_call | solution.py:183
  22.8 1.6 %dress_rows.4 = (f32[160,1920]{1,0:T(8,128)S(1)}, s32[8,128]{1,0:T(8,128)S(1)}) custom-call(bf16[160,1920]{1,0:T(8,128)(2,1)S(1)} %owned_rows.2.refs_1_.amplitudes, bf16[1920,2048]{1,0:T(8,128)(2,1)S(1)} %spread_panel.5.dense.other, bf16[2048,1920]{1,0:T(8,128)(2,1)S(1)} %get-tuple-element.22.fock), custom_call_target="tpu_custom_call" | custom-call | tf_op jit(solution)/shard_map/dress_rows/pallas_call | solution.py:307
  24.4 8.5 %collective-permute-done.4.refs_0_ = bf16[480,512]{1,0:T(8,128)(2,1)S(1)} collective-permute-done((bf16[480,512]{1,0:T(8,128)(2,1)S(1)}, bf16[480,512]{1,0:T(8,128)(2,1)S(1)}, u32[]{:S(2)}, u32[]{:S(2)}) %collective-permute-start.4) | collective-permute-done | bytes 491552 | tf_op jit(solution)/shard_map/ppermute | solution.py:351
  32.8 0.4 collective-permute-start.6
  33.3 1.6 %spread_panel.6.other = bf16[1920,2048]{1,0:T(8,128)(2,1)S(1)} custom-call(s32[8]{0:T(128)} %sizes.9, s32[1]{0:T(128)S(6)} %copy.24.pair, bf16[480,512]{1,0:T(8,128)(2,1)S(1)} %after.3.folded, bf16[1920,2048]{1,0:T(8,128)(2,1)S(1)} %spread_panel.5.dense.other), custom_call_target="tpu_custom_call", output_to_operand_aliasing={{}: (3, {})} | custom-call | tf_op jit(solution)/shard_map/spread_panel/pallas_call | solution.py:183
  34.9 0.0 collective-permute-done.6.folded
  34.9 1.6 %spread_panel.7.dense = bf16[1920,2048]{1,0:T(8,128)(2,1)S(1)} custom-call(s32[8]{0:T(128)} %sizes.9, s32[1]{0:T(128)S(6)} %copy.24.pair, bf16[480,512]{1,0:T(8,128)(2,1)S(1)} %collective-permute-done.6.folded, bf16[1920,2048]{1,0:T(8,128)(2,1)S(1)} %spread_panel.6.other), custom_call_target="tpu_custom_call", output_to_operand_aliasing={{}: (3, {})} | custom-call | tf_op jit(solution)/shard_map/spread_panel/pallas_call | solution.py:183
  36.5 2.3 %dress_rows.5.refs_0_ = bf16[480,1920]{1,0:T(8,128)(2,1)} custom-call(bf16[160,1920]{1,0:T(8,128)(2,1)S(1)} %owned_rows.2.refs_1_.amplitudes, bf16[1920,2048]{1,0:T(8,128)(2,1)S(1)} %spread_panel.7.dense, bf16[2048,1920]{1,0:T(8,128)(2,1)S(1)} %get-tuple-element.22.fock, f32[160,1920]{1,0:T(8,128)S(1)} %get-tuple-element.24.refs_0_), custom_call_target="tpu_custom_call" | custom-call | tf_op jit(solution)/shard_map/dress_rows/pallas_call | solution.py:307
  38.8 0.0 collective-permute-done.3.amplitudes
  38.8 3.6 %dress_rows.6 = (bf16[480,1920]{1,0:T(8,128)(2,1)}, s32[8,128]{1,0:T(8,128)S(1)}) custom-call(bf16[160,1920]{1,0:T(8,128)(2,1)S(1)} %collective-permute-done.3.amplitudes, bf16[1920,2048]{1,0:T(8,128)(2,1)S(1)} %spread_panel.7.dense, bf16[2048,1920]{1,0:T(8,128)(2,1)S(1)} %get-tuple-element.22.fock, ...), custom_call_target="tpu_custom_call", output_to_operand_aliasing={{0}: (3, {})} | custom-call | tf_op jit(solution)/shard_map/dress_rows/pallas_call | solution.py:307
  42.4 0.0 collective-permute-done.2.received
  42.5 3.7 %dress_rows.7 = bf16[480,1920]{1,0:T(8,128)(2,1)} custom-call(bf16[160,1920]{1,0:T(8,128)(2,1)S(1)} %owned_rows.3.amplitudes, bf16[1920,2048]{1,0:T(8,128)(2,1)S(1)} %spread_panel.7.dense, bf16[2048,1920]{1,0:T(8,128)(2,1)S(1)} %get-tuple-element.22.fock, bf16[480,1920]{1,0:T(8,128)(2,1)} %get-tuple-element.26.refs_0_), custom_call_target="tpu_custom_call", output_to_operand_aliasing={{}: (3, {})} | custom-call | tf_op jit(solution)/shard_map/dress_rows/pallas_call | solution.py:307
  (5 shorter events, 0.1 us)
Async XLA Ops:
  1.2 18.4 %collective-permute-start.1 = (bf16[160,1920]{1,0:T(8,128)(2,1)S(1)}, bf16[160,1920]{1,0:T(8,128)(2,1)S(1)}, u32[]{:S(2)}, u32[]{:S(2)}) collective-permute-start(bf16[160,1920]{1,0:T(8,128)(2,1)S(1)} %get-tuple-element.17.kept), channel_id=1, source_target_pairs={{8,1},{16,2},{26,3},{12,5},{20,6},{30,7},{1,8},{18,10},{24,11},{5,... | collective-permute-start | bytes 1843208 | tf_op jit(solution)/shard_map/ppermute | solution.py:364
  2.5 10.6 %collective-permute-start = (bf16[80,1920]{1,0:T(8,128)(2,1)S(1)}, bf16[80,1920]{1,0:T(8,128)(2,1)S(1)}, u32[]{:S(2)}, u32[]{:S(2)}) collective-permute-start(bf16[80,1920]{1,0:T(8,128)(2,1)S(1)} %get-tuple-element.16), channel_id=1, source_target_pairs={{4,0},{5,1},{6,2},{7,3},{0,4},{1,5},{2,6},{3,7},{12,8},{13,9},{14,... | collective-permute-start | bytes 921608 | tf_op jit(solution)/shard_map/ppermute | solution.py:357
  6.2 15.0 %collective-permute-start.5 = (bf16[480,512]{1,0:T(8,128)(2,1)S(1)}, bf16[480,512]{1,0:T(8,128)(2,1)S(1)}, u32[]{:S(2)}, u32[]{:S(2)}) collective-permute-start(bf16[480,512]{1,0:T(8,128)(2,1)S(1)} %get-tuple-element.20), channel_id=1, source_target_pairs={{1,0},{0,1},{3,2},{2,3},{5,4},{4,5},{7,6},{6,7},{9,8},{8,9},{11,10... | collective-permute-start | bytes 1474568 | tf_op jit(solution)/shard_map/ppermute | solution.py:352
  8.5 24.3 %collective-permute-start.4 = (bf16[480,512]{1,0:T(8,128)(2,1)S(1)}, bf16[480,512]{1,0:T(8,128)(2,1)S(1)}, u32[]{:S(2)}, u32[]{:S(2)}) collective-permute-start(bf16[480,512]{1,0:T(8,128)(2,1)S(1)} %get-tuple-element.18.folded), channel_id=1, source_target_pairs={{2,0},{3,1},{0,2},{1,3},{6,4},{7,5},{4,6},{5,7},{10,8},{11,9},{8,1... | collective-permute-start | bytes 1474568 | tf_op jit(solution)/shard_map/ppermute | solution.py:351
  19.6 19.2 %collective-permute-start.3 = (bf16[160,1920]{1,0:T(8,128)(2,1)S(1)}, bf16[160,1920]{1,0:T(8,128)(2,1)S(1)}, u32[]{:S(2)}, u32[]{:S(2)}) collective-permute-start(bf16[160,1920]{1,0:T(8,128)(2,1)S(1)} %owned_rows.2.refs_1_.amplitudes), channel_id=1, source_target_pairs={{4,0},{5,1},{6,2},{7,3},{0,4},{1,5},{2,6},{3,7},{12,8},{13,9},{14,... | collective-permute-start | bytes 1843208 | tf_op jit(solution)/shard_map/ppermute | solution.py:368
  19.9 22.5 %collective-permute-start.2 = (bf16[160,1920]{1,0:T(8,128)(2,1)S(1)}, bf16[160,1920]{1,0:T(8,128)(2,1)S(1)}, u32[]{:S(2)}, u32[]{:S(2)}) collective-permute-start(bf16[160,1920]{1,0:T(8,128)(2,1)S(1)} %after.2.kept), channel_id=1, source_target_pairs={{8,1},{16,2},{26,3},{12,5},{20,6},{30,7},{1,8},{18,10},{24,11},{5,... | collective-permute-start | bytes 1843208 | tf_op jit(solution)/shard_map/ppermute | solution.py:367
  32.8 2.1 %collective-permute-start.6 = (bf16[480,512]{1,0:T(8,128)(2,1)S(1)}, bf16[480,512]{1,0:T(8,128)(2,1)S(1)}, u32[]{:S(2)}, u32[]{:S(2)}) collective-permute-start(bf16[480,512]{1,0:T(8,128)(2,1)S(1)} %after.3.folded), channel_id=1, source_target_pairs={{1,0},{0,1},{3,2},{2,3},{5,4},{4,5},{7,6},{6,7},{9,8},{8,9},{11,10... | collective-permute-start | bytes 1474568 | tf_op jit(solution)/shard_map/ppermute | solution.py:374

commit v12 on v11

--- a/solution.py
+++ b/solution.py
@@ -62,14 +62,18 @@
     )(pltpu.with_memory_space_constraint(whole, pltpu.HBM))
 
 
-def fold_kernel(chunk, sizes, pair, source, folded, again, panel, bounds, sems):
+def fold_kernel(chunk, pair, sizes_in, source, folded, again, token, panel, sizes, bounds, sems):
     quarter, virtuals = panel.shape
     fold = folded.shape[1]
+    small = pltpu.make_async_copy(sizes_in, sizes, sems.at[quarter // chunk])
+    small.start()
     copies = []
     for k in range(quarter // chunk):
         rows = pl.ds(k * chunk, chunk)
         copies.append(pltpu.make_async_copy(source.at[rows], panel.at[rows], sems.at[k]))
         copies[-1].start()
+    token[...] = jnp.zeros_like(token)
+    small.wait()
     fill_bounds(sizes, bounds)
     start = lax.axis_index("grp") * quarter
     step = 32 if chunk % 32 == 0 else SUBLANES
@@ -97,58 +101,35 @@
 def fold_panel(panel, sizes, pair, fold):
     quarter, virtuals = panel.shape
     chunk = quarter // 5 if quarter % (5 * SUBLANES) == 0 else quarter
-    smem = pl.BlockSpec(memory_space=pltpu.SMEM)
     return pl.pallas_call(
         functools.partial(fold_kernel, chunk),
-        out_shape=[pltpu.VMEM((quarter, fold), panel.dtype)] * 2,
-        in_specs=[smem, smem, pl.BlockSpec(memory_space=pl.ANY)],
-        out_specs=[pl.BlockSpec(memory_space=pltpu.VMEM)] * 2,
+        out_shape=[pltpu.VMEM((quarter, fold), panel.dtype)] * 2 + [TOKEN],
+        in_specs=[pl.BlockSpec(memory_space=pltpu.SMEM)] + [pl.BlockSpec(memory_space=pl.ANY)] * 2,
+        out_specs=[pl.BlockSpec(memory_space=pltpu.VMEM)] * 3,
         scratch_shapes=[
             pltpu.VMEM((quarter, virtuals), panel.dtype),
+            pltpu.SMEM(sizes.shape, jnp.int32),
             pltpu.SMEM((sizes.shape[0] + 1,), jnp.int32),
-            pltpu.SemaphoreType.DMA((quarter // chunk,)),
+            pltpu.SemaphoreType.DMA((quarter // chunk + 1,)),
         ],
         compiler_params=pltpu.CompilerParams(vmem_limit_bytes=8 * MIB),
         cost_estimate=NOTHING,
         name="fold_panel",
-    )(sizes, pair, pltpu.with_memory_space_constraint(panel, pltpu.HBM))
-
-
-def spread_kernel(slot, groups, first, signed, sizes, pair, folded, other, dense, *refs):
-    if signed:
-        refs[0][...] = jnp.zeros_like(refs[0])
-        refs = refs[1:]
-    if first:
-        fock_out, bounds, turned, sems = refs
-    else:
-        bounds, turned = refs
+    )(pair, sizes, pltpu.with_memory_space_constraint(panel, pltpu.HBM))
+
+
+def place_panel(slot, folded, ranges, dense, turned):
     quarter, fold = folded.shape
-    virtuals, total = dense.shape
-    width = total // groups
-    group = lax.axis_index("grp")
-    copies = []
-    if first:
-        for k in range(groups):
-            start = pl.multiple_of(jnp.bitwise_xor(group, k) * quarter, SUBLANES)
-            copies.append(pltpu.make_async_copy(
-                other.at[pl.ds(start, quarter)], fock_out.at[pl.ds(k * width, quarter)], sems.at[k]
-            ))
-            copies[-1].start()
-            if width > quarter:
-                fock_out[k * width + quarter:(k + 1) * width, :] = jnp.zeros(
-                    (width - quarter, virtuals), fock_out.dtype
-                )
-    fill_bounds(sizes, bounds)
+    virtuals = dense.shape[0]
+    width = turned.shape[1]
+    columns = slice(slot * width, (slot + 1) * width)
     step = 32
     values = folded[...].astype(jnp.float32)
     if width > quarter:
         values = jnp.concatenate([values, jnp.zeros((width - quarter, fold), jnp.float32)])
     turned[...] = values.T
-    start = jnp.bitwise_xor(group, slot) * quarter
-    b = start + lax.broadcasted_iota(jnp.int32, (8, width), 1)
-    low, high = wanted_range(b, pair, bounds, sizes.shape[0])
-    low = jnp.concatenate([low] * (step // 8))
-    high = jnp.concatenate([high] * (step // 8))
+    low = jnp.concatenate([ranges[0, :, columns]] * (step // 8))
+    high = jnp.concatenate([ranges[1, :, columns]] * (step // 8))
 
     @pl.loop(0, virtuals // step, unroll=4)
     def _(i):
@@ -156,41 +137,87 @@
         source = pl.multiple_of(lax.rem(row, fold), step)
         c = row + lax.broadcasted_iota(jnp.int32, (step, width), 0)
         kept = jnp.where((c >= low) & (c < high), turned[pl.ds(source, step), :], 0.0)
-        dense[pl.ds(row, step), slot * width:(slot + 1) * width] = kept.astype(dense.dtype)
-
+        dense[pl.ds(row, step), columns] = kept.astype(dense.dtype)
+
+
+def first_spread_kernel(
+    groups, sizes, pair, folded, fock, dense, fock_out, ranges, token, bounds, turned, sems
+):
+    quarter = folded.shape[0]
+    virtuals = dense.shape[0]
+    width = turned.shape[1]
+    group = lax.axis_index("grp")
+    copies = []
+    for k in range(groups):
+        start = pl.multiple_of(jnp.bitwise_xor(group, k) * quarter, SUBLANES)
+        copies.append(pltpu.make_async_copy(
+            fock.at[pl.ds(start, quarter)], fock_out.at[pl.ds(k * width, quarter)], sems.at[k]
+        ))
+        copies[-1].start()
+        if width > quarter:
+            fock_out[k * width + quarter:(k + 1) * width, :] = jnp.zeros(
+                (width - quarter, virtuals), fock_out.dtype
+            )
+    token[...] = jnp.zeros_like(token)
+    fill_bounds(sizes, bounds)
+    for k in range(groups):
+        start = jnp.bitwise_xor(group, k) * quarter
+        b = start + lax.broadcasted_iota(jnp.int32, (8, width), 1)
+        low, high = wanted_range(b, pair, bounds, sizes.shape[0])
+        ranges[0, :, k * width:(k + 1) * width] = low
+        ranges[1, :, k * width:(k + 1) * width] = high
+    place_panel(0, folded, ranges, dense, turned)
     for copy in copies:
         copy.wait()
 
 
-def spread(slot, groups, folded, sizes, pair, *, fock=None, dense=None, signed=False):
+def first_spread(groups, folded, fock, sizes, pair):
     quarter, fold = folded.shape
-    first = dense is None
-    virtuals = fock.shape[0] if first else dense.shape[0]
+    virtuals = fock.shape[0]
     width = rounded(quarter, LANES)
     smem = pl.BlockSpec(memory_space=pltpu.SMEM)
     vmem = pl.BlockSpec(memory_space=pltpu.VMEM)
-    out_shape = [pltpu.VMEM((virtuals, groups * width), folded.dtype)] + [TOKEN] * signed
-    scratch = [
-        pltpu.SMEM((sizes.shape[0] + 1,), jnp.int32),
-        pltpu.VMEM((fold, width), jnp.float32),
-    ]
-    if first:
-        out_shape.append(pltpu.VMEM((groups * width, virtuals), fock.dtype))
-        scratch.append(pltpu.SemaphoreType.DMA((groups,)))
-        other = pltpu.with_memory_space_constraint(fock, pltpu.HBM)
-    else:
-        other = pltpu.with_memory_space_constraint(dense, pltpu.VMEM)
-    return pl.pallas_call(
-        functools.partial(spread_kernel, slot, groups, first, signed),
-        out_shape=out_shape,
+    return pl.pallas_call(
+        functools.partial(first_spread_kernel, groups),
+        out_shape=[
+            pltpu.VMEM((virtuals, groups * width), folded.dtype),
+            pltpu.VMEM((groups * width, virtuals), fock.dtype),
+            pltpu.VMEM((2, 8, groups * width), jnp.int32),
+            TOKEN,
+        ],
         in_specs=[smem, smem, vmem, pl.BlockSpec(memory_space=pl.ANY)],
-        out_specs=[vmem] * len(out_shape),
-        input_output_aliases={} if first else {3: 0},
-        scratch_shapes=scratch,
+        out_specs=[vmem] * 4,
+        scratch_shapes=[
+            pltpu.SMEM((sizes.shape[0] + 1,), jnp.int32),
+            pltpu.VMEM((fold, width), jnp.float32),
+            pltpu.SemaphoreType.DMA((groups,)),
+        ],
         compiler_params=pltpu.CompilerParams(vmem_limit_bytes=8 * MIB),
         cost_estimate=NOTHING,
+        name="first_spread",
+    )(sizes, pair, folded, pltpu.with_memory_space_constraint(fock, pltpu.HBM))
+
+
+def spread_kernel(slot, folded, ranges, before, dense, turned):
+    place_panel(slot, folded, ranges, dense, turned)
+
+
+def spread(slot, folded, ranges, dense):
+    fold = folded.shape[1]
+    width = rounded(folded.shape[0], LANES)
+    vmem = pl.BlockSpec(memory_space=pltpu.VMEM)
+    pinned = [pltpu.with_memory_space_constraint(x, pltpu.VMEM) for x in (ranges, dense)]
+    return pl.pallas_call(
+        functools.partial(spread_kernel, slot),
+        out_shape=pltpu.VMEM(dense.shape, dense.dtype),
+        in_specs=[vmem, vmem, pl.BlockSpec(memory_space=pl.ANY)],
+        out_specs=vmem,
+        input_output_aliases={2: 0},
+        scratch_shapes=[pltpu.VMEM((fold, width), jnp.float32)],
+        compiler_params=pltpu.CompilerParams(vmem_limit_bytes=8 * MIB),
+        cost_estimate=NOTHING,
         name="spread_panel",
-    )(sizes, pair, folded, other)
+    )(folded, *pinned)
 
 
 def after(array, *others):
@@ -347,33 +374,33 @@
         panel = jnp.swapaxes(hole_panel[:, 0, :], 0, 1)
         irrep_sizes = pltpu.with_memory_space_constraint(irrep_sizes, pltpu.HBM)
 
-        own, own_again = fold_panel(panel, irrep_sizes, pair_irreps, fold)
+        own, own_again, token = fold_panel(panel, irrep_sizes, pair_irreps, fold)
         across = lax.ppermute(own, axes, to_slot(2))
         beside = lax.ppermute(own_again, axes, to_slot(1))
 
         early = rounded(rows * 2 // 3, SUBLANES) if rows % SUBLANES == 0 else rows
         if early < rows:
             top, low = cut(amplitudes, (early, rows - early))
+            low = after(low, token)
             lows = [low] + [lax.ppermute(low, axes, to_member(by)) for by in range(1, members)]
             lows = jnp.concatenate(lows)
         else:
             top = amplitudes
 
-        spread_one = functools.partial(spread, sizes=irrep_sizes, pair=pair_irreps)
-        dense, token, fock = spread_one(0, groups, own, fock=virt_fock, signed=True)
+        dense, fock, ranges, token = first_spread(groups, own, virt_fock, irrep_sizes, pair_irreps)
         top = owned(lax.ppermute(top, axes, to_group), top, members, token)
         if early < rows:
             lows = after(lows, top)
             late = lax.ppermute(lows, axes, to_group)
         tops = [top] + [lax.ppermute(top, axes, to_member(by)) for by in range(1, members)]
-        dense, = spread_one(1, groups, beside, dense=dense)
+        dense = spread(1, beside, ranges, dense)
         near = 2 * dense.shape[1] // groups
         if early < rows:
             sums, token = dress(top, dense, fock, columns=(0, near), signed=True)
             across = after(across, token)
         both = lax.ppermute(across, axes, to_slot(1))
-        dense, = spread_one(2, groups, across, dense=dense)
-        dense, = spread_one(3, groups, both, dense=dense)
+        dense = spread(2, across, ranges, dense)
+        dense = spread(3, both, ranges, dense)
 
         if early < rows:
             place = dict(rows=rows, members=members, out_rows=out_rows)

time: 46.4 us -> 45.6 us (0.983)
  Pallas kernels: 23.8 us -> 21.2 us
  waiting for transfers between devices: 14.9 us -> 16.8 us
    pallas_call x4, Pallas kernels: 8.84 us -> 6.86 us  [the longest x1 4 us: first_spread(): pl.pallas_call(functools.partial(first_spread_kernel, groups), out_shape=...]
    ppermute x1, waiting for transfers between devices: 6.42 us -> 7.14 us  [local(): top = owned(lax.ppermute(top, axes, to_group), top, members, token)]
    ppermute x1, waiting for transfers between devices: 8.47 us -> 9.13 us  [local(): across = lax.ppermute(own, axes, to_slot(2))]
    pallas_call x1, Pallas kernels: 2.7 us -> 2.05 us  [fold_panel(): pl.pallas_call(functools.partial(fold_kernel, chunk), out_shape=[pltpu.VM...]
    ppermute x1, waiting for transfers between devices: 0.01 us -> 0.53 us  [local(): both = lax.ppermute(across, axes, to_slot(1))]
  transfers between devices with their start and end apart: 7 -> 7, of which waited for: 2 -> 3; matrix products, arithmetic and copies ran while one was open for 0% -> 0% of each run, Pallas kernels for 41% -> 36%
where the time goes in v12:
time: 45.6 us; the launch traced here: 45.4 us
  Pallas kernels  21.2 us (46%)
  waiting for transfers between devices  16.8 us (37%)
  starting transfers between devices  6.47 us (14%)
  between operations  0.8 us (2%)
    pallas_call x4, Pallas kernels, dress(): pl.pallas_call(functools.partial(dress_kernel, job), out_shape=out_shape...  11.1 us
    ppermute x1, waiting for transfers between devices, local(): across = lax.ppermute(own, axes, to_slot(2))  9.13 us
    ppermute x1, waiting for transfers between devices, local(): top = owned(lax.ppermute(top, axes, to_group), top, members, token)  7.14 us
    pallas_call x1, Pallas kernels, first_spread(): pl.pallas_call(functools.partial(first_spread_kernel, groups), out_shape=...  4 us
    pallas_call x3, Pallas kernels, spread(): pl.pallas_call(functools.partial(spread_kernel, slot), out_shape=pltpu.VM...  2.85 us
    ppermute x1, starting transfers between devices, local(): beside = lax.ppermute(own_again, axes, to_slot(1))  2.3 us
    pallas_call x1, Pallas kernels, fold_panel(): pl.pallas_call(functools.partial(fold_kernel, chunk), out_shape=[pltpu.VM...  2.05 us
    ppermute x1, starting transfers between devices, local(): top = owned(lax.ppermute(top, axes, to_group), top, members, token)  1.29 us
  transfers between devices with their start and end apart: 7, of which 3 were waited for; matrix products, arithmetic and copies ran while one was open for 0% of the time, Pallas kernels for 36%

profile of v12, /device:TPU:27, one launch (start us, length us, event | category | flops | bytes accessed | tf_op | source)
XLA Modules:
  0.0 45.4 jit_solution(411851572943013657)
XLA Ops:
  0.0 1.2 %cut_rows.1 = (bf16[160,1920]{1,0:T(8,128)(2,1)S(1)}, bf16[80,1920]{1,0:T(8,128)(2,1)S(1)}) custom-call(bf16[240,1920]{1,0:T(8,128)(2,1)} %whole.1), custom_call_target="tpu_custom_call" | custom-call | tf_op jit(solution)/shard_map/cut_rows/pallas_call | solution.py:53
  1.2 1.3 %collective-permute-start.1 = (bf16[160,1920]{1,0:T(8,128)(2,1)S(1)}, bf16[160,1920]{1,0:T(8,128)(2,1)S(1)}, u32[]{:S(2)}, u32[]{:S(2)}) collective-permute-start(bf16[160,1920]{1,0:T(8,128)(2,1)S(1)} %get-tuple-element.20.kept), channel_id=1, source_target_pairs={{8,1},{16,2},{26,3},{12,5},{20,6},{30,7},{1,8},{18,10},{24,11},{5,... | collective-permute-start | bytes 1843208 | tf_op jit(solution)/shard_map/ppermute | solution.py:391
  3.1 2.0 %fold_panel.1 = (bf16[480,512]{1,0:T(8,128)(2,1)S(1)}, bf16[480,512]{1,0:T(8,128)(2,1)S(1)}, s32[8,128]{1,0:T(8,128)S(1)}) custom-call(s32[1]{0:T(128)S(6)} %copy.26.pair, s32[8]{0:T(128)} %sizes.1, bf16[480,1920]{1,0:T(8,128)(2,1)} %bitcast.4), custom_call_target="tpu_custom_call" | custom-call | tf_op jit(solution)/shard_map/fold_panel/pallas_call | solution.py:104
  5.2 0.3 collective-permute-start
  5.5 2.3 %collective-permute-start.5 = (bf16[480,512]{1,0:T(8,128)(2,1)S(1)}, bf16[480,512]{1,0:T(8,128)(2,1)S(1)}, u32[]{:S(2)}, u32[]{:S(2)}) collective-permute-start(bf16[480,512]{1,0:T(8,128)(2,1)S(1)} %get-tuple-element.23), channel_id=1, source_target_pairs={{1,0},{0,1},{3,2},{2,3},{5,4},{4,5},{7,6},{6,7},{9,8},{8,9},{11,10... | collective-permute-start | bytes 1474568 | tf_op jit(solution)/shard_map/ppermute | solution.py:379
  7.8 0.5 %collective-permute-start.4 = (bf16[480,512]{1,0:T(8,128)(2,1)S(1)}, bf16[480,512]{1,0:T(8,128)(2,1)S(1)}, u32[]{:S(2)}, u32[]{:S(2)}) collective-permute-start(bf16[480,512]{1,0:T(8,128)(2,1)S(1)} %get-tuple-element.21.folded), channel_id=1, source_target_pairs={{2,0},{3,1},{0,2},{1,3},{6,4},{7,5},{4,6},{5,7},{10,8},{11,9},{8,1... | collective-permute-start | bytes 1474568 | tf_op jit(solution)/shard_map/ppermute | solution.py:378
  8.3 4.0 %first_spread.1 = (bf16[1920,2048]{1,0:T(8,128)(2,1)S(1)}, bf16[2048,1920]{1,0:T(8,128)(2,1)S(1)}, s32[2,8,2048]{2,1,0:T(8,128)S(1)}, s32[8,128]{1,0:T(8,128)S(1)}) custom-call(s32[8]{0:T(128)} %sizes.1, s32[1]{0:T(128)S(6)} %copy.26.pair, bf16[480,512]{1,0:T(8,128)(2,1)S(1)} %get-tuple-element.21.folded, bf16[1920,1920]{1,0:T(8,128)(2,1)} %fock.1), custom_call_target="tpu_custom_call" | custom-call | tf_op jit(solution)/shard_map/first_spread/pallas_call | solution.py:180
  12.3 0.0 collective-permute-done
  12.4 7.1 %collective-permute-done.1.received = bf16[160,1920]{1,0:T(8,128)(2,1)S(1)} collective-permute-done((bf16[160,1920]{1,0:T(8,128)(2,1)S(1)}, bf16[160,1920]{1,0:T(8,128)(2,1)S(1)}, u32[]{:S(2)}, u32[]{:S(2)}) %collective-permute-start.1) | collective-permute-done | bytes 614432 | tf_op jit(solution)/shard_map/ppermute | solution.py:391
  19.6 0.3 collective-permute-start.3
  19.9 1.3 %collective-permute-start.2 = (bf16[160,1920]{1,0:T(8,128)(2,1)S(1)}, bf16[160,1920]{1,0:T(8,128)(2,1)S(1)}, u32[]{:S(2)}, u32[]{:S(2)}) collective-permute-start(bf16[160,1920]{1,0:T(8,128)(2,1)S(1)} %after.4.kept), channel_id=1, source_target_pairs={{8,1},{16,2},{26,3},{12,5},{20,6},{30,7},{1,8},{18,10},{24,11},{5,... | collective-permute-start | bytes 1843208 | tf_op jit(solution)/shard_map/ppermute | solution.py:394
  21.2 0.0 collective-permute-done.5.folded
  21.2 1.0 %spread_panel.3.dense.before = bf16[1920,2048]{1,0:T(8,128)(2,1)S(1)} custom-call(bf16[480,512]{1,0:T(8,128)(2,1)S(1)} %collective-permute-done.5.folded, s32[2,8,2048]{2,1,0:T(8,128)S(1)} %get-tuple-element.24.ranges, bf16[1920,2048]{1,0:T(8,128)(2,1)S(1)} %get-tuple-element.25.before), custom_call_target="tpu_custom_call", output_to_operand_aliasing={{}: (2, {})} | custom-call | tf_op jit(solution)/shard_map/spread_panel/pallas_call | solution.py:210
  22.1 1.6 %dress_rows.4 = (f32[160,1920]{1,0:T(8,128)S(1)}, s32[8,128]{1,0:T(8,128)S(1)}) custom-call(bf16[160,1920]{1,0:T(8,128)(2,1)S(1)} %owned_rows.2.refs_1_.amplitudes, bf16[1920,2048]{1,0:T(8,128)(2,1)S(1)} %spread_panel.3.dense.before, bf16[2048,1920]{1,0:T(8,128)(2,1)S(1)} %get-tuple-element.26.fock), custom_call_target="tpu_custom_call" | custom-call | tf_op jit(solution)/shard_map/dress_rows/pallas_call | solution.py:334
  23.7 9.1 %collective-permute-done.4.refs_0_ = bf16[480,512]{1,0:T(8,128)(2,1)S(1)} collective-permute-done((bf16[480,512]{1,0:T(8,128)(2,1)S(1)}, bf16[480,512]{1,0:T(8,128)(2,1)S(1)}, u32[]{:S(2)}, u32[]{:S(2)}) %collective-permute-start.4) | collective-permute-done | bytes 491552 | tf_op jit(solution)/shard_map/ppermute | solution.py:378
  32.8 0.4 collective-permute-start.6
  33.3 0.9 %spread_panel.4.before = bf16[1920,2048]{1,0:T(8,128)(2,1)S(1)} custom-call(bf16[480,512]{1,0:T(8,128)(2,1)S(1)} %after.5.folded, s32[2,8,2048]{2,1,0:T(8,128)S(1)} %get-tuple-element.24.ranges, bf16[1920,2048]{1,0:T(8,128)(2,1)S(1)} %spread_panel.3.dense.before), custom_call_target="tpu_custom_call", output_to_operand_aliasing={{}: (2, {})} | custom-call | tf_op jit(solution)/shard_map/spread_panel/pallas_call | solution.py:210
  34.2 0.5 %collective-permute-done.6.folded = bf16[480,512]{1,0:T(8,128)(2,1)S(1)} collective-permute-done((bf16[480,512]{1,0:T(8,128)(2,1)S(1)}, bf16[480,512]{1,0:T(8,128)(2,1)S(1)}, u32[]{:S(2)}, u32[]{:S(2)}) %collective-permute-start.6) | collective-permute-done | bytes 491552 | tf_op jit(solution)/shard_map/ppermute | solution.py:401
  34.8 0.9 %spread_panel.5.dense = bf16[1920,2048]{1,0:T(8,128)(2,1)S(1)} custom-call(bf16[480,512]{1,0:T(8,128)(2,1)S(1)} %collective-permute-done.6.folded, s32[2,8,2048]{2,1,0:T(8,128)S(1)} %get-tuple-element.24.ranges, bf16[1920,2048]{1,0:T(8,128)(2,1)S(1)} %spread_panel.4.before), custom_call_target="tpu_custom_call", output_to_operand_aliasing={{}: (2, {})} | custom-call | tf_op jit(solution)/shard_map/spread_panel/pallas_call | solution.py:210
  35.7 2.3 %dress_rows.5.refs_0_ = bf16[480,1920]{1,0:T(8,128)(2,1)} custom-call(bf16[160,1920]{1,0:T(8,128)(2,1)S(1)} %owned_rows.2.refs_1_.amplitudes, bf16[1920,2048]{1,0:T(8,128)(2,1)S(1)} %spread_panel.5.dense, bf16[2048,1920]{1,0:T(8,128)(2,1)S(1)} %get-tuple-element.26.fock, f32[160,1920]{1,0:T(8,128)S(1)} %get-tuple-element.28.refs_0_), custom_call_target="tpu_custom_call" | custom-call | tf_op jit(solution)/shard_map/dress_rows/pallas_call | solution.py:334
  38.0 0.0 collective-permute-done.3.amplitudes
  38.0 3.6 %dress_rows.6 = (bf16[480,1920]{1,0:T(8,128)(2,1)}, s32[8,128]{1,0:T(8,128)S(1)}) custom-call(bf16[160,1920]{1,0:T(8,128)(2,1)S(1)} %collective-permute-done.3.amplitudes, bf16[1920,2048]{1,0:T(8,128)(2,1)S(1)} %spread_panel.5.dense, bf16[2048,1920]{1,0:T(8,128)(2,1)S(1)} %get-tuple-element.26.fock, ...), custom_call_target="tpu_custom_call", output_to_operand_aliasing={{0}: (3, {})} | custom-call | tf_op jit(solution)/shard_map/dress_rows/pallas_call | solution.py:334
  41.6 0.0 collective-permute-done.2.received
  41.7 3.7 %dress_rows.7 = bf16[480,1920]{1,0:T(8,128)(2,1)} custom-call(bf16[160,1920]{1,0:T(8,128)(2,1)S(1)} %owned_rows.3.amplitudes, bf16[1920,2048]{1,0:T(8,128)(2,1)S(1)} %spread_panel.5.dense, bf16[2048,1920]{1,0:T(8,128)(2,1)S(1)} %get-tuple-element.26.fock, bf16[480,1920]{1,0:T(8,128)(2,1)} %get-tuple-element.30.refs_0_), custom_call_target="tpu_custom_call", output_to_operand_aliasing={{}: (3, {})} | custom-call | tf_op jit(solution)/shard_map/dress_rows/pallas_call | solution.py:334
  (6 shorter events, 0.1 us)
Async XLA Ops:
  1.2 18.4 %collective-permute-start.1 = (bf16[160,1920]{1,0:T(8,128)(2,1)S(1)}, bf16[160,1920]{1,0:T(8,128)(2,1)S(1)}, u32[]{:S(2)}, u32[]{:S(2)}) collective-permute-start(bf16[160,1920]{1,0:T(8,128)(2,1)S(1)} %get-tuple-element.20.kept), channel_id=1, source_target_pairs={{8,1},{16,2},{26,3},{12,5},{20,6},{30,7},{1,8},{18,10},{24,11},{5,... | collective-permute-start | bytes 1843208 | tf_op jit(solution)/shard_map/ppermute | solution.py:391
  5.2 7.2 %collective-permute-start = (bf16[80,1920]{1,0:T(8,128)(2,1)S(1)}, bf16[80,1920]{1,0:T(8,128)(2,1)S(1)}, u32[]{:S(2)}, u32[]{:S(2)}) collective-permute-start(bf16[80,1920]{1,0:T(8,128)(2,1)S(1)} %after.3), channel_id=1, source_target_pairs={{4,0},{5,1},{6,2},{7,3},{0,4},{1,5},{2,6},{3,7},{12,8},{13,9},{14,... | collective-permute-start | bytes 921608 | tf_op jit(solution)/shard_map/ppermute | solution.py:385
  5.5 15.7 %collective-permute-start.5 = (bf16[480,512]{1,0:T(8,128)(2,1)S(1)}, bf16[480,512]{1,0:T(8,128)(2,1)S(1)}, u32[]{:S(2)}, u32[]{:S(2)}) collective-permute-start(bf16[480,512]{1,0:T(8,128)(2,1)S(1)} %get-tuple-element.23), channel_id=1, source_target_pairs={{1,0},{0,1},{3,2},{2,3},{5,4},{4,5},{7,6},{6,7},{9,8},{8,9},{11,10... | collective-permute-start | bytes 1474568 | tf_op jit(solution)/shard_map/ppermute | solution.py:379
  7.8 25.0 %collective-permute-start.4 = (bf16[480,512]{1,0:T(8,128)(2,1)S(1)}, bf16[480,512]{1,0:T(8,128)(2,1)S(1)}, u32[]{:S(2)}, u32[]{:S(2)}) collective-permute-start(bf16[480,512]{1,0:T(8,128)(2,1)S(1)} %get-tuple-element.21.folded), channel_id=1, source_target_pairs={{2,0},{3,1},{0,2},{1,3},{6,4},{7,5},{4,6},{5,7},{10,8},{11,9},{8,1... | collective-permute-start | bytes 1474568 | tf_op jit(solution)/shard_map/ppermute | solution.py:378
  19.6 18.4 %collective-permute-start.3 = (bf16[160,1920]{1,0:T(8,128)(2,1)S(1)}, bf16[160,1920]{1,0:T(8,128)(2,1)S(1)}, u32[]{:S(2)}, u32[]{:S(2)}) collective-permute-start(bf16[160,1920]{1,0:T(8,128)(2,1)S(1)} %owned_rows.2.refs_1_.amplitudes), channel_id=1, source_target_pairs={{4,0},{5,1},{6,2},{7,3},{0,4},{1,5},{2,6},{3,7},{12,8},{13,9},{14,... | collective-permute-start | bytes 1843208 | tf_op jit(solution)/shard_map/ppermute | solution.py:395
  19.9 21.7 %collective-permute-start.2 = (bf16[160,1920]{1,0:T(8,128)(2,1)S(1)}, bf16[160,1920]{1,0:T(8,128)(2,1)S(1)}, u32[]{:S(2)}, u32[]{:S(2)}) collective-permute-start(bf16[160,1920]{1,0:T(8,128)(2,1)S(1)} %after.4.kept), channel_id=1, source_target_pairs={{8,1},{16,2},{26,3},{12,5},{20,6},{30,7},{1,8},{18,10},{24,11},{5,... | collective-permute-start | bytes 1843208 | tf_op jit(solution)/shard_map/ppermute | solution.py:394
  32.8 1.9 %collective-permute-start.6 = (bf16[480,512]{1,0:T(8,128)(2,1)S(1)}, bf16[480,512]{1,0:T(8,128)(2,1)S(1)}, u32[]{:S(2)}, u32[]{:S(2)}) collective-permute-start(bf16[480,512]{1,0:T(8,128)(2,1)S(1)} %after.5.folded), channel_id=1, source_target_pairs={{1,0},{0,1},{3,2},{2,3},{5,4},{4,5},{7,6},{6,7},{9,8},{8,9},{11,10... | collective-permute-start | bytes 1474568 | tf_op jit(solution)/shard_map/ppermute | solution.py:401

commit v13 on v12

--- a/solution.py
+++ b/solution.py
@@ -36,33 +36,42 @@
     return low, high
 
 
-def cut_kernel(whole, *refs):
-    pieces, sems = refs[:-1], refs[-1]
-    copies, first = [], 0
-    for k, piece in enumerate(pieces):
-        size = piece.shape[0]
-        copies.append(pltpu.make_async_copy(whole.at[pl.ds(first, size)], piece, sems.at[k]))
+def copies_of(source, first, target, sems):
+    count = sems.shape[0]
+    step = rounded(-(-target.shape[0] // count), SUBLANES)
+    copies = []
+    for k, begin in enumerate(range(0, target.shape[0], step)):
+        size = min(step, target.shape[0] - begin)
+        copies.append(pltpu.make_async_copy(
+            source.at[pl.ds(first + begin, size)], target.at[pl.ds(begin, size)], sems.at[k]
+        ))
         copies[-1].start()
-        first += size
-    for copy in copies:
-        copy.wait()
-
-
-def cut(whole, sizes):
-    vmem = pl.BlockSpec(memory_space=pltpu.VMEM)
+    return copies
+
+
+def cut_kernel(whole, piece, sems):
+    for copy in copies_of(whole, 0, piece, sems):
+        copy.wait()
+
+
+def cut(whole, size):
     return pl.pallas_call(
         cut_kernel,
-        out_shape=[pltpu.VMEM((size, whole.shape[1]), whole.dtype) for size in sizes],
+        out_shape=pltpu.VMEM((size, whole.shape[1]), whole.dtype),
         in_specs=[pl.BlockSpec(memory_space=pl.ANY)],
-        out_specs=[vmem] * len(sizes),
-        scratch_shapes=[pltpu.SemaphoreType.DMA((len(sizes),))],
+        out_specs=pl.BlockSpec(memory_space=pltpu.VMEM),
+        scratch_shapes=[pltpu.SemaphoreType.DMA((5,))],
         compiler_params=pltpu.CompilerParams(vmem_limit_bytes=4 * MIB),
         cost_estimate=NOTHING,
         name="cut_rows",
-    )(pltpu.with_memory_space_constraint(whole, pltpu.HBM))
-
-
-def fold_kernel(chunk, pair, sizes_in, source, folded, again, token, panel, sizes, bounds, sems):
+    )(whole)
+
+
+def fold_kernel(chunk, late, pair, sizes_in, source, *refs):
+    if late:
+        amplitudes, folded, again, low, panel, sizes, bounds, sems, low_sems = refs
+    else:
+        folded, again, panel, sizes, bounds, sems = refs
     quarter, virtuals = panel.shape
     fold = folded.shape[1]
     small = pltpu.make_async_copy(sizes_in, sizes, sems.at[quarter // chunk])
@@ -72,7 +81,7 @@
         rows = pl.ds(k * chunk, chunk)
         copies.append(pltpu.make_async_copy(source.at[rows], panel.at[rows], sems.at[k]))
         copies[-1].start()
-    token[...] = jnp.zeros_like(token)
+    lows = copies_of(amplitudes, late, low, low_sems) if late else []
     small.wait()
     fill_bounds(sizes, bounds)
     start = lax.axis_index("grp") * quarter
@@ -97,25 +106,37 @@
                 folded[here, place:place + LANES] = total
                 again[here, place:place + LANES] = total
 
-
-def fold_panel(panel, sizes, pair, fold):
+    for copy in lows:
+        copy.wait()
+
+
+def fold_panel(panel, sizes, pair, fold, amplitudes, late):
     quarter, virtuals = panel.shape
     chunk = quarter // 5 if quarter % (5 * SUBLANES) == 0 else quarter
-    return pl.pallas_call(
-        functools.partial(fold_kernel, chunk),
-        out_shape=[pltpu.VMEM((quarter, fold), panel.dtype)] * 2 + [TOKEN],
-        in_specs=[pl.BlockSpec(memory_space=pltpu.SMEM)] + [pl.BlockSpec(memory_space=pl.ANY)] * 2,
-        out_specs=[pl.BlockSpec(memory_space=pltpu.VMEM)] * 3,
-        scratch_shapes=[
-            pltpu.VMEM((quarter, virtuals), panel.dtype),
-            pltpu.SMEM(sizes.shape, jnp.int32),
-            pltpu.SMEM((sizes.shape[0] + 1,), jnp.int32),
-            pltpu.SemaphoreType.DMA((quarter // chunk + 1,)),
-        ],
+    vmem = pl.BlockSpec(memory_space=pltpu.VMEM)
+    anywhere = pl.BlockSpec(memory_space=pl.ANY)
+    out_shape = [pltpu.VMEM((quarter, fold), panel.dtype)] * 2
+    scratch = [
+        pltpu.VMEM((quarter, virtuals), panel.dtype),
+        pltpu.SMEM(sizes.shape, jnp.int32),
+        pltpu.SMEM((sizes.shape[0] + 1,), jnp.int32),
+        pltpu.SemaphoreType.DMA((quarter // chunk + 1,)),
+    ]
+    extra = []
+    if late:
+        out_shape.append(pltpu.VMEM((amplitudes.shape[0] - late, virtuals), amplitudes.dtype))
+        scratch.append(pltpu.SemaphoreType.DMA((2,)))
+        extra.append(amplitudes)
+    return pl.pallas_call(
+        functools.partial(fold_kernel, chunk, late),
+        out_shape=out_shape,
+        in_specs=[pl.BlockSpec(memory_space=pltpu.SMEM)] + [anywhere] * (2 + len(extra)),
+        out_specs=[vmem] * len(out_shape),
+        scratch_shapes=scratch,
         compiler_params=pltpu.CompilerParams(vmem_limit_bytes=8 * MIB),
         cost_estimate=NOTHING,
         name="fold_panel",
-    )(pair, sizes, pltpu.with_memory_space_constraint(panel, pltpu.HBM))
+    )(pair, sizes, pltpu.with_memory_space_constraint(panel, pltpu.HBM), *extra)
 
 
 def place_panel(slot, folded, ranges, dense, turned):
@@ -374,35 +395,35 @@
         panel = jnp.swapaxes(hole_panel[:, 0, :], 0, 1)
         irrep_sizes = pltpu.with_memory_space_constraint(irrep_sizes, pltpu.HBM)
 
-        own, own_again, token = fold_panel(panel, irrep_sizes, pair_irreps, fold)
+        early = rounded(rows * 2 // 3, SUBLANES) if rows % SUBLANES == 0 else 0
+        if early:
+            amplitudes = pltpu.with_memory_space_constraint(amplitudes, pltpu.HBM)
+            top = cut(amplitudes, early)
+        else:
+            top = amplitudes
+        own, own_again, *low = fold_panel(panel, irrep_sizes, pair_irreps, fold, amplitudes, early)
         across = lax.ppermute(own, axes, to_slot(2))
         beside = lax.ppermute(own_again, axes, to_slot(1))
-
-        early = rounded(rows * 2 // 3, SUBLANES) if rows % SUBLANES == 0 else rows
-        if early < rows:
-            top, low = cut(amplitudes, (early, rows - early))
-            low = after(low, token)
-            lows = [low] + [lax.ppermute(low, axes, to_member(by)) for by in range(1, members)]
-            lows = jnp.concatenate(lows)
-        else:
-            top = amplitudes
+        if early:
+            low = low[0]
+            swapped = [lax.ppermute(low, axes, to_member(by)) for by in range(1, members)]
 
         dense, fock, ranges, token = first_spread(groups, own, virt_fock, irrep_sizes, pair_irreps)
         top = owned(lax.ppermute(top, axes, to_group), top, members, token)
-        if early < rows:
-            lows = after(lows, top)
+        if early:
+            lows = jnp.concatenate([after(piece, top) for piece in [low] + swapped])
             late = lax.ppermute(lows, axes, to_group)
         tops = [top] + [lax.ppermute(top, axes, to_member(by)) for by in range(1, members)]
         dense = spread(1, beside, ranges, dense)
         near = 2 * dense.shape[1] // groups
-        if early < rows:
+        if early:
             sums, token = dress(top, dense, fock, columns=(0, near), signed=True)
             across = after(across, token)
         both = lax.ppermute(across, axes, to_slot(1))
         dense = spread(2, across, ranges, dense)
         dense = spread(3, both, ranges, dense)
 
-        if early < rows:
+        if early:
             place = dict(rows=rows, members=members, out_rows=out_rows)
             result, = dress(
                 top, dense, fock, columns=(near, dense.shape[1]), sums=sums, spans=((0, 0, early),),

time: 45.6 us -> 45.6 us (level)
  no operation moved by 1% of the time
where the time goes in v13:
time: 45.6 us; the launch traced here: 45.4 us
  Pallas kernels  21.3 us (47%)
  waiting for transfers between devices  16.8 us (37%)
  starting transfers between devices  6.49 us (14%)
  between operations  0.79 us (2%)
    pallas_call x4, Pallas kernels, dress(): pl.pallas_call(functools.partial(dress_kernel, job), out_shape=out_shape...  11.1 us
    ppermute x1, waiting for transfers between devices, local(): across = lax.ppermute(own, axes, to_slot(2))  9.05 us
    ppermute x1, waiting for transfers between devices, local(): top = owned(lax.ppermute(top, axes, to_group), top, members, token)  7.19 us
    pallas_call x1, Pallas kernels, first_spread(): pl.pallas_call(functools.partial(first_spread_kernel, groups), out_shape=...  4 us
    pallas_call x3, Pallas kernels, spread(): pl.pallas_call(functools.partial(spread_kernel, slot), out_shape=pltpu.VM...  2.85 us
    ppermute x1, starting transfers between devices, local(): beside = lax.ppermute(own_again, axes, to_slot(1))  2.3 us
    pallas_call x1, Pallas kernels, fold_panel(): pl.pallas_call(functools.partial(fold_kernel, chunk, late), out_shape=out...  2.07 us
    ppermute x1, starting transfers between devices, local(): top = owned(lax.ppermute(top, axes, to_group), top, members, token)  1.29 us
  transfers between devices with their start and end apart: 7, of which 3 were waited for; matrix products, arithmetic and copies ran while one was open for 0% of the time, Pallas kernels for 36%

profile of v13, /device:TPU:27, one launch (start us, length us, event | category | flops | bytes accessed | tf_op | source)
XLA Modules:
  0.0 45.4 jit_solution(174250687141893083)
XLA Ops:
  0.0 1.2 %cut_rows.1.kept = bf16[160,1920]{1,0:T(8,128)(2,1)S(1)} custom-call(bf16[240,1920]{1,0:T(8,128)(2,1)} %whole.1), custom_call_target="tpu_custom_call" | custom-call | tf_op jit(solution)/shard_map/cut_rows/pallas_call | solution.py:58
  1.2 1.3 %collective-permute-start = (bf16[160,1920]{1,0:T(8,128)(2,1)S(1)}, bf16[160,1920]{1,0:T(8,128)(2,1)S(1)}, u32[]{:S(2)}, u32[]{:S(2)}) collective-permute-start(bf16[160,1920]{1,0:T(8,128)(2,1)S(1)} %cut_rows.1.kept), channel_id=1, source_target_pairs={{8,1},{16,2},{26,3},{12,5},{20,6},{30,7},{1,8},{18,10},{24,11},{5,... | collective-permute-start | bytes 1843208 | tf_op jit(solution)/shard_map/ppermute | solution.py:412
  3.1 2.1 %fold_panel.1 = (bf16[480,512]{1,0:T(8,128)(2,1)S(1)}, bf16[480,512]{1,0:T(8,128)(2,1)S(1)}, bf16[80,1920]{1,0:T(8,128)(2,1)S(1)}) custom-call(s32[1]{0:T(128)S(6)} %copy.26.pair, s32[8]{0:T(128)} %sizes.1, bf16[480,1920]{1,0:T(8,128)(2,1)} %bitcast.4, bf16[240,1920]{1,0:T(8,128)(2,1)} %whole.1), custom_call_target="tpu_custom_call" | custom-call | tf_op jit(solution)/shard_map/fold_panel/pallas_call | solution.py:130
  5.2 0.3 collective-permute-start.1
  5.5 2.3 %collective-permute-start.5 = (bf16[480,512]{1,0:T(8,128)(2,1)S(1)}, bf16[480,512]{1,0:T(8,128)(2,1)S(1)}, u32[]{:S(2)}, u32[]{:S(2)}) collective-permute-start(bf16[480,512]{1,0:T(8,128)(2,1)S(1)} %get-tuple-element.19), channel_id=1, source_target_pairs={{1,0},{0,1},{3,2},{2,3},{5,4},{4,5},{7,6},{6,7},{9,8},{8,9},{11,10... | collective-permute-start | bytes 1474568 | tf_op jit(solution)/shard_map/ppermute | solution.py:406
  7.8 0.5 %collective-permute-start.4 = (bf16[480,512]{1,0:T(8,128)(2,1)S(1)}, bf16[480,512]{1,0:T(8,128)(2,1)S(1)}, u32[]{:S(2)}, u32[]{:S(2)}) collective-permute-start(bf16[480,512]{1,0:T(8,128)(2,1)S(1)} %get-tuple-element.17.folded), channel_id=1, source_target_pairs={{2,0},{3,1},{0,2},{1,3},{6,4},{7,5},{4,6},{5,7},{10,8},{11,9},{8,1... | collective-permute-start | bytes 1474568 | tf_op jit(solution)/shard_map/ppermute | solution.py:405
  8.4 4.0 %first_spread.1 = (bf16[1920,2048]{1,0:T(8,128)(2,1)S(1)}, bf16[2048,1920]{1,0:T(8,128)(2,1)S(1)}, s32[2,8,2048]{2,1,0:T(8,128)S(1)}, s32[8,128]{1,0:T(8,128)S(1)}) custom-call(s32[8]{0:T(128)} %sizes.1, s32[1]{0:T(128)S(6)} %copy.26.pair, bf16[480,512]{1,0:T(8,128)(2,1)S(1)} %get-tuple-element.17.folded, bf16[1920,1920]{1,0:T(8,128)(2,1)} %fock.1), custom_call_target="tpu_custom_call" | custom-call | tf_op jit(solution)/shard_map/first_spread/pallas_call | solution.py:201
  12.4 7.2 %collective-permute-done.received = bf16[160,1920]{1,0:T(8,128)(2,1)S(1)} collective-permute-done((bf16[160,1920]{1,0:T(8,128)(2,1)S(1)}, bf16[160,1920]{1,0:T(8,128)(2,1)S(1)}, u32[]{:S(2)}, u32[]{:S(2)}) %collective-permute-start) | collective-permute-done | bytes 614432 | tf_op jit(solution)/shard_map/ppermute | solution.py:412
  19.6 0.3 collective-permute-start.3
  19.9 0.0 collective-permute-done.1.refs_0_
  20.0 1.3 %collective-permute-start.2 = (bf16[160,1920]{1,0:T(8,128)(2,1)S(1)}, bf16[160,1920]{1,0:T(8,128)(2,1)S(1)}, u32[]{:S(2)}, u32[]{:S(2)}) collective-permute-start(bf16[160,1920]{1,0:T(8,128)(2,1)S(1)} %pad_maximum_fusion.kept), channel_id=1, source_target_pairs={{8,1},{16,2},{26,3},{12,5},{20,6},{30,7},{1,8},{18,10},{24,11},{5,... | collective-permute-start | bytes 1843208 | tf_op jit(solution)/shard_map/ppermute | solution.py:415
  21.3 0.0 collective-permute-done.5.folded
  21.3 1.0 %spread_panel.3.dense.before = bf16[1920,2048]{1,0:T(8,128)(2,1)S(1)} custom-call(bf16[480,512]{1,0:T(8,128)(2,1)S(1)} %collective-permute-done.5.folded, s32[2,8,2048]{2,1,0:T(8,128)S(1)} %get-tuple-element.20.ranges, bf16[1920,2048]{1,0:T(8,128)(2,1)S(1)} %get-tuple-element.21.before), custom_call_target="tpu_custom_call", output_to_operand_aliasing={{}: (2, {})} | custom-call | tf_op jit(solution)/shard_map/spread_panel/pallas_call | solution.py:231
  22.2 1.6 %dress_rows.4 = (f32[160,1920]{1,0:T(8,128)S(1)}, s32[8,128]{1,0:T(8,128)S(1)}) custom-call(bf16[160,1920]{1,0:T(8,128)(2,1)S(1)} %owned_rows.2.refs_1_.amplitudes, bf16[1920,2048]{1,0:T(8,128)(2,1)S(1)} %spread_panel.3.dense.before, bf16[2048,1920]{1,0:T(8,128)(2,1)S(1)} %get-tuple-element.22.fock), custom_call_target="tpu_custom_call" | custom-call | tf_op jit(solution)/shard_map/dress_rows/pallas_call | solution.py:355
  23.8 9.0 %collective-permute-done.4.refs_0_ = bf16[480,512]{1,0:T(8,128)(2,1)S(1)} collective-permute-done((bf16[480,512]{1,0:T(8,128)(2,1)S(1)}, bf16[480,512]{1,0:T(8,128)(2,1)S(1)}, u32[]{:S(2)}, u32[]{:S(2)}) %collective-permute-start.4) | collective-permute-done | bytes 491552 | tf_op jit(solution)/shard_map/ppermute | solution.py:405
  32.9 0.4 collective-permute-start.6
  33.3 0.9 %spread_panel.4.before = bf16[1920,2048]{1,0:T(8,128)(2,1)S(1)} custom-call(bf16[480,512]{1,0:T(8,128)(2,1)S(1)} %after.5.folded, s32[2,8,2048]{2,1,0:T(8,128)S(1)} %get-tuple-element.20.ranges, bf16[1920,2048]{1,0:T(8,128)(2,1)S(1)} %spread_panel.3.dense.before), custom_call_target="tpu_custom_call", output_to_operand_aliasing={{}: (2, {})} | custom-call | tf_op jit(solution)/shard_map/spread_panel/pallas_call | solution.py:231
  34.3 0.5 %collective-permute-done.6.folded = bf16[480,512]{1,0:T(8,128)(2,1)S(1)} collective-permute-done((bf16[480,512]{1,0:T(8,128)(2,1)S(1)}, bf16[480,512]{1,0:T(8,128)(2,1)S(1)}, u32[]{:S(2)}, u32[]{:S(2)}) %collective-permute-start.6) | collective-permute-done | bytes 491552 | tf_op jit(solution)/shard_map/ppermute | solution.py:422
  34.8 0.9 %spread_panel.5.dense = bf16[1920,2048]{1,0:T(8,128)(2,1)S(1)} custom-call(bf16[480,512]{1,0:T(8,128)(2,1)S(1)} %collective-permute-done.6.folded, s32[2,8,2048]{2,1,0:T(8,128)S(1)} %get-tuple-element.20.ranges, bf16[1920,2048]{1,0:T(8,128)(2,1)S(1)} %spread_panel.4.before), custom_call_target="tpu_custom_call", output_to_operand_aliasing={{}: (2, {})} | custom-call | tf_op jit(solution)/shard_map/spread_panel/pallas_call | solution.py:231
  35.7 2.3 %dress_rows.5.refs_0_ = bf16[480,1920]{1,0:T(8,128)(2,1)} custom-call(bf16[160,1920]{1,0:T(8,128)(2,1)S(1)} %owned_rows.2.refs_1_.amplitudes, bf16[1920,2048]{1,0:T(8,128)(2,1)S(1)} %spread_panel.5.dense, bf16[2048,1920]{1,0:T(8,128)(2,1)S(1)} %get-tuple-element.22.fock, f32[160,1920]{1,0:T(8,128)S(1)} %get-tuple-element.24.refs_0_), custom_call_target="tpu_custom_call" | custom-call | tf_op jit(solution)/shard_map/dress_rows/pallas_call | solution.py:355
  38.0 0.0 collective-permute-done.3.amplitudes
  38.0 3.6 %dress_rows.6 = (bf16[480,1920]{1,0:T(8,128)(2,1)}, s32[8,128]{1,0:T(8,128)S(1)}) custom-call(bf16[160,1920]{1,0:T(8,128)(2,1)S(1)} %collective-permute-done.3.amplitudes, bf16[1920,2048]{1,0:T(8,128)(2,1)S(1)} %spread_panel.5.dense, bf16[2048,1920]{1,0:T(8,128)(2,1)S(1)} %get-tuple-element.22.fock, ...), custom_call_target="tpu_custom_call", output_to_operand_aliasing={{0}: (3, {})} | custom-call | tf_op jit(solution)/shard_map/dress_rows/pallas_call | solution.py:355
  41.6 0.0 collective-permute-done.2.received
  41.7 3.7 %dress_rows.7 = bf16[480,1920]{1,0:T(8,128)(2,1)} custom-call(bf16[160,1920]{1,0:T(8,128)(2,1)S(1)} %owned_rows.3.amplitudes, bf16[1920,2048]{1,0:T(8,128)(2,1)S(1)} %spread_panel.5.dense, bf16[2048,1920]{1,0:T(8,128)(2,1)S(1)} %get-tuple-element.22.fock, bf16[480,1920]{1,0:T(8,128)(2,1)} %get-tuple-element.26.refs_0_), custom_call_target="tpu_custom_call", output_to_operand_aliasing={{}: (3, {})} | custom-call | tf_op jit(solution)/shard_map/dress_rows/pallas_call | solution.py:355
  (6 shorter events, 0.1 us)
Async XLA Ops:
  1.2 18.4 %collective-permute-start = (bf16[160,1920]{1,0:T(8,128)(2,1)S(1)}, bf16[160,1920]{1,0:T(8,128)(2,1)S(1)}, u32[]{:S(2)}, u32[]{:S(2)}) collective-permute-start(bf16[160,1920]{1,0:T(8,128)(2,1)S(1)} %cut_rows.1.kept), channel_id=1, source_target_pairs={{8,1},{16,2},{26,3},{12,5},{20,6},{30,7},{1,8},{18,10},{24,11},{5,... | collective-permute-start | bytes 1843208 | tf_op jit(solution)/shard_map/ppermute | solution.py:412
  5.2 14.7 %collective-permute-start.1 = (bf16[80,1920]{1,0:T(8,128)(2,1)S(1)}, bf16[80,1920]{1,0:T(8,128)(2,1)S(1)}, u32[]{:S(2)}, u32[]{:S(2)}) collective-permute-start(bf16[80,1920]{1,0:T(8,128)(2,1)S(1)} %get-tuple-element.16.refs_0_), channel_id=1, source_target_pairs={{4,0},{5,1},{6,2},{7,3},{0,4},{1,5},{2,6},{3,7},{12,8},{13,9},{14,... | collective-permute-start | bytes 921608 | tf_op jit(solution)/shard_map/ppermute | solution.py:409
  5.5 15.7 %collective-permute-start.5 = (bf16[480,512]{1,0:T(8,128)(2,1)S(1)}, bf16[480,512]{1,0:T(8,128)(2,1)S(1)}, u32[]{:S(2)}, u32[]{:S(2)}) collective-permute-start(bf16[480,512]{1,0:T(8,128)(2,1)S(1)} %get-tuple-element.19), channel_id=1, source_target_pairs={{1,0},{0,1},{3,2},{2,3},{5,4},{4,5},{7,6},{6,7},{9,8},{8,9},{11,10... | collective-permute-start | bytes 1474568 | tf_op jit(solution)/shard_map/ppermute | solution.py:406
  7.8 25.0 %collective-permute-start.4 = (bf16[480,512]{1,0:T(8,128)(2,1)S(1)}, bf16[480,512]{1,0:T(8,128)(2,1)S(1)}, u32[]{:S(2)}, u32[]{:S(2)}) collective-permute-start(bf16[480,512]{1,0:T(8,128)(2,1)S(1)} %get-tuple-element.17.folded), channel_id=1, source_target_pairs={{2,0},{3,1},{0,2},{1,3},{6,4},{7,5},{4,6},{5,7},{10,8},{11,9},{8,1... | collective-permute-start | bytes 1474568 | tf_op jit(solution)/shard_map/ppermute | solution.py:405
  19.6 18.4 %collective-permute-start.3 = (bf16[160,1920]{1,0:T(8,128)(2,1)S(1)}, bf16[160,1920]{1,0:T(8,128)(2,1)S(1)}, u32[]{:S(2)}, u32[]{:S(2)}) collective-permute-start(bf16[160,1920]{1,0:T(8,128)(2,1)S(1)} %owned_rows.2.refs_1_.amplitudes), channel_id=1, source_target_pairs={{4,0},{5,1},{6,2},{7,3},{0,4},{1,5},{2,6},{3,7},{12,8},{13,9},{14,... | collective-permute-start | bytes 1843208 | tf_op jit(solution)/shard_map/ppermute | solution.py:416
  20.0 21.7 %collective-permute-start.2 = (bf16[160,1920]{1,0:T(8,128)(2,1)S(1)}, bf16[160,1920]{1,0:T(8,128)(2,1)S(1)}, u32[]{:S(2)}, u32[]{:S(2)}) collective-permute-start(bf16[160,1920]{1,0:T(8,128)(2,1)S(1)} %pad_maximum_fusion.kept), channel_id=1, source_target_pairs={{8,1},{16,2},{26,3},{12,5},{20,6},{30,7},{1,8},{18,10},{24,11},{5,... | collective-permute-start | bytes 1843208 | tf_op jit(solution)/shard_map/ppermute | solution.py:415
  32.9 1.9 %collective-permute-start.6 = (bf16[480,512]{1,0:T(8,128)(2,1)S(1)}, bf16[480,512]{1,0:T(8,128)(2,1)S(1)}, u32[]{:S(2)}, u32[]{:S(2)}) collective-permute-start(bf16[480,512]{1,0:T(8,128)(2,1)S(1)} %after.5.folded), channel_id=1, source_target_pairs={{1,0},{0,1},{3,2},{2,3},{5,4},{4,5},{7,6},{6,7},{9,8},{8,9},{11,10... | collective-permute-start | bytes 1474568 | tf_op jit(solution)/shard_map/ppermute | solution.py:422

commit v14 on v13

--- a/solution.py
+++ b/solution.py
@@ -375,7 +375,7 @@
     everyone = [(h, l, g) for h in range(groups) for l in range(members) for g in range(groups)]
 
     if groups == 4:
-        copies = ((None, 1, 0, 3), (0, None, 2, 1), (0, 2, None, 3), (2, 0, 3, None))
+        copies = ((None, 0, 3, 1), (0, None, 1, 3), (0, 2, None, 3), (2, 0, 3, None))
     else:
         copies = [[None if h == g else h for h in range(groups)] for g in range(groups)]
     to_group = [

time: 45.6 us -> 45.3 us (level)
  the two profiles are of different devices: /device:TPU:27 before, /device:TPU:4 now
where the time goes in v14:
time: 45.3 us; the launch traced here: 45.1 us
  Pallas kernels  21.3 us (47%)
  waiting for transfers between devices  12.7 us (28%)
  starting transfers between devices  10.3 us (23%)
  between operations  0.77 us (2%)
    pallas_call x4, Pallas kernels, dress(): pl.pallas_call(functools.partial(dress_kernel, job), out_shape=out_shape...  11.1 us
    ppermute x1, waiting for transfers between devices, local(): top = owned(lax.ppermute(top, axes, to_group), top, members, token)  6.37 us
    pallas_call x1, Pallas kernels, first_spread(): pl.pallas_call(functools.partial(first_spread_kernel, groups), out_shape=...  4 us
    ppermute x1, starting transfers between devices, local(): beside = lax.ppermute(own_again, axes, to_slot(1))  2.98 us
    pallas_call x3, Pallas kernels, spread(): pl.pallas_call(functools.partial(spread_kernel, slot), out_shape=pltpu.VM...  2.85 us
    ppermute x1, waiting for transfers between devices, local(): lax.ppermute(top, axes, to_member(by))  2.65 us
    pallas_call x1, Pallas kernels, fold_panel(): pl.pallas_call(functools.partial(fold_kernel, chunk, late), out_shape=out...  2.07 us
    ppermute x1, waiting for transfers between devices, local(): across = lax.ppermute(own, axes, to_slot(2))  1.71 us
  transfers between devices with their start and end apart: 7, of which 5 were waited for; matrix products, arithmetic and copies ran while one was open for 0% of the time, Pallas kernels for 36%

profile of v14, /device:TPU:4, one launch (start us, length us, event | category | flops | bytes accessed | tf_op | source)
XLA Modules:
  0.0 45.1 jit_solution(14490808182213919620)
XLA Ops:
  0.0 1.2 %cut_rows.1.kept = bf16[160,1920]{1,0:T(8,128)(2,1)S(1)} custom-call(bf16[240,1920]{1,0:T(8,128)(2,1)} %whole.1), custom_call_target="tpu_custom_call" | custom-call | tf_op jit(solution)/shard_map/cut_rows/pallas_call | solution.py:58
  1.2 1.3 %collective-permute-start = (bf16[160,1920]{1,0:T(8,128)(2,1)S(1)}, bf16[160,1920]{1,0:T(8,128)(2,1)S(1)}, u32[]{:S(2)}, u32[]{:S(2)}) collective-permute-start(bf16[160,1920]{1,0:T(8,128)(2,1)S(1)} %cut_rows.1.kept), channel_id=1, source_target_pairs={{8,1},{16,2},{26,3},{12,5},{20,6},{30,7},{0,8},{18,10},{24,11},{4,... | collective-permute-start | bytes 1843208 | tf_op jit(solution)/shard_map/ppermute | solution.py:412
  3.1 2.1 %fold_panel.1 = (bf16[480,512]{1,0:T(8,128)(2,1)S(1)}, bf16[480,512]{1,0:T(8,128)(2,1)S(1)}, bf16[80,1920]{1,0:T(8,128)(2,1)S(1)}) custom-call(s32[1]{0:T(128)S(6)} %copy.26.pair, s32[8]{0:T(128)} %sizes.1, bf16[480,1920]{1,0:T(8,128)(2,1)} %bitcast.4, bf16[240,1920]{1,0:T(8,128)(2,1)} %whole.1), custom_call_target="tpu_custom_call" | custom-call | tf_op jit(solution)/shard_map/fold_panel/pallas_call | solution.py:130
  5.2 1.6 %collective-permute-start.1 = (bf16[80,1920]{1,0:T(8,128)(2,1)S(1)}, bf16[80,1920]{1,0:T(8,128)(2,1)S(1)}, u32[]{:S(2)}, u32[]{:S(2)}) collective-permute-start(bf16[80,1920]{1,0:T(8,128)(2,1)S(1)} %get-tuple-element.16.refs_0_), channel_id=1, source_target_pairs={{4,0},{5,1},{6,2},{7,3},{0,4},{1,5},{2,6},{3,7},{12,8},{13,9},{14,... | collective-permute-start | bytes 921608 | tf_op jit(solution)/shard_map/ppermute | solution.py:409
  6.8 3.0 %collective-permute-start.5 = (bf16[480,512]{1,0:T(8,128)(2,1)S(1)}, bf16[480,512]{1,0:T(8,128)(2,1)S(1)}, u32[]{:S(2)}, u32[]{:S(2)}) collective-permute-start(bf16[480,512]{1,0:T(8,128)(2,1)S(1)} %get-tuple-element.19), channel_id=1, source_target_pairs={{1,0},{0,1},{3,2},{2,3},{5,4},{4,5},{7,6},{6,7},{9,8},{8,9},{11,10... | collective-permute-start | bytes 1474568 | tf_op jit(solution)/shard_map/ppermute | solution.py:406
  9.8 1.6 %collective-permute-start.4 = (bf16[480,512]{1,0:T(8,128)(2,1)S(1)}, bf16[480,512]{1,0:T(8,128)(2,1)S(1)}, u32[]{:S(2)}, u32[]{:S(2)}) collective-permute-start(bf16[480,512]{1,0:T(8,128)(2,1)S(1)} %get-tuple-element.17.folded), channel_id=1, source_target_pairs={{2,0},{3,1},{0,2},{1,3},{6,4},{7,5},{4,6},{5,7},{10,8},{11,9},{8,1... | collective-permute-start | bytes 1474568 | tf_op jit(solution)/shard_map/ppermute | solution.py:405
  11.3 4.0 %first_spread.1 = (bf16[1920,2048]{1,0:T(8,128)(2,1)S(1)}, bf16[2048,1920]{1,0:T(8,128)(2,1)S(1)}, s32[2,8,2048]{2,1,0:T(8,128)S(1)}, s32[8,128]{1,0:T(8,128)S(1)}) custom-call(s32[8]{0:T(128)} %sizes.1, s32[1]{0:T(128)S(6)} %copy.26.pair, bf16[480,512]{1,0:T(8,128)(2,1)S(1)} %get-tuple-element.17.folded, bf16[1920,1920]{1,0:T(8,128)(2,1)} %fock.1), custom_call_target="tpu_custom_call" | custom-call | tf_op jit(solution)/shard_map/first_spread/pallas_call | solution.py:201
  15.3 6.4 %collective-permute-done.received = bf16[160,1920]{1,0:T(8,128)(2,1)S(1)} collective-permute-done((bf16[160,1920]{1,0:T(8,128)(2,1)S(1)}, bf16[160,1920]{1,0:T(8,128)(2,1)S(1)}, u32[]{:S(2)}, u32[]{:S(2)}) %collective-permute-start) | collective-permute-done | bytes 614432 | tf_op jit(solution)/shard_map/ppermute | solution.py:412
  21.7 1.6 %collective-permute-start.3 = (bf16[160,1920]{1,0:T(8,128)(2,1)S(1)}, bf16[160,1920]{1,0:T(8,128)(2,1)S(1)}, u32[]{:S(2)}, u32[]{:S(2)}) collective-permute-start(bf16[160,1920]{1,0:T(8,128)(2,1)S(1)} %owned_rows.2.refs_1_.amplitudes), channel_id=1, source_target_pairs={{4,0},{5,1},{6,2},{7,3},{0,4},{1,5},{2,6},{3,7},{12,8},{13,9},{14,... | collective-permute-start | bytes 1843208 | tf_op jit(solution)/shard_map/ppermute | solution.py:416
  23.3 0.0 collective-permute-done.1.refs_0_
  23.3 1.3 %collective-permute-start.2 = (bf16[160,1920]{1,0:T(8,128)(2,1)S(1)}, bf16[160,1920]{1,0:T(8,128)(2,1)S(1)}, u32[]{:S(2)}, u32[]{:S(2)}) collective-permute-start(bf16[160,1920]{1,0:T(8,128)(2,1)S(1)} %pad_maximum_fusion.kept), channel_id=1, source_target_pairs={{8,1},{16,2},{26,3},{12,5},{20,6},{30,7},{0,8},{18,10},{24,11},{4,... | collective-permute-start | bytes 1843208 | tf_op jit(solution)/shard_map/ppermute | solution.py:415
  24.6 0.0 collective-permute-done.5.folded
  24.7 1.0 %spread_panel.3.dense.before = bf16[1920,2048]{1,0:T(8,128)(2,1)S(1)} custom-call(bf16[480,512]{1,0:T(8,128)(2,1)S(1)} %collective-permute-done.5.folded, s32[2,8,2048]{2,1,0:T(8,128)S(1)} %get-tuple-element.20.ranges, bf16[1920,2048]{1,0:T(8,128)(2,1)S(1)} %get-tuple-element.21.before), custom_call_target="tpu_custom_call", output_to_operand_aliasing={{}: (2, {})} | custom-call | tf_op jit(solution)/shard_map/spread_panel/pallas_call | solution.py:231
  25.6 1.6 %dress_rows.4 = (f32[160,1920]{1,0:T(8,128)S(1)}, s32[8,128]{1,0:T(8,128)S(1)}) custom-call(bf16[160,1920]{1,0:T(8,128)(2,1)S(1)} %owned_rows.2.refs_1_.amplitudes, bf16[1920,2048]{1,0:T(8,128)(2,1)S(1)} %spread_panel.3.dense.before, bf16[2048,1920]{1,0:T(8,128)(2,1)S(1)} %get-tuple-element.22.fock), custom_call_target="tpu_custom_call" | custom-call | tf_op jit(solution)/shard_map/dress_rows/pallas_call | solution.py:355
  27.2 1.7 %collective-permute-done.4.refs_0_ = bf16[480,512]{1,0:T(8,128)(2,1)S(1)} collective-permute-done((bf16[480,512]{1,0:T(8,128)(2,1)S(1)}, bf16[480,512]{1,0:T(8,128)(2,1)S(1)}, u32[]{:S(2)}, u32[]{:S(2)}) %collective-permute-start.4) | collective-permute-done | bytes 491552 | tf_op jit(solution)/shard_map/ppermute | solution.py:405
  28.9 0.0 collective-permute-start.6
  28.9 1.0 %spread_panel.4.before = bf16[1920,2048]{1,0:T(8,128)(2,1)S(1)} custom-call(bf16[480,512]{1,0:T(8,128)(2,1)S(1)} %after.5.folded, s32[2,8,2048]{2,1,0:T(8,128)S(1)} %get-tuple-element.20.ranges, bf16[1920,2048]{1,0:T(8,128)(2,1)S(1)} %spread_panel.3.dense.before), custom_call_target="tpu_custom_call", output_to_operand_aliasing={{}: (2, {})} | custom-call | tf_op jit(solution)/shard_map/spread_panel/pallas_call | solution.py:231
  29.9 0.9 %collective-permute-done.6.folded = bf16[480,512]{1,0:T(8,128)(2,1)S(1)} collective-permute-done((bf16[480,512]{1,0:T(8,128)(2,1)S(1)}, bf16[480,512]{1,0:T(8,128)(2,1)S(1)}, u32[]{:S(2)}, u32[]{:S(2)}) %collective-permute-start.6) | collective-permute-done | bytes 491552 | tf_op jit(solution)/shard_map/ppermute | solution.py:422
  30.8 0.9 %spread_panel.5.dense = bf16[1920,2048]{1,0:T(8,128)(2,1)S(1)} custom-call(bf16[480,512]{1,0:T(8,128)(2,1)S(1)} %collective-permute-done.6.folded, s32[2,8,2048]{2,1,0:T(8,128)S(1)} %get-tuple-element.20.ranges, bf16[1920,2048]{1,0:T(8,128)(2,1)S(1)} %spread_panel.4.before), custom_call_target="tpu_custom_call", output_to_operand_aliasing={{}: (2, {})} | custom-call | tf_op jit(solution)/shard_map/spread_panel/pallas_call | solution.py:231
  31.7 2.3 %dress_rows.5.refs_0_ = bf16[480,1920]{1,0:T(8,128)(2,1)} custom-call(bf16[160,1920]{1,0:T(8,128)(2,1)S(1)} %owned_rows.2.refs_1_.amplitudes, bf16[1920,2048]{1,0:T(8,128)(2,1)S(1)} %spread_panel.5.dense, bf16[2048,1920]{1,0:T(8,128)(2,1)S(1)} %get-tuple-element.22.fock, f32[160,1920]{1,0:T(8,128)S(1)} %get-tuple-element.24.refs_0_), custom_call_target="tpu_custom_call" | custom-call | tf_op jit(solution)/shard_map/dress_rows/pallas_call | solution.py:355
  34.0 2.6 %collective-permute-done.3.amplitudes = bf16[160,1920]{1,0:T(8,128)(2,1)S(1)} collective-permute-done((bf16[160,1920]{1,0:T(8,128)(2,1)S(1)}, bf16[160,1920]{1,0:T(8,128)(2,1)S(1)}, u32[]{:S(2)}, u32[]{:S(2)}) %collective-permute-start.3) | collective-permute-done | bytes 614432 | tf_op jit(solution)/shard_map/ppermute | solution.py:416
  36.7 3.6 %dress_rows.6 = (bf16[480,1920]{1,0:T(8,128)(2,1)}, s32[8,128]{1,0:T(8,128)S(1)}) custom-call(bf16[160,1920]{1,0:T(8,128)(2,1)S(1)} %collective-permute-done.3.amplitudes, bf16[1920,2048]{1,0:T(8,128)(2,1)S(1)} %spread_panel.5.dense, bf16[2048,1920]{1,0:T(8,128)(2,1)S(1)} %get-tuple-element.22.fock, ...), custom_call_target="tpu_custom_call", output_to_operand_aliasing={{0}: (3, {})} | custom-call | tf_op jit(solution)/shard_map/dress_rows/pallas_call | solution.py:355
  40.3 1.1 %collective-permute-done.2.received = bf16[160,1920]{1,0:T(8,128)(2,1)S(1)} collective-permute-done((bf16[160,1920]{1,0:T(8,128)(2,1)S(1)}, bf16[160,1920]{1,0:T(8,128)(2,1)S(1)}, u32[]{:S(2)}, u32[]{:S(2)}) %collective-permute-start.2) | collective-permute-done | bytes 614432 | tf_op jit(solution)/shard_map/ppermute | solution.py:415
  41.4 3.7 %dress_rows.7 = bf16[480,1920]{1,0:T(8,128)(2,1)} custom-call(bf16[160,1920]{1,0:T(8,128)(2,1)S(1)} %owned_rows.3.amplitudes, bf16[1920,2048]{1,0:T(8,128)(2,1)S(1)} %spread_panel.5.dense, bf16[2048,1920]{1,0:T(8,128)(2,1)S(1)} %get-tuple-element.22.fock, bf16[480,1920]{1,0:T(8,128)(2,1)} %get-tuple-element.26.refs_0_), custom_call_target="tpu_custom_call", output_to_operand_aliasing={{}: (3, {})} | custom-call | tf_op jit(solution)/shard_map/dress_rows/pallas_call | solution.py:355
  (6 shorter events, 0.1 us)
Async XLA Ops:
  1.2 20.5 %collective-permute-start = (bf16[160,1920]{1,0:T(8,128)(2,1)S(1)}, bf16[160,1920]{1,0:T(8,128)(2,1)S(1)}, u32[]{:S(2)}, u32[]{:S(2)}) collective-permute-start(bf16[160,1920]{1,0:T(8,128)(2,1)S(1)} %cut_rows.1.kept), channel_id=1, source_target_pairs={{8,1},{16,2},{26,3},{12,5},{20,6},{30,7},{0,8},{18,10},{24,11},{4,... | collective-permute-start | bytes 1843208 | tf_op jit(solution)/shard_map/ppermute | solution.py:412
  5.2 18.1 %collective-permute-start.1 = (bf16[80,1920]{1,0:T(8,128)(2,1)S(1)}, bf16[80,1920]{1,0:T(8,128)(2,1)S(1)}, u32[]{:S(2)}, u32[]{:S(2)}) collective-permute-start(bf16[80,1920]{1,0:T(8,128)(2,1)S(1)} %get-tuple-element.16.refs_0_), channel_id=1, source_target_pairs={{4,0},{5,1},{6,2},{7,3},{0,4},{1,5},{2,6},{3,7},{12,8},{13,9},{14,... | collective-permute-start | bytes 921608 | tf_op jit(solution)/shard_map/ppermute | solution.py:409
  6.8 17.9 %collective-permute-start.5 = (bf16[480,512]{1,0:T(8,128)(2,1)S(1)}, bf16[480,512]{1,0:T(8,128)(2,1)S(1)}, u32[]{:S(2)}, u32[]{:S(2)}) collective-permute-start(bf16[480,512]{1,0:T(8,128)(2,1)S(1)} %get-tuple-element.19), channel_id=1, source_target_pairs={{1,0},{0,1},{3,2},{2,3},{5,4},{4,5},{7,6},{6,7},{9,8},{8,9},{11,10... | collective-permute-start | bytes 1474568 | tf_op jit(solution)/shard_map/ppermute | solution.py:406
  9.8 19.2 %collective-permute-start.4 = (bf16[480,512]{1,0:T(8,128)(2,1)S(1)}, bf16[480,512]{1,0:T(8,128)(2,1)S(1)}, u32[]{:S(2)}, u32[]{:S(2)}) collective-permute-start(bf16[480,512]{1,0:T(8,128)(2,1)S(1)} %get-tuple-element.17.folded), channel_id=1, source_target_pairs={{2,0},{3,1},{0,2},{1,3},{6,4},{7,5},{4,6},{5,7},{10,8},{11,9},{8,1... | collective-permute-start | bytes 1474568 | tf_op jit(solution)/shard_map/ppermute | solution.py:405
  21.7 14.9 %collective-permute-start.3 = (bf16[160,1920]{1,0:T(8,128)(2,1)S(1)}, bf16[160,1920]{1,0:T(8,128)(2,1)S(1)}, u32[]{:S(2)}, u32[]{:S(2)}) collective-permute-start(bf16[160,1920]{1,0:T(8,128)(2,1)S(1)} %owned_rows.2.refs_1_.amplitudes), channel_id=1, source_target_pairs={{4,0},{5,1},{6,2},{7,3},{0,4},{1,5},{2,6},{3,7},{12,8},{13,9},{14,... | collective-permute-start | bytes 1843208 | tf_op jit(solution)/shard_map/ppermute | solution.py:416
  23.3 18.0 %collective-permute-start.2 = (bf16[160,1920]{1,0:T(8,128)(2,1)S(1)}, bf16[160,1920]{1,0:T(8,128)(2,1)S(1)}, u32[]{:S(2)}, u32[]{:S(2)}) collective-permute-start(bf16[160,1920]{1,0:T(8,128)(2,1)S(1)} %pad_maximum_fusion.kept), channel_id=1, source_target_pairs={{8,1},{16,2},{26,3},{12,5},{20,6},{30,7},{0,8},{18,10},{24,11},{4,... | collective-permute-start | bytes 1843208 | tf_op jit(solution)/shard_map/ppermute | solution.py:415
  28.9 1.9 %collective-permute-start.6 = (bf16[480,512]{1,0:T(8,128)(2,1)S(1)}, bf16[480,512]{1,0:T(8,128)(2,1)S(1)}, u32[]{:S(2)}, u32[]{:S(2)}) collective-permute-start(bf16[480,512]{1,0:T(8,128)(2,1)S(1)} %after.5.folded), channel_id=1, source_target_pairs={{1,0},{0,1},{3,2},{2,3},{5,4},{4,5},{7,6},{6,7},{9,8},{8,9},{11,10... | collective-permute-start | bytes 1474568 | tf_op jit(solution)/shard_map/ppermute | solution.py:422

commit v15 on v14

--- a/solution.py
+++ b/solution.py
@@ -49,29 +49,30 @@
     return copies
 
 
-def cut_kernel(whole, piece, sems):
-    for copy in copies_of(whole, 0, piece, sems):
+def cut_kernel(whole, top, low, sems, low_sems):
+    copies = copies_of(whole, 0, top, sems) + copies_of(whole, top.shape[0], low, low_sems)
+    for copy in copies:
         copy.wait()
 
 
 def cut(whole, size):
+    vmem = pl.BlockSpec(memory_space=pltpu.VMEM)
     return pl.pallas_call(
         cut_kernel,
-        out_shape=pltpu.VMEM((size, whole.shape[1]), whole.dtype),
+        out_shape=[
+            pltpu.VMEM((height, whole.shape[1]), whole.dtype)
+            for height in (size, whole.shape[0] - size)
+        ],
         in_specs=[pl.BlockSpec(memory_space=pl.ANY)],
-        out_specs=pl.BlockSpec(memory_space=pltpu.VMEM),
-        scratch_shapes=[pltpu.SemaphoreType.DMA((5,))],
+        out_specs=[vmem] * 2,
+        scratch_shapes=[pltpu.SemaphoreType.DMA((3,)), pltpu.SemaphoreType.DMA((2,))],
         compiler_params=pltpu.CompilerParams(vmem_limit_bytes=4 * MIB),
         cost_estimate=NOTHING,
         name="cut_rows",
     )(whole)
 
 
-def fold_kernel(chunk, late, pair, sizes_in, source, *refs):
-    if late:
-        amplitudes, folded, again, low, panel, sizes, bounds, sems, low_sems = refs
-    else:
-        folded, again, panel, sizes, bounds, sems = refs
+def fold_kernel(chunk, pair, sizes_in, source, folded, again, panel, sizes, bounds, sems):
     quarter, virtuals = panel.shape
     fold = folded.shape[1]
     small = pltpu.make_async_copy(sizes_in, sizes, sems.at[quarter // chunk])
@@ -81,7 +82,6 @@
         rows = pl.ds(k * chunk, chunk)
         copies.append(pltpu.make_async_copy(source.at[rows], panel.at[rows], sems.at[k]))
         copies[-1].start()
-    lows = copies_of(amplitudes, late, low, low_sems) if late else []
     small.wait()
     fill_bounds(sizes, bounds)
     start = lax.axis_index("grp") * quarter
@@ -106,11 +106,8 @@
                 folded[here, place:place + LANES] = total
                 again[here, place:place + LANES] = total
 
-    for copy in lows:
-        copy.wait()
-
-
-def fold_panel(panel, sizes, pair, fold, amplitudes, late):
+
+def fold_panel(panel, sizes, pair, fold):
     quarter, virtuals = panel.shape
     chunk = quarter // 5 if quarter % (5 * SUBLANES) == 0 else quarter
     vmem = pl.BlockSpec(memory_space=pltpu.VMEM)
@@ -122,21 +119,16 @@
         pltpu.SMEM((sizes.shape[0] + 1,), jnp.int32),
         pltpu.SemaphoreType.DMA((quarter // chunk + 1,)),
     ]
-    extra = []
-    if late:
-        out_shape.append(pltpu.VMEM((amplitudes.shape[0] - late, virtuals), amplitudes.dtype))
-        scratch.append(pltpu.SemaphoreType.DMA((2,)))
-        extra.append(amplitudes)
-    return pl.pallas_call(
-        functools.partial(fold_kernel, chunk, late),
+    return pl.pallas_call(
+        functools.partial(fold_kernel, chunk),
         out_shape=out_shape,
-        in_specs=[pl.BlockSpec(memory_space=pltpu.SMEM)] + [anywhere] * (2 + len(extra)),
-        out_specs=[vmem] * len(out_shape),
+        in_specs=[pl.BlockSpec(memory_space=pltpu.SMEM)] + [anywhere] * 2,
+        out_specs=[vmem] * 2,
         scratch_shapes=scratch,
         compiler_params=pltpu.CompilerParams(vmem_limit_bytes=8 * MIB),
         cost_estimate=NOTHING,
         name="fold_panel",
-    )(pair, sizes, pltpu.with_memory_space_constraint(panel, pltpu.HBM), *extra)
+    )(pair, sizes, pltpu.with_memory_space_constraint(panel, pltpu.HBM))
 
 
 def place_panel(slot, folded, ranges, dense, turned):
@@ -395,24 +387,23 @@
         panel = jnp.swapaxes(hole_panel[:, 0, :], 0, 1)
         irrep_sizes = pltpu.with_memory_space_constraint(irrep_sizes, pltpu.HBM)
 
-        early = rounded(rows * 2 // 3, SUBLANES) if rows % SUBLANES == 0 else 0
+        early = rounded(rows * 3 // 5, SUBLANES) if rows % SUBLANES == 0 else 0
         if early:
             amplitudes = pltpu.with_memory_space_constraint(amplitudes, pltpu.HBM)
-            top = cut(amplitudes, early)
+            top, low = cut(amplitudes, early)
         else:
             top = amplitudes
-        own, own_again, *low = fold_panel(panel, irrep_sizes, pair_irreps, fold, amplitudes, early)
+        own, own_again = fold_panel(panel, irrep_sizes, pair_irreps, fold)
         across = lax.ppermute(own, axes, to_slot(2))
         beside = lax.ppermute(own_again, axes, to_slot(1))
         if early:
-            low = low[0]
             swapped = [lax.ppermute(low, axes, to_member(by)) for by in range(1, members)]
 
         dense, fock, ranges, token = first_spread(groups, own, virt_fock, irrep_sizes, pair_irreps)
+        if early:
+            lows = jnp.concatenate([after(piece, token) for piece in [low] + swapped])
+            late = lax.ppermute(lows, axes, to_group)
         top = owned(lax.ppermute(top, axes, to_group), top, members, token)
-        if early:
-            lows = jnp.concatenate([after(piece, top) for piece in [low] + swapped])
-            late = lax.ppermute(lows, axes, to_group)
         tops = [top] + [lax.ppermute(top, axes, to_member(by)) for by in range(1, members)]
         dense = spread(1, beside, ranges, dense)
         near = 2 * dense.shape[1] // groups

time: 45.3 us -> 47.4 us (1.046)
  waiting for transfers between devices: 12.7 us -> 15.1 us
  starting transfers between devices: 10.3 us -> 9.7 us
    ppermute x1, waiting for transfers between devices: 6.37 us -> 12.7 us  [local(): top = owned(lax.ppermute(top, axes, to_group), top, members, token)]
    ppermute x1, waiting for transfers between devices: 1.71 us -> 0.01 us  [local(): across = lax.ppermute(own, axes, to_slot(2))]
    ppermute x1, waiting for transfers between devices: 2.65 us -> 1.45 us  [local(): lax.ppermute(top, axes, to_member(by))]
    ppermute x1, waiting for transfers between devices: 1.1 us -> 0.01 us  [local(): late = lax.ppermute(lows, axes, to_group)]
    ppermute x1, starting transfers between devices: 1.55 us -> 0.6 us  [local(): lax.ppermute(top, axes, to_member(by))]
  transfers between devices with their start and end apart: 7 -> 7, of which waited for: 5 -> 3; matrix products, arithmetic and copies ran while one was open for 0% -> 0% of each run, Pallas kernels for 36% -> 34%
where the time goes in v15:
time: 47.4 us; the launch traced here: 47.2 us
  Pallas kernels  21.5 us (45%)
  waiting for transfers between devices  15.1 us (32%)
  starting transfers between devices  9.7 us (20%)
  between operations  0.81 us (2%)
    ppermute x1, waiting for transfers between devices, local(): top = owned(lax.ppermute(top, axes, to_group), top, members, token)  12.7 us
    pallas_call x4, Pallas kernels, dress(): pl.pallas_call(functools.partial(dress_kernel, job), out_shape=out_shape...  11.3 us
    pallas_call x1, Pallas kernels, first_spread(): pl.pallas_call(functools.partial(first_spread_kernel, groups), out_shape=...  4 us
    ppermute x1, starting transfers between devices, local(): beside = lax.ppermute(own_again, axes, to_slot(1))  3.33 us
    pallas_call x3, Pallas kernels, spread(): pl.pallas_call(functools.partial(spread_kernel, slot), out_shape=pltpu.VM...  2.85 us
    pallas_call x1, Pallas kernels, fold_panel(): pl.pallas_call(functools.partial(fold_kernel, chunk), out_shape=out_shape...  2.05 us
    ppermute x1, starting transfers between devices, local(): across = lax.ppermute(own, axes, to_slot(2))  1.58 us
    ppermute x1, starting transfers between devices, local(): lax.ppermute(low, axes, to_member(by))  1.56 us
  transfers between devices with their start and end apart: 7, of which 3 were waited for; matrix products, arithmetic and copies ran while one was open for 0% of the time, Pallas kernels for 34%

profile of v15, /device:TPU:4, one launch (start us, length us, event | category | flops | bytes accessed | tf_op | source)
XLA Modules:
  0.0 47.2 jit_solution(7632556602564752288)
XLA Ops:
  0.0 1.3 %cut_rows.1 = (bf16[144,1920]{1,0:T(8,128)(2,1)S(1)}, bf16[96,1920]{1,0:T(8,128)(2,1)S(1)}) custom-call(bf16[240,1920]{1,0:T(8,128)(2,1)} %whole.1), custom_call_target="tpu_custom_call" | custom-call | tf_op jit(solution)/shard_map/cut_rows/pallas_call | solution.py:60
  1.3 1.6 %collective-permute-start = (bf16[96,1920]{1,0:T(8,128)(2,1)S(1)}, bf16[96,1920]{1,0:T(8,128)(2,1)S(1)}, u32[]{:S(2)}, u32[]{:S(2)}) collective-permute-start(bf16[96,1920]{1,0:T(8,128)(2,1)S(1)} %get-tuple-element.17.refs_0_), channel_id=1, source_target_pairs={{4,0},{5,1},{6,2},{7,3},{0,4},{1,5},{2,6},{3,7},{12,8},{13,9},{14,... | collective-permute-start | bytes 1105928 | tf_op jit(solution)/shard_map/ppermute | solution.py:400
  2.9 1.3 %collective-permute-start.2 = (bf16[144,1920]{1,0:T(8,128)(2,1)S(1)}, bf16[144,1920]{1,0:T(8,128)(2,1)S(1)}, u32[]{:S(2)}, u32[]{:S(2)}) collective-permute-start(bf16[144,1920]{1,0:T(8,128)(2,1)S(1)} %get-tuple-element.20.kept), channel_id=1, source_target_pairs={{8,1},{16,2},{26,3},{12,5},{20,6},{30,7},{0,8},{18,10},{24,11},{4,... | collective-permute-start | bytes 1658888 | tf_op jit(solution)/shard_map/ppermute | solution.py:406
  4.8 2.0 %fold_panel.1 = (bf16[480,512]{1,0:T(8,128)(2,1)S(1)}, bf16[480,512]{1,0:T(8,128)(2,1)S(1)}) custom-call(s32[1]{0:T(128)S(6)} %copy.26.pair, s32[8]{0:T(128)} %sizes.1, bf16[480,1920]{1,0:T(8,128)(2,1)} %bitcast.4), custom_call_target="tpu_custom_call" | custom-call | tf_op jit(solution)/shard_map/fold_panel/pallas_call | solution.py:122
  6.9 3.3 %collective-permute-start.5 = (bf16[480,512]{1,0:T(8,128)(2,1)S(1)}, bf16[480,512]{1,0:T(8,128)(2,1)S(1)}, u32[]{:S(2)}, u32[]{:S(2)}) collective-permute-start(bf16[480,512]{1,0:T(8,128)(2,1)S(1)} %get-tuple-element.21), channel_id=1, source_target_pairs={{1,0},{0,1},{3,2},{2,3},{5,4},{4,5},{7,6},{6,7},{9,8},{8,9},{11,10... | collective-permute-start | bytes 1474568 | tf_op jit(solution)/shard_map/ppermute | solution.py:398
  10.2 1.6 %collective-permute-start.4 = (bf16[480,512]{1,0:T(8,128)(2,1)S(1)}, bf16[480,512]{1,0:T(8,128)(2,1)S(1)}, u32[]{:S(2)}, u32[]{:S(2)}) collective-permute-start(bf16[480,512]{1,0:T(8,128)(2,1)S(1)} %get-tuple-element.18.folded), channel_id=1, source_target_pairs={{2,0},{3,1},{0,2},{1,3},{6,4},{7,5},{4,6},{5,7},{10,8},{11,9},{8,1... | collective-permute-start | bytes 1474568 | tf_op jit(solution)/shard_map/ppermute | solution.py:397
  11.8 4.0 %first_spread.1 = (bf16[1920,2048]{1,0:T(8,128)(2,1)S(1)}, bf16[2048,1920]{1,0:T(8,128)(2,1)S(1)}, s32[2,8,2048]{2,1,0:T(8,128)S(1)}, s32[8,128]{1,0:T(8,128)S(1)}) custom-call(s32[8]{0:T(128)} %sizes.1, s32[1]{0:T(128)S(6)} %copy.26.pair, bf16[480,512]{1,0:T(8,128)(2,1)S(1)} %get-tuple-element.18.folded, bf16[1920,1920]{1,0:T(8,128)(2,1)} %fock.1), custom_call_target="tpu_custom_call" | custom-call | tf_op jit(solution)/shard_map/first_spread/pallas_call | solution.py:193
  15.8 0.0 collective-permute-done.refs_0_
  15.8 0.1 pad_maximum_fusion.kept
  15.9 1.3 %collective-permute-start.1 = (bf16[192,1920]{1,0:T(8,128)(2,1)S(1)}, bf16[192,1920]{1,0:T(8,128)(2,1)S(1)}, u32[]{:S(2)}, u32[]{:S(2)}) collective-permute-start(bf16[192,1920]{1,0:T(8,128)(2,1)S(1)} %pad_maximum_fusion.kept), channel_id=1, source_target_pairs={{8,1},{16,2},{26,3},{12,5},{20,6},{30,7},{0,8},{18,10},{24,11},{4,... | collective-permute-start | bytes 2211848 | tf_op jit(solution)/shard_map/ppermute | solution.py:405
  17.2 12.7 %collective-permute-done.2.received = bf16[144,1920]{1,0:T(8,128)(2,1)S(1)} collective-permute-done((bf16[144,1920]{1,0:T(8,128)(2,1)S(1)}, bf16[144,1920]{1,0:T(8,128)(2,1)S(1)}, u32[]{:S(2)}, u32[]{:S(2)}) %collective-permute-start.2) | collective-permute-done | bytes 552992 | tf_op jit(solution)/shard_map/ppermute | solution.py:406
  29.9 0.6 %collective-permute-start.3 = (bf16[144,1920]{1,0:T(8,128)(2,1)S(1)}, bf16[144,1920]{1,0:T(8,128)(2,1)S(1)}, u32[]{:S(2)}, u32[]{:S(2)}) collective-permute-start(bf16[144,1920]{1,0:T(8,128)(2,1)S(1)} %owned_rows.2.amplitudes), channel_id=1, source_target_pairs={{4,0},{5,1},{6,2},{7,3},{0,4},{1,5},{2,6},{3,7},{12,8},{13,9},{14,... | collective-permute-start | bytes 1658888 | tf_op jit(solution)/shard_map/ppermute | solution.py:407
  30.5 0.0 collective-permute-done.5.folded
  30.5 0.9 %spread_panel.3.dense.before = bf16[1920,2048]{1,0:T(8,128)(2,1)S(1)} custom-call(bf16[480,512]{1,0:T(8,128)(2,1)S(1)} %collective-permute-done.5.folded, s32[2,8,2048]{2,1,0:T(8,128)S(1)} %get-tuple-element.22.ranges, bf16[1920,2048]{1,0:T(8,128)(2,1)S(1)} %get-tuple-element.23.before), custom_call_target="tpu_custom_call", output_to_operand_aliasing={{}: (2, {})} | custom-call | tf_op jit(solution)/shard_map/spread_panel/pallas_call | solution.py:223
  31.5 1.5 %dress_rows.4 = (f32[144,1920]{1,0:T(8,128)S(1)}, s32[8,128]{1,0:T(8,128)S(1)}) custom-call(bf16[144,1920]{1,0:T(8,128)(2,1)S(1)} %owned_rows.2.amplitudes, bf16[1920,2048]{1,0:T(8,128)(2,1)S(1)} %spread_panel.3.dense.before, bf16[2048,1920]{1,0:T(8,128)(2,1)S(1)} %get-tuple-element.24.fock), custom_call_target="tpu_custom_call" | custom-call | tf_op jit(solution)/shard_map/dress_rows/pallas_call | solution.py:347
  32.9 0.0 collective-permute-done.4.refs_0_
  33.0 0.1 collective-permute-start.6
  33.0 1.0 %spread_panel.4.before = bf16[1920,2048]{1,0:T(8,128)(2,1)S(1)} custom-call(bf16[480,512]{1,0:T(8,128)(2,1)S(1)} %after.5.folded, s32[2,8,2048]{2,1,0:T(8,128)S(1)} %get-tuple-element.22.ranges, bf16[1920,2048]{1,0:T(8,128)(2,1)S(1)} %spread_panel.3.dense.before), custom_call_target="tpu_custom_call", output_to_operand_aliasing={{}: (2, {})} | custom-call | tf_op jit(solution)/shard_map/spread_panel/pallas_call | solution.py:223
  34.0 0.9 %collective-permute-done.6.folded = bf16[480,512]{1,0:T(8,128)(2,1)S(1)} collective-permute-done((bf16[480,512]{1,0:T(8,128)(2,1)S(1)}, bf16[480,512]{1,0:T(8,128)(2,1)S(1)}, u32[]{:S(2)}, u32[]{:S(2)}) %collective-permute-start.6) | collective-permute-done | bytes 491552 | tf_op jit(solution)/shard_map/ppermute | solution.py:413
  34.9 0.9 %spread_panel.5.dense = bf16[1920,2048]{1,0:T(8,128)(2,1)S(1)} custom-call(bf16[480,512]{1,0:T(8,128)(2,1)S(1)} %collective-permute-done.6.folded, s32[2,8,2048]{2,1,0:T(8,128)S(1)} %get-tuple-element.22.ranges, bf16[1920,2048]{1,0:T(8,128)(2,1)S(1)} %spread_panel.4.before), custom_call_target="tpu_custom_call", output_to_operand_aliasing={{}: (2, {})} | custom-call | tf_op jit(solution)/shard_map/spread_panel/pallas_call | solution.py:223
  35.8 2.2 %dress_rows.5.refs_0_ = bf16[480,1920]{1,0:T(8,128)(2,1)} custom-call(bf16[144,1920]{1,0:T(8,128)(2,1)S(1)} %owned_rows.2.amplitudes, bf16[1920,2048]{1,0:T(8,128)(2,1)S(1)} %spread_panel.5.dense, bf16[2048,1920]{1,0:T(8,128)(2,1)S(1)} %get-tuple-element.24.fock, f32[144,1920]{1,0:T(8,128)S(1)} %get-tuple-element.26.refs_0_), custom_call_target="tpu_custom_call" | custom-call | tf_op jit(solution)/shard_map/dress_rows/pallas_call | solution.py:347
  38.0 1.4 %collective-permute-done.3.amplitudes = bf16[144,1920]{1,0:T(8,128)(2,1)S(1)} collective-permute-done((bf16[144,1920]{1,0:T(8,128)(2,1)S(1)}, bf16[144,1920]{1,0:T(8,128)(2,1)S(1)}, u32[]{:S(2)}, u32[]{:S(2)}) %collective-permute-start.3) | collective-permute-done | bytes 552992 | tf_op jit(solution)/shard_map/ppermute | solution.py:407
  39.5 3.4 %dress_rows.6 = (bf16[480,1920]{1,0:T(8,128)(2,1)}, s32[8,128]{1,0:T(8,128)S(1)}) custom-call(bf16[144,1920]{1,0:T(8,128)(2,1)S(1)} %collective-permute-done.3.amplitudes, bf16[1920,2048]{1,0:T(8,128)(2,1)S(1)} %spread_panel.5.dense, bf16[2048,1920]{1,0:T(8,128)(2,1)S(1)} %get-tuple-element.24.fock, ...), custom_call_target="tpu_custom_call", output_to_operand_aliasing={{0}: (3, {})} | custom-call | tf_op jit(solution)/shard_map/dress_rows/pallas_call | solution.py:347
  42.9 0.0 collective-permute-done.1.received
  42.9 4.2 %dress_rows.7 = bf16[480,1920]{1,0:T(8,128)(2,1)} custom-call(bf16[192,1920]{1,0:T(8,128)(2,1)S(1)} %owned_rows.3.amplitudes, bf16[1920,2048]{1,0:T(8,128)(2,1)S(1)} %spread_panel.5.dense, bf16[2048,1920]{1,0:T(8,128)(2,1)S(1)} %get-tuple-element.24.fock, bf16[480,1920]{1,0:T(8,128)(2,1)} %get-tuple-element.28.refs_0_), custom_call_target="tpu_custom_call", output_to_operand_aliasing={{}: (3, {})} | custom-call | tf_op jit(solution)/shard_map/dress_rows/pallas_call | solution.py:347
  (5 shorter events, 0.0 us)
Async XLA Ops:
  1.3 14.5 %collective-permute-start = (bf16[96,1920]{1,0:T(8,128)(2,1)S(1)}, bf16[96,1920]{1,0:T(8,128)(2,1)S(1)}, u32[]{:S(2)}, u32[]{:S(2)}) collective-permute-start(bf16[96,1920]{1,0:T(8,128)(2,1)S(1)} %get-tuple-element.17.refs_0_), channel_id=1, source_target_pairs={{4,0},{5,1},{6,2},{7,3},{0,4},{1,5},{2,6},{3,7},{12,8},{13,9},{14,... | collective-permute-start | bytes 1105928 | tf_op jit(solution)/shard_map/ppermute | solution.py:400
  2.9 27.0 %collective-permute-start.2 = (bf16[144,1920]{1,0:T(8,128)(2,1)S(1)}, bf16[144,1920]{1,0:T(8,128)(2,1)S(1)}, u32[]{:S(2)}, u32[]{:S(2)}) collective-permute-start(bf16[144,1920]{1,0:T(8,128)(2,1)S(1)} %get-tuple-element.20.kept), channel_id=1, source_target_pairs={{8,1},{16,2},{26,3},{12,5},{20,6},{30,7},{0,8},{18,10},{24,11},{4,... | collective-permute-start | bytes 1658888 | tf_op jit(solution)/shard_map/ppermute | solution.py:406
  6.9 23.7 %collective-permute-start.5 = (bf16[480,512]{1,0:T(8,128)(2,1)S(1)}, bf16[480,512]{1,0:T(8,128)(2,1)S(1)}, u32[]{:S(2)}, u32[]{:S(2)}) collective-permute-start(bf16[480,512]{1,0:T(8,128)(2,1)S(1)} %get-tuple-element.21), channel_id=1, source_target_pairs={{1,0},{0,1},{3,2},{2,3},{5,4},{4,5},{7,6},{6,7},{9,8},{8,9},{11,10... | collective-permute-start | bytes 1474568 | tf_op jit(solution)/shard_map/ppermute | solution.py:398
  10.2 22.8 %collective-permute-start.4 = (bf16[480,512]{1,0:T(8,128)(2,1)S(1)}, bf16[480,512]{1,0:T(8,128)(2,1)S(1)}, u32[]{:S(2)}, u32[]{:S(2)}) collective-permute-start(bf16[480,512]{1,0:T(8,128)(2,1)S(1)} %get-tuple-element.18.folded), channel_id=1, source_target_pairs={{2,0},{3,1},{0,2},{1,3},{6,4},{7,5},{4,6},{5,7},{10,8},{11,9},{8,1... | collective-permute-start | bytes 1474568 | tf_op jit(solution)/shard_map/ppermute | solution.py:397
  15.9 27.0 %collective-permute-start.1 = (bf16[192,1920]{1,0:T(8,128)(2,1)S(1)}, bf16[192,1920]{1,0:T(8,128)(2,1)S(1)}, u32[]{:S(2)}, u32[]{:S(2)}) collective-permute-start(bf16[192,1920]{1,0:T(8,128)(2,1)S(1)} %pad_maximum_fusion.kept), channel_id=1, source_target_pairs={{8,1},{16,2},{26,3},{12,5},{20,6},{30,7},{0,8},{18,10},{24,11},{4,... | collective-permute-start | bytes 2211848 | tf_op jit(solution)/shard_map/ppermute | solution.py:405
  29.9 9.6 %collective-permute-start.3 = (bf16[144,1920]{1,0:T(8,128)(2,1)S(1)}, bf16[144,1920]{1,0:T(8,128)(2,1)S(1)}, u32[]{:S(2)}, u32[]{:S(2)}) collective-permute-start(bf16[144,1920]{1,0:T(8,128)(2,1)S(1)} %owned_rows.2.amplitudes), channel_id=1, source_target_pairs={{4,0},{5,1},{6,2},{7,3},{0,4},{1,5},{2,6},{3,7},{12,8},{13,9},{14,... | collective-permute-start | bytes 1658888 | tf_op jit(solution)/shard_map/ppermute | solution.py:407
  33.0 1.9 %collective-permute-start.6 = (bf16[480,512]{1,0:T(8,128)(2,1)S(1)}, bf16[480,512]{1,0:T(8,128)(2,1)S(1)}, u32[]{:S(2)}, u32[]{:S(2)}) collective-permute-start(bf16[480,512]{1,0:T(8,128)(2,1)S(1)} %after.5.folded), channel_id=1, source_target_pairs={{1,0},{0,1},{3,2},{2,3},{5,4},{4,5},{7,6},{6,7},{9,8},{8,9},{11,10... | collective-permute-start | bytes 1474568 | tf_op jit(solution)/shard_map/ppermute | solution.py:413

commit v16 on v14

--- a/solution.py
+++ b/solution.py
@@ -284,6 +284,17 @@
     return [(first, min(tile, total - first)) for first in range(0, total, tile)]
 
 
+def ending_small(total, tile):
+    tiles, first = [], 0
+    while first < total:
+        left = total - first
+        size = tile if left >= 2 * tile or left < 2 * LANES else rounded(left * 2 // 3, LANES)
+        size = min(size, tile, left)
+        tiles.append((first, size))
+        first += size
+    return tiles
+
+
 def dress_kernel(job, amplitudes, dense, fock, *refs):
     columns, spans, rows, members, has_sums, has_base, signed = job
     if has_sums:
@@ -309,7 +320,7 @@
             for by, offset, _ in spans
         ]
     copies = []
-    for t, (first, tile) in enumerate(column_tiles(virtuals, 512)):
+    for t, (first, tile) in enumerate(ending_small(virtuals, 512)):
         here = slice(first, first + tile)
         total = jnp.dot(
             coupled[...], fock[begin:end, here], preferred_element_type=jnp.float32
@@ -347,7 +358,7 @@
         out_shape = [jax.ShapeDtypeStruct((out_rows, virtuals), amplitudes.dtype)]
         scratch += [
             pltpu.VMEM((height, virtuals), amplitudes.dtype),
-            pltpu.SemaphoreType.DMA((len(spans), len(column_tiles(virtuals, 512)))),
+            pltpu.SemaphoreType.DMA((len(spans), len(ending_small(virtuals, 512)))),
         ]
     else:
         out_shape = [pltpu.VMEM((height, virtuals), jnp.float32)]
@@ -375,7 +386,7 @@
     everyone = [(h, l, g) for h in range(groups) for l in range(members) for g in range(groups)]
 
     if groups == 4:
-        copies = ((None, 0, 3, 1), (0, None, 1, 3), (0, 2, None, 3), (2, 0, 3, None))
+        copies = ((None, 0, 3, 1), (2, None, 1, 3), (0, 2, None, 1), (2, 0, 3, None))
     else:
         copies = [[None if h == g else h for h in range(groups)] for g in range(groups)]
     to_group = [

time: 45.3 us -> 45.4 us (level)
  no operation moved by 1% of the time
where the time goes in v16:
time: 45.4 us; the launch traced here: 45.2 us
  Pallas kernels  21.3 us (47%)
  waiting for transfers between devices  12.8 us (28%)
  starting transfers between devices  10.3 us (23%)
  between operations  0.77 us (2%)
    pallas_call x4, Pallas kernels, dress(): pl.pallas_call(functools.partial(dress_kernel, job), out_shape=out_shape...  11.1 us
    ppermute x1, waiting for transfers between devices, local(): top = owned(lax.ppermute(top, axes, to_group), top, members, token)  6.37 us
    pallas_call x1, Pallas kernels, first_spread(): pl.pallas_call(functools.partial(first_spread_kernel, groups), out_shape=...  4 us
    ppermute x1, starting transfers between devices, local(): beside = lax.ppermute(own_again, axes, to_slot(1))  2.98 us
    pallas_call x3, Pallas kernels, spread(): pl.pallas_call(functools.partial(spread_kernel, slot), out_shape=pltpu.VM...  2.85 us
    ppermute x1, waiting for transfers between devices, local(): lax.ppermute(top, axes, to_member(by))  2.65 us
    pallas_call x1, Pallas kernels, fold_panel(): pl.pallas_call(functools.partial(fold_kernel, chunk, late), out_shape=out...  2.07 us
    ppermute x1, waiting for transfers between devices, local(): across = lax.ppermute(own, axes, to_slot(2))  1.71 us
  transfers between devices with their start and end apart: 7, of which 5 were waited for; matrix products, arithmetic and copies ran while one was open for 0% of the time, Pallas kernels for 36%

profile of v16, /device:TPU:4, one launch (start us, length us, event | category | flops | bytes accessed | tf_op | source)
XLA Modules:
  0.0 45.2 jit_solution(17198199889757885968)
XLA Ops:
  0.0 1.2 %cut_rows.1.kept = bf16[160,1920]{1,0:T(8,128)(2,1)S(1)} custom-call(bf16[240,1920]{1,0:T(8,128)(2,1)} %whole.1), custom_call_target="tpu_custom_call" | custom-call | tf_op jit(solution)/shard_map/cut_rows/pallas_call | solution.py:58
  1.2 1.3 %collective-permute-start = (bf16[160,1920]{1,0:T(8,128)(2,1)S(1)}, bf16[160,1920]{1,0:T(8,128)(2,1)S(1)}, u32[]{:S(2)}, u32[]{:S(2)}) collective-permute-start(bf16[160,1920]{1,0:T(8,128)(2,1)S(1)} %cut_rows.1.kept), channel_id=1, source_target_pairs={{10,1},{16,2},{26,3},{14,5},{20,6},{30,7},{0,8},{18,10},{24,11},{4... | collective-permute-start | bytes 1843208 | tf_op jit(solution)/shard_map/ppermute | solution.py:423
  3.1 2.1 %fold_panel.1 = (bf16[480,512]{1,0:T(8,128)(2,1)S(1)}, bf16[480,512]{1,0:T(8,128)(2,1)S(1)}, bf16[80,1920]{1,0:T(8,128)(2,1)S(1)}) custom-call(s32[1]{0:T(128)S(6)} %copy.26.pair, s32[8]{0:T(128)} %sizes.1, bf16[480,1920]{1,0:T(8,128)(2,1)} %bitcast.4, bf16[240,1920]{1,0:T(8,128)(2,1)} %whole.1), custom_call_target="tpu_custom_call" | custom-call | tf_op jit(solution)/shard_map/fold_panel/pallas_call | solution.py:130
  5.2 1.6 %collective-permute-start.1 = (bf16[80,1920]{1,0:T(8,128)(2,1)S(1)}, bf16[80,1920]{1,0:T(8,128)(2,1)S(1)}, u32[]{:S(2)}, u32[]{:S(2)}) collective-permute-start(bf16[80,1920]{1,0:T(8,128)(2,1)S(1)} %get-tuple-element.16.refs_0_), channel_id=1, source_target_pairs={{4,0},{5,1},{6,2},{7,3},{0,4},{1,5},{2,6},{3,7},{12,8},{13,9},{14,... | collective-permute-start | bytes 921608 | tf_op jit(solution)/shard_map/ppermute | solution.py:420
  6.8 3.0 %collective-permute-start.5 = (bf16[480,512]{1,0:T(8,128)(2,1)S(1)}, bf16[480,512]{1,0:T(8,128)(2,1)S(1)}, u32[]{:S(2)}, u32[]{:S(2)}) collective-permute-start(bf16[480,512]{1,0:T(8,128)(2,1)S(1)} %get-tuple-element.19), channel_id=1, source_target_pairs={{1,0},{0,1},{3,2},{2,3},{5,4},{4,5},{7,6},{6,7},{9,8},{8,9},{11,10... | collective-permute-start | bytes 1474568 | tf_op jit(solution)/shard_map/ppermute | solution.py:417
  9.8 1.6 %collective-permute-start.4 = (bf16[480,512]{1,0:T(8,128)(2,1)S(1)}, bf16[480,512]{1,0:T(8,128)(2,1)S(1)}, u32[]{:S(2)}, u32[]{:S(2)}) collective-permute-start(bf16[480,512]{1,0:T(8,128)(2,1)S(1)} %get-tuple-element.17.folded), channel_id=1, source_target_pairs={{2,0},{3,1},{0,2},{1,3},{6,4},{7,5},{4,6},{5,7},{10,8},{11,9},{8,1... | collective-permute-start | bytes 1474568 | tf_op jit(solution)/shard_map/ppermute | solution.py:416
  11.3 4.0 %first_spread.1 = (bf16[1920,2048]{1,0:T(8,128)(2,1)S(1)}, bf16[2048,1920]{1,0:T(8,128)(2,1)S(1)}, s32[2,8,2048]{2,1,0:T(8,128)S(1)}, s32[8,128]{1,0:T(8,128)S(1)}) custom-call(s32[8]{0:T(128)} %sizes.1, s32[1]{0:T(128)S(6)} %copy.26.pair, bf16[480,512]{1,0:T(8,128)(2,1)S(1)} %get-tuple-element.17.folded, bf16[1920,1920]{1,0:T(8,128)(2,1)} %fock.1), custom_call_target="tpu_custom_call" | custom-call | tf_op jit(solution)/shard_map/first_spread/pallas_call | solution.py:201
  15.3 6.4 %collective-permute-done.received = bf16[160,1920]{1,0:T(8,128)(2,1)S(1)} collective-permute-done((bf16[160,1920]{1,0:T(8,128)(2,1)S(1)}, bf16[160,1920]{1,0:T(8,128)(2,1)S(1)}, u32[]{:S(2)}, u32[]{:S(2)}) %collective-permute-start) | collective-permute-done | bytes 614432 | tf_op jit(solution)/shard_map/ppermute | solution.py:423
  21.7 1.6 %collective-permute-start.3 = (bf16[160,1920]{1,0:T(8,128)(2,1)S(1)}, bf16[160,1920]{1,0:T(8,128)(2,1)S(1)}, u32[]{:S(2)}, u32[]{:S(2)}) collective-permute-start(bf16[160,1920]{1,0:T(8,128)(2,1)S(1)} %owned_rows.2.refs_1_.amplitudes), channel_id=1, source_target_pairs={{4,0},{5,1},{6,2},{7,3},{0,4},{1,5},{2,6},{3,7},{12,8},{13,9},{14,... | collective-permute-start | bytes 1843208 | tf_op jit(solution)/shard_map/ppermute | solution.py:427
  23.3 0.0 collective-permute-done.1.refs_0_
  23.3 1.3 %collective-permute-start.2 = (bf16[160,1920]{1,0:T(8,128)(2,1)S(1)}, bf16[160,1920]{1,0:T(8,128)(2,1)S(1)}, u32[]{:S(2)}, u32[]{:S(2)}) collective-permute-start(bf16[160,1920]{1,0:T(8,128)(2,1)S(1)} %pad_maximum_fusion.kept), channel_id=1, source_target_pairs={{10,1},{16,2},{26,3},{14,5},{20,6},{30,7},{0,8},{18,10},{24,11},{4... | collective-permute-start | bytes 1843208 | tf_op jit(solution)/shard_map/ppermute | solution.py:426
  24.6 0.0 collective-permute-done.5.folded
  24.7 1.0 %spread_panel.3.dense.before = bf16[1920,2048]{1,0:T(8,128)(2,1)S(1)} custom-call(bf16[480,512]{1,0:T(8,128)(2,1)S(1)} %collective-permute-done.5.folded, s32[2,8,2048]{2,1,0:T(8,128)S(1)} %get-tuple-element.20.ranges, bf16[1920,2048]{1,0:T(8,128)(2,1)S(1)} %get-tuple-element.21.before), custom_call_target="tpu_custom_call", output_to_operand_aliasing={{}: (2, {})} | custom-call | tf_op jit(solution)/shard_map/spread_panel/pallas_call | solution.py:231
  25.6 1.6 %dress_rows.4 = (f32[160,1920]{1,0:T(8,128)S(1)}, s32[8,128]{1,0:T(8,128)S(1)}) custom-call(bf16[160,1920]{1,0:T(8,128)(2,1)S(1)} %owned_rows.2.refs_1_.amplitudes, bf16[1920,2048]{1,0:T(8,128)(2,1)S(1)} %spread_panel.3.dense.before, bf16[2048,1920]{1,0:T(8,128)(2,1)S(1)} %get-tuple-element.22.fock), custom_call_target="tpu_custom_call" | custom-call | tf_op jit(solution)/shard_map/dress_rows/pallas_call | solution.py:366
  27.2 1.7 %collective-permute-done.4.refs_0_ = bf16[480,512]{1,0:T(8,128)(2,1)S(1)} collective-permute-done((bf16[480,512]{1,0:T(8,128)(2,1)S(1)}, bf16[480,512]{1,0:T(8,128)(2,1)S(1)}, u32[]{:S(2)}, u32[]{:S(2)}) %collective-permute-start.4) | collective-permute-done | bytes 491552 | tf_op jit(solution)/shard_map/ppermute | solution.py:416
  28.9 0.0 collective-permute-start.6
  28.9 1.0 %spread_panel.4.before = bf16[1920,2048]{1,0:T(8,128)(2,1)S(1)} custom-call(bf16[480,512]{1,0:T(8,128)(2,1)S(1)} %after.5.folded, s32[2,8,2048]{2,1,0:T(8,128)S(1)} %get-tuple-element.20.ranges, bf16[1920,2048]{1,0:T(8,128)(2,1)S(1)} %spread_panel.3.dense.before), custom_call_target="tpu_custom_call", output_to_operand_aliasing={{}: (2, {})} | custom-call | tf_op jit(solution)/shard_map/spread_panel/pallas_call | solution.py:231
  29.9 0.9 %collective-permute-done.6.folded = bf16[480,512]{1,0:T(8,128)(2,1)S(1)} collective-permute-done((bf16[480,512]{1,0:T(8,128)(2,1)S(1)}, bf16[480,512]{1,0:T(8,128)(2,1)S(1)}, u32[]{:S(2)}, u32[]{:S(2)}) %collective-permute-start.6) | collective-permute-done | bytes 491552 | tf_op jit(solution)/shard_map/ppermute | solution.py:433
  30.8 0.9 %spread_panel.5.dense = bf16[1920,2048]{1,0:T(8,128)(2,1)S(1)} custom-call(bf16[480,512]{1,0:T(8,128)(2,1)S(1)} %collective-permute-done.6.folded, s32[2,8,2048]{2,1,0:T(8,128)S(1)} %get-tuple-element.20.ranges, bf16[1920,2048]{1,0:T(8,128)(2,1)S(1)} %spread_panel.4.before), custom_call_target="tpu_custom_call", output_to_operand_aliasing={{}: (2, {})} | custom-call | tf_op jit(solution)/shard_map/spread_panel/pallas_call | solution.py:231
  31.7 2.3 %dress_rows.5.refs_0_ = bf16[480,1920]{1,0:T(8,128)(2,1)} custom-call(bf16[160,1920]{1,0:T(8,128)(2,1)S(1)} %owned_rows.2.refs_1_.amplitudes, bf16[1920,2048]{1,0:T(8,128)(2,1)S(1)} %spread_panel.5.dense, bf16[2048,1920]{1,0:T(8,128)(2,1)S(1)} %get-tuple-element.22.fock, f32[160,1920]{1,0:T(8,128)S(1)} %get-tuple-element.24.refs_0_), custom_call_target="tpu_custom_call" | custom-call | tf_op jit(solution)/shard_map/dress_rows/pallas_call | solution.py:366
  34.0 2.6 %collective-permute-done.3.amplitudes = bf16[160,1920]{1,0:T(8,128)(2,1)S(1)} collective-permute-done((bf16[160,1920]{1,0:T(8,128)(2,1)S(1)}, bf16[160,1920]{1,0:T(8,128)(2,1)S(1)}, u32[]{:S(2)}, u32[]{:S(2)}) %collective-permute-start.3) | collective-permute-done | bytes 614432 | tf_op jit(solution)/shard_map/ppermute | solution.py:427
  36.7 3.6 %dress_rows.6 = (bf16[480,1920]{1,0:T(8,128)(2,1)}, s32[8,128]{1,0:T(8,128)S(1)}) custom-call(bf16[160,1920]{1,0:T(8,128)(2,1)S(1)} %collective-permute-done.3.amplitudes, bf16[1920,2048]{1,0:T(8,128)(2,1)S(1)} %spread_panel.5.dense, bf16[2048,1920]{1,0:T(8,128)(2,1)S(1)} %get-tuple-element.22.fock, ...), custom_call_target="tpu_custom_call", output_to_operand_aliasing={{0}: (3, {})} | custom-call | tf_op jit(solution)/shard_map/dress_rows/pallas_call | solution.py:366
  40.3 1.2 %collective-permute-done.2.received = bf16[160,1920]{1,0:T(8,128)(2,1)S(1)} collective-permute-done((bf16[160,1920]{1,0:T(8,128)(2,1)S(1)}, bf16[160,1920]{1,0:T(8,128)(2,1)S(1)}, u32[]{:S(2)}, u32[]{:S(2)}) %collective-permute-start.2) | collective-permute-done | bytes 614432 | tf_op jit(solution)/shard_map/ppermute | solution.py:426
  41.5 3.7 %dress_rows.7 = bf16[480,1920]{1,0:T(8,128)(2,1)} custom-call(bf16[160,1920]{1,0:T(8,128)(2,1)S(1)} %owned_rows.3.amplitudes, bf16[1920,2048]{1,0:T(8,128)(2,1)S(1)} %spread_panel.5.dense, bf16[2048,1920]{1,0:T(8,128)(2,1)S(1)} %get-tuple-element.22.fock, bf16[480,1920]{1,0:T(8,128)(2,1)} %get-tuple-element.26.refs_0_), custom_call_target="tpu_custom_call", output_to_operand_aliasing={{}: (3, {})} | custom-call | tf_op jit(solution)/shard_map/dress_rows/pallas_call | solution.py:366
  (6 shorter events, 0.1 us)
Async XLA Ops:
  1.2 20.5 %collective-permute-start = (bf16[160,1920]{1,0:T(8,128)(2,1)S(1)}, bf16[160,1920]{1,0:T(8,128)(2,1)S(1)}, u32[]{:S(2)}, u32[]{:S(2)}) collective-permute-start(bf16[160,1920]{1,0:T(8,128)(2,1)S(1)} %cut_rows.1.kept), channel_id=1, source_target_pairs={{10,1},{16,2},{26,3},{14,5},{20,6},{30,7},{0,8},{18,10},{24,11},{4... | collective-permute-start | bytes 1843208 | tf_op jit(solution)/shard_map/ppermute | solution.py:423
  5.2 18.1 %collective-permute-start.1 = (bf16[80,1920]{1,0:T(8,128)(2,1)S(1)}, bf16[80,1920]{1,0:T(8,128)(2,1)S(1)}, u32[]{:S(2)}, u32[]{:S(2)}) collective-permute-start(bf16[80,1920]{1,0:T(8,128)(2,1)S(1)} %get-tuple-element.16.refs_0_), channel_id=1, source_target_pairs={{4,0},{5,1},{6,2},{7,3},{0,4},{1,5},{2,6},{3,7},{12,8},{13,9},{14,... | collective-permute-start | bytes 921608 | tf_op jit(solution)/shard_map/ppermute | solution.py:420
  6.8 17.9 %collective-permute-start.5 = (bf16[480,512]{1,0:T(8,128)(2,1)S(1)}, bf16[480,512]{1,0:T(8,128)(2,1)S(1)}, u32[]{:S(2)}, u32[]{:S(2)}) collective-permute-start(bf16[480,512]{1,0:T(8,128)(2,1)S(1)} %get-tuple-element.19), channel_id=1, source_target_pairs={{1,0},{0,1},{3,2},{2,3},{5,4},{4,5},{7,6},{6,7},{9,8},{8,9},{11,10... | collective-permute-start | bytes 1474568 | tf_op jit(solution)/shard_map/ppermute | solution.py:417
  9.8 19.2 %collective-permute-start.4 = (bf16[480,512]{1,0:T(8,128)(2,1)S(1)}, bf16[480,512]{1,0:T(8,128)(2,1)S(1)}, u32[]{:S(2)}, u32[]{:S(2)}) collective-permute-start(bf16[480,512]{1,0:T(8,128)(2,1)S(1)} %get-tuple-element.17.folded), channel_id=1, source_target_pairs={{2,0},{3,1},{0,2},{1,3},{6,4},{7,5},{4,6},{5,7},{10,8},{11,9},{8,1... | collective-permute-start | bytes 1474568 | tf_op jit(solution)/shard_map/ppermute | solution.py:416
  21.7 14.9 %collective-permute-start.3 = (bf16[160,1920]{1,0:T(8,128)(2,1)S(1)}, bf16[160,1920]{1,0:T(8,128)(2,1)S(1)}, u32[]{:S(2)}, u32[]{:S(2)}) collective-permute-start(bf16[160,1920]{1,0:T(8,128)(2,1)S(1)} %owned_rows.2.refs_1_.amplitudes), channel_id=1, source_target_pairs={{4,0},{5,1},{6,2},{7,3},{0,4},{1,5},{2,6},{3,7},{12,8},{13,9},{14,... | collective-permute-start | bytes 1843208 | tf_op jit(solution)/shard_map/ppermute | solution.py:427
  23.3 18.1 %collective-permute-start.2 = (bf16[160,1920]{1,0:T(8,128)(2,1)S(1)}, bf16[160,1920]{1,0:T(8,128)(2,1)S(1)}, u32[]{:S(2)}, u32[]{:S(2)}) collective-permute-start(bf16[160,1920]{1,0:T(8,128)(2,1)S(1)} %pad_maximum_fusion.kept), channel_id=1, source_target_pairs={{10,1},{16,2},{26,3},{14,5},{20,6},{30,7},{0,8},{18,10},{24,11},{4... | collective-permute-start | bytes 1843208 | tf_op jit(solution)/shard_map/ppermute | solution.py:426
  28.9 1.9 %collective-permute-start.6 = (bf16[480,512]{1,0:T(8,128)(2,1)S(1)}, bf16[480,512]{1,0:T(8,128)(2,1)S(1)}, u32[]{:S(2)}, u32[]{:S(2)}) collective-permute-start(bf16[480,512]{1,0:T(8,128)(2,1)S(1)} %after.5.folded), channel_id=1, source_target_pairs={{1,0},{0,1},{3,2},{2,3},{5,4},{4,5},{7,6},{6,7},{9,8},{8,9},{11,10... | collective-permute-start | bytes 1474568 | tf_op jit(solution)/shard_map/ppermute | solution.py:433

commit v17 on v14

--- a/solution.py
+++ b/solution.py
@@ -375,12 +375,14 @@
     everyone = [(h, l, g) for h in range(groups) for l in range(members) for g in range(groups)]
 
     if groups == 4:
-        copies = ((None, 0, 3, 1), (0, None, 1, 3), (0, 2, None, 3), (2, 0, 3, None))
+        early_copies = ((None, 0, 3, 1), (0, None, 1, 3), (0, 2, None, 3), (2, 0, 3, None))
+        late_copies = ((None, 0, 1, 3), (0, None, 3, 1), (2, 0, None, 3), (0, 2, 3, None))
     else:
-        copies = [[None if h == g else h for h in range(groups)] for g in range(groups)]
-    to_group = [
-        (device(g, l, copies[g][h]), device(h, l, g)) for h, l, g in everyone if h != g
-    ]
+        early_copies = [[None if h == g else h for h in range(groups)] for g in range(groups)]
+        late_copies = early_copies
+
+    def to_group(copies):
+        return [(device(g, l, copies[g][h]), device(h, l, g)) for h, l, g in everyone if h != g]
 
     def to_member(by):
         return [(device(h, (l + by) % members, g), device(h, l, g)) for h, l, g in everyone]
@@ -409,10 +411,10 @@
             swapped = [lax.ppermute(low, axes, to_member(by)) for by in range(1, members)]
 
         dense, fock, ranges, token = first_spread(groups, own, virt_fock, irrep_sizes, pair_irreps)
-        top = owned(lax.ppermute(top, axes, to_group), top, members, token)
+        top = owned(lax.ppermute(top, axes, to_group(early_copies)), top, members, token)
         if early:
             lows = jnp.concatenate([after(piece, top) for piece in [low] + swapped])
-            late = lax.ppermute(lows, axes, to_group)
+            late = lax.ppermute(lows, axes, to_group(late_copies))
         tops = [top] + [lax.ppermute(top, axes, to_member(by)) for by in range(1, members)]
         dense = spread(1, beside, ranges, dense)
         near = 2 * dense.shape[1] // groups

time: 45.3 us -> 45.5 us (level)
  starting transfers between devices: 10.3 us -> 10.8 us
    ppermute x1, starting transfers between devices: 0.01 us -> 0.5 us  [local(): both = lax.ppermute(across, axes, to_slot(1))]
where the time goes in v17:
time: 45.5 us; the launch traced here: 45.3 us
  Pallas kernels  21.3 us (47%)
  waiting for transfers between devices  12.5 us (27%)
  starting transfers between devices  10.8 us (24%)
  between operations  0.77 us (2%)
    pallas_call x4, Pallas kernels, dress(): pl.pallas_call(functools.partial(dress_kernel, job), out_shape=out_shape...  11.1 us
    ppermute x1, waiting for transfers between devices, local(): lax.ppermute(top, axes, to_group(early_copies))  6.37 us
    pallas_call x1, Pallas kernels, first_spread(): pl.pallas_call(functools.partial(first_spread_kernel, groups), out_shape=...  4 us
    ppermute x1, starting transfers between devices, local(): beside = lax.ppermute(own_again, axes, to_slot(1))  2.98 us
    pallas_call x3, Pallas kernels, spread(): pl.pallas_call(functools.partial(spread_kernel, slot), out_shape=pltpu.VM...  2.85 us
    ppermute x1, waiting for transfers between devices, local(): lax.ppermute(top, axes, to_member(by))  2.52 us
    pallas_call x1, Pallas kernels, fold_panel(): pl.pallas_call(functools.partial(fold_kernel, chunk, late), out_shape=out...  2.07 us
    ppermute x1, waiting for transfers between devices, local(): across = lax.ppermute(own, axes, to_slot(2))  1.71 us
  transfers between devices with their start and end apart: 7, of which 5 were waited for; matrix products, arithmetic and copies ran while one was open for 0% of the time, Pallas kernels for 36%

profile of v17, /device:TPU:4, one launch (start us, length us, event | category | flops | bytes accessed | tf_op | source)
XLA Modules:
  0.0 45.3 jit_solution(7149194392898804123)
XLA Ops:
  0.0 1.2 %cut_rows.1.kept = bf16[160,1920]{1,0:T(8,128)(2,1)S(1)} custom-call(bf16[240,1920]{1,0:T(8,128)(2,1)} %whole.1), custom_call_target="tpu_custom_call" | custom-call | tf_op jit(solution)/shard_map/cut_rows/pallas_call | solution.py:58
  1.2 1.3 %collective-permute-start = (bf16[160,1920]{1,0:T(8,128)(2,1)S(1)}, bf16[160,1920]{1,0:T(8,128)(2,1)S(1)}, u32[]{:S(2)}, u32[]{:S(2)}) collective-permute-start(bf16[160,1920]{1,0:T(8,128)(2,1)S(1)} %cut_rows.1.kept), channel_id=1, source_target_pairs={{8,1},{16,2},{26,3},{12,5},{20,6},{30,7},{0,8},{18,10},{24,11},{4,... | collective-permute-start | bytes 1843208 | tf_op jit(solution)/shard_map/ppermute | solution.py:414
  3.1 2.1 %fold_panel.1 = (bf16[480,512]{1,0:T(8,128)(2,1)S(1)}, bf16[480,512]{1,0:T(8,128)(2,1)S(1)}, bf16[80,1920]{1,0:T(8,128)(2,1)S(1)}) custom-call(s32[1]{0:T(128)S(6)} %copy.26.pair, s32[8]{0:T(128)} %sizes.1, bf16[480,1920]{1,0:T(8,128)(2,1)} %bitcast.4, bf16[240,1920]{1,0:T(8,128)(2,1)} %whole.1), custom_call_target="tpu_custom_call" | custom-call | tf_op jit(solution)/shard_map/fold_panel/pallas_call | solution.py:130
  5.2 1.6 %collective-permute-start.1 = (bf16[80,1920]{1,0:T(8,128)(2,1)S(1)}, bf16[80,1920]{1,0:T(8,128)(2,1)S(1)}, u32[]{:S(2)}, u32[]{:S(2)}) collective-permute-start(bf16[80,1920]{1,0:T(8,128)(2,1)S(1)} %get-tuple-element.16.refs_0_), channel_id=1, source_target_pairs={{4,0},{5,1},{6,2},{7,3},{0,4},{1,5},{2,6},{3,7},{12,8},{13,9},{14,... | collective-permute-start | bytes 921608 | tf_op jit(solution)/shard_map/ppermute | solution.py:411
  6.8 3.0 %collective-permute-start.5 = (bf16[480,512]{1,0:T(8,128)(2,1)S(1)}, bf16[480,512]{1,0:T(8,128)(2,1)S(1)}, u32[]{:S(2)}, u32[]{:S(2)}) collective-permute-start(bf16[480,512]{1,0:T(8,128)(2,1)S(1)} %get-tuple-element.19), channel_id=1, source_target_pairs={{1,0},{0,1},{3,2},{2,3},{5,4},{4,5},{7,6},{6,7},{9,8},{8,9},{11,10... | collective-permute-start | bytes 1474568 | tf_op jit(solution)/shard_map/ppermute | solution.py:408
  9.8 1.6 %collective-permute-start.4 = (bf16[480,512]{1,0:T(8,128)(2,1)S(1)}, bf16[480,512]{1,0:T(8,128)(2,1)S(1)}, u32[]{:S(2)}, u32[]{:S(2)}) collective-permute-start(bf16[480,512]{1,0:T(8,128)(2,1)S(1)} %get-tuple-element.17.folded), channel_id=1, source_target_pairs={{2,0},{3,1},{0,2},{1,3},{6,4},{7,5},{4,6},{5,7},{10,8},{11,9},{8,1... | collective-permute-start | bytes 1474568 | tf_op jit(solution)/shard_map/ppermute | solution.py:407
  11.3 4.0 %first_spread.1 = (bf16[1920,2048]{1,0:T(8,128)(2,1)S(1)}, bf16[2048,1920]{1,0:T(8,128)(2,1)S(1)}, s32[2,8,2048]{2,1,0:T(8,128)S(1)}, s32[8,128]{1,0:T(8,128)S(1)}) custom-call(s32[8]{0:T(128)} %sizes.1, s32[1]{0:T(128)S(6)} %copy.26.pair, bf16[480,512]{1,0:T(8,128)(2,1)S(1)} %get-tuple-element.17.folded, bf16[1920,1920]{1,0:T(8,128)(2,1)} %fock.1), custom_call_target="tpu_custom_call" | custom-call | tf_op jit(solution)/shard_map/first_spread/pallas_call | solution.py:201
  15.3 6.4 %collective-permute-done.received = bf16[160,1920]{1,0:T(8,128)(2,1)S(1)} collective-permute-done((bf16[160,1920]{1,0:T(8,128)(2,1)S(1)}, bf16[160,1920]{1,0:T(8,128)(2,1)S(1)}, u32[]{:S(2)}, u32[]{:S(2)}) %collective-permute-start) | collective-permute-done | bytes 614432 | tf_op jit(solution)/shard_map/ppermute | solution.py:414
  21.7 1.6 %collective-permute-start.3 = (bf16[160,1920]{1,0:T(8,128)(2,1)S(1)}, bf16[160,1920]{1,0:T(8,128)(2,1)S(1)}, u32[]{:S(2)}, u32[]{:S(2)}) collective-permute-start(bf16[160,1920]{1,0:T(8,128)(2,1)S(1)} %owned_rows.2.refs_1_.amplitudes), channel_id=1, source_target_pairs={{4,0},{5,1},{6,2},{7,3},{0,4},{1,5},{2,6},{3,7},{12,8},{13,9},{14,... | collective-permute-start | bytes 1843208 | tf_op jit(solution)/shard_map/ppermute | solution.py:418
  23.3 0.0 collective-permute-done.1.refs_0_
  23.3 1.3 %collective-permute-start.2 = (bf16[160,1920]{1,0:T(8,128)(2,1)S(1)}, bf16[160,1920]{1,0:T(8,128)(2,1)S(1)}, u32[]{:S(2)}, u32[]{:S(2)}) collective-permute-start(bf16[160,1920]{1,0:T(8,128)(2,1)S(1)} %pad_maximum_fusion.kept), channel_id=1, source_target_pairs={{8,1},{18,2},{24,3},{12,5},{22,6},{28,7},{0,8},{16,10},{26,11},{4,... | collective-permute-start | bytes 1843208 | tf_op jit(solution)/shard_map/ppermute | solution.py:417
  24.6 0.0 collective-permute-done.5.folded
  24.7 1.0 %spread_panel.3.dense.before = bf16[1920,2048]{1,0:T(8,128)(2,1)S(1)} custom-call(bf16[480,512]{1,0:T(8,128)(2,1)S(1)} %collective-permute-done.5.folded, s32[2,8,2048]{2,1,0:T(8,128)S(1)} %get-tuple-element.20.ranges, bf16[1920,2048]{1,0:T(8,128)(2,1)S(1)} %get-tuple-element.21.before), custom_call_target="tpu_custom_call", output_to_operand_aliasing={{}: (2, {})} | custom-call | tf_op jit(solution)/shard_map/spread_panel/pallas_call | solution.py:231
  25.6 1.6 %dress_rows.4 = (f32[160,1920]{1,0:T(8,128)S(1)}, s32[8,128]{1,0:T(8,128)S(1)}) custom-call(bf16[160,1920]{1,0:T(8,128)(2,1)S(1)} %owned_rows.2.refs_1_.amplitudes, bf16[1920,2048]{1,0:T(8,128)(2,1)S(1)} %spread_panel.3.dense.before, bf16[2048,1920]{1,0:T(8,128)(2,1)S(1)} %get-tuple-element.22.fock), custom_call_target="tpu_custom_call" | custom-call | tf_op jit(solution)/shard_map/dress_rows/pallas_call | solution.py:355
  27.2 1.7 %collective-permute-done.4.refs_0_ = bf16[480,512]{1,0:T(8,128)(2,1)S(1)} collective-permute-done((bf16[480,512]{1,0:T(8,128)(2,1)S(1)}, bf16[480,512]{1,0:T(8,128)(2,1)S(1)}, u32[]{:S(2)}, u32[]{:S(2)}) %collective-permute-start.4) | collective-permute-done | bytes 491552 | tf_op jit(solution)/shard_map/ppermute | solution.py:407
  28.9 0.5 %collective-permute-start.6 = (bf16[480,512]{1,0:T(8,128)(2,1)S(1)}, bf16[480,512]{1,0:T(8,128)(2,1)S(1)}, u32[]{:S(2)}, u32[]{:S(2)}) collective-permute-start(bf16[480,512]{1,0:T(8,128)(2,1)S(1)} %after.5.folded), channel_id=1, source_target_pairs={{1,0},{0,1},{3,2},{2,3},{5,4},{4,5},{7,6},{6,7},{9,8},{8,9},{11,10... | collective-permute-start | bytes 1474568 | tf_op jit(solution)/shard_map/ppermute | solution.py:424
  29.4 0.9 %spread_panel.4.before = bf16[1920,2048]{1,0:T(8,128)(2,1)S(1)} custom-call(bf16[480,512]{1,0:T(8,128)(2,1)S(1)} %after.5.folded, s32[2,8,2048]{2,1,0:T(8,128)S(1)} %get-tuple-element.20.ranges, bf16[1920,2048]{1,0:T(8,128)(2,1)S(1)} %spread_panel.3.dense.before), custom_call_target="tpu_custom_call", output_to_operand_aliasing={{}: (2, {})} | custom-call | tf_op jit(solution)/shard_map/spread_panel/pallas_call | solution.py:231
  30.4 0.5 %collective-permute-done.6.folded = bf16[480,512]{1,0:T(8,128)(2,1)S(1)} collective-permute-done((bf16[480,512]{1,0:T(8,128)(2,1)S(1)}, bf16[480,512]{1,0:T(8,128)(2,1)S(1)}, u32[]{:S(2)}, u32[]{:S(2)}) %collective-permute-start.6) | collective-permute-done | bytes 491552 | tf_op jit(solution)/shard_map/ppermute | solution.py:424
  30.9 0.9 %spread_panel.5.dense = bf16[1920,2048]{1,0:T(8,128)(2,1)S(1)} custom-call(bf16[480,512]{1,0:T(8,128)(2,1)S(1)} %collective-permute-done.6.folded, s32[2,8,2048]{2,1,0:T(8,128)S(1)} %get-tuple-element.20.ranges, bf16[1920,2048]{1,0:T(8,128)(2,1)S(1)} %spread_panel.4.before), custom_call_target="tpu_custom_call", output_to_operand_aliasing={{}: (2, {})} | custom-call | tf_op jit(solution)/shard_map/spread_panel/pallas_call | solution.py:231
  31.9 2.3 %dress_rows.5.refs_0_ = bf16[480,1920]{1,0:T(8,128)(2,1)} custom-call(bf16[160,1920]{1,0:T(8,128)(2,1)S(1)} %owned_rows.2.refs_1_.amplitudes, bf16[1920,2048]{1,0:T(8,128)(2,1)S(1)} %spread_panel.5.dense, bf16[2048,1920]{1,0:T(8,128)(2,1)S(1)} %get-tuple-element.22.fock, f32[160,1920]{1,0:T(8,128)S(1)} %get-tuple-element.24.refs_0_), custom_call_target="tpu_custom_call" | custom-call | tf_op jit(solution)/shard_map/dress_rows/pallas_call | solution.py:355
  34.1 2.5 %collective-permute-done.3.amplitudes = bf16[160,1920]{1,0:T(8,128)(2,1)S(1)} collective-permute-done((bf16[160,1920]{1,0:T(8,128)(2,1)S(1)}, bf16[160,1920]{1,0:T(8,128)(2,1)S(1)}, u32[]{:S(2)}, u32[]{:S(2)}) %collective-permute-start.3) | collective-permute-done | bytes 614432 | tf_op jit(solution)/shard_map/ppermute | solution.py:418
  36.7 3.6 %dress_rows.6 = (bf16[480,1920]{1,0:T(8,128)(2,1)}, s32[8,128]{1,0:T(8,128)S(1)}) custom-call(bf16[160,1920]{1,0:T(8,128)(2,1)S(1)} %collective-permute-done.3.amplitudes, bf16[1920,2048]{1,0:T(8,128)(2,1)S(1)} %spread_panel.5.dense, bf16[2048,1920]{1,0:T(8,128)(2,1)S(1)} %get-tuple-element.22.fock, ...), custom_call_target="tpu_custom_call", output_to_operand_aliasing={{0}: (3, {})} | custom-call | tf_op jit(solution)/shard_map/dress_rows/pallas_call | solution.py:355
  40.3 1.3 %collective-permute-done.2.received = bf16[160,1920]{1,0:T(8,128)(2,1)S(1)} collective-permute-done((bf16[160,1920]{1,0:T(8,128)(2,1)S(1)}, bf16[160,1920]{1,0:T(8,128)(2,1)S(1)}, u32[]{:S(2)}, u32[]{:S(2)}) %collective-permute-start.2) | collective-permute-done | bytes 614432 | tf_op jit(solution)/shard_map/ppermute | solution.py:417
  41.6 3.7 %dress_rows.7 = bf16[480,1920]{1,0:T(8,128)(2,1)} custom-call(bf16[160,1920]{1,0:T(8,128)(2,1)S(1)} %owned_rows.3.amplitudes, bf16[1920,2048]{1,0:T(8,128)(2,1)S(1)} %spread_panel.5.dense, bf16[2048,1920]{1,0:T(8,128)(2,1)S(1)} %get-tuple-element.22.fock, bf16[480,1920]{1,0:T(8,128)(2,1)} %get-tuple-element.26.refs_0_), custom_call_target="tpu_custom_call", output_to_operand_aliasing={{}: (3, {})} | custom-call | tf_op jit(solution)/shard_map/dress_rows/pallas_call | solution.py:355
  (6 shorter events, 0.1 us)
Async XLA Ops:
  1.2 20.5 %collective-permute-start = (bf16[160,1920]{1,0:T(8,128)(2,1)S(1)}, bf16[160,1920]{1,0:T(8,128)(2,1)S(1)}, u32[]{:S(2)}, u32[]{:S(2)}) collective-permute-start(bf16[160,1920]{1,0:T(8,128)(2,1)S(1)} %cut_rows.1.kept), channel_id=1, source_target_pairs={{8,1},{16,2},{26,3},{12,5},{20,6},{30,7},{0,8},{18,10},{24,11},{4,... | collective-permute-start | bytes 1843208 | tf_op jit(solution)/shard_map/ppermute | solution.py:414
  5.2 18.1 %collective-permute-start.1 = (bf16[80,1920]{1,0:T(8,128)(2,1)S(1)}, bf16[80,1920]{1,0:T(8,128)(2,1)S(1)}, u32[]{:S(2)}, u32[]{:S(2)}) collective-permute-start(bf16[80,1920]{1,0:T(8,128)(2,1)S(1)} %get-tuple-element.16.refs_0_), channel_id=1, source_target_pairs={{4,0},{5,1},{6,2},{7,3},{0,4},{1,5},{2,6},{3,7},{12,8},{13,9},{14,... | collective-permute-start | bytes 921608 | tf_op jit(solution)/shard_map/ppermute | solution.py:411
  6.8 17.9 %collective-permute-start.5 = (bf16[480,512]{1,0:T(8,128)(2,1)S(1)}, bf16[480,512]{1,0:T(8,128)(2,1)S(1)}, u32[]{:S(2)}, u32[]{:S(2)}) collective-permute-start(bf16[480,512]{1,0:T(8,128)(2,1)S(1)} %get-tuple-element.19), channel_id=1, source_target_pairs={{1,0},{0,1},{3,2},{2,3},{5,4},{4,5},{7,6},{6,7},{9,8},{8,9},{11,10... | collective-permute-start | bytes 1474568 | tf_op jit(solution)/shard_map/ppermute | solution.py:408
  9.8 19.2 %collective-permute-start.4 = (bf16[480,512]{1,0:T(8,128)(2,1)S(1)}, bf16[480,512]{1,0:T(8,128)(2,1)S(1)}, u32[]{:S(2)}, u32[]{:S(2)}) collective-permute-start(bf16[480,512]{1,0:T(8,128)(2,1)S(1)} %get-tuple-element.17.folded), channel_id=1, source_target_pairs={{2,0},{3,1},{0,2},{1,3},{6,4},{7,5},{4,6},{5,7},{10,8},{11,9},{8,1... | collective-permute-start | bytes 1474568 | tf_op jit(solution)/shard_map/ppermute | solution.py:407
  21.7 14.9 %collective-permute-start.3 = (bf16[160,1920]{1,0:T(8,128)(2,1)S(1)}, bf16[160,1920]{1,0:T(8,128)(2,1)S(1)}, u32[]{:S(2)}, u32[]{:S(2)}) collective-permute-start(bf16[160,1920]{1,0:T(8,128)(2,1)S(1)} %owned_rows.2.refs_1_.amplitudes), channel_id=1, source_target_pairs={{4,0},{5,1},{6,2},{7,3},{0,4},{1,5},{2,6},{3,7},{12,8},{13,9},{14,... | collective-permute-start | bytes 1843208 | tf_op jit(solution)/shard_map/ppermute | solution.py:418
  23.3 18.3 %collective-permute-start.2 = (bf16[160,1920]{1,0:T(8,128)(2,1)S(1)}, bf16[160,1920]{1,0:T(8,128)(2,1)S(1)}, u32[]{:S(2)}, u32[]{:S(2)}) collective-permute-start(bf16[160,1920]{1,0:T(8,128)(2,1)S(1)} %pad_maximum_fusion.kept), channel_id=1, source_target_pairs={{8,1},{18,2},{24,3},{12,5},{22,6},{28,7},{0,8},{16,10},{26,11},{4,... | collective-permute-start | bytes 1843208 | tf_op jit(solution)/shard_map/ppermute | solution.py:417
  28.9 2.0 %collective-permute-start.6 = (bf16[480,512]{1,0:T(8,128)(2,1)S(1)}, bf16[480,512]{1,0:T(8,128)(2,1)S(1)}, u32[]{:S(2)}, u32[]{:S(2)}) collective-permute-start(bf16[480,512]{1,0:T(8,128)(2,1)S(1)} %after.5.folded), channel_id=1, source_target_pairs={{1,0},{0,1},{3,2},{2,3},{5,4},{4,5},{7,6},{6,7},{9,8},{8,9},{11,10... | collective-permute-start | bytes 1474568 | tf_op jit(solution)/shard_map/ppermute | solution.py:424

commit v18 on v14

--- a/solution.py
+++ b/solution.py
@@ -67,11 +67,10 @@
     )(whole)
 
 
-def fold_kernel(chunk, late, pair, sizes_in, source, *refs):
-    if late:
-        amplitudes, folded, again, low, panel, sizes, bounds, sems, low_sems = refs
-    else:
-        folded, again, panel, sizes, bounds, sems = refs
+def fold_kernel(chunk, starts, pair, sizes_in, source, *refs):
+    if starts:
+        amplitudes, refs, piece_sems = refs[0], refs[1:-1], refs[-1]
+    folded, again, *pieces, panel, sizes, bounds, sems = refs
     quarter, virtuals = panel.shape
     fold = folded.shape[1]
     small = pltpu.make_async_copy(sizes_in, sizes, sems.at[quarter // chunk])
@@ -81,7 +80,9 @@
         rows = pl.ds(k * chunk, chunk)
         copies.append(pltpu.make_async_copy(source.at[rows], panel.at[rows], sems.at[k]))
         copies[-1].start()
-    lows = copies_of(amplitudes, late, low, low_sems) if late else []
+    piece_copies = []
+    for k, (first, piece) in enumerate(zip(starts, pieces)):
+        piece_copies += copies_of(amplitudes, first, piece, piece_sems.at[pl.ds(2 * k, 2)])
     small.wait()
     fill_bounds(sizes, bounds)
     start = lax.axis_index("grp") * quarter
@@ -106,11 +107,11 @@
                 folded[here, place:place + LANES] = total
                 again[here, place:place + LANES] = total
 
-    for copy in lows:
-        copy.wait()
-
-
-def fold_panel(panel, sizes, pair, fold, amplitudes, late):
+    for copy in piece_copies:
+        copy.wait()
+
+
+def fold_panel(panel, sizes, pair, fold, amplitudes, starts):
     quarter, virtuals = panel.shape
     chunk = quarter // 5 if quarter % (5 * SUBLANES) == 0 else quarter
     vmem = pl.BlockSpec(memory_space=pltpu.VMEM)
@@ -123,12 +124,13 @@
         pltpu.SemaphoreType.DMA((quarter // chunk + 1,)),
     ]
     extra = []
-    if late:
-        out_shape.append(pltpu.VMEM((amplitudes.shape[0] - late, virtuals), amplitudes.dtype))
-        scratch.append(pltpu.SemaphoreType.DMA((2,)))
+    if starts:
+        for first, end in zip(starts, (*starts[1:], amplitudes.shape[0])):
+            out_shape.append(pltpu.VMEM((end - first, virtuals), amplitudes.dtype))
+        scratch.append(pltpu.SemaphoreType.DMA((2 * len(starts),)))
         extra.append(amplitudes)
     return pl.pallas_call(
-        functools.partial(fold_kernel, chunk, late),
+        functools.partial(fold_kernel, chunk, starts),
         out_shape=out_shape,
         in_specs=[pl.BlockSpec(memory_space=pltpu.SMEM)] + [anywhere] * (2 + len(extra)),
         out_specs=[vmem] * len(out_shape),
@@ -139,16 +141,16 @@
     )(pair, sizes, pltpu.with_memory_space_constraint(panel, pltpu.HBM), *extra)
 
 
-def place_panel(slot, folded, ranges, dense, turned):
-    quarter, fold = folded.shape
+def place_panel(slot, parts, ranges, dense, turned):
+    quarter, fold = sum(part.shape[0] for part in parts), parts[0].shape[1]
     virtuals = dense.shape[0]
     width = turned.shape[1]
     columns = slice(slot * width, (slot + 1) * width)
     step = 32
-    values = folded[...].astype(jnp.float32)
+    values = [part[...].astype(jnp.float32) for part in parts]
     if width > quarter:
-        values = jnp.concatenate([values, jnp.zeros((width - quarter, fold), jnp.float32)])
-    turned[...] = values.T
+        values.append(jnp.zeros((width - quarter, fold), jnp.float32))
+    turned[...] = jnp.concatenate(values).T
     low = jnp.concatenate([ranges[0, :, columns]] * (step // 8))
     high = jnp.concatenate([ranges[1, :, columns]] * (step // 8))
 
@@ -187,7 +189,7 @@
         low, high = wanted_range(b, pair, bounds, sizes.shape[0])
         ranges[0, :, k * width:(k + 1) * width] = low
         ranges[1, :, k * width:(k + 1) * width] = high
-    place_panel(0, folded, ranges, dense, turned)
+    place_panel(0, [folded], ranges, dense, turned)
     for copy in copies:
         copy.wait()
 
@@ -219,26 +221,27 @@
     )(sizes, pair, folded, pltpu.with_memory_space_constraint(fock, pltpu.HBM))
 
 
-def spread_kernel(slot, folded, ranges, before, dense, turned):
-    place_panel(slot, folded, ranges, dense, turned)
-
-
-def spread(slot, folded, ranges, dense):
-    fold = folded.shape[1]
-    width = rounded(folded.shape[0], LANES)
+def spread_kernel(slot, count, *refs):
+    parts, (ranges, _, dense, turned) = refs[:count], refs[count:]
+    place_panel(slot, parts, ranges, dense, turned)
+
+
+def spread(slot, parts, ranges, dense):
+    fold = parts[0].shape[1]
+    width = rounded(sum(part.shape[0] for part in parts), LANES)
     vmem = pl.BlockSpec(memory_space=pltpu.VMEM)
     pinned = [pltpu.with_memory_space_constraint(x, pltpu.VMEM) for x in (ranges, dense)]
     return pl.pallas_call(
-        functools.partial(spread_kernel, slot),
+        functools.partial(spread_kernel, slot, len(parts)),
         out_shape=pltpu.VMEM(dense.shape, dense.dtype),
-        in_specs=[vmem, vmem, pl.BlockSpec(memory_space=pl.ANY)],
+        in_specs=[vmem] * (len(parts) + 1) + [pl.BlockSpec(memory_space=pl.ANY)],
         out_specs=vmem,
-        input_output_aliases={2: 0},
+        input_output_aliases={len(parts) + 1: 0},
         scratch_shapes=[pltpu.VMEM((fold, width), jnp.float32)],
         compiler_params=pltpu.CompilerParams(vmem_limit_bytes=8 * MIB),
         cost_estimate=NOTHING,
         name="spread_panel",
-    )(folded, *pinned)
+    )(*parts, *pinned)
 
 
 def after(array, *others):
@@ -395,51 +398,60 @@
         panel = jnp.swapaxes(hole_panel[:, 0, :], 0, 1)
         irrep_sizes = pltpu.with_memory_space_constraint(irrep_sizes, pltpu.HBM)
 
-        early = rounded(rows * 2 // 3, SUBLANES) if rows % SUBLANES == 0 else 0
-        if early:
+        piece = rounded(rows * 2 // 5, SUBLANES) if rows % SUBLANES == 0 else 0
+        early = rounded(rows * 7 // 10, SUBLANES)
+        if piece:
             amplitudes = pltpu.with_memory_space_constraint(amplitudes, pltpu.HBM)
-            top = cut(amplitudes, early)
+            first = cut(amplitudes, piece)
+            starts = (piece, early)
         else:
-            top = amplitudes
-        own, own_again, *low = fold_panel(panel, irrep_sizes, pair_irreps, fold, amplitudes, early)
+            first, starts = amplitudes, ()
+        own, own_again, *pieces = fold_panel(
+            panel, irrep_sizes, pair_irreps, fold, amplitudes, starts
+        )
         across = lax.ppermute(own, axes, to_slot(2))
         beside = lax.ppermute(own_again, axes, to_slot(1))
-        if early:
-            low = low[0]
-            swapped = [lax.ppermute(low, axes, to_member(by)) for by in range(1, members)]
+        if piece:
+            second, late = pieces
+            lates = [late] + [lax.ppermute(late, axes, to_member(by)) for by in range(1, members)]
 
         dense, fock, ranges, token = first_spread(groups, own, virt_fock, irrep_sizes, pair_irreps)
-        top = owned(lax.ppermute(top, axes, to_group), top, members, token)
-        if early:
-            lows = jnp.concatenate([after(piece, top) for piece in [low] + swapped])
-            late = lax.ppermute(lows, axes, to_group)
-        tops = [top] + [lax.ppermute(top, axes, to_member(by)) for by in range(1, members)]
-        dense = spread(1, beside, ranges, dense)
+        first = owned(lax.ppermute(first, axes, to_group), first, members, token)
+        firsts = [lax.ppermute(first, axes, to_member(by)) for by in range(1, members)]
+        if piece:
+            second = owned(lax.ppermute(second, axes, to_group), second, members, first)
+            seconds = [lax.ppermute(second, axes, to_member(by)) for by in range(1, members)]
+            lates = jnp.concatenate([after(rows_of, second) for rows_of in lates])
+            sent = lax.ppermute(lates, axes, to_group)
+        dense = spread(1, [beside], ranges, dense)
         near = 2 * dense.shape[1] // groups
-        if early:
-            sums, token = dress(top, dense, fock, columns=(0, near), signed=True)
+        if piece:
+            mine = jnp.concatenate([first, second])
+            sums, token = dress(mine, dense, fock, columns=(0, near), signed=True)
             across = after(across, token)
-        both = lax.ppermute(across, axes, to_slot(1))
-        dense = spread(2, across, ranges, dense)
+        cuts = [rounded(across.shape[0] // 2, SUBLANES)] if piece else []
+        both = [lax.ppermute(part, axes, to_slot(1)) for part in jnp.split(across, cuts)]
+        dense = spread(2, [across], ranges, dense)
         dense = spread(3, both, ranges, dense)
 
-        if early:
+        if piece:
             place = dict(rows=rows, members=members, out_rows=out_rows)
-            result, = dress(
-                top, dense, fock, columns=(near, dense.shape[1]), sums=sums, spans=((0, 0, early),),
-                **place,
+            result, token = dress(
+                mine, dense, fock, columns=(near, dense.shape[1]), sums=sums,
+                spans=((0, 0, early),), signed=True, **place,
             )
             for by in range(1, members):
-                result, *token = dress(
-                    tops[by], dense, fock, spans=((by, 0, early),), base=result,
-                    signed=by == members - 1, **place,
+                other = [after(part, token) for part in (firsts[by - 1], seconds[by - 1])]
+                result, token = dress(
+                    jnp.concatenate(other), dense, fock,
+                    spans=((by, 0, early),), base=result, signed=True, **place,
                 )
-            lows = owned(late, lows, members, *token)
+            lates = owned(sent, lates, members, token)
             spans = tuple((by, early, rows - early) for by in range(members))
-            result, = dress(lows, dense, fock, spans=spans, base=result, **place)
+            result, = dress(lates, dense, fock, spans=spans, base=result, **place)
         else:
             member = lax.axis_index("blk") % members
-            ordered = jnp.roll(jnp.stack(tops), member, axis=0).reshape(out_rows, virtuals)
+            ordered = jnp.roll(jnp.stack([first, *firsts]), member, axis=0).reshape(out_rows, virtuals)
             result, = dress(ordered, dense, fock, spans=((0, 0, out_rows),), out_rows=out_rows)
         return result[:, None, :]
 

time: 45.3 us -> 47 us (1.038)
  the two profiles are of different devices: /device:TPU:4 before, /device:TPU:13 now
where the time goes in v18:
time: 47 us; the launch traced here: 46.8 us
  Pallas kernels  21.2 us (45%)
  starting transfers between devices  17.9 us (38%)
  waiting for transfers between devices  6.58 us (14%)
  between operations  0.84 us (2%)
    pallas_call x4, Pallas kernels, dress(): pl.pallas_call(functools.partial(dress_kernel, job), out_shape=out_shape...  11.1 us
    ppermute x1, starting transfers between devices, local(): sent = lax.ppermute(lates, axes, to_group)  5.72 us
    ppermute x1, starting transfers between devices, local(): first = owned(lax.ppermute(first, axes, to_group), first, members, token)  4.16 us
    ppermute x1, waiting for transfers between devices, local(): across = lax.ppermute(own, axes, to_slot(2))  4.11 us
    pallas_call x1, Pallas kernels, first_spread(): pl.pallas_call(functools.partial(first_spread_kernel, groups), out_shape=...  4 us
    pallas_call x3, Pallas kernels, spread(): pl.pallas_call(functools.partial(spread_kernel, slot, len(parts)), out_sh...  2.85 us
    ppermute x1, starting transfers between devices, local(): across = lax.ppermute(own, axes, to_slot(2))  2.69 us
    pallas_call x1, Pallas kernels, fold_panel(): pl.pallas_call(functools.partial(fold_kernel, chunk, starts), out_shape=o...  2.09 us
  transfers between devices with their start and end apart: 10, of which 4 were waited for; matrix products, arithmetic and copies ran while one was open for 0% of the time, Pallas kernels for 36%

profile of v18, /device:TPU:13, one launch (start us, length us, event | category | flops | bytes accessed | tf_op | source)
XLA Modules:
  0.0 46.8 jit_solution(5152533848663366383)
XLA Ops:
  0.0 1.1 %cut_rows.1.kept = bf16[96,1920]{1,0:T(8,128)(2,1)S(1)} custom-call(bf16[240,1920]{1,0:T(8,128)(2,1)} %whole.1), custom_call_target="tpu_custom_call" | custom-call | tf_op jit(solution)/shard_map/cut_rows/pallas_call | solution.py:58
  1.1 4.2 %collective-permute-start.1 = (bf16[96,1920]{1,0:T(8,128)(2,1)S(1)}, bf16[96,1920]{1,0:T(8,128)(2,1)S(1)}, u32[]{:S(2)}, u32[]{:S(2)}) collective-permute-start(bf16[96,1920]{1,0:T(8,128)(2,1)S(1)} %cut_rows.1.kept), channel_id=1, source_target_pairs={{8,1},{16,2},{26,3},{12,5},{20,6},{30,7},{0,8},{18,10},{24,11},{4,... | collective-permute-start | bytes 1105928 | tf_op jit(solution)/shard_map/ppermute | solution.py:419
  5.9 2.1 %fold_panel.1 = (bf16[480,512]{1,0:T(8,128)(2,1)S(1)}, bf16[480,512]{1,0:T(8,128)(2,1)S(1)}, bf16[80,1920]{1,0:T(8,128)(2,1)S(1)}, bf16[64,1920]{1,0:T(8,128)(2,1)S(1)}) custom-call(s32[1]{0:T(128)S(6)} %copy.32.pair, s32[8]{0:T(128)} %sizes.1, bf16[480,1920]{1,0:T(8,128)(2,1)} %bitcast.4, bf16[240,1920]{1,0:T(8,128)(2,1)} %whole.1), custom_call_target="tpu_custom_call" | custom-call | tf_op jit(solution)/shard_map/fold_panel/pallas_call | solution.py:132
  8.0 1.9 %collective-permute-start = (bf16[80,1920]{1,0:T(8,128)(2,1)S(1)}, bf16[80,1920]{1,0:T(8,128)(2,1)S(1)}, u32[]{:S(2)}, u32[]{:S(2)}) collective-permute-start(bf16[80,1920]{1,0:T(8,128)(2,1)S(1)} %get-tuple-element.20.kept), channel_id=1, source_target_pairs={{8,1},{16,2},{26,3},{12,5},{20,6},{30,7},{0,8},{18,10},{24,11},{4,... | collective-permute-start | bytes 921608 | tf_op jit(solution)/shard_map/ppermute | solution.py:422
  9.9 1.3 %collective-permute-start.2 = (bf16[64,1920]{1,0:T(8,128)(2,1)S(1)}, bf16[64,1920]{1,0:T(8,128)(2,1)S(1)}, u32[]{:S(2)}, u32[]{:S(2)}) collective-permute-start(bf16[64,1920]{1,0:T(8,128)(2,1)S(1)} %get-tuple-element.19.refs_0_), channel_id=1, source_target_pairs={{4,0},{5,1},{6,2},{7,3},{0,4},{1,5},{2,6},{3,7},{12,8},{13,9},{14,... | collective-permute-start | bytes 737288 | tf_op jit(solution)/shard_map/ppermute | solution.py:416
  11.2 0.0 collective-permute-start.6
  11.2 2.7 %collective-permute-start.5 = (bf16[480,512]{1,0:T(8,128)(2,1)S(1)}, bf16[480,512]{1,0:T(8,128)(2,1)S(1)}, u32[]{:S(2)}, u32[]{:S(2)}) collective-permute-start(bf16[480,512]{1,0:T(8,128)(2,1)S(1)} %get-tuple-element.21.folded), channel_id=1, source_target_pairs={{2,0},{3,1},{0,2},{1,3},{6,4},{7,5},{4,6},{5,7},{10,8},{11,9},{8,1... | collective-permute-start | bytes 1474568 | tf_op jit(solution)/shard_map/ppermute | solution.py:412
  13.9 4.0 %first_spread.1 = (bf16[1920,2048]{1,0:T(8,128)(2,1)S(1)}, bf16[2048,1920]{1,0:T(8,128)(2,1)S(1)}, s32[2,8,2048]{2,1,0:T(8,128)S(1)}, s32[8,128]{1,0:T(8,128)S(1)}) custom-call(s32[8]{0:T(128)} %sizes.1, s32[1]{0:T(128)S(6)} %copy.32.pair, bf16[480,512]{1,0:T(8,128)(2,1)S(1)} %get-tuple-element.21.folded, bf16[1920,1920]{1,0:T(8,128)(2,1)} %fock.1), custom_call_target="tpu_custom_call" | custom-call | tf_op jit(solution)/shard_map/first_spread/pallas_call | solution.py:203
  17.9 0.0 collective-permute-done.1.received
  17.9 0.3 collective-permute-start.4
  18.3 2.0 %collective-permute-done.received = bf16[80,1920]{1,0:T(8,128)(2,1)S(1)} collective-permute-done((bf16[80,1920]{1,0:T(8,128)(2,1)S(1)}, bf16[80,1920]{1,0:T(8,128)(2,1)S(1)}, u32[]{:S(2)}, u32[]{:S(2)}) %collective-permute-start) | collective-permute-done | bytes 307232 | tf_op jit(solution)/shard_map/ppermute | solution.py:422
  20.3 1.3 %collective-permute-start.9 = (bf16[80,1920]{1,0:T(8,128)(2,1)S(1)}, bf16[80,1920]{1,0:T(8,128)(2,1)S(1)}, u32[]{:S(2)}, u32[]{:S(2)}) collective-permute-start(bf16[80,1920]{1,0:T(8,128)(2,1)S(1)} %owned_rows.4.refs_1_), channel_id=1, source_target_pairs={{4,0},{5,1},{6,2},{7,3},{0,4},{1,5},{2,6},{3,7},{12,8},{13,9},{14,... | collective-permute-start | bytes 921608 | tf_op jit(solution)/shard_map/ppermute | solution.py:423
  21.5 0.0 collective-permute-done.2.refs_0_
  21.6 5.7 %collective-permute-start.3 = (bf16[128,1920]{1,0:T(8,128)(2,1)S(1)}, bf16[128,1920]{1,0:T(8,128)(2,1)S(1)}, u32[]{:S(2)}, u32[]{:S(2)}) collective-permute-start(bf16[128,1920]{1,0:T(8,128)(2,1)S(1)} %pad_maximum_fusion.2.kept), channel_id=1, source_target_pairs={{8,1},{16,2},{26,3},{12,5},{20,6},{30,7},{0,8},{18,10},{24,11},{4,... | collective-permute-start | bytes 1474568 | tf_op jit(solution)/shard_map/ppermute | solution.py:425
  27.3 0.1 pad_maximum_fusion.amplitudes
  27.4 0.0 collective-permute-done.6.refs_0_
  27.4 1.0 %spread_panel.3.dense.refs_2_ = bf16[1920,2048]{1,0:T(8,128)(2,1)S(1)} custom-call(bf16[480,512]{1,0:T(8,128)(2,1)S(1)} %collective-permute-done.6.refs_0_, s32[2,8,2048]{2,1,0:T(8,128)S(1)} %get-tuple-element.24.refs_1_.refs_2_, bf16[1920,2048]{1,0:T(8,128)(2,1)S(1)} %get-tuple-element.25.refs_2_), custom_call_target="tpu_custom_call", output_to_operand_aliasing={{}: (2, {})} | custom-call | tf_op jit(solution)/shard_map/spread_panel/pallas_call | solution.py:234
  28.3 1.7 %dress_rows.4 = (f32[176,1920]{1,0:T(8,128)S(1)}, s32[8,128]{1,0:T(8,128)S(1)}) custom-call(bf16[176,1920]{1,0:T(8,128)(2,1)S(1)} %pad_maximum_fusion.amplitudes, bf16[1920,2048]{1,0:T(8,128)(2,1)S(1)} %spread_panel.3.dense.refs_2_, bf16[2048,1920]{1,0:T(8,128)(2,1)S(1)} %get-tuple-element.26.fock), custom_call_target="tpu_custom_call" | custom-call | tf_op jit(solution)/shard_map/dress_rows/pallas_call | solution.py:358
  30.0 4.1 %collective-permute-done.5.refs_0_ = bf16[480,512]{1,0:T(8,128)(2,1)S(1)} collective-permute-done((bf16[480,512]{1,0:T(8,128)(2,1)S(1)}, bf16[480,512]{1,0:T(8,128)(2,1)S(1)}, u32[]{:S(2)}, u32[]{:S(2)}) %collective-permute-start.5) | collective-permute-done | bytes 491552 | tf_op jit(solution)/shard_map/ppermute | solution.py:412
  34.2 0.5 %collective-permute-start.7 = (bf16[240,512]{1,0:T(8,128)(2,1)S(1)}, bf16[240,512]{1,0:T(8,128)(2,1)S(1)}, u32[]{:S(2)}, u32[]{:S(2)}) collective-permute-start(bf16[240,512]{1,0:T(8,128)(2,1)S(1)} %get-tuple-element.34), channel_id=1, source_target_pairs={{1,0},{0,1},{3,2},{2,3},{5,4},{4,5},{7,6},{6,7},{9,8},{8,9},{11,10... | collective-permute-start | bytes 737288 | tf_op jit(solution)/shard_map/ppermute | solution.py:433
  34.7 0.1 collective-permute-start.8
  34.8 0.9 %spread_panel.4.refs_3_ = bf16[1920,2048]{1,0:T(8,128)(2,1)S(1)} custom-call(bf16[480,512]{1,0:T(8,128)(2,1)S(1)} %after.7.refs_0_, s32[2,8,2048]{2,1,0:T(8,128)S(1)} %get-tuple-element.24.refs_1_.refs_2_, bf16[1920,2048]{1,0:T(8,128)(2,1)S(1)} %spread_panel.3.dense.refs_2_), custom_call_target="tpu_custom_call", output_to_operand_aliasing={{}: (2, {})} | custom-call | tf_op jit(solution)/shard_map/spread_panel/pallas_call | solution.py:234
  35.7 0.1 collective-permute-done.7.refs_0_
  35.8 0.4 collective-permute-done.8.refs_1_
  36.2 0.9 %spread_panel.5.dense = bf16[1920,2048]{1,0:T(8,128)(2,1)S(1)} custom-call(bf16[240,512]{1,0:T(8,128)(2,1)S(1)} %collective-permute-done.7.refs_0_, bf16[240,512]{1,0:T(8,128)(2,1)S(1)} %collective-permute-done.8.refs_1_, s32[2,8,2048]{2,1,0:T(8,128)S(1)} %get-tuple-element.24.refs_1_.refs_2_, ...), custom_call_target="tpu_custom_call", output_to_operand_aliasing={{}: (3, {})} | custom-call | tf_op jit(solution)/shard_map/spread_panel/pallas_call | solution.py:234
  37.1 2.4 %dress_rows.5 = (bf16[480,1920]{1,0:T(8,128)(2,1)}, s32[8,128]{1,0:T(8,128)S(1)}) custom-call(bf16[176,1920]{1,0:T(8,128)(2,1)S(1)} %pad_maximum_fusion.amplitudes, bf16[1920,2048]{1,0:T(8,128)(2,1)S(1)} %spread_panel.5.dense, bf16[2048,1920]{1,0:T(8,128)(2,1)S(1)} %get-tuple-element.26.fock, f32[176,1920]{1,0:T(8,128)S(1)} %get-tuple-element.28.refs_0_), custom_call_target="tpu_custom_call" | custom-call | tf_op jit(solution)/shard_map/dress_rows/pallas_call | solution.py:358
  39.5 0.0 collective-permute-done.4.refs_0_
  39.5 0.0 collective-permute-done.9.refs_0_
  39.5 0.1 pad_maximum_fusion.1.amplitudes
  39.6 3.9 %dress_rows.6 = (bf16[480,1920]{1,0:T(8,128)(2,1)}, s32[8,128]{1,0:T(8,128)S(1)}) custom-call(bf16[176,1920]{1,0:T(8,128)(2,1)S(1)} %pad_maximum_fusion.1.amplitudes, bf16[1920,2048]{1,0:T(8,128)(2,1)S(1)} %spread_panel.5.dense, bf16[2048,1920]{1,0:T(8,128)(2,1)S(1)} %get-tuple-element.26.fock, ...), custom_call_target="tpu_custom_call", output_to_operand_aliasing={{0}: (3, {})} | custom-call | tf_op jit(solution)/shard_map/dress_rows/pallas_call | solution.py:358
  43.5 0.0 collective-permute-done.3.received
  43.6 3.2 %dress_rows.7 = bf16[480,1920]{1,0:T(8,128)(2,1)} custom-call(bf16[128,1920]{1,0:T(8,128)(2,1)S(1)} %owned_rows.5.amplitudes, bf16[1920,2048]{1,0:T(8,128)(2,1)S(1)} %spread_panel.5.dense, bf16[2048,1920]{1,0:T(8,128)(2,1)S(1)} %get-tuple-element.26.fock, bf16[480,1920]{1,0:T(8,128)(2,1)} %get-tuple-element.32.refs_0_), custom_call_target="tpu_custom_call", output_to_operand_aliasing={{}: (3, {})} | custom-call | tf_op jit(solution)/shard_map/dress_rows/pallas_call | solution.py:358
  (10 shorter events, 0.1 us)
Async XLA Ops:
  1.1 16.8 %collective-permute-start.1 = (bf16[96,1920]{1,0:T(8,128)(2,1)S(1)}, bf16[96,1920]{1,0:T(8,128)(2,1)S(1)}, u32[]{:S(2)}, u32[]{:S(2)}) collective-permute-start(bf16[96,1920]{1,0:T(8,128)(2,1)S(1)} %cut_rows.1.kept), channel_id=1, source_target_pairs={{8,1},{16,2},{26,3},{12,5},{20,6},{30,7},{0,8},{18,10},{24,11},{4,... | collective-permute-start | bytes 1105928 | tf_op jit(solution)/shard_map/ppermute | solution.py:419
  8.0 12.3 %collective-permute-start = (bf16[80,1920]{1,0:T(8,128)(2,1)S(1)}, bf16[80,1920]{1,0:T(8,128)(2,1)S(1)}, u32[]{:S(2)}, u32[]{:S(2)}) collective-permute-start(bf16[80,1920]{1,0:T(8,128)(2,1)S(1)} %get-tuple-element.20.kept), channel_id=1, source_target_pairs={{8,1},{16,2},{26,3},{12,5},{20,6},{30,7},{0,8},{18,10},{24,11},{4,... | collective-permute-start | bytes 921608 | tf_op jit(solution)/shard_map/ppermute | solution.py:422
  9.9 11.6 %collective-permute-start.2 = (bf16[64,1920]{1,0:T(8,128)(2,1)S(1)}, bf16[64,1920]{1,0:T(8,128)(2,1)S(1)}, u32[]{:S(2)}, u32[]{:S(2)}) collective-permute-start(bf16[64,1920]{1,0:T(8,128)(2,1)S(1)} %get-tuple-element.19.refs_0_), channel_id=1, source_target_pairs={{4,0},{5,1},{6,2},{7,3},{0,4},{1,5},{2,6},{3,7},{12,8},{13,9},{14,... | collective-permute-start | bytes 737288 | tf_op jit(solution)/shard_map/ppermute | solution.py:416
  11.2 16.2 %collective-permute-start.6 = (bf16[480,512]{1,0:T(8,128)(2,1)S(1)}, bf16[480,512]{1,0:T(8,128)(2,1)S(1)}, u32[]{:S(2)}, u32[]{:S(2)}) collective-permute-start(bf16[480,512]{1,0:T(8,128)(2,1)S(1)} %get-tuple-element.23), channel_id=1, source_target_pairs={{1,0},{0,1},{3,2},{2,3},{5,4},{4,5},{7,6},{6,7},{9,8},{8,9},{11,10... | collective-permute-start | bytes 1474568 | tf_op jit(solution)/shard_map/ppermute | solution.py:413
  11.2 22.9 %collective-permute-start.5 = (bf16[480,512]{1,0:T(8,128)(2,1)S(1)}, bf16[480,512]{1,0:T(8,128)(2,1)S(1)}, u32[]{:S(2)}, u32[]{:S(2)}) collective-permute-start(bf16[480,512]{1,0:T(8,128)(2,1)S(1)} %get-tuple-element.21.folded), channel_id=1, source_target_pairs={{2,0},{3,1},{0,2},{1,3},{6,4},{7,5},{4,6},{5,7},{10,8},{11,9},{8,1... | collective-permute-start | bytes 1474568 | tf_op jit(solution)/shard_map/ppermute | solution.py:412
  17.9 21.6 %collective-permute-start.4 = (bf16[96,1920]{1,0:T(8,128)(2,1)S(1)}, bf16[96,1920]{1,0:T(8,128)(2,1)S(1)}, u32[]{:S(2)}, u32[]{:S(2)}) collective-permute-start(bf16[96,1920]{1,0:T(8,128)(2,1)S(1)} %owned_rows.3.refs_0_), channel_id=1, source_target_pairs={{4,0},{5,1},{6,2},{7,3},{0,4},{1,5},{2,6},{3,7},{12,8},{13,9},{14,... | collective-permute-start | bytes 1105928 | tf_op jit(solution)/shard_map/ppermute | solution.py:420
  20.3 19.3 %collective-permute-start.9 = (bf16[80,1920]{1,0:T(8,128)(2,1)S(1)}, bf16[80,1920]{1,0:T(8,128)(2,1)S(1)}, u32[]{:S(2)}, u32[]{:S(2)}) collective-permute-start(bf16[80,1920]{1,0:T(8,128)(2,1)S(1)} %owned_rows.4.refs_1_), channel_id=1, source_target_pairs={{4,0},{5,1},{6,2},{7,3},{0,4},{1,5},{2,6},{3,7},{12,8},{13,9},{14,... | collective-permute-start | bytes 921608 | tf_op jit(solution)/shard_map/ppermute | solution.py:423
  21.6 22.0 %collective-permute-start.3 = (bf16[128,1920]{1,0:T(8,128)(2,1)S(1)}, bf16[128,1920]{1,0:T(8,128)(2,1)S(1)}, u32[]{:S(2)}, u32[]{:S(2)}) collective-permute-start(bf16[128,1920]{1,0:T(8,128)(2,1)S(1)} %pad_maximum_fusion.2.kept), channel_id=1, source_target_pairs={{8,1},{16,2},{26,3},{12,5},{20,6},{30,7},{0,8},{18,10},{24,11},{4,... | collective-permute-start | bytes 1474568 | tf_op jit(solution)/shard_map/ppermute | solution.py:425
  34.2 1.6 %collective-permute-start.7 = (bf16[240,512]{1,0:T(8,128)(2,1)S(1)}, bf16[240,512]{1,0:T(8,128)(2,1)S(1)}, u32[]{:S(2)}, u32[]{:S(2)}) collective-permute-start(bf16[240,512]{1,0:T(8,128)(2,1)S(1)} %get-tuple-element.34), channel_id=1, source_target_pairs={{1,0},{0,1},{3,2},{2,3},{5,4},{4,5},{7,6},{6,7},{9,8},{8,9},{11,10... | collective-permute-start | bytes 737288 | tf_op jit(solution)/shard_map/ppermute | solution.py:433
  34.7 1.5 %collective-permute-start.8 = (bf16[240,512]{1,0:T(8,128)(2,1)S(1)}, bf16[240,512]{1,0:T(8,128)(2,1)S(1)}, u32[]{:S(2)}, u32[]{:S(2)}) collective-permute-start(bf16[240,512]{1,0:T(8,128)(2,1)S(1)} %get-tuple-element.33), channel_id=1, source_target_pairs={{1,0},{0,1},{3,2},{2,3},{5,4},{4,5},{7,6},{6,7},{9,8},{8,9},{11,10... | collective-permute-start | bytes 737288 | tf_op jit(solution)/shard_map/ppermute | solution.py:433

commit v19 on v18

--- a/solution.py
+++ b/solution.py
@@ -398,8 +398,8 @@
         panel = jnp.swapaxes(hole_panel[:, 0, :], 0, 1)
         irrep_sizes = pltpu.with_memory_space_constraint(irrep_sizes, pltpu.HBM)
 
-        piece = rounded(rows * 2 // 5, SUBLANES) if rows % SUBLANES == 0 else 0
-        early = rounded(rows * 7 // 10, SUBLANES)
+        piece = rounded(rows * 7 // 15, SUBLANES) if rows % SUBLANES == 0 else 0
+        early = rounded(rows * 4 // 5, SUBLANES)
         if piece:
             amplitudes = pltpu.with_memory_space_constraint(amplitudes, pltpu.HBM)
             first = cut(amplitudes, piece)
@@ -441,14 +441,16 @@
                 spans=((0, 0, early),), signed=True, **place,
             )
             for by in range(1, members):
-                other = [after(part, token) for part in (firsts[by - 1], seconds[by - 1])]
                 result, token = dress(
-                    jnp.concatenate(other), dense, fock,
-                    spans=((by, 0, early),), base=result, signed=True, **place,
+                    after(firsts[by - 1], token), dense, fock, spans=((by, 0, piece),), base=result,
+                    signed=True, **place,
                 )
-            lates = owned(sent, lates, members, token)
-            spans = tuple((by, early, rows - early) for by in range(members))
-            result, = dress(lates, dense, fock, spans=spans, base=result, **place)
+            last = [after(part, token) for part in seconds] + [owned(sent, lates, members, token)]
+            spans = [(by, piece, early - piece) for by in range(1, members)]
+            spans += [(by, early, rows - early) for by in range(members)]
+            result, = dress(
+                jnp.concatenate(last), dense, fock, spans=tuple(spans), base=result, **place
+            )
         else:
             member = lax.axis_index("blk") % members
             ordered = jnp.roll(jnp.stack([first, *firsts]), member, axis=0).reshape(out_rows, virtuals)

time: 47 us -> 46.4 us (0.987)
  the two profiles are of different devices: /device:TPU:13 before, /device:TPU:0 now
where the time goes in v19:
time: 46.4 us; the launch traced here: 46.2 us
  Pallas kernels  22 us (47%)
  starting transfers between devices  20.4 us (44%)
  waiting for transfers between devices  2.8 us (6%)
  between operations  0.84 us (2%)
    pallas_call x4, Pallas kernels, dress(): pl.pallas_call(functools.partial(dress_kernel, job), out_shape=out_shape...  11.4 us
    ppermute x1, starting transfers between devices, local(): first = owned(lax.ppermute(first, axes, to_group), first, members, token)  4.95 us
    ppermute x1, starting transfers between devices, local(): sent = lax.ppermute(lates, axes, to_group)  4.34 us
    pallas_call x1, Pallas kernels, first_spread(): pl.pallas_call(functools.partial(first_spread_kernel, groups), out_shape=...  4 us
    pallas_call x3, Pallas kernels, spread(): pl.pallas_call(functools.partial(spread_kernel, slot, len(parts)), out_sh...  2.85 us
    ppermute x1, starting transfers between devices, local(): beside = lax.ppermute(own_again, axes, to_slot(1))  2.56 us
    pallas_call x1, Pallas kernels, fold_panel(): pl.pallas_call(functools.partial(fold_kernel, chunk, starts), out_shape=o...  2.09 us
    ppermute x1, starting transfers between devices, local(): second = owned(lax.ppermute(second, axes, to_group), second, members, first)  1.91 us
  transfers between devices with their start and end apart: 10, of which 4 were waited for; matrix products, arithmetic and copies ran while one was open for 0% of the time, Pallas kernels for 36%

profile of v19, /device:TPU:0, one launch (start us, length us, event | category | flops | bytes accessed | tf_op | source)
XLA Modules:
  0.0 46.2 jit_solution(6552495370033635665)
XLA Ops:
  0.0 1.1 %cut_rows.1.kept = bf16[112,1920]{1,0:T(8,128)(2,1)S(1)} custom-call(bf16[240,1920]{1,0:T(8,128)(2,1)} %whole.1), custom_call_target="tpu_custom_call" | custom-call | tf_op jit(solution)/shard_map/cut_rows/pallas_call | solution.py:58
  1.1 5.0 %collective-permute-start.1 = (bf16[112,1920]{1,0:T(8,128)(2,1)S(1)}, bf16[112,1920]{1,0:T(8,128)(2,1)S(1)}, u32[]{:S(2)}, u32[]{:S(2)}) collective-permute-start(bf16[112,1920]{1,0:T(8,128)(2,1)S(1)} %cut_rows.1.kept), channel_id=1, source_target_pairs={{8,1},{16,2},{26,3},{12,5},{20,6},{30,7},{0,8},{18,10},{24,11},{4,... | collective-permute-start | bytes 1290248 | tf_op jit(solution)/shard_map/ppermute | solution.py:419
  6.7 2.1 %fold_panel.1 = (bf16[480,512]{1,0:T(8,128)(2,1)S(1)}, bf16[480,512]{1,0:T(8,128)(2,1)S(1)}, bf16[80,1920]{1,0:T(8,128)(2,1)S(1)}, bf16[48,1920]{1,0:T(8,128)(2,1)S(1)}) custom-call(s32[1]{0:T(128)S(6)} %copy.32.pair, s32[8]{0:T(128)} %sizes.1, bf16[480,1920]{1,0:T(8,128)(2,1)} %bitcast.4, bf16[240,1920]{1,0:T(8,128)(2,1)} %whole.1), custom_call_target="tpu_custom_call" | custom-call | tf_op jit(solution)/shard_map/fold_panel/pallas_call | solution.py:132
  8.8 1.9 %collective-permute-start = (bf16[80,1920]{1,0:T(8,128)(2,1)S(1)}, bf16[80,1920]{1,0:T(8,128)(2,1)S(1)}, u32[]{:S(2)}, u32[]{:S(2)}) collective-permute-start(bf16[80,1920]{1,0:T(8,128)(2,1)S(1)} %get-tuple-element.19.kept), channel_id=1, source_target_pairs={{8,1},{16,2},{26,3},{12,5},{20,6},{30,7},{0,8},{18,10},{24,11},{4,... | collective-permute-start | bytes 921608 | tf_op jit(solution)/shard_map/ppermute | solution.py:422
  10.7 1.6 %collective-permute-start.8 = (bf16[48,1920]{1,0:T(8,128)(2,1)S(1)}, bf16[48,1920]{1,0:T(8,128)(2,1)S(1)}, u32[]{:S(2)}, u32[]{:S(2)}) collective-permute-start(bf16[48,1920]{1,0:T(8,128)(2,1)S(1)} %get-tuple-element.31.refs_0_), channel_id=1, source_target_pairs={{4,0},{5,1},{6,2},{7,3},{0,4},{1,5},{2,6},{3,7},{12,8},{13,9},{14,... | collective-permute-start | bytes 552968 | tf_op jit(solution)/shard_map/ppermute | solution.py:416
  12.3 2.6 %collective-permute-start.5 = (bf16[480,512]{1,0:T(8,128)(2,1)S(1)}, bf16[480,512]{1,0:T(8,128)(2,1)S(1)}, u32[]{:S(2)}, u32[]{:S(2)}) collective-permute-start(bf16[480,512]{1,0:T(8,128)(2,1)S(1)} %get-tuple-element.22), channel_id=1, source_target_pairs={{1,0},{0,1},{3,2},{2,3},{5,4},{4,5},{7,6},{6,7},{9,8},{8,9},{11,10... | collective-permute-start | bytes 1474568 | tf_op jit(solution)/shard_map/ppermute | solution.py:413
  14.8 1.0 %collective-permute-start.4 = (bf16[480,512]{1,0:T(8,128)(2,1)S(1)}, bf16[480,512]{1,0:T(8,128)(2,1)S(1)}, u32[]{:S(2)}, u32[]{:S(2)}) collective-permute-start(bf16[480,512]{1,0:T(8,128)(2,1)S(1)} %get-tuple-element.20.folded), channel_id=1, source_target_pairs={{2,0},{3,1},{0,2},{1,3},{6,4},{7,5},{4,6},{5,7},{10,8},{11,9},{8,1... | collective-permute-start | bytes 1474568 | tf_op jit(solution)/shard_map/ppermute | solution.py:412
  15.8 4.0 %first_spread.1 = (bf16[1920,2048]{1,0:T(8,128)(2,1)S(1)}, bf16[2048,1920]{1,0:T(8,128)(2,1)S(1)}, s32[2,8,2048]{2,1,0:T(8,128)S(1)}, s32[8,128]{1,0:T(8,128)S(1)}) custom-call(s32[8]{0:T(128)} %sizes.1, s32[1]{0:T(128)S(6)} %copy.32.pair, bf16[480,512]{1,0:T(8,128)(2,1)S(1)} %get-tuple-element.20.folded, bf16[1920,1920]{1,0:T(8,128)(2,1)} %fock.1), custom_call_target="tpu_custom_call" | custom-call | tf_op jit(solution)/shard_map/first_spread/pallas_call | solution.py:203
  19.8 0.0 collective-permute-done.1.received
  19.9 0.3 owned_rows.3.refs_0_
  20.1 0.6 %collective-permute-start.3 = (bf16[112,1920]{1,0:T(8,128)(2,1)S(1)}, bf16[112,1920]{1,0:T(8,128)(2,1)S(1)}, u32[]{:S(2)}, u32[]{:S(2)}) collective-permute-start(bf16[112,1920]{1,0:T(8,128)(2,1)S(1)} %owned_rows.3.refs_0_), channel_id=1, source_target_pairs={{4,0},{5,1},{6,2},{7,3},{0,4},{1,5},{2,6},{3,7},{12,8},{13,9},{14,... | collective-permute-start | bytes 1290248 | tf_op jit(solution)/shard_map/ppermute | solution.py:420
  20.7 0.6 %collective-permute-done.received = bf16[80,1920]{1,0:T(8,128)(2,1)S(1)} collective-permute-done((bf16[80,1920]{1,0:T(8,128)(2,1)S(1)}, bf16[80,1920]{1,0:T(8,128)(2,1)S(1)}, u32[]{:S(2)}, u32[]{:S(2)}) %collective-permute-start) | collective-permute-done | bytes 307232 | tf_op jit(solution)/shard_map/ppermute | solution.py:422
  21.4 0.1 owned_rows.4.refs_1_
  21.4 1.6 %collective-permute-start.2 = (bf16[80,1920]{1,0:T(8,128)(2,1)S(1)}, bf16[80,1920]{1,0:T(8,128)(2,1)S(1)}, u32[]{:S(2)}, u32[]{:S(2)}) collective-permute-start(bf16[80,1920]{1,0:T(8,128)(2,1)S(1)} %owned_rows.4.refs_1_), channel_id=1, source_target_pairs={{4,0},{5,1},{6,2},{7,3},{0,4},{1,5},{2,6},{3,7},{12,8},{13,9},{14,... | collective-permute-start | bytes 921608 | tf_op jit(solution)/shard_map/ppermute | solution.py:423
  23.0 0.0 collective-permute-done.8.refs_0_
  23.0 4.3 %collective-permute-start.9 = (bf16[96,1920]{1,0:T(8,128)(2,1)S(1)}, bf16[96,1920]{1,0:T(8,128)(2,1)S(1)}, u32[]{:S(2)}, u32[]{:S(2)}) collective-permute-start(bf16[96,1920]{1,0:T(8,128)(2,1)S(1)} %pad_maximum_fusion.2.kept), channel_id=1, source_target_pairs={{8,1},{16,2},{26,3},{12,5},{20,6},{30,7},{0,8},{18,10},{24,11},{4,... | collective-permute-start | bytes 1105928 | tf_op jit(solution)/shard_map/ppermute | solution.py:425
  27.4 0.1 pad_maximum_fusion.amplitudes
  27.5 1.0 %spread_panel.3.dense.refs_2_ = bf16[1920,2048]{1,0:T(8,128)(2,1)S(1)} custom-call(bf16[480,512]{1,0:T(8,128)(2,1)S(1)} %collective-permute-done.5.refs_0_, s32[2,8,2048]{2,1,0:T(8,128)S(1)} %get-tuple-element.23.refs_1_.refs_2_, bf16[1920,2048]{1,0:T(8,128)(2,1)S(1)} %get-tuple-element.24.refs_2_), custom_call_target="tpu_custom_call", output_to_operand_aliasing={{}: (2, {})} | custom-call | tf_op jit(solution)/shard_map/spread_panel/pallas_call | solution.py:234
  28.4 1.8 %dress_rows.4 = (f32[192,1920]{1,0:T(8,128)S(1)}, s32[8,128]{1,0:T(8,128)S(1)}) custom-call(bf16[192,1920]{1,0:T(8,128)(2,1)S(1)} %pad_maximum_fusion.amplitudes, bf16[1920,2048]{1,0:T(8,128)(2,1)S(1)} %spread_panel.3.dense.refs_2_, bf16[2048,1920]{1,0:T(8,128)(2,1)S(1)} %get-tuple-element.25.fock), custom_call_target="tpu_custom_call" | custom-call | tf_op jit(solution)/shard_map/dress_rows/pallas_call | solution.py:358
  30.3 1.7 %collective-permute-done.4.refs_0_ = bf16[480,512]{1,0:T(8,128)(2,1)S(1)} collective-permute-done((bf16[480,512]{1,0:T(8,128)(2,1)S(1)}, bf16[480,512]{1,0:T(8,128)(2,1)S(1)}, u32[]{:S(2)}, u32[]{:S(2)}) %collective-permute-start.4) | collective-permute-done | bytes 491552 | tf_op jit(solution)/shard_map/ppermute | solution.py:412
  32.0 1.8 %collective-permute-start.6 = (bf16[240,512]{1,0:T(8,128)(2,1)S(1)}, bf16[240,512]{1,0:T(8,128)(2,1)S(1)}, u32[]{:S(2)}, u32[]{:S(2)}) collective-permute-start(bf16[240,512]{1,0:T(8,128)(2,1)S(1)} %get-tuple-element.34), channel_id=1, source_target_pairs={{1,0},{0,1},{3,2},{2,3},{5,4},{4,5},{7,6},{6,7},{9,8},{8,9},{11,10... | collective-permute-start | bytes 737288 | tf_op jit(solution)/shard_map/ppermute | solution.py:433
  33.8 0.1 collective-permute-start.7
  33.9 0.9 %spread_panel.4.refs_3_ = bf16[1920,2048]{1,0:T(8,128)(2,1)S(1)} custom-call(bf16[480,512]{1,0:T(8,128)(2,1)S(1)} %after.5.refs_0_, s32[2,8,2048]{2,1,0:T(8,128)S(1)} %get-tuple-element.23.refs_1_.refs_2_, bf16[1920,2048]{1,0:T(8,128)(2,1)S(1)} %spread_panel.3.dense.refs_2_), custom_call_target="tpu_custom_call", output_to_operand_aliasing={{}: (2, {})} | custom-call | tf_op jit(solution)/shard_map/spread_panel/pallas_call | solution.py:234
  34.9 0.1 collective-permute-done.6.refs_0_
  35.0 0.4 collective-permute-done.7.refs_1_
  35.3 0.9 %spread_panel.5.dense = bf16[1920,2048]{1,0:T(8,128)(2,1)S(1)} custom-call(bf16[240,512]{1,0:T(8,128)(2,1)S(1)} %collective-permute-done.6.refs_0_, bf16[240,512]{1,0:T(8,128)(2,1)S(1)} %collective-permute-done.7.refs_1_, s32[2,8,2048]{2,1,0:T(8,128)S(1)} %get-tuple-element.23.refs_1_.refs_2_, ...), custom_call_target="tpu_custom_call", output_to_operand_aliasing={{}: (3, {})} | custom-call | tf_op jit(solution)/shard_map/spread_panel/pallas_call | solution.py:234
  36.3 2.5 %dress_rows.5 = (bf16[480,1920]{1,0:T(8,128)(2,1)}, s32[8,128]{1,0:T(8,128)S(1)}) custom-call(bf16[192,1920]{1,0:T(8,128)(2,1)S(1)} %pad_maximum_fusion.amplitudes, bf16[1920,2048]{1,0:T(8,128)(2,1)S(1)} %spread_panel.5.dense, bf16[2048,1920]{1,0:T(8,128)(2,1)S(1)} %get-tuple-element.25.fock, f32[192,1920]{1,0:T(8,128)S(1)} %get-tuple-element.27.refs_0_), custom_call_target="tpu_custom_call" | custom-call | tf_op jit(solution)/shard_map/dress_rows/pallas_call | solution.py:358
  38.9 3.0 %dress_rows.6 = (bf16[480,1920]{1,0:T(8,128)(2,1)}, s32[8,128]{1,0:T(8,128)S(1)}) custom-call(bf16[112,1920]{1,0:T(8,128)(2,1)S(1)} %after.6.amplitudes, bf16[1920,2048]{1,0:T(8,128)(2,1)S(1)} %spread_panel.5.dense, bf16[2048,1920]{1,0:T(8,128)(2,1)S(1)} %get-tuple-element.25.fock, ...), custom_call_target="tpu_custom_call", output_to_operand_aliasing={{0}: (3, {})} | custom-call | tf_op jit(solution)/shard_map/dress_rows/pallas_call | solution.py:358
  41.9 0.0 collective-permute-done.9.received
  41.9 0.2 owned_rows.5
  42.1 0.1 pad_maximum_fusion.1.amplitudes
  42.2 4.0 %dress_rows.7 = bf16[480,1920]{1,0:T(8,128)(2,1)} custom-call(bf16[176,1920]{1,0:T(8,128)(2,1)S(1)} %pad_maximum_fusion.1.amplitudes, bf16[1920,2048]{1,0:T(8,128)(2,1)S(1)} %spread_panel.5.dense, bf16[2048,1920]{1,0:T(8,128)(2,1)S(1)} %get-tuple-element.25.fock, bf16[480,1920]{1,0:T(8,128)(2,1)} %get-tuple-element.32.refs_0_), custom_call_target="tpu_custom_call", output_to_operand_aliasing={{}: (3, {})} | custom-call | tf_op jit(solution)/shard_map/dress_rows/pallas_call | solution.py:358
  (10 shorter events, 0.1 us)
Async XLA Ops:
  1.1 18.8 %collective-permute-start.1 = (bf16[112,1920]{1,0:T(8,128)(2,1)S(1)}, bf16[112,1920]{1,0:T(8,128)(2,1)S(1)}, u32[]{:S(2)}, u32[]{:S(2)}) collective-permute-start(bf16[112,1920]{1,0:T(8,128)(2,1)S(1)} %cut_rows.1.kept), channel_id=1, source_target_pairs={{8,1},{16,2},{26,3},{12,5},{20,6},{30,7},{0,8},{18,10},{24,11},{4,... | collective-permute-start | bytes 1290248 | tf_op jit(solution)/shard_map/ppermute | solution.py:419
  8.8 12.6 %collective-permute-start = (bf16[80,1920]{1,0:T(8,128)(2,1)S(1)}, bf16[80,1920]{1,0:T(8,128)(2,1)S(1)}, u32[]{:S(2)}, u32[]{:S(2)}) collective-permute-start(bf16[80,1920]{1,0:T(8,128)(2,1)S(1)} %get-tuple-element.19.kept), channel_id=1, source_target_pairs={{8,1},{16,2},{26,3},{12,5},{20,6},{30,7},{0,8},{18,10},{24,11},{4,... | collective-permute-start | bytes 921608 | tf_op jit(solution)/shard_map/ppermute | solution.py:422
  10.7 12.3 %collective-permute-start.8 = (bf16[48,1920]{1,0:T(8,128)(2,1)S(1)}, bf16[48,1920]{1,0:T(8,128)(2,1)S(1)}, u32[]{:S(2)}, u32[]{:S(2)}) collective-permute-start(bf16[48,1920]{1,0:T(8,128)(2,1)S(1)} %get-tuple-element.31.refs_0_), channel_id=1, source_target_pairs={{4,0},{5,1},{6,2},{7,3},{0,4},{1,5},{2,6},{3,7},{12,8},{13,9},{14,... | collective-permute-start | bytes 552968 | tf_op jit(solution)/shard_map/ppermute | solution.py:416
  12.3 15.2 %collective-permute-start.5 = (bf16[480,512]{1,0:T(8,128)(2,1)S(1)}, bf16[480,512]{1,0:T(8,128)(2,1)S(1)}, u32[]{:S(2)}, u32[]{:S(2)}) collective-permute-start(bf16[480,512]{1,0:T(8,128)(2,1)S(1)} %get-tuple-element.22), channel_id=1, source_target_pairs={{1,0},{0,1},{3,2},{2,3},{5,4},{4,5},{7,6},{6,7},{9,8},{8,9},{11,10... | collective-permute-start | bytes 1474568 | tf_op jit(solution)/shard_map/ppermute | solution.py:413
  14.8 17.1 %collective-permute-start.4 = (bf16[480,512]{1,0:T(8,128)(2,1)S(1)}, bf16[480,512]{1,0:T(8,128)(2,1)S(1)}, u32[]{:S(2)}, u32[]{:S(2)}) collective-permute-start(bf16[480,512]{1,0:T(8,128)(2,1)S(1)} %get-tuple-element.20.folded), channel_id=1, source_target_pairs={{2,0},{3,1},{0,2},{1,3},{6,4},{7,5},{4,6},{5,7},{10,8},{11,9},{8,1... | collective-permute-start | bytes 1474568 | tf_op jit(solution)/shard_map/ppermute | solution.py:412
  20.1 18.7 %collective-permute-start.3 = (bf16[112,1920]{1,0:T(8,128)(2,1)S(1)}, bf16[112,1920]{1,0:T(8,128)(2,1)S(1)}, u32[]{:S(2)}, u32[]{:S(2)}) collective-permute-start(bf16[112,1920]{1,0:T(8,128)(2,1)S(1)} %owned_rows.3.refs_0_), channel_id=1, source_target_pairs={{4,0},{5,1},{6,2},{7,3},{0,4},{1,5},{2,6},{3,7},{12,8},{13,9},{14,... | collective-permute-start | bytes 1290248 | tf_op jit(solution)/shard_map/ppermute | solution.py:420
  21.4 20.5 %collective-permute-start.2 = (bf16[80,1920]{1,0:T(8,128)(2,1)S(1)}, bf16[80,1920]{1,0:T(8,128)(2,1)S(1)}, u32[]{:S(2)}, u32[]{:S(2)}) collective-permute-start(bf16[80,1920]{1,0:T(8,128)(2,1)S(1)} %owned_rows.4.refs_1_), channel_id=1, source_target_pairs={{4,0},{5,1},{6,2},{7,3},{0,4},{1,5},{2,6},{3,7},{12,8},{13,9},{14,... | collective-permute-start | bytes 921608 | tf_op jit(solution)/shard_map/ppermute | solution.py:423
  23.0 18.9 %collective-permute-start.9 = (bf16[96,1920]{1,0:T(8,128)(2,1)S(1)}, bf16[96,1920]{1,0:T(8,128)(2,1)S(1)}, u32[]{:S(2)}, u32[]{:S(2)}) collective-permute-start(bf16[96,1920]{1,0:T(8,128)(2,1)S(1)} %pad_maximum_fusion.2.kept), channel_id=1, source_target_pairs={{8,1},{16,2},{26,3},{12,5},{20,6},{30,7},{0,8},{18,10},{24,11},{4,... | collective-permute-start | bytes 1105928 | tf_op jit(solution)/shard_map/ppermute | solution.py:425
  32.0 3.0 %collective-permute-start.6 = (bf16[240,512]{1,0:T(8,128)(2,1)S(1)}, bf16[240,512]{1,0:T(8,128)(2,1)S(1)}, u32[]{:S(2)}, u32[]{:S(2)}) collective-permute-start(bf16[240,512]{1,0:T(8,128)(2,1)S(1)} %get-tuple-element.34), channel_id=1, source_target_pairs={{1,0},{0,1},{3,2},{2,3},{5,4},{4,5},{7,6},{6,7},{9,8},{8,9},{11,10... | collective-permute-start | bytes 737288 | tf_op jit(solution)/shard_map/ppermute | solution.py:433
  33.8 1.5 %collective-permute-start.7 = (bf16[240,512]{1,0:T(8,128)(2,1)S(1)}, bf16[240,512]{1,0:T(8,128)(2,1)S(1)}, u32[]{:S(2)}, u32[]{:S(2)}) collective-permute-start(bf16[240,512]{1,0:T(8,128)(2,1)S(1)} %get-tuple-element.33), channel_id=1, source_target_pairs={{1,0},{0,1},{3,2},{2,3},{5,4},{4,5},{7,6},{6,7},{9,8},{8,9},{11,10... | collective-permute-start | bytes 737288 | tf_op jit(solution)/shard_map/ppermute | solution.py:433

commit v20 on v19

--- a/solution.py
+++ b/solution.py
@@ -440,13 +440,11 @@
                 mine, dense, fock, columns=(near, dense.shape[1]), sums=sums,
                 spans=((0, 0, early),), signed=True, **place,
             )
-            for by in range(1, members):
-                result, token = dress(
-                    after(firsts[by - 1], token), dense, fock, spans=((by, 0, piece),), base=result,
-                    signed=True, **place,
-                )
-            last = [after(part, token) for part in seconds] + [owned(sent, lates, members, token)]
-            spans = [(by, piece, early - piece) for by in range(1, members)]
+            last = []
+            for parts in zip(firsts, seconds):
+                last += [after(part, token) for part in parts]
+            last.append(owned(sent, lates, members, token))
+            spans = [(by, 0, early) for by in range(1, members)]
             spans += [(by, early, rows - early) for by in range(members)]
             result, = dress(
                 jnp.concatenate(last), dense, fock, spans=tuple(spans), base=result, **place

time: 46.4 us -> 45.3 us (0.976)
  the two profiles are of different devices: /device:TPU:0 before, /device:TPU:4 now
where the time goes in v20:
time: 45.3 us; the launch traced here: 44.6 us
  Pallas kernels  20.3 us (45%)
  starting transfers between devices  15 us (33%)
  waiting for transfers between devices  8.23 us (18%)
  between operations  0.83 us (2%)
    pallas_call x3, Pallas kernels, dress(): pl.pallas_call(functools.partial(dress_kernel, job), out_shape=out_shape...  10.3 us
    ppermute x1, starting transfers between devices, local(): beside = lax.ppermute(own_again, axes, to_slot(1))  4.89 us
    pallas_call x1, Pallas kernels, first_spread(): pl.pallas_call(functools.partial(first_spread_kernel, groups), out_shape=...  4 us
    ppermute x1, waiting for transfers between devices, local(): first = owned(lax.ppermute(first, axes, to_group), first, members, token)  3.04 us
    pallas_call x3, Pallas kernels, spread(): pl.pallas_call(functools.partial(spread_kernel, slot, len(parts)), out_sh...  2.85 us
    pallas_call x1, Pallas kernels, fold_panel(): pl.pallas_call(functools.partial(fold_kernel, chunk, starts), out_shape=o...  2.09 us
    ppermute x1, waiting for transfers between devices, local(): second = owned(lax.ppermute(second, axes, to_group), second, members, first)  1.72 us
    ppermute x1, waiting for transfers between devices, local(): sent = lax.ppermute(lates, axes, to_group)  1.63 us
  transfers between devices with their start and end apart: 10, of which 5 were waited for; matrix products, arithmetic and copies ran while one was open for 0% of the time, Pallas kernels for 30%

profile of v20, /device:TPU:4, one launch (start us, length us, event | category | flops | bytes accessed | tf_op | source)
XLA Modules:
  0.0 44.6 jit_solution(11945459986960325850)
XLA Ops:
  0.0 1.1 %cut_rows.1.kept = bf16[112,1920]{1,0:T(8,128)(2,1)S(1)} custom-call(bf16[240,1920]{1,0:T(8,128)(2,1)} %refs_0_.1), custom_call_target="tpu_custom_call" | custom-call | tf_op jit(solution)/shard_map/cut_rows/pallas_call | solution.py:58
  1.1 1.3 %collective-permute-start = (bf16[112,1920]{1,0:T(8,128)(2,1)S(1)}, bf16[112,1920]{1,0:T(8,128)(2,1)S(1)}, u32[]{:S(2)}, u32[]{:S(2)}) collective-permute-start(bf16[112,1920]{1,0:T(8,128)(2,1)S(1)} %cut_rows.1.kept), channel_id=1, source_target_pairs={{8,1},{16,2},{26,3},{12,5},{20,6},{30,7},{0,8},{18,10},{24,11},{4,... | collective-permute-start | bytes 1290248 | tf_op jit(solution)/shard_map/ppermute | solution.py:419
  3.0 2.1 %fold_panel.1 = (bf16[480,512]{1,0:T(8,128)(2,1)S(1)}, bf16[480,512]{1,0:T(8,128)(2,1)S(1)}, bf16[80,1920]{1,0:T(8,128)(2,1)S(1)}, bf16[48,1920]{1,0:T(8,128)(2,1)S(1)}) custom-call(s32[1]{0:T(128)S(6)} %copy.30.pair, s32[8]{0:T(128)} %sizes.1, bf16[480,1920]{1,0:T(8,128)(2,1)} %bitcast.4, bf16[240,1920]{1,0:T(8,128)(2,1)} %refs_0_.1), custom_call_target="tpu_custom_call" | custom-call | tf_op jit(solution)/shard_map/fold_panel/pallas_call | solution.py:132
  5.1 1.3 %collective-permute-start.2 = (bf16[80,1920]{1,0:T(8,128)(2,1)S(1)}, bf16[80,1920]{1,0:T(8,128)(2,1)S(1)}, u32[]{:S(2)}, u32[]{:S(2)}) collective-permute-start(bf16[80,1920]{1,0:T(8,128)(2,1)S(1)} %get-tuple-element.19.kept), channel_id=1, source_target_pairs={{8,1},{16,2},{26,3},{12,5},{20,6},{30,7},{0,8},{18,10},{24,11},{4,... | collective-permute-start | bytes 921608 | tf_op jit(solution)/shard_map/ppermute | solution.py:422
  6.4 1.6 %collective-permute-start.8 = (bf16[48,1920]{1,0:T(8,128)(2,1)S(1)}, bf16[48,1920]{1,0:T(8,128)(2,1)S(1)}, u32[]{:S(2)}, u32[]{:S(2)}) collective-permute-start(bf16[48,1920]{1,0:T(8,128)(2,1)S(1)} %get-tuple-element.27.refs_0_), channel_id=1, source_target_pairs={{4,0},{5,1},{6,2},{7,3},{0,4},{1,5},{2,6},{3,7},{12,8},{13,9},{14,... | collective-permute-start | bytes 552968 | tf_op jit(solution)/shard_map/ppermute | solution.py:416
  8.0 4.9 %collective-permute-start.4 = (bf16[480,512]{1,0:T(8,128)(2,1)S(1)}, bf16[480,512]{1,0:T(8,128)(2,1)S(1)}, u32[]{:S(2)}, u32[]{:S(2)}) collective-permute-start(bf16[480,512]{1,0:T(8,128)(2,1)S(1)} %get-tuple-element.20), channel_id=1, source_target_pairs={{1,0},{0,1},{3,2},{2,3},{5,4},{4,5},{7,6},{6,7},{9,8},{8,9},{11,10... | collective-permute-start | bytes 1474568 | tf_op jit(solution)/shard_map/ppermute | solution.py:413
  12.9 1.0 %collective-permute-start.3 = (bf16[480,512]{1,0:T(8,128)(2,1)S(1)}, bf16[480,512]{1,0:T(8,128)(2,1)S(1)}, u32[]{:S(2)}, u32[]{:S(2)}) collective-permute-start(bf16[480,512]{1,0:T(8,128)(2,1)S(1)} %get-tuple-element.17.folded), channel_id=1, source_target_pairs={{2,0},{3,1},{0,2},{1,3},{6,4},{7,5},{4,6},{5,7},{10,8},{11,9},{8,1... | collective-permute-start | bytes 1474568 | tf_op jit(solution)/shard_map/ppermute | solution.py:412
  13.9 4.0 %first_spread.1 = (bf16[1920,2048]{1,0:T(8,128)(2,1)S(1)}, bf16[2048,1920]{1,0:T(8,128)(2,1)S(1)}, s32[2,8,2048]{2,1,0:T(8,128)S(1)}, s32[8,128]{1,0:T(8,128)S(1)}) custom-call(s32[8]{0:T(128)} %sizes.1, s32[1]{0:T(128)S(6)} %copy.30.pair, bf16[480,512]{1,0:T(8,128)(2,1)S(1)} %get-tuple-element.17.folded, bf16[1920,1920]{1,0:T(8,128)(2,1)} %fock.1), custom_call_target="tpu_custom_call" | custom-call | tf_op jit(solution)/shard_map/first_spread/pallas_call | solution.py:203
  17.9 3.0 %collective-permute-done.received = bf16[112,1920]{1,0:T(8,128)(2,1)S(1)} collective-permute-done((bf16[112,1920]{1,0:T(8,128)(2,1)S(1)}, bf16[112,1920]{1,0:T(8,128)(2,1)S(1)}, u32[]{:S(2)}, u32[]{:S(2)}) %collective-permute-start) | collective-permute-done | bytes 430112 | tf_op jit(solution)/shard_map/ppermute | solution.py:419
  21.0 1.6 %collective-permute-start.1 = (bf16[112,1920]{1,0:T(8,128)(2,1)S(1)}, bf16[112,1920]{1,0:T(8,128)(2,1)S(1)}, u32[]{:S(2)}, u32[]{:S(2)}) collective-permute-start(bf16[112,1920]{1,0:T(8,128)(2,1)S(1)} %owned_rows.3.refs_0_), channel_id=1, source_target_pairs={{4,0},{5,1},{6,2},{7,3},{0,4},{1,5},{2,6},{3,7},{12,8},{13,9},{14,... | collective-permute-start | bytes 1290248 | tf_op jit(solution)/shard_map/ppermute | solution.py:420
  22.5 1.7 %collective-permute-done.2.received = bf16[80,1920]{1,0:T(8,128)(2,1)S(1)} collective-permute-done((bf16[80,1920]{1,0:T(8,128)(2,1)S(1)}, bf16[80,1920]{1,0:T(8,128)(2,1)S(1)}, u32[]{:S(2)}, u32[]{:S(2)}) %collective-permute-start.2) | collective-permute-done | bytes 307232 | tf_op jit(solution)/shard_map/ppermute | solution.py:422
  24.2 1.6 %collective-permute-start.7 = (bf16[80,1920]{1,0:T(8,128)(2,1)S(1)}, bf16[80,1920]{1,0:T(8,128)(2,1)S(1)}, u32[]{:S(2)}, u32[]{:S(2)}) collective-permute-start(bf16[80,1920]{1,0:T(8,128)(2,1)S(1)} %owned_rows.4.refs_1_), channel_id=1, source_target_pairs={{4,0},{5,1},{6,2},{7,3},{0,4},{1,5},{2,6},{3,7},{12,8},{13,9},{14,... | collective-permute-start | bytes 921608 | tf_op jit(solution)/shard_map/ppermute | solution.py:423
  25.8 0.0 collective-permute-done.8.refs_0_
  25.8 1.3 %collective-permute-start.9 = (bf16[96,1920]{1,0:T(8,128)(2,1)S(1)}, bf16[96,1920]{1,0:T(8,128)(2,1)S(1)}, u32[]{:S(2)}, u32[]{:S(2)}) collective-permute-start(bf16[96,1920]{1,0:T(8,128)(2,1)S(1)} %pad_maximum_fusion.2.kept), channel_id=1, source_target_pairs={{8,1},{16,2},{26,3},{12,5},{20,6},{30,7},{0,8},{18,10},{24,11},{4,... | collective-permute-start | bytes 1105928 | tf_op jit(solution)/shard_map/ppermute | solution.py:425
  27.1 0.1 pad_maximum_fusion.1.amplitudes
  27.2 0.0 collective-permute-done.4.refs_0_
  27.2 1.0 %spread_panel.3.dense.refs_2_ = bf16[1920,2048]{1,0:T(8,128)(2,1)S(1)} custom-call(bf16[480,512]{1,0:T(8,128)(2,1)S(1)} %collective-permute-done.4.refs_0_, s32[2,8,2048]{2,1,0:T(8,128)S(1)} %get-tuple-element.21.refs_1_.refs_2_, bf16[1920,2048]{1,0:T(8,128)(2,1)S(1)} %get-tuple-element.22.refs_2_), custom_call_target="tpu_custom_call", output_to_operand_aliasing={{}: (2, {})} | custom-call | tf_op jit(solution)/shard_map/spread_panel/pallas_call | solution.py:234
  28.2 1.8 %dress_rows.3 = (f32[192,1920]{1,0:T(8,128)S(1)}, s32[8,128]{1,0:T(8,128)S(1)}) custom-call(bf16[192,1920]{1,0:T(8,128)(2,1)S(1)} %pad_maximum_fusion.1.amplitudes, bf16[1920,2048]{1,0:T(8,128)(2,1)S(1)} %spread_panel.3.dense.refs_2_, bf16[2048,1920]{1,0:T(8,128)(2,1)S(1)} %get-tuple-element.23.fock), custom_call_target="tpu_custom_call" | custom-call | tf_op jit(solution)/shard_map/dress_rows/pallas_call | solution.py:358
  30.0 1.4 %collective-permute-done.3.refs_0_ = bf16[480,512]{1,0:T(8,128)(2,1)S(1)} collective-permute-done((bf16[480,512]{1,0:T(8,128)(2,1)S(1)}, bf16[480,512]{1,0:T(8,128)(2,1)S(1)}, u32[]{:S(2)}, u32[]{:S(2)}) %collective-permute-start.3) | collective-permute-done | bytes 491552 | tf_op jit(solution)/shard_map/ppermute | solution.py:412
  31.5 0.1 collective-permute-start.5
  31.6 0.5 %collective-permute-start.6 = (bf16[240,512]{1,0:T(8,128)(2,1)S(1)}, bf16[240,512]{1,0:T(8,128)(2,1)S(1)}, u32[]{:S(2)}, u32[]{:S(2)}) collective-permute-start(bf16[240,512]{1,0:T(8,128)(2,1)S(1)} %get-tuple-element.29), channel_id=1, source_target_pairs={{1,0},{0,1},{3,2},{2,3},{5,4},{4,5},{7,6},{6,7},{9,8},{8,9},{11,10... | collective-permute-start | bytes 737288 | tf_op jit(solution)/shard_map/ppermute | solution.py:433
  32.1 0.9 %spread_panel.4.refs_3_ = bf16[1920,2048]{1,0:T(8,128)(2,1)S(1)} custom-call(bf16[480,512]{1,0:T(8,128)(2,1)S(1)} %after.5.refs_0_, s32[2,8,2048]{2,1,0:T(8,128)S(1)} %get-tuple-element.21.refs_1_.refs_2_, bf16[1920,2048]{1,0:T(8,128)(2,1)S(1)} %spread_panel.3.dense.refs_2_), custom_call_target="tpu_custom_call", output_to_operand_aliasing={{}: (2, {})} | custom-call | tf_op jit(solution)/shard_map/spread_panel/pallas_call | solution.py:234
  33.0 0.0 collective-permute-done.5.refs_0_
  33.1 0.4 collective-permute-done.6.refs_1_
  33.4 0.9 %spread_panel.5.dense = bf16[1920,2048]{1,0:T(8,128)(2,1)S(1)} custom-call(bf16[240,512]{1,0:T(8,128)(2,1)S(1)} %collective-permute-done.5.refs_0_, bf16[240,512]{1,0:T(8,128)(2,1)S(1)} %collective-permute-done.6.refs_1_, s32[2,8,2048]{2,1,0:T(8,128)S(1)} %get-tuple-element.21.refs_1_.refs_2_, ...), custom_call_target="tpu_custom_call", output_to_operand_aliasing={{}: (3, {})} | custom-call | tf_op jit(solution)/shard_map/spread_panel/pallas_call | solution.py:234
  34.4 2.6 %dress_rows.4 = (bf16[480,1920]{1,0:T(8,128)(2,1)}, s32[8,128]{1,0:T(8,128)S(1)}) custom-call(bf16[192,1920]{1,0:T(8,128)(2,1)S(1)} %pad_maximum_fusion.1.amplitudes, bf16[1920,2048]{1,0:T(8,128)(2,1)S(1)} %spread_panel.5.dense, bf16[2048,1920]{1,0:T(8,128)(2,1)S(1)} %get-tuple-element.23.fock, f32[192,1920]{1,0:T(8,128)S(1)} %get-tuple-element.25.refs_0_), custom_call_target="tpu_custom_call" | custom-call | tf_op jit(solution)/shard_map/dress_rows/pallas_call | solution.py:358
  37.0 0.0 collective-permute-done.7.refs_0_
  37.0 1.6 %collective-permute-done.9.received = bf16[96,1920]{1,0:T(8,128)(2,1)S(1)} collective-permute-done((bf16[96,1920]{1,0:T(8,128)(2,1)S(1)}, bf16[96,1920]{1,0:T(8,128)(2,1)S(1)}, u32[]{:S(2)}, u32[]{:S(2)}) %collective-permute-start.9) | collective-permute-done | bytes 368672 | tf_op jit(solution)/shard_map/ppermute | solution.py:425
  38.6 0.0 collective-permute-done.1.refs_0_
  38.6 0.1 pad_maximum_fusion.amplitudes
  38.7 5.9 %dress_rows.5 = bf16[480,1920]{1,0:T(8,128)(2,1)} custom-call(bf16[288,1920]{1,0:T(8,128)(2,1)S(1)} %pad_maximum_fusion.amplitudes, bf16[1920,2048]{1,0:T(8,128)(2,1)S(1)} %spread_panel.5.dense, bf16[2048,1920]{1,0:T(8,128)(2,1)S(1)} %get-tuple-element.23.fock, bf16[480,1920]{1,0:T(8,128)(2,1)} %get-tuple-element.28.refs_0_), custom_call_target="tpu_custom_call", output_to_operand_aliasing={{}: (3, {})} | custom-call | tf_op jit(solution)/shard_map/dress_rows/pallas_call | solution.py:358
  (10 shorter events, 0.1 us)
Async XLA Ops:
  1.1 19.9 %collective-permute-start = (bf16[112,1920]{1,0:T(8,128)(2,1)S(1)}, bf16[112,1920]{1,0:T(8,128)(2,1)S(1)}, u32[]{:S(2)}, u32[]{:S(2)}) collective-permute-start(bf16[112,1920]{1,0:T(8,128)(2,1)S(1)} %cut_rows.1.kept), channel_id=1, source_target_pairs={{8,1},{16,2},{26,3},{12,5},{20,6},{30,7},{0,8},{18,10},{24,11},{4,... | collective-permute-start | bytes 1290248 | tf_op jit(solution)/shard_map/ppermute | solution.py:419
  5.1 19.1 %collective-permute-start.2 = (bf16[80,1920]{1,0:T(8,128)(2,1)S(1)}, bf16[80,1920]{1,0:T(8,128)(2,1)S(1)}, u32[]{:S(2)}, u32[]{:S(2)}) collective-permute-start(bf16[80,1920]{1,0:T(8,128)(2,1)S(1)} %get-tuple-element.19.kept), channel_id=1, source_target_pairs={{8,1},{16,2},{26,3},{12,5},{20,6},{30,7},{0,8},{18,10},{24,11},{4,... | collective-permute-start | bytes 921608 | tf_op jit(solution)/shard_map/ppermute | solution.py:422
  6.4 19.4 %collective-permute-start.8 = (bf16[48,1920]{1,0:T(8,128)(2,1)S(1)}, bf16[48,1920]{1,0:T(8,128)(2,1)S(1)}, u32[]{:S(2)}, u32[]{:S(2)}) collective-permute-start(bf16[48,1920]{1,0:T(8,128)(2,1)S(1)} %get-tuple-element.27.refs_0_), channel_id=1, source_target_pairs={{4,0},{5,1},{6,2},{7,3},{0,4},{1,5},{2,6},{3,7},{12,8},{13,9},{14,... | collective-permute-start | bytes 552968 | tf_op jit(solution)/shard_map/ppermute | solution.py:416
  8.0 19.2 %collective-permute-start.4 = (bf16[480,512]{1,0:T(8,128)(2,1)S(1)}, bf16[480,512]{1,0:T(8,128)(2,1)S(1)}, u32[]{:S(2)}, u32[]{:S(2)}) collective-permute-start(bf16[480,512]{1,0:T(8,128)(2,1)S(1)} %get-tuple-element.20), channel_id=1, source_target_pairs={{1,0},{0,1},{3,2},{2,3},{5,4},{4,5},{7,6},{6,7},{9,8},{8,9},{11,10... | collective-permute-start | bytes 1474568 | tf_op jit(solution)/shard_map/ppermute | solution.py:413
  12.9 18.6 %collective-permute-start.3 = (bf16[480,512]{1,0:T(8,128)(2,1)S(1)}, bf16[480,512]{1,0:T(8,128)(2,1)S(1)}, u32[]{:S(2)}, u32[]{:S(2)}) collective-permute-start(bf16[480,512]{1,0:T(8,128)(2,1)S(1)} %get-tuple-element.17.folded), channel_id=1, source_target_pairs={{2,0},{3,1},{0,2},{1,3},{6,4},{7,5},{4,6},{5,7},{10,8},{11,9},{8,1... | collective-permute-start | bytes 1474568 | tf_op jit(solution)/shard_map/ppermute | solution.py:412
  21.0 17.7 %collective-permute-start.1 = (bf16[112,1920]{1,0:T(8,128)(2,1)S(1)}, bf16[112,1920]{1,0:T(8,128)(2,1)S(1)}, u32[]{:S(2)}, u32[]{:S(2)}) collective-permute-start(bf16[112,1920]{1,0:T(8,128)(2,1)S(1)} %owned_rows.3.refs_0_), channel_id=1, source_target_pairs={{4,0},{5,1},{6,2},{7,3},{0,4},{1,5},{2,6},{3,7},{12,8},{13,9},{14,... | collective-permute-start | bytes 1290248 | tf_op jit(solution)/shard_map/ppermute | solution.py:420
  24.2 12.7 %collective-permute-start.7 = (bf16[80,1920]{1,0:T(8,128)(2,1)S(1)}, bf16[80,1920]{1,0:T(8,128)(2,1)S(1)}, u32[]{:S(2)}, u32[]{:S(2)}) collective-permute-start(bf16[80,1920]{1,0:T(8,128)(2,1)S(1)} %owned_rows.4.refs_1_), channel_id=1, source_target_pairs={{4,0},{5,1},{6,2},{7,3},{0,4},{1,5},{2,6},{3,7},{12,8},{13,9},{14,... | collective-permute-start | bytes 921608 | tf_op jit(solution)/shard_map/ppermute | solution.py:423
  25.8 12.8 %collective-permute-start.9 = (bf16[96,1920]{1,0:T(8,128)(2,1)S(1)}, bf16[96,1920]{1,0:T(8,128)(2,1)S(1)}, u32[]{:S(2)}, u32[]{:S(2)}) collective-permute-start(bf16[96,1920]{1,0:T(8,128)(2,1)S(1)} %pad_maximum_fusion.2.kept), channel_id=1, source_target_pairs={{8,1},{16,2},{26,3},{12,5},{20,6},{30,7},{0,8},{18,10},{24,11},{4,... | collective-permute-start | bytes 1105928 | tf_op jit(solution)/shard_map/ppermute | solution.py:425
  31.5 1.6 %collective-permute-start.5 = (bf16[240,512]{1,0:T(8,128)(2,1)S(1)}, bf16[240,512]{1,0:T(8,128)(2,1)S(1)}, u32[]{:S(2)}, u32[]{:S(2)}) collective-permute-start(bf16[240,512]{1,0:T(8,128)(2,1)S(1)} %get-tuple-element.30), channel_id=1, source_target_pairs={{1,0},{0,1},{3,2},{2,3},{5,4},{4,5},{7,6},{6,7},{9,8},{8,9},{11,10... | collective-permute-start | bytes 737288 | tf_op jit(solution)/shard_map/ppermute | solution.py:433
  31.6 1.9 %collective-permute-start.6 = (bf16[240,512]{1,0:T(8,128)(2,1)S(1)}, bf16[240,512]{1,0:T(8,128)(2,1)S(1)}, u32[]{:S(2)}, u32[]{:S(2)}) collective-permute-start(bf16[240,512]{1,0:T(8,128)(2,1)S(1)} %get-tuple-element.29), channel_id=1, source_target_pairs={{1,0},{0,1},{3,2},{2,3},{5,4},{4,5},{7,6},{6,7},{9,8},{8,9},{11,10... | collective-permute-start | bytes 737288 | tf_op jit(solution)/shard_map/ppermute | solution.py:433

commit v21 on v19

--- a/solution.py
+++ b/solution.py
@@ -398,8 +398,8 @@
         panel = jnp.swapaxes(hole_panel[:, 0, :], 0, 1)
         irrep_sizes = pltpu.with_memory_space_constraint(irrep_sizes, pltpu.HBM)
 
-        piece = rounded(rows * 7 // 15, SUBLANES) if rows % SUBLANES == 0 else 0
-        early = rounded(rows * 4 // 5, SUBLANES)
+        piece = rounded(rows * 2 // 5, SUBLANES) if rows % SUBLANES == 0 else 0
+        early = rounded(rows * 7 // 10, SUBLANES)
         if piece:
             amplitudes = pltpu.with_memory_space_constraint(amplitudes, pltpu.HBM)
             first = cut(amplitudes, piece)
@@ -419,32 +419,32 @@
         first = owned(lax.ppermute(first, axes, to_group), first, members, token)
         firsts = [lax.ppermute(first, axes, to_member(by)) for by in range(1, members)]
         if piece:
-            second = owned(lax.ppermute(second, axes, to_group), second, members, first)
-            seconds = [lax.ppermute(second, axes, to_member(by)) for by in range(1, members)]
-            lates = jnp.concatenate([after(rows_of, second) for rows_of in lates])
+            lates = jnp.concatenate([after(rows_of, first) for rows_of in lates])
             sent = lax.ppermute(lates, axes, to_group)
         dense = spread(1, [beside], ranges, dense)
         near = 2 * dense.shape[1] // groups
         if piece:
-            mine = jnp.concatenate([first, second])
-            sums, token = dress(mine, dense, fock, columns=(0, near), signed=True)
+            sums, token = dress(first, dense, fock, columns=(0, near), signed=True)
             across = after(across, token)
         cuts = [rounded(across.shape[0] // 2, SUBLANES)] if piece else []
         both = [lax.ppermute(part, axes, to_slot(1)) for part in jnp.split(across, cuts)]
+        if piece:
+            second = owned(lax.ppermute(second, axes, to_group), second, members, across)
+            seconds = [lax.ppermute(second, axes, to_member(by)) for by in range(1, members)]
         dense = spread(2, [across], ranges, dense)
         dense = spread(3, both, ranges, dense)
 
         if piece:
             place = dict(rows=rows, members=members, out_rows=out_rows)
             result, token = dress(
-                mine, dense, fock, columns=(near, dense.shape[1]), sums=sums,
-                spans=((0, 0, early),), signed=True, **place,
+                first, dense, fock, columns=(near, dense.shape[1]), sums=sums,
+                spans=((0, 0, piece),), signed=True, **place,
             )
-            for by in range(1, members):
-                result, token = dress(
-                    after(firsts[by - 1], token), dense, fock, spans=((by, 0, piece),), base=result,
-                    signed=True, **place,
-                )
+            parts = [second] + [after(part, token) for part in firsts]
+            spans = [(0, piece, early - piece)] + [(by, 0, piece) for by in range(1, members)]
+            result, token = dress(
+                jnp.concatenate(parts), dense, fock, spans=tuple(spans), base=result, signed=True, **place
+            )
             last = [after(part, token) for part in seconds] + [owned(sent, lates, members, token)]
             spans = [(by, piece, early - piece) for by in range(1, members)]
             spans += [(by, early, rows - early) for by in range(members)]

time: 46.4 us -> 46.2 us (level)
  the two profiles are of different devices: /device:TPU:0 before, /device:TPU:24 now
where the time goes in v21:
time: 46.2 us; the launch traced here: 46 us
  Pallas kernels  21.9 us (47%)
  starting transfers between devices  15.4 us (33%)
  waiting for transfers between devices  7.6 us (16%)
  between operations  0.87 us (2%)
    pallas_call x4, Pallas kernels, dress(): pl.pallas_call(functools.partial(dress_kernel, job), out_shape=out_shape...  11.8 us
    ppermute x1, waiting for transfers between devices, local(): across = lax.ppermute(own, axes, to_slot(2))  7.58 us
    pallas_call x1, Pallas kernels, first_spread(): pl.pallas_call(functools.partial(first_spread_kernel, groups), out_shape=...  4.01 us
    ppermute x1, starting transfers between devices, local(): sent = lax.ppermute(lates, axes, to_group)  3.41 us
    ppermute x1, starting transfers between devices, local(): lax.ppermute(second, axes, to_group)  3.15 us
    pallas_call x3, Pallas kernels, spread(): pl.pallas_call(functools.partial(spread_kernel, slot, len(parts)), out_sh...  2.85 us
    ppermute x1, starting transfers between devices, local(): lax.ppermute(second, axes, to_member(by))  2.64 us
    ppermute x1, starting transfers between devices, local(): first = owned(lax.ppermute(first, axes, to_group), first, members, token)  2.64 us
  transfers between devices with their start and end apart: 10, of which 1 were waited for; matrix products, arithmetic and copies ran while one was open for 0% of the time, Pallas kernels for 35%

profile of v21, /device:TPU:24, one launch (start us, length us, event | category | flops | bytes accessed | tf_op | source)
XLA Modules:
  0.0 46.0 jit_solution(16901200000554487200)
XLA Ops:
  0.0 1.1 %cut_rows.1.kept = bf16[96,1920]{1,0:T(8,128)(2,1)S(1)} custom-call(bf16[240,1920]{1,0:T(8,128)(2,1)} %whole.1), custom_call_target="tpu_custom_call" | custom-call | tf_op jit(solution)/shard_map/cut_rows/pallas_call | solution.py:58
  1.1 2.6 %collective-permute-start.2 = (bf16[96,1920]{1,0:T(8,128)(2,1)S(1)}, bf16[96,1920]{1,0:T(8,128)(2,1)S(1)}, u32[]{:S(2)}, u32[]{:S(2)}) collective-permute-start(bf16[96,1920]{1,0:T(8,128)(2,1)S(1)} %cut_rows.1.kept), channel_id=1, source_target_pairs={{8,1},{16,2},{26,3},{12,5},{20,6},{30,7},{0,8},{18,10},{24,11},{4,... | collective-permute-start | bytes 1105928 | tf_op jit(solution)/shard_map/ppermute | solution.py:419
  4.4 2.1 %fold_panel.1 = (bf16[480,512]{1,0:T(8,128)(2,1)S(1)}, bf16[480,512]{1,0:T(8,128)(2,1)S(1)}, bf16[80,1920]{1,0:T(8,128)(2,1)S(1)}, bf16[64,1920]{1,0:T(8,128)(2,1)S(1)}) custom-call(s32[1]{0:T(128)S(6)} %copy.32.pair, s32[8]{0:T(128)} %sizes.1, bf16[480,1920]{1,0:T(8,128)(2,1)} %bitcast.4, bf16[240,1920]{1,0:T(8,128)(2,1)} %whole.1), custom_call_target="tpu_custom_call" | custom-call | tf_op jit(solution)/shard_map/fold_panel/pallas_call | solution.py:132
  6.5 0.1 collective-permute-start.3
  6.5 0.9 %collective-permute-start.1 = (bf16[480,512]{1,0:T(8,128)(2,1)S(1)}, bf16[480,512]{1,0:T(8,128)(2,1)S(1)}, u32[]{:S(2)}, u32[]{:S(2)}) collective-permute-start(bf16[480,512]{1,0:T(8,128)(2,1)S(1)} %get-tuple-element.20.folded), channel_id=1, source_target_pairs={{2,0},{3,1},{0,2},{1,3},{6,4},{7,5},{4,6},{5,7},{10,8},{11,9},{8,1... | collective-permute-start | bytes 1474568 | tf_op jit(solution)/shard_map/ppermute | solution.py:412
  7.4 1.5 %collective-permute-start.8 = (bf16[64,1920]{1,0:T(8,128)(2,1)S(1)}, bf16[64,1920]{1,0:T(8,128)(2,1)S(1)}, u32[]{:S(2)}, u32[]{:S(2)}) collective-permute-start(bf16[64,1920]{1,0:T(8,128)(2,1)S(1)} %get-tuple-element.31.refs_0_), channel_id=1, source_target_pairs={{4,0},{5,1},{6,2},{7,3},{0,4},{1,5},{2,6},{3,7},{12,8},{13,9},{14,... | collective-permute-start | bytes 737288 | tf_op jit(solution)/shard_map/ppermute | solution.py:416
  8.9 3.1 %collective-permute-start = (bf16[80,1920]{1,0:T(8,128)(2,1)S(1)}, bf16[80,1920]{1,0:T(8,128)(2,1)S(1)}, u32[]{:S(2)}, u32[]{:S(2)}) collective-permute-start(bf16[80,1920]{1,0:T(8,128)(2,1)S(1)} %get-tuple-element.19.kept), channel_id=1, source_target_pairs={{8,1},{16,2},{26,3},{12,5},{20,6},{30,7},{0,8},{18,10},{24,11},{4,... | collective-permute-start | bytes 921608 | tf_op jit(solution)/shard_map/ppermute | solution.py:432
  12.1 4.0 %first_spread.1 = (bf16[1920,2048]{1,0:T(8,128)(2,1)S(1)}, bf16[2048,1920]{1,0:T(8,128)(2,1)S(1)}, s32[2,8,2048]{2,1,0:T(8,128)S(1)}, s32[8,128]{1,0:T(8,128)S(1)}) custom-call(s32[8]{0:T(128)} %sizes.1, s32[1]{0:T(128)S(6)} %copy.32.pair, bf16[480,512]{1,0:T(8,128)(2,1)S(1)} %get-tuple-element.20.folded, bf16[1920,1920]{1,0:T(8,128)(2,1)} %fock.1), custom_call_target="tpu_custom_call" | custom-call | tf_op jit(solution)/shard_map/first_spread/pallas_call | solution.py:203
  16.1 0.0 collective-permute-done.2.received
  16.1 0.6 %collective-permute-start.5 = (bf16[96,1920]{1,0:T(8,128)(2,1)S(1)}, bf16[96,1920]{1,0:T(8,128)(2,1)S(1)}, u32[]{:S(2)}, u32[]{:S(2)}) collective-permute-start(bf16[96,1920]{1,0:T(8,128)(2,1)S(1)} %owned_rows.3.amplitudes.refs_1_), channel_id=1, source_target_pairs={{4,0},{5,1},{6,2},{7,3},{0,4},{1,5},{2,6},{3,7},{12,8},{13,9},{14,... | collective-permute-start | bytes 1105928 | tf_op jit(solution)/shard_map/ppermute | solution.py:420
  16.7 0.0 collective-permute-done.8.refs_0_
  16.8 3.4 %collective-permute-start.9 = (bf16[128,1920]{1,0:T(8,128)(2,1)S(1)}, bf16[128,1920]{1,0:T(8,128)(2,1)S(1)}, u32[]{:S(2)}, u32[]{:S(2)}) collective-permute-start(bf16[128,1920]{1,0:T(8,128)(2,1)S(1)} %pad_maximum_fusion.2.kept), channel_id=1, source_target_pairs={{8,1},{16,2},{26,3},{12,5},{20,6},{30,7},{0,8},{18,10},{24,11},{4,... | collective-permute-start | bytes 1474568 | tf_op jit(solution)/shard_map/ppermute | solution.py:423
  20.2 0.0 collective-permute-done.3.refs_0_
  20.2 1.0 %spread_panel.3.dense.refs_2_ = bf16[1920,2048]{1,0:T(8,128)(2,1)S(1)} custom-call(bf16[480,512]{1,0:T(8,128)(2,1)S(1)} %collective-permute-done.3.refs_0_, s32[2,8,2048]{2,1,0:T(8,128)S(1)} %get-tuple-element.23.refs_1_.refs_2_, bf16[1920,2048]{1,0:T(8,128)(2,1)S(1)} %get-tuple-element.24.refs_2_), custom_call_target="tpu_custom_call", output_to_operand_aliasing={{}: (2, {})} | custom-call | tf_op jit(solution)/shard_map/spread_panel/pallas_call | solution.py:234
  21.2 1.3 %dress_rows.4 = (f32[96,1920]{1,0:T(8,128)S(1)}, s32[8,128]{1,0:T(8,128)S(1)}) custom-call(bf16[96,1920]{1,0:T(8,128)(2,1)S(1)} %owned_rows.3.amplitudes.refs_1_, bf16[1920,2048]{1,0:T(8,128)(2,1)S(1)} %spread_panel.3.dense.refs_2_, bf16[2048,1920]{1,0:T(8,128)(2,1)S(1)} %get-tuple-element.25.fock), custom_call_target="tpu_custom_call" | custom-call | tf_op jit(solution)/shard_map/dress_rows/pallas_call | solution.py:358
  22.5 7.6 %collective-permute-done.1.refs_0_ = bf16[480,512]{1,0:T(8,128)(2,1)S(1)} collective-permute-done((bf16[480,512]{1,0:T(8,128)(2,1)S(1)}, bf16[480,512]{1,0:T(8,128)(2,1)S(1)}, u32[]{:S(2)}, u32[]{:S(2)}) %collective-permute-start.1) | collective-permute-done | bytes 491552 | tf_op jit(solution)/shard_map/ppermute | solution.py:412
  30.1 0.1 collective-permute-start.6
  30.2 0.5 %collective-permute-start.7 = (bf16[240,512]{1,0:T(8,128)(2,1)S(1)}, bf16[240,512]{1,0:T(8,128)(2,1)S(1)}, u32[]{:S(2)}, u32[]{:S(2)}) collective-permute-start(bf16[240,512]{1,0:T(8,128)(2,1)S(1)} %get-tuple-element.33), channel_id=1, source_target_pairs={{1,0},{0,1},{3,2},{2,3},{5,4},{4,5},{7,6},{6,7},{9,8},{8,9},{11,10... | collective-permute-start | bytes 737288 | tf_op jit(solution)/shard_map/ppermute | solution.py:430
  30.6 0.0 collective-permute-done.received
  30.7 2.6 %collective-permute-start.4 = (bf16[80,1920]{1,0:T(8,128)(2,1)S(1)}, bf16[80,1920]{1,0:T(8,128)(2,1)S(1)}, u32[]{:S(2)}, u32[]{:S(2)}) collective-permute-start(bf16[80,1920]{1,0:T(8,128)(2,1)S(1)} %owned_rows.4), channel_id=1, source_target_pairs={{4,0},{5,1},{6,2},{7,3},{0,4},{1,5},{2,6},{3,7},{12,8},{13,9},{14,... | collective-permute-start | bytes 921608 | tf_op jit(solution)/shard_map/ppermute | solution.py:433
  33.3 0.9 %spread_panel.4.refs_3_ = bf16[1920,2048]{1,0:T(8,128)(2,1)S(1)} custom-call(bf16[480,512]{1,0:T(8,128)(2,1)S(1)} %after.5.refs_0_, s32[2,8,2048]{2,1,0:T(8,128)S(1)} %get-tuple-element.23.refs_1_.refs_2_, bf16[1920,2048]{1,0:T(8,128)(2,1)S(1)} %spread_panel.3.dense.refs_2_), custom_call_target="tpu_custom_call", output_to_operand_aliasing={{}: (2, {})} | custom-call | tf_op jit(solution)/shard_map/spread_panel/pallas_call | solution.py:234
  34.3 0.0 collective-permute-done.6.refs_0_
  34.3 0.0 collective-permute-done.7.refs_1_
  34.3 1.0 %spread_panel.5.dense = bf16[1920,2048]{1,0:T(8,128)(2,1)S(1)} custom-call(bf16[240,512]{1,0:T(8,128)(2,1)S(1)} %collective-permute-done.6.refs_0_, bf16[240,512]{1,0:T(8,128)(2,1)S(1)} %collective-permute-done.7.refs_1_, s32[2,8,2048]{2,1,0:T(8,128)S(1)} %get-tuple-element.23.refs_1_.refs_2_, ...), custom_call_target="tpu_custom_call", output_to_operand_aliasing={{}: (3, {})} | custom-call | tf_op jit(solution)/shard_map/spread_panel/pallas_call | solution.py:234
  35.3 2.0 %dress_rows.5 = (bf16[480,1920]{1,0:T(8,128)(2,1)}, s32[8,128]{1,0:T(8,128)S(1)}) custom-call(bf16[96,1920]{1,0:T(8,128)(2,1)S(1)} %owned_rows.3.amplitudes.refs_1_, bf16[1920,2048]{1,0:T(8,128)(2,1)S(1)} %spread_panel.5.dense, bf16[2048,1920]{1,0:T(8,128)(2,1)S(1)} %get-tuple-element.25.fock, f32[96,1920]{1,0:T(8,128)S(1)} %get-tuple-element.27.refs_0_), custom_call_target="tpu_custom_call" | custom-call | tf_op jit(solution)/shard_map/dress_rows/pallas_call | solution.py:358
  37.2 0.0 collective-permute-done.5.refs_0_
  37.3 0.1 pad_maximum_fusion.1.amplitudes
  37.3 4.0 %dress_rows.6 = (bf16[480,1920]{1,0:T(8,128)(2,1)}, s32[8,128]{1,0:T(8,128)S(1)}) custom-call(bf16[176,1920]{1,0:T(8,128)(2,1)S(1)} %pad_maximum_fusion.1.amplitudes, bf16[1920,2048]{1,0:T(8,128)(2,1)S(1)} %spread_panel.5.dense, bf16[2048,1920]{1,0:T(8,128)(2,1)S(1)} %get-tuple-element.25.fock, ...), custom_call_target="tpu_custom_call", output_to_operand_aliasing={{0}: (3, {})} | custom-call | tf_op jit(solution)/shard_map/dress_rows/pallas_call | solution.py:358
  41.3 0.0 collective-permute-done.4.refs_0_
  41.3 0.0 collective-permute-done.9.received
  41.3 0.1 pad_maximum_fusion.amplitudes
  41.4 4.5 %dress_rows.7 = bf16[480,1920]{1,0:T(8,128)(2,1)} custom-call(bf16[208,1920]{1,0:T(8,128)(2,1)S(1)} %pad_maximum_fusion.amplitudes, bf16[1920,2048]{1,0:T(8,128)(2,1)S(1)} %spread_panel.5.dense, bf16[2048,1920]{1,0:T(8,128)(2,1)S(1)} %get-tuple-element.25.fock, bf16[480,1920]{1,0:T(8,128)(2,1)} %get-tuple-element.32.refs_0_), custom_call_target="tpu_custom_call", output_to_operand_aliasing={{}: (3, {})} | custom-call | tf_op jit(solution)/shard_map/dress_rows/pallas_call | solution.py:358
  (10 shorter events, 0.1 us)
Async XLA Ops:
  1.1 15.0 %collective-permute-start.2 = (bf16[96,1920]{1,0:T(8,128)(2,1)S(1)}, bf16[96,1920]{1,0:T(8,128)(2,1)S(1)}, u32[]{:S(2)}, u32[]{:S(2)}) collective-permute-start(bf16[96,1920]{1,0:T(8,128)(2,1)S(1)} %cut_rows.1.kept), channel_id=1, source_target_pairs={{8,1},{16,2},{26,3},{12,5},{20,6},{30,7},{0,8},{18,10},{24,11},{4,... | collective-permute-start | bytes 1105928 | tf_op jit(solution)/shard_map/ppermute | solution.py:419
  6.5 13.7 %collective-permute-start.3 = (bf16[480,512]{1,0:T(8,128)(2,1)S(1)}, bf16[480,512]{1,0:T(8,128)(2,1)S(1)}, u32[]{:S(2)}, u32[]{:S(2)}) collective-permute-start(bf16[480,512]{1,0:T(8,128)(2,1)S(1)} %get-tuple-element.22), channel_id=1, source_target_pairs={{1,0},{0,1},{3,2},{2,3},{5,4},{4,5},{7,6},{6,7},{9,8},{8,9},{11,10... | collective-permute-start | bytes 1474568 | tf_op jit(solution)/shard_map/ppermute | solution.py:413
  6.5 23.5 %collective-permute-start.1 = (bf16[480,512]{1,0:T(8,128)(2,1)S(1)}, bf16[480,512]{1,0:T(8,128)(2,1)S(1)}, u32[]{:S(2)}, u32[]{:S(2)}) collective-permute-start(bf16[480,512]{1,0:T(8,128)(2,1)S(1)} %get-tuple-element.20.folded), channel_id=1, source_target_pairs={{2,0},{3,1},{0,2},{1,3},{6,4},{7,5},{4,6},{5,7},{10,8},{11,9},{8,1... | collective-permute-start | bytes 1474568 | tf_op jit(solution)/shard_map/ppermute | solution.py:412
  7.4 9.3 %collective-permute-start.8 = (bf16[64,1920]{1,0:T(8,128)(2,1)S(1)}, bf16[64,1920]{1,0:T(8,128)(2,1)S(1)}, u32[]{:S(2)}, u32[]{:S(2)}) collective-permute-start(bf16[64,1920]{1,0:T(8,128)(2,1)S(1)} %get-tuple-element.31.refs_0_), channel_id=1, source_target_pairs={{4,0},{5,1},{6,2},{7,3},{0,4},{1,5},{2,6},{3,7},{12,8},{13,9},{14,... | collective-permute-start | bytes 737288 | tf_op jit(solution)/shard_map/ppermute | solution.py:416
  8.9 21.7 %collective-permute-start = (bf16[80,1920]{1,0:T(8,128)(2,1)S(1)}, bf16[80,1920]{1,0:T(8,128)(2,1)S(1)}, u32[]{:S(2)}, u32[]{:S(2)}) collective-permute-start(bf16[80,1920]{1,0:T(8,128)(2,1)S(1)} %get-tuple-element.19.kept), channel_id=1, source_target_pairs={{8,1},{16,2},{26,3},{12,5},{20,6},{30,7},{0,8},{18,10},{24,11},{4,... | collective-permute-start | bytes 921608 | tf_op jit(solution)/shard_map/ppermute | solution.py:432
  16.1 21.1 %collective-permute-start.5 = (bf16[96,1920]{1,0:T(8,128)(2,1)S(1)}, bf16[96,1920]{1,0:T(8,128)(2,1)S(1)}, u32[]{:S(2)}, u32[]{:S(2)}) collective-permute-start(bf16[96,1920]{1,0:T(8,128)(2,1)S(1)} %owned_rows.3.amplitudes.refs_1_), channel_id=1, source_target_pairs={{4,0},{5,1},{6,2},{7,3},{0,4},{1,5},{2,6},{3,7},{12,8},{13,9},{14,... | collective-permute-start | bytes 1105928 | tf_op jit(solution)/shard_map/ppermute | solution.py:420
  16.8 24.5 %collective-permute-start.9 = (bf16[128,1920]{1,0:T(8,128)(2,1)S(1)}, bf16[128,1920]{1,0:T(8,128)(2,1)S(1)}, u32[]{:S(2)}, u32[]{:S(2)}) collective-permute-start(bf16[128,1920]{1,0:T(8,128)(2,1)S(1)} %pad_maximum_fusion.2.kept), channel_id=1, source_target_pairs={{8,1},{16,2},{26,3},{12,5},{20,6},{30,7},{0,8},{18,10},{24,11},{4,... | collective-permute-start | bytes 1474568 | tf_op jit(solution)/shard_map/ppermute | solution.py:423
  30.1 4.2 %collective-permute-start.6 = (bf16[240,512]{1,0:T(8,128)(2,1)S(1)}, bf16[240,512]{1,0:T(8,128)(2,1)S(1)}, u32[]{:S(2)}, u32[]{:S(2)}) collective-permute-start(bf16[240,512]{1,0:T(8,128)(2,1)S(1)} %get-tuple-element.34), channel_id=1, source_target_pairs={{1,0},{0,1},{3,2},{2,3},{5,4},{4,5},{7,6},{6,7},{9,8},{8,9},{11,10... | collective-permute-start | bytes 737288 | tf_op jit(solution)/shard_map/ppermute | solution.py:430
  30.2 4.1 %collective-permute-start.7 = (bf16[240,512]{1,0:T(8,128)(2,1)S(1)}, bf16[240,512]{1,0:T(8,128)(2,1)S(1)}, u32[]{:S(2)}, u32[]{:S(2)}) collective-permute-start(bf16[240,512]{1,0:T(8,128)(2,1)S(1)} %get-tuple-element.33), channel_id=1, source_target_pairs={{1,0},{0,1},{3,2},{2,3},{5,4},{4,5},{7,6},{6,7},{9,8},{8,9},{11,10... | collective-permute-start | bytes 737288 | tf_op jit(solution)/shard_map/ppermute | solution.py:430
  30.7 10.6 %collective-permute-start.4 = (bf16[80,1920]{1,0:T(8,128)(2,1)S(1)}, bf16[80,1920]{1,0:T(8,128)(2,1)S(1)}, u32[]{:S(2)}, u32[]{:S(2)}) collective-permute-start(bf16[80,1920]{1,0:T(8,128)(2,1)S(1)} %owned_rows.4), channel_id=1, source_target_pairs={{4,0},{5,1},{6,2},{7,3},{0,4},{1,5},{2,6},{3,7},{12,8},{13,9},{14,... | collective-permute-start | bytes 921608 | tf_op jit(solution)/shard_map/ppermute | solution.py:433

commit v22 on v14

--- a/solution.py
+++ b/solution.py
@@ -296,7 +296,7 @@
     virtuals = dense.shape[0]
     begin, end = columns
     coupled = refs[0]
-    for first, tile in column_tiles(end - begin, 512):
+    for first, tile in column_tiles(end - begin, 1024):
         coupled[:, first:first + tile] = jnp.dot(
             amplitudes[...], dense[:, begin + first:begin + first + tile],
             preferred_element_type=jnp.float32,
@@ -309,7 +309,7 @@
             for by, offset, _ in spans
         ]
     copies = []
-    for t, (first, tile) in enumerate(column_tiles(virtuals, 512)):
+    for t, (first, tile) in enumerate(column_tiles(virtuals, 640)):
         here = slice(first, first + tile)
         total = jnp.dot(
             coupled[...], fock[begin:end, here], preferred_element_type=jnp.float32
@@ -347,7 +347,7 @@
         out_shape = [jax.ShapeDtypeStruct((out_rows, virtuals), amplitudes.dtype)]
         scratch += [
             pltpu.VMEM((height, virtuals), amplitudes.dtype),
-            pltpu.SemaphoreType.DMA((len(spans), len(column_tiles(virtuals, 512)))),
+            pltpu.SemaphoreType.DMA((len(spans), len(column_tiles(virtuals, 640)))),
         ]
     else:
         out_shape = [pltpu.VMEM((height, virtuals), jnp.float32)]

time: 45.3 us -> 45.5 us (level)
  Pallas kernels: 21.3 us -> 21.8 us
    pallas_call x4, Pallas kernels: 11.1 us -> 11.7 us  [dress(): pl.pallas_call(functools.partial(dress_kernel, job), out_shape=out_shape...]
  transfers between devices with their start and end apart: 7 -> 7, of which waited for: 5 -> 5; matrix products, arithmetic and copies ran while one was open for 0% -> 0% of each run, Pallas kernels for 36% -> 37%
where the time goes in v22:
time: 45.5 us; the launch traced here: 45.2 us
  Pallas kernels  21.8 us (48%)
  waiting for transfers between devices  12.4 us (27%)
  starting transfers between devices  10.3 us (23%)
  between operations  0.77 us (2%)
    pallas_call x4, Pallas kernels, dress(): pl.pallas_call(functools.partial(dress_kernel, job), out_shape=out_shape...  11.7 us
    ppermute x1, waiting for transfers between devices, local(): top = owned(lax.ppermute(top, axes, to_group), top, members, token)  6.37 us
    pallas_call x1, Pallas kernels, first_spread(): pl.pallas_call(functools.partial(first_spread_kernel, groups), out_shape=...  4 us
    ppermute x1, starting transfers between devices, local(): beside = lax.ppermute(own_again, axes, to_slot(1))  2.98 us
    pallas_call x3, Pallas kernels, spread(): pl.pallas_call(functools.partial(spread_kernel, slot), out_shape=pltpu.VM...  2.85 us
    ppermute x1, waiting for transfers between devices, local(): lax.ppermute(top, axes, to_member(by))  2.53 us
    pallas_call x1, Pallas kernels, fold_panel(): pl.pallas_call(functools.partial(fold_kernel, chunk, late), out_shape=out...  2.07 us
    ppermute x1, waiting for transfers between devices, local(): across = lax.ppermute(own, axes, to_slot(2))  1.65 us
  transfers between devices with their start and end apart: 7, of which 5 were waited for; matrix products, arithmetic and copies ran while one was open for 0% of the time, Pallas kernels for 37%

profile of v22, /device:TPU:4, one launch (start us, length us, event | category | flops | bytes accessed | tf_op | source)
XLA Modules:
  0.0 45.2 jit_solution(13603286448282550197)
XLA Ops:
  0.0 1.2 %cut_rows.1.kept = bf16[160,1920]{1,0:T(8,128)(2,1)S(1)} custom-call(bf16[240,1920]{1,0:T(8,128)(2,1)} %whole.1), custom_call_target="tpu_custom_call" | custom-call | tf_op jit(solution)/shard_map/cut_rows/pallas_call | solution.py:58
  1.2 1.3 %collective-permute-start = (bf16[160,1920]{1,0:T(8,128)(2,1)S(1)}, bf16[160,1920]{1,0:T(8,128)(2,1)S(1)}, u32[]{:S(2)}, u32[]{:S(2)}) collective-permute-start(bf16[160,1920]{1,0:T(8,128)(2,1)S(1)} %cut_rows.1.kept), channel_id=1, source_target_pairs={{8,1},{16,2},{26,3},{12,5},{20,6},{30,7},{0,8},{18,10},{24,11},{4,... | collective-permute-start | bytes 1843208 | tf_op jit(solution)/shard_map/ppermute | solution.py:412
  3.1 2.1 %fold_panel.1 = (bf16[480,512]{1,0:T(8,128)(2,1)S(1)}, bf16[480,512]{1,0:T(8,128)(2,1)S(1)}, bf16[80,1920]{1,0:T(8,128)(2,1)S(1)}) custom-call(s32[1]{0:T(128)S(6)} %copy.26.pair, s32[8]{0:T(128)} %sizes.1, bf16[480,1920]{1,0:T(8,128)(2,1)} %bitcast.4, bf16[240,1920]{1,0:T(8,128)(2,1)} %whole.1), custom_call_target="tpu_custom_call" | custom-call | tf_op jit(solution)/shard_map/fold_panel/pallas_call | solution.py:130
  5.2 1.6 %collective-permute-start.1 = (bf16[80,1920]{1,0:T(8,128)(2,1)S(1)}, bf16[80,1920]{1,0:T(8,128)(2,1)S(1)}, u32[]{:S(2)}, u32[]{:S(2)}) collective-permute-start(bf16[80,1920]{1,0:T(8,128)(2,1)S(1)} %get-tuple-element.16.refs_0_), channel_id=1, source_target_pairs={{4,0},{5,1},{6,2},{7,3},{0,4},{1,5},{2,6},{3,7},{12,8},{13,9},{14,... | collective-permute-start | bytes 921608 | tf_op jit(solution)/shard_map/ppermute | solution.py:409
  6.8 3.0 %collective-permute-start.5 = (bf16[480,512]{1,0:T(8,128)(2,1)S(1)}, bf16[480,512]{1,0:T(8,128)(2,1)S(1)}, u32[]{:S(2)}, u32[]{:S(2)}) collective-permute-start(bf16[480,512]{1,0:T(8,128)(2,1)S(1)} %get-tuple-element.19), channel_id=1, source_target_pairs={{1,0},{0,1},{3,2},{2,3},{5,4},{4,5},{7,6},{6,7},{9,8},{8,9},{11,10... | collective-permute-start | bytes 1474568 | tf_op jit(solution)/shard_map/ppermute | solution.py:406
  9.8 1.6 %collective-permute-start.4 = (bf16[480,512]{1,0:T(8,128)(2,1)S(1)}, bf16[480,512]{1,0:T(8,128)(2,1)S(1)}, u32[]{:S(2)}, u32[]{:S(2)}) collective-permute-start(bf16[480,512]{1,0:T(8,128)(2,1)S(1)} %get-tuple-element.17.folded), channel_id=1, source_target_pairs={{2,0},{3,1},{0,2},{1,3},{6,4},{7,5},{4,6},{5,7},{10,8},{11,9},{8,1... | collective-permute-start | bytes 1474568 | tf_op jit(solution)/shard_map/ppermute | solution.py:405
  11.3 4.0 %first_spread.1 = (bf16[1920,2048]{1,0:T(8,128)(2,1)S(1)}, bf16[2048,1920]{1,0:T(8,128)(2,1)S(1)}, s32[2,8,2048]{2,1,0:T(8,128)S(1)}, s32[8,128]{1,0:T(8,128)S(1)}) custom-call(s32[8]{0:T(128)} %sizes.1, s32[1]{0:T(128)S(6)} %copy.26.pair, bf16[480,512]{1,0:T(8,128)(2,1)S(1)} %get-tuple-element.17.folded, bf16[1920,1920]{1,0:T(8,128)(2,1)} %fock.1), custom_call_target="tpu_custom_call" | custom-call | tf_op jit(solution)/shard_map/first_spread/pallas_call | solution.py:201
  15.3 6.4 %collective-permute-done.received = bf16[160,1920]{1,0:T(8,128)(2,1)S(1)} collective-permute-done((bf16[160,1920]{1,0:T(8,128)(2,1)S(1)}, bf16[160,1920]{1,0:T(8,128)(2,1)S(1)}, u32[]{:S(2)}, u32[]{:S(2)}) %collective-permute-start) | collective-permute-done | bytes 614432 | tf_op jit(solution)/shard_map/ppermute | solution.py:412
  21.7 1.6 %collective-permute-start.3 = (bf16[160,1920]{1,0:T(8,128)(2,1)S(1)}, bf16[160,1920]{1,0:T(8,128)(2,1)S(1)}, u32[]{:S(2)}, u32[]{:S(2)}) collective-permute-start(bf16[160,1920]{1,0:T(8,128)(2,1)S(1)} %owned_rows.2.refs_1_.amplitudes), channel_id=1, source_target_pairs={{4,0},{5,1},{6,2},{7,3},{0,4},{1,5},{2,6},{3,7},{12,8},{13,9},{14,... | collective-permute-start | bytes 1843208 | tf_op jit(solution)/shard_map/ppermute | solution.py:416
  23.3 0.0 collective-permute-done.1.refs_0_
  23.3 1.3 %collective-permute-start.2 = (bf16[160,1920]{1,0:T(8,128)(2,1)S(1)}, bf16[160,1920]{1,0:T(8,128)(2,1)S(1)}, u32[]{:S(2)}, u32[]{:S(2)}) collective-permute-start(bf16[160,1920]{1,0:T(8,128)(2,1)S(1)} %pad_maximum_fusion.kept), channel_id=1, source_target_pairs={{8,1},{16,2},{26,3},{12,5},{20,6},{30,7},{0,8},{18,10},{24,11},{4,... | collective-permute-start | bytes 1843208 | tf_op jit(solution)/shard_map/ppermute | solution.py:415
  24.6 0.0 collective-permute-done.5.folded
  24.7 1.0 %spread_panel.3.dense.before = bf16[1920,2048]{1,0:T(8,128)(2,1)S(1)} custom-call(bf16[480,512]{1,0:T(8,128)(2,1)S(1)} %collective-permute-done.5.folded, s32[2,8,2048]{2,1,0:T(8,128)S(1)} %get-tuple-element.20.ranges, bf16[1920,2048]{1,0:T(8,128)(2,1)S(1)} %get-tuple-element.21.before), custom_call_target="tpu_custom_call", output_to_operand_aliasing={{}: (2, {})} | custom-call | tf_op jit(solution)/shard_map/spread_panel/pallas_call | solution.py:231
  25.6 1.6 %dress_rows.4 = (f32[160,1920]{1,0:T(8,128)S(1)}, s32[8,128]{1,0:T(8,128)S(1)}) custom-call(bf16[160,1920]{1,0:T(8,128)(2,1)S(1)} %owned_rows.2.refs_1_.amplitudes, bf16[1920,2048]{1,0:T(8,128)(2,1)S(1)} %spread_panel.3.dense.before, bf16[2048,1920]{1,0:T(8,128)(2,1)S(1)} %get-tuple-element.22.fock), custom_call_target="tpu_custom_call" | custom-call | tf_op jit(solution)/shard_map/dress_rows/pallas_call | solution.py:355
  27.3 1.6 %collective-permute-done.4.refs_0_ = bf16[480,512]{1,0:T(8,128)(2,1)S(1)} collective-permute-done((bf16[480,512]{1,0:T(8,128)(2,1)S(1)}, bf16[480,512]{1,0:T(8,128)(2,1)S(1)}, u32[]{:S(2)}, u32[]{:S(2)}) %collective-permute-start.4) | collective-permute-done | bytes 491552 | tf_op jit(solution)/shard_map/ppermute | solution.py:405
  28.9 0.0 collective-permute-start.6
  28.9 1.0 %spread_panel.4.before = bf16[1920,2048]{1,0:T(8,128)(2,1)S(1)} custom-call(bf16[480,512]{1,0:T(8,128)(2,1)S(1)} %after.5.folded, s32[2,8,2048]{2,1,0:T(8,128)S(1)} %get-tuple-element.20.ranges, bf16[1920,2048]{1,0:T(8,128)(2,1)S(1)} %spread_panel.3.dense.before), custom_call_target="tpu_custom_call", output_to_operand_aliasing={{}: (2, {})} | custom-call | tf_op jit(solution)/shard_map/spread_panel/pallas_call | solution.py:231
  29.9 0.9 %collective-permute-done.6.folded = bf16[480,512]{1,0:T(8,128)(2,1)S(1)} collective-permute-done((bf16[480,512]{1,0:T(8,128)(2,1)S(1)}, bf16[480,512]{1,0:T(8,128)(2,1)S(1)}, u32[]{:S(2)}, u32[]{:S(2)}) %collective-permute-start.6) | collective-permute-done | bytes 491552 | tf_op jit(solution)/shard_map/ppermute | solution.py:422
  30.8 0.9 %spread_panel.5.dense = bf16[1920,2048]{1,0:T(8,128)(2,1)S(1)} custom-call(bf16[480,512]{1,0:T(8,128)(2,1)S(1)} %collective-permute-done.6.folded, s32[2,8,2048]{2,1,0:T(8,128)S(1)} %get-tuple-element.20.ranges, bf16[1920,2048]{1,0:T(8,128)(2,1)S(1)} %spread_panel.4.before), custom_call_target="tpu_custom_call", output_to_operand_aliasing={{}: (2, {})} | custom-call | tf_op jit(solution)/shard_map/spread_panel/pallas_call | solution.py:231
  31.7 2.4 %dress_rows.5.refs_0_ = bf16[480,1920]{1,0:T(8,128)(2,1)} custom-call(bf16[160,1920]{1,0:T(8,128)(2,1)S(1)} %owned_rows.2.refs_1_.amplitudes, bf16[1920,2048]{1,0:T(8,128)(2,1)S(1)} %spread_panel.5.dense, bf16[2048,1920]{1,0:T(8,128)(2,1)S(1)} %get-tuple-element.22.fock, f32[160,1920]{1,0:T(8,128)S(1)} %get-tuple-element.24.refs_0_), custom_call_target="tpu_custom_call" | custom-call | tf_op jit(solution)/shard_map/dress_rows/pallas_call | solution.py:355
  34.1 2.5 %collective-permute-done.3.amplitudes = bf16[160,1920]{1,0:T(8,128)(2,1)S(1)} collective-permute-done((bf16[160,1920]{1,0:T(8,128)(2,1)S(1)}, bf16[160,1920]{1,0:T(8,128)(2,1)S(1)}, u32[]{:S(2)}, u32[]{:S(2)}) %collective-permute-start.3) | collective-permute-done | bytes 614432 | tf_op jit(solution)/shard_map/ppermute | solution.py:416
  36.7 3.8 %dress_rows.6 = (bf16[480,1920]{1,0:T(8,128)(2,1)}, s32[8,128]{1,0:T(8,128)S(1)}) custom-call(bf16[160,1920]{1,0:T(8,128)(2,1)S(1)} %collective-permute-done.3.amplitudes, bf16[1920,2048]{1,0:T(8,128)(2,1)S(1)} %spread_panel.5.dense, bf16[2048,1920]{1,0:T(8,128)(2,1)S(1)} %get-tuple-element.22.fock, ...), custom_call_target="tpu_custom_call", output_to_operand_aliasing={{0}: (3, {})} | custom-call | tf_op jit(solution)/shard_map/dress_rows/pallas_call | solution.py:355
  40.5 0.9 %collective-permute-done.2.received = bf16[160,1920]{1,0:T(8,128)(2,1)S(1)} collective-permute-done((bf16[160,1920]{1,0:T(8,128)(2,1)S(1)}, bf16[160,1920]{1,0:T(8,128)(2,1)S(1)}, u32[]{:S(2)}, u32[]{:S(2)}) %collective-permute-start.2) | collective-permute-done | bytes 614432 | tf_op jit(solution)/shard_map/ppermute | solution.py:415
  41.4 3.9 %dress_rows.7 = bf16[480,1920]{1,0:T(8,128)(2,1)} custom-call(bf16[160,1920]{1,0:T(8,128)(2,1)S(1)} %owned_rows.3.amplitudes, bf16[1920,2048]{1,0:T(8,128)(2,1)S(1)} %spread_panel.5.dense, bf16[2048,1920]{1,0:T(8,128)(2,1)S(1)} %get-tuple-element.22.fock, bf16[480,1920]{1,0:T(8,128)(2,1)} %get-tuple-element.26.refs_0_), custom_call_target="tpu_custom_call", output_to_operand_aliasing={{}: (3, {})} | custom-call | tf_op jit(solution)/shard_map/dress_rows/pallas_call | solution.py:355
  (6 shorter events, 0.1 us)
Async XLA Ops:
  1.2 20.5 %collective-permute-start = (bf16[160,1920]{1,0:T(8,128)(2,1)S(1)}, bf16[160,1920]{1,0:T(8,128)(2,1)S(1)}, u32[]{:S(2)}, u32[]{:S(2)}) collective-permute-start(bf16[160,1920]{1,0:T(8,128)(2,1)S(1)} %cut_rows.1.kept), channel_id=1, source_target_pairs={{8,1},{16,2},{26,3},{12,5},{20,6},{30,7},{0,8},{18,10},{24,11},{4,... | collective-permute-start | bytes 1843208 | tf_op jit(solution)/shard_map/ppermute | solution.py:412
  5.2 18.1 %collective-permute-start.1 = (bf16[80,1920]{1,0:T(8,128)(2,1)S(1)}, bf16[80,1920]{1,0:T(8,128)(2,1)S(1)}, u32[]{:S(2)}, u32[]{:S(2)}) collective-permute-start(bf16[80,1920]{1,0:T(8,128)(2,1)S(1)} %get-tuple-element.16.refs_0_), channel_id=1, source_target_pairs={{4,0},{5,1},{6,2},{7,3},{0,4},{1,5},{2,6},{3,7},{12,8},{13,9},{14,... | collective-permute-start | bytes 921608 | tf_op jit(solution)/shard_map/ppermute | solution.py:409
  6.8 17.9 %collective-permute-start.5 = (bf16[480,512]{1,0:T(8,128)(2,1)S(1)}, bf16[480,512]{1,0:T(8,128)(2,1)S(1)}, u32[]{:S(2)}, u32[]{:S(2)}) collective-permute-start(bf16[480,512]{1,0:T(8,128)(2,1)S(1)} %get-tuple-element.19), channel_id=1, source_target_pairs={{1,0},{0,1},{3,2},{2,3},{5,4},{4,5},{7,6},{6,7},{9,8},{8,9},{11,10... | collective-permute-start | bytes 1474568 | tf_op jit(solution)/shard_map/ppermute | solution.py:406
  9.8 19.2 %collective-permute-start.4 = (bf16[480,512]{1,0:T(8,128)(2,1)S(1)}, bf16[480,512]{1,0:T(8,128)(2,1)S(1)}, u32[]{:S(2)}, u32[]{:S(2)}) collective-permute-start(bf16[480,512]{1,0:T(8,128)(2,1)S(1)} %get-tuple-element.17.folded), channel_id=1, source_target_pairs={{2,0},{3,1},{0,2},{1,3},{6,4},{7,5},{4,6},{5,7},{10,8},{11,9},{8,1... | collective-permute-start | bytes 1474568 | tf_op jit(solution)/shard_map/ppermute | solution.py:405
  21.7 14.9 %collective-permute-start.3 = (bf16[160,1920]{1,0:T(8,128)(2,1)S(1)}, bf16[160,1920]{1,0:T(8,128)(2,1)S(1)}, u32[]{:S(2)}, u32[]{:S(2)}) collective-permute-start(bf16[160,1920]{1,0:T(8,128)(2,1)S(1)} %owned_rows.2.refs_1_.amplitudes), channel_id=1, source_target_pairs={{4,0},{5,1},{6,2},{7,3},{0,4},{1,5},{2,6},{3,7},{12,8},{13,9},{14,... | collective-permute-start | bytes 1843208 | tf_op jit(solution)/shard_map/ppermute | solution.py:416
  23.3 18.0 %collective-permute-start.2 = (bf16[160,1920]{1,0:T(8,128)(2,1)S(1)}, bf16[160,1920]{1,0:T(8,128)(2,1)S(1)}, u32[]{:S(2)}, u32[]{:S(2)}) collective-permute-start(bf16[160,1920]{1,0:T(8,128)(2,1)S(1)} %pad_maximum_fusion.kept), channel_id=1, source_target_pairs={{8,1},{16,2},{26,3},{12,5},{20,6},{30,7},{0,8},{18,10},{24,11},{4,... | collective-permute-start | bytes 1843208 | tf_op jit(solution)/shard_map/ppermute | solution.py:415
  28.9 1.9 %collective-permute-start.6 = (bf16[480,512]{1,0:T(8,128)(2,1)S(1)}, bf16[480,512]{1,0:T(8,128)(2,1)S(1)}, u32[]{:S(2)}, u32[]{:S(2)}) collective-permute-start(bf16[480,512]{1,0:T(8,128)(2,1)S(1)} %after.5.folded), channel_id=1, source_target_pairs={{1,0},{0,1},{3,2},{2,3},{5,4},{4,5},{7,6},{6,7},{9,8},{8,9},{11,10... | collective-permute-start | bytes 1474568 | tf_op jit(solution)/shard_map/ppermute | solution.py:422
